TPU v7x, 32 devices: a whole 2x2x4 slice. The times are simulated.
32 devices in a mesh: group: 1, req: 4 (over z), head: 4 (over y, x), pool: 2 (over core).
Axes of the slice: x: 2, y: 2, z: 4, core: 2. Of those that a mesh axis runs over, the one named last changes fastest.
Arguments:
- queries: bfloat16 [192, 4096], P(('group', 'req'), 'head'), may hold values from -128 to 128
- new_entries: bfloat16 [192, 2, 4, 256], P(('group', 'req'), None, 'head'), may hold values from -6 to 6
- cache_pages: bfloat16 [4, 416, 16, 256], P('head', ('group', 'req', 'pool')), may hold values from -6 to 6
- page_table: int32 [192, 2, 1], P(('group', 'req'), 'pool'), may hold values from 0 to 51, as said below
- cached_length: int32 [192, 2], P(('group', 'req'), 'pool'), may hold values from 1 to 16, as said below
- leave_slots: int32 [32], P(('group', 'req', 'pool')), may hold values from 0 to 50, as said below
- arrive_slots: int32 [32], P(('group', 'req', 'pool')), may hold values from 0 to 51, as said below
- residual: bfloat16 [192, 2048], P(('group', 'req', 'head')), may hold values from -5 to 5
- norm_gain: float32 [2048], replicated, may hold values from 0.5 to 1.5
- output_weight: bfloat16 [4096, 2048], P(('head', 'pool')), may hold values from -0.25 to 0.25
- expert_choice: int32 [192, 8], P(('group', 'req', 'head')), may hold values from 0 to 15, all different within a row; in each aligned block of 12 rows (0 to 11, 12 to 23, ...) at most 12 rows name the same one
- route_weight: float32 [192, 8], P(('group', 'req', 'head')), may hold values from 0.2 to 1
- gate_up: bfloat16 [16, 2, 384, 2048], P(('req', 'head'), None, 'pool'), may hold values from -0.125 to 0.125
- down_weight: bfloat16 [16, 384, 2048], P(('req', 'head'), 'pool'), may hold values from -0.3125 to 0.3125
Outputs:
- decoded: bfloat16 [192, 2048], P(('group', 'req', 'head'), 'pool')
Inputs may be any that keep to these rules, and one draw needn't show every extreme that they name: `page_table`: within each block of one index of req and one pool, the 48 entries name distinct slots, none of them among that block's leave_slots. `leave_slots`: each block's 4 entries are distinct. `arrive_slots`: each block's 4 entries are distinct slots that its page table names. `cached_length`: in every block of 48 requests and each pool some request has 16. `expert_choice`: each row names 8 distinct experts; in each aligned block of 12 rows no expert is named more than 12 times, a bound that some block reaches.
All inputs are finite; a program needn't handle non-finite values.
Results may differ from a plain program's by a relative error of at most 0.023.
Values may be sent and summed in bfloat16 or wider, within the bound.
No kernel may reach another device: no remote copies, remote signals or barrier semaphores. Data moves between devices by JAX's collectives and lax.ppermute only.
A program may use at most 64 MiB of HBM per device.

v0:
```python
import jax
import jax.numpy as jnp
from jax import lax
from jax.sharding import PartitionSpec as P


def swapped(value, axis, apart):
    mask = 2**apart
    pairs = [(source, source ^ mask) for source in range(lax.axis_size(axis))]
    return lax.ppermute(value, axis, pairs)


def combined_all(shard, axis, join):
    gathered = jax.tree.map(
        lambda a, kind: lax.all_gather(a.astype(kind), axis),
        shard,
        (jnp.bfloat16, jnp.bfloat16, jnp.bfloat16),
    )

    def take(source):
        return jax.tree.map(
            lambda a, own: lax.dynamic_index_in_dim(a, source, 0, False).astype(own.dtype),
            gathered,
            shard,
        )

    return lax.fori_loop(
        1, lax.axis_size(axis), lambda source, state: join(state, take(source)), take(0)
    )


def merge_parts(earlier, later):
    first_max, first_denominator, first_value = earlier
    second_max, second_denominator, second_value = later
    largest = jnp.maximum(first_max, second_max)
    first_scale = jnp.exp(first_max - largest)
    second_scale = jnp.exp(second_max - largest)
    denominator = first_denominator * first_scale + second_denominator * second_scale
    weighted = first_value * first_scale[..., None] + second_value * second_scale[..., None]
    return (largest, denominator, weighted)


def local(
    queries,
    new_entries,
    cache_pages,
    page_table,
    cached_length,
    leave_slots,
    arrive_slots,
    residual,
    norm_gain,
    output_weight,
    expert_choice,
    route_weight,
    gate_up,
    down_weight,
):
    batch_size = queries.shape[0]
    group_count = cache_pages.shape[0]
    head_dim = new_entries.shape[3] // 2
    group_size = queries.shape[1] // (group_count * head_dim)
    pool_index = lax.axis_index("pool")
    outgoing = cache_pages[:, leave_slots]
    arrived = swapped(outgoing, "pool", 0)
    current = cache_pages.at[:, arrive_slots].set(arrived)
    context = current[:, page_table[:, 0, :]]
    context = context.reshape(group_count, batch_size, -1, 2 * head_dim)
    context_keys = context[..., :head_dim]
    context_values = context[..., head_dim:]
    grouped_queries = queries.reshape(batch_size, group_count, group_size, head_dim)
    score_scale = head_dim ** (-0.5)
    attention_scores = (
        jnp.einsum(
            "bgqd,gbtd->bgqt", grouped_queries, context_keys, preferred_element_type=jnp.float32
        )
        * score_scale
    )
    positions = jnp.arange(context.shape[2], dtype=jnp.int32)
    valid_mask = positions[None, :] < cached_length
    attention_scores = jnp.where(valid_mask[:, None, None, :], attention_scores, -jnp.inf)
    fresh_scores = (
        jnp.einsum(
            "bgqd,bsgd->bgqs",
            grouped_queries,
            new_entries[..., :head_dim],
            preferred_element_type=jnp.float32,
        )
        * score_scale
    )
    fresh_scores = jnp.where(pool_index == 0, fresh_scores, -jnp.inf)
    largest = jnp.maximum(jnp.max(attention_scores, axis=-1), jnp.max(fresh_scores, axis=-1))
    local_weights = jnp.exp(attention_scores - largest[..., None])
    fresh_weights = jnp.exp(fresh_scores - largest[..., None])
    denominator = jnp.sum(local_weights, axis=-1) + jnp.sum(fresh_weights, axis=-1)
    weighted = jnp.einsum("bgqt,gbtd->bgqd", local_weights, context_values.astype(jnp.float32))
    weighted = weighted + jnp.einsum(
        "bgqs,bsgd->bgqd", fresh_weights, new_entries[..., head_dim:].astype(jnp.float32)
    )
    largest, denominator, weighted = combined_all(
        (largest, denominator, weighted), "pool", merge_parts
    )
    attended = (weighted / denominator[..., None]).reshape(batch_size, -1).astype(jnp.bfloat16)
    head_width = output_weight.shape[0]
    own_heads = lax.dynamic_slice_in_dim(attended, pool_index * head_width, head_width, 1)
    partial_value = jnp.dot(own_heads, output_weight, preferred_element_type=jnp.float32)
    rows_here = residual.shape[0]
    summed = lax.psum(partial_value.astype(jnp.bfloat16), ("head", "pool")).astype(jnp.float32)
    attention = lax.dynamic_slice_in_dim(summed, lax.axis_index("head") * rows_here, rows_here, 0)
    hidden = residual.astype(jnp.float32) + attention
    normed = (
        hidden * lax.rsqrt(jnp.mean(hidden * hidden, axis=-1, keepdims=True) + 1e-06) * norm_gain
    ).astype(jnp.bfloat16)
    expert_count = lax.axis_size("req") * lax.axis_size("head")
    top_count = expert_choice.shape[1]
    capacity = max(
        2, min(rows_here, (2 * rows_here * top_count + expert_count - 1) // expert_count)
    )
    flat_choice = expert_choice.reshape(-1)
    expert_hits = (
        flat_choice[:, None] == jnp.arange(expert_count, dtype=jnp.int32)[None, :]
    ).astype(jnp.int32)
    earlier = jnp.cumsum(expert_hits, axis=0) - expert_hits
    slot_index = jnp.sum(earlier * expert_hits, axis=1)
    target = flat_choice * capacity + slot_index
    placed = (
        target[:, None] == jnp.arange(expert_count * capacity, dtype=jnp.int32)[None, :]
    ).astype(jnp.float32)
    placed = placed.reshape(rows_here, top_count, expert_count * capacity)
    dispatch = jnp.sum(placed, axis=1).astype(jnp.bfloat16)
    combine_matrix = jnp.sum(placed * route_weight[:, :, None], axis=1)
    outgoing_rows = jnp.einsum("re,rd->ed", dispatch, normed, preferred_element_type=jnp.float32)
    outgoing_rows = outgoing_rows.astype(jnp.bfloat16).reshape(expert_count, capacity, -1)
    model_width = normed.shape[1]
    half_width = model_width // lax.axis_size("pool")
    projection = gate_up[0].reshape(-1, model_width)
    hidden_size = projection.shape[0] // 2
    received = lax.all_to_all(
        outgoing_rows, ("req", "head"), split_axis=0, concat_axis=0, tiled=True
    )
    sources = received.shape[0]
    item_count = received.shape[1]
    flat_rows = received.reshape(sources * item_count, model_width)
    projected = jnp.einsum("nd,fd->nf", flat_rows, projection, preferred_element_type=jnp.float32)
    activated = (jax.nn.silu(projected[:, :hidden_size]) * projected[:, hidden_size:]).astype(
        jnp.bfloat16
    )
    part_sum = jnp.dot(activated, down_weight[0], preferred_element_type=jnp.float32).reshape(
        sources, item_count, model_width
    )
    column_sum = lax.psum_scatter(
        part_sum.astype(jnp.bfloat16), "pool", scatter_dimension=2, tiled=True
    )
    returned = lax.all_to_all(column_sum, ("req", "head"), split_axis=0, concat_axis=0, tiled=True)
    gathered = returned.reshape(expert_count * capacity, half_width).astype(jnp.float32)
    expert_mix = jnp.dot(combine_matrix, gathered, precision=lax.Precision.HIGHEST)
    own_columns = lax.dynamic_slice_in_dim(hidden, pool_index * half_width, half_width, 1)
    return (own_columns + expert_mix).astype(jnp.bfloat16)


def solution(mesh):
    return jax.shard_map(
        local,
        mesh=mesh,
        in_specs=(
            P(("group", "req"), "head"),
            P(("group", "req"), None, "head", None),
            P("head", ("group", "req", "pool"), None, None),
            P(("group", "req"), "pool", None),
            P(("group", "req"), "pool"),
            P(("group", "req", "pool")),
            P(("group", "req", "pool")),
            P(("group", "req", "head"), None),
            P(),
            P(("head", "pool"), None),
            P(("group", "req", "head"), None),
            P(("group", "req", "head"), None),
            P(("req", "head"), None, "pool", None),
            P(("req", "head"), "pool", None),
        ),
        out_specs=P(("group", "req", "head"), "pool"),
        check_vma=False,
    )
```

profile of v0, /device:TPU:0, one launch (start us, length us, event | category | flops | bytes accessed | tf_op | source)
XLA Modules:
  0.0 159.3 jit_solution(2999815218880634779)
XLA Ops:
  6.5 1.2 copy.73
  7.7 0.7 compare_select_fusion.1
  9.5 0.7 fusion.23
  10.8 0.7 iota_compare_fusion.2
  11.5 0.8 copy.59
  12.9 0.9 copy.64
  13.8 1.0 fusion.25
  16.8 1.8 %all-gather.3 = bf16[2,48,8]{1,2,0:T(8,128)(2,1)S(1)} all-gather(bf16[1,48,8]{1,2,0:T(8,128)(2,1)S(1)} %copy.54), channel_id=3, replica_groups=mesh['group'=1,'req'=4,'head'=4,'pool'=2] {'pool'}, dimensions={0}, use_global_device_ids=true | all-gather | bytes 2304 | tf_op jit(solution)/shard_map/all_gather | solution.py:15
  18.9 1.8 %all-gather.4 = bf16[2,48,8]{1,2,0:T(8,128)(2,1)S(1)} all-gather(bf16[1,48,8]{1,2,0:T(8,128)(2,1)S(1)} %copy.57), channel_id=4, replica_groups=mesh['group'=1,'req'=4,'head'=4,'pool'=2] {'pool'}, dimensions={0}, use_global_device_ids=true | all-gather | bytes 2304 | tf_op jit(solution)/shard_map/all_gather | solution.py:15
  21.2 1.9 %all-gather = bf16[96,8,128]{2,1,0:T(8,128)(2,1)S(1)} all-gather(bf16[48,8,128]{2,1,0:T(8,128)(2,1)S(1)} %fusion.2), channel_id=2, replica_groups=mesh['group'=1,'req'=4,'head'=4,'pool'=2] {'pool'}, dimensions={0}, use_global_device_ids=true | all-gather | bytes 294912 | tf_op jit(solution)/shard_map/all_gather | solution.py:15
  23.4 1.2 convolution_convert_fusion.2
  24.8 55.8 %all-reduce.2.cloned.1.call-done = bf16[48,2048]{1,0:T(8,128)(2,1)} async-done(((bf16[48,2048]{1,0:T(8,128)(2,1)}), bf16[48,2048]{1,0:T(8,128)(2,1)}) %all-reduce.2.cloned.1.call-update) | async-done | bytes 196624 | tf_op jit(solution)/shard_map/psum | solution.py:108
  80.6 1.0 multiply_reduce_fusion
  81.6 1.3 convolution_convert_fusion.1
  82.9 1.3 reshape.273
  84.2 30.5 %all_to_all.10 = bf16[16,12,2048]{2,1,0:T(8,128)(2,1)} all-to-all(bf16[16,12,2048]{2,1,0:T(8,128)(2,1)S(1)} %reshape.273), channel_id=1, replica_groups=mesh['group'=1,'req'=4,'head'=4,'pool'=2] {'req','head'}, dimensions={0} | all-to-all | bytes 1572864 | tf_op jit(solution)/shard_map/all_to_all | solution.py:138
  114.6 1.3 reshape.274
  116.0 2.1 %fusion.26 = f32[192,384]{1,0:T(8,128)S(1)} fusion(bf16[192,2048]{1,0:T(8,128)(2,1)S(1)} %reshape.274, bf16[384,2048]{1,0:T(8,128)(2,1)} %bitcast.85), kind=kOutput, calls=%fused_computation.71 | convolution fusion | flops 301989888 | bytes 2654208 | tf_op jit(solution)/shard_map/nd,fd->nf/dot_general | solution.py:144
  118.2 2.4 %convolution_convert_fusion = bf16[16,12,2048]{2,0,1:T(8,128)(2,1)} fusion(bf16[1,192,2048]{2,1,0:T(8,128)(2,1)} %param.27, bf16[16,12,192]{2,1,0:T(8,128)(2,1)S(1)} %dot_general.36), kind=kOutput, calls=%fused_computation.3 | convolution fusion | flops 151388160 | bytes 1646592 | tf_op jit(solution)/shard_map/dot_general | solution.py:148
  120.6 6.6 %reduce-scatter.2.cloned.1.call-done = bf16[16,12,1024]{2,0,1:T(8,128)(2,1)} async-done(((bf16[16,12,2048]{2,0,1:T(8,128)(2,1)}), bf16[16,12,1024]{2,0,1:T(8,128)(2,1)}) %reduce-scatter.2.cloned.1.call-update) | async-done | bytes 393232 | tf_op jit(solution)/shard_map/reduce_scatter | solution.py:151
  127.3 2.0 %copy.63 = bf16[16,12,1024]{2,1,0:T(8,128)(2,1)} copy(bf16[16,12,1024]{2,0,1:T(8,128)(2,1)} %reduce-scatter.2.cloned.1.call-done) | data formatting | bytes 786432 | tf_op jit(solution)/shard_map/reduce_scatter | solution.py:151
  129.3 6.8 %all-to-all-start.1 = ((bf16[16,12,1024]{2,1,0:T(8,128)(2,1)}), bf16[16,12,1024]{2,1,0:T(8,128)(2,1)S(1)}, u32[]{:S(2)}, u32[]{:S(2)}) async-start(bf16[16,12,1024]{2,1,0:T(8,128)(2,1)} %copy.63), calls=%async_computation.2 | async-start | bytes 1048576 | tf_op jit(solution)/shard_map/all_to_all | solution.py:154
  136.0 15.5 %all-to-all-done.1 = bf16[16,12,1024]{2,1,0:T(8,128)(2,1)S(1)} async-done(((bf16[16,12,1024]{2,1,0:T(8,128)(2,1)}), bf16[16,12,1024]{2,1,0:T(8,128)(2,1)S(1)}, u32[]{:S(2)}, u32[]{:S(2)}) %all-to-all-start.1) | async-done | bytes 393248 | tf_op jit(solution)/shard_map/all_to_all | solution.py:154
  151.6 0.9 fusion.4
  (49 shorter events, 5.8 us)
Async XLA Ops:
  6.5 16.9 %copy-start = (bf16[512,2048]{1,0:T(8,128)(2,1)S(1)}, bf16[512,2048]{1,0:T(8,128)(2,1)}, u32[]{:S(2)}) copy-start(bf16[512,2048]{1,0:T(8,128)(2,1)} %param.23) | copy-start | bytes 6291460
  6.5 10.0 %copy-start.2 = (bf16[48,2,1,256]{3,1,2,0:T(2,128)(2,1)S(1)}, bf16[48,2,1,256]{3,1,2,0:T(2,128)(2,1)}, u32[]{:S(2)}) copy-start(bf16[48,2,1,256]{3,1,2,0:T(2,128)(2,1)} %param.15) | copy-start | bytes 147460
  6.5 8.2 %copy-start.4 = (f32[12,8]{0,1:T(8,128)S(1)}, f32[12,8]{0,1:T(8,128)}, u32[]{:S(2)}) copy-start(f32[12,8]{0,1:T(8,128)} %param.25) | copy-start | bytes 1156
  6.5 74.0 %all-reduce.2.cloned.1.call-start = ((), (), s32[]{:S(2)}) async-start(), calls=%async_computation.3 | async-start | bytes 393216 | tf_op jit(solution)/shard_map/psum | solution.py:108
  8.9 5.9 %collective-permute-start = (bf16[1,4,16,256]{3,2,1,0:T(8,128)(2,1)S(1)}, bf16[1,4,16,256]{3,2,1,0:T(8,128)(2,1)S(1)}, u32[]{:S(2)}, u32[]{:S(2)}) collective-permute-start(bf16[1,4,16,256]{3,2,1,0:T(8,128)(2,1)S(1)} %bitcast.94), channel_id=1, source_target_pairs={{0,1},{1,0},{2,3},{3,2},{4,5},{5,4},{6,7},{7,6},{8,9},{9,8},{10,11... | collective-permute-start | bytes 98312 | tf_op jit(solution)/shard_map/ppermute | solution.py:10
  23.2 57.4 %copy-start.1 = (bf16[12,2048]{1,0:T(8,128)(2,1)S(1)}, bf16[12,2048]{1,0:T(8,128)(2,1)}, u32[]{:S(2)}) copy-start(bf16[12,2048]{1,0:T(8,128)(2,1)} %param.21) | copy-start | bytes 147460
  23.4 58.2 %copy-start.3 = (f32[2048]{0:T(1024)S(1)}, f32[2048]{0:T(1024)}, u32[]{:S(2)}) copy-start(f32[2048]{0:T(1024)} %param.22) | copy-start | bytes 24580
  24.6 102.6 %reduce-scatter.2.cloned.1.call-start = ((), (), s32[]{:S(2)}) async-start(), calls=%async_computation.4 | async-start | bytes 1179648 | tf_op jit(solution)/shard_map/reduce_scatter | solution.py:151
  129.3 22.2 %all-to-all-start.1 = ((bf16[16,12,1024]{2,1,0:T(8,128)(2,1)}), bf16[16,12,1024]{2,1,0:T(8,128)(2,1)S(1)}, u32[]{:S(2)}, u32[]{:S(2)}) async-start(bf16[16,12,1024]{2,1,0:T(8,128)(2,1)} %copy.63), calls=%async_computation.2 | async-start | bytes 1048576 | tf_op jit(solution)/shard_map/all_to_all | solution.py:154
Sparse Core Ops, SparseCore 0:
  24.8 55.7 all-reduce.1
  120.7 6.4 reduce-scatter.1
where the time goes:
time: 160 us; the launch traced here: 159 us
  waiting for transfers between devices  77.9 us (49%)
  blocking collectives  36 us (22%)
  between operations  13.6 us (8%)
  local copies, waits for them, and re-layouts  10 us (6%)
  matrix products  9.56 us (6%)
  starting transfers between devices  7.32 us (5%)
  other arithmetic  4.95 us (3%)
    psum x1, waiting for transfers between devices, local(): lax.psum(partial_value.astype(jnp.bfloat16), ('head', 'pool'))  55.8 us
    all_to_all x1, blocking collectives, local(): lax.all_to_all(outgoing_rows, ('req', 'head'), split_axis=0, concat_axis=...  30.5 us
    all_to_all x1, waiting for transfers between devices, local(): lax.all_to_all(column_sum, ('req', 'head'), split_axis=0, concat_axis=0,...  15.5 us
    all_to_all x1, starting transfers between devices, local(): lax.all_to_all(column_sum, ('req', 'head'), split_axis=0, concat_axis=0,...  6.76 us
    reduce_scatter x1, waiting for transfers between devices, local(): lax.psum_scatter(part_sum.astype(jnp.bfloat16), 'pool', scatter_dimension...  6.63 us
    all_gather x3, blocking collectives, combined_all(): lax.all_gather(a.astype(kind), axis)  5.51 us
  transfers between devices with their start and end apart: 4, of which 3 were waited for; matrix products, arithmetic and copies ran while one was open for 3% of the time, Pallas kernels for 0%

commit v1 on v0

v1 whole, which is shorter than its diff:
```python
import functools

import jax
import jax.numpy as jnp
import numpy as np
from jax import lax
from jax.experimental import pallas as pl
from jax.experimental.pallas import tpu as pltpu
from jax.sharding import PartitionSpec as P

F32 = jnp.float32
BF16 = jnp.bfloat16
VMEM_LIMIT = 56 * 2**20
LANES = 128


def send(value, axes, step):
    size = lax.axis_size(axes)
    return lax.ppermute(value, axes, [(i, i ^ step) for i in range(size)])


def dot(a, b, contract=((1,), (0,))):
    return lax.dot_general(a, b, (contract, ((), ())), preferred_element_type=F32)


def kernel_call(body, out_shape, args, scratch=()):
    return pl.pallas_call(
        body,
        out_shape=out_shape,
        in_specs=[pl.BlockSpec(memory_space=pltpu.VMEM)] * len(args),
        out_specs=jax.tree.map(lambda _: pl.BlockSpec(memory_space=pltpu.VMEM), out_shape),
        scratch_shapes=list(scratch),
        compiler_params=pltpu.CompilerParams(vmem_limit_bytes=VMEM_LIMIT),
    )(*args)


def column(row, start, count):
    lane = lax.broadcasted_iota(jnp.int32, (count, row.shape[1]), 1)
    line = lax.broadcasted_iota(jnp.int32, (count, row.shape[1]), 0)
    return jnp.sum(jnp.where(lane == line + start, row, 0.0), axis=1, keepdims=True)


def attend_kernel(sizes, q_ref, new_ref, own_ref, other_ref, own_ints_ref, other_ints_ref, residual_ref, weight_ref, *rest):
    requests, pages, moved, page, heads, pools, head_dim = sizes
    outs, partial_ref = rest[:-1], rest[-1]
    slots = own_ref.shape[0] // page
    here = lax.axis_index("pool")
    me = lax.axis_index("head") * pools + here
    group = q_ref.shape[1] // head_dim // pools
    rows = requests // pools
    columns = weight_ref.shape[1] // heads

    ints = [own_ints_ref[...].astype(F32), other_ints_ref[...].astype(F32)]
    live_from, live_count = [], []
    for q in range(2):
        row, across = ints[q], ints[1 - q]
        base = pages * requests
        length = column(row, base, requests)
        for j in range(pages):
            slot = column(row, j * requests, requests)
            source = slot + float(q * slots)
            for k in range(moved):
                leave = column(across, base + requests + k, 1)
                arrive = column(row, base + requests + moved + k, 1)
                source = jnp.where(slot == arrive, leave + float((1 - q) * slots), source)
            live_from.append((source * float(page)).astype(jnp.int32))
            live_count.append(jnp.clip(length - float(j * page), 0.0, float(page)).astype(jnp.int32))

    def cache_mask(offset, count):
        entry = lax.broadcasted_iota(jnp.int32, (requests, count), 1) + offset
        mask = None
        for start, amount in zip(live_from, live_count):
            apart = entry - start
            one = (apart >= 0) & (apart < amount)
            mask = one if mask is None else mask | one
        return mask

    count = own_ref.shape[0]
    fresh = new_ref.shape[0] // requests
    entry = lax.broadcasted_iota(jnp.int32, (requests, new_ref.shape[0]), 1)
    first = lax.broadcasted_iota(jnp.int32, (requests, new_ref.shape[0]), 0) * fresh
    masks = [cache_mask(0, count), cache_mask(count, count), (entry >= first) & (entry < first + fresh)]
    queries = jnp.concatenate(
        [
            q_ref[:, pl.ds(pl.multiple_of((here * group + g) * head_dim, LANES), head_dim)]
            for g in range(group)
        ],
        axis=0,
    )
    scale = head_dim ** (-0.5)
    scores = []
    for ref, mask in zip((own_ref, other_ref, new_ref), masks):
        score = dot(queries, ref[:, :head_dim], ((1,), (1,))) * scale
        bias = jnp.where(mask, 0.0, -jnp.inf)
        scores.append(score + jnp.concatenate([bias] * group, axis=0))
    largest = functools.reduce(
        jnp.maximum, [jnp.max(score, axis=1, keepdims=True) for score in scores]
    )
    total, value = 0.0, 0.0
    for ref, score in zip((own_ref, other_ref, new_ref), scores):
        weights = jnp.exp(score - largest)
        total = total + jnp.sum(weights, axis=1, keepdims=True)
        value = value + dot(weights.astype(BF16), ref[:, head_dim:])
    value = (value / total).astype(BF16)
    attended = jnp.concatenate(
        [value[g * requests : (g + 1) * requests] for g in range(group)], axis=1
    )
    partial_ref[...] = dot(attended, weight_ref[...]) + residual_ref[...].astype(F32)
    for step, out in enumerate(outs):
        to = me ^ step
        to_head, to_pool = to // pools, to % pools
        out[...] = partial_ref[
            pl.ds(pl.multiple_of(to_pool * rows, 8), rows),
            pl.ds(pl.multiple_of(to_head * columns, LANES), columns),
        ].astype(BF16)


def expert_kernel(sizes, *refs):
    heads, pools, rows_here = sizes
    blocks, refs = refs[:heads], refs[heads:]
    gates, ups, downs, refs = refs[:pools], refs[pools : 2 * pools], refs[2 * pools : 3 * pools], refs[3 * pools :]
    gain_ref, order_ref, route_ref = refs[:3]
    outs, sum_ref = refs[3:-1], refs[-1]
    head, pool = lax.axis_index("head"), lax.axis_index("pool")
    planes, plane_rows, columns = blocks[0].shape
    width = heads * columns
    squares = 0.0
    gate = [0.0] * pools
    up = [0.0] * pools
    for step in range(heads):
        start = pl.multiple_of((head ^ step) * columns, LANES)
        block = blocks[step][...].astype(F32).reshape(planes * plane_rows, columns)
        squares = squares + jnp.sum(block * block, axis=1, keepdims=True)
        block = (block * gain_ref[:, pl.ds(start, columns)]).astype(BF16)
        for half in range(pools):
            gate[half] = gate[half] + dot(block, gates[half][:, pl.ds(start, columns)], ((1,), (1,)))
            up[half] = up[half] + dot(block, ups[half][:, pl.ds(start, columns)], ((1,), (1,)))
    scale = lax.rsqrt(squares / width + 1e-06)
    result = 0.0
    for half in range(pools):
        g, u = gate[half] * scale, up[half] * scale
        activated = (g / (1.0 + jnp.exp(-g)) * u).astype(BF16)
        activated = (dot(order_ref[...], activated) * route_ref[...]).astype(BF16)
        result = result + dot(activated, downs[half][...])
    sum_ref[...] = result
    hidden = blocks[0][0].astype(F32)
    own = pl.ds(pl.multiple_of(head * columns, LANES), columns)
    parts = plane_rows // rows_here
    for a in range(parts):
        at = slice(a * planes * rows_here, a * planes * rows_here + rows_here)
        sum_ref[at, own] = sum_ref[at, own] + hidden[a * rows_here : (a + 1) * rows_here]
    rows, half = planes * rows_here, width // pools
    for step, out in enumerate(outs):
        to = head ^ step
        a, b = to // pools, to % pools
        out[...] = sum_ref[
            pl.ds(pl.multiple_of(a * rows, 8), rows), pl.ds(pl.multiple_of(b * half, LANES), half)
        ].astype(BF16)


def local(
    queries,
    new_entries,
    cache_pages,
    page_table,
    cached_length,
    leave_slots,
    arrive_slots,
    residual,
    norm_gain,
    output_weight,
    expert_choice,
    route_weight,
    gate_up,
    down_weight,
):
    pools, heads, planes = lax.axis_size("pool"), lax.axis_size("head"), lax.axis_size("req")
    experts = heads * planes
    requests = queries.shape[0]
    slots, page, entry = cache_pages.shape[1:]
    head_dim = entry // 2
    moved = leave_slots.shape[0]
    pages = page_table.shape[2]
    rows_here, width = residual.shape
    head, pool, plane = lax.axis_index("head"), lax.axis_index("pool"), lax.axis_index("req")
    both = ("head", "pool")

    own_cache = cache_pages.reshape(slots * page, entry)
    other_cache = send(own_cache, "pool", 1)
    ints = jnp.concatenate(
        [page_table[:, 0, j] for j in range(pages)]
        + [cached_length.reshape(-1), leave_slots, arrive_slots]
    )
    ints = jnp.pad(ints, (0, -ints.shape[0] % LANES)).reshape(1, -1)
    other_ints = send(ints, "pool", 1)

    choice = expert_choice[:, :, None] == jnp.arange(experts, dtype=jnp.int32)[None, None, :]
    mix = jnp.sum(jnp.where(choice, route_weight[:, :, None], 0.0), axis=1)
    mix = jnp.stack([mix] + [send(mix, "req", step) for step in range(1, planes)])
    mix = jnp.stack([mix] + [send(mix, "head", step) for step in range(1, heads)])
    mix = lax.dynamic_index_in_dim(mix, plane * heads + head, 3, False)
    parts = heads // pools
    route = jnp.stack(
        [
            lax.dynamic_index_in_dim(mix, (pool * parts + a) ^ head, 0, False)
            for a in range(parts)
        ]
    ).reshape(-1, 1)

    added = lax.dynamic_update_slice_in_dim(
        jnp.zeros((requests, width), BF16),
        jnp.where(pool == 0, residual, jnp.zeros_like(residual)),
        head * rows_here,
        0,
    )
    sizes = (requests, pages, moved, page, heads, pools, head_dim)
    args = (
        queries,
        new_entries.reshape(-1, entry),
        own_cache,
        other_cache,
        ints,
        other_ints,
        added,
        output_weight,
    )
    piece = jax.ShapeDtypeStruct((requests // pools, width // heads), BF16)
    pieces = kernel_call(
        functools.partial(attend_kernel, sizes),
        [piece] * (heads * pools),
        args,
        [pltpu.VMEM((requests, width), F32)],
    )
    arrived = [pieces[0]] + [send(pieces[step], both, step) for step in range(1, heads * pools)]
    hidden = sum(value.astype(F32) for value in arrived).astype(BF16)

    held = lax.optimization_barrier((gate_up, down_weight, other_cache))
    other_gate_up, other_down = send(held[0], "pool", 1), send(held[1], "pool", 1)

    block = jnp.stack([hidden] + [send(hidden, "req", step) for step in range(1, planes)])
    blocks = [block] + [send(block, "head", step) for step in range(1, heads)]

    order = np.zeros((planes * parts * rows_here,) * 2, np.float32)
    for a in range(parts):
        for r in range(planes):
            for i in range(rows_here):
                order[(a * planes + r) * rows_here + i, (r * parts + a) * rows_here + i] = 1.0
    piece = jax.ShapeDtypeStruct((planes * rows_here, width // pools), BF16)
    args = (
        *blocks,
        gate_up[0, 0],
        other_gate_up[0, 0],
        gate_up[0, 1],
        other_gate_up[0, 1],
        down_weight[0],
        other_down[0],
        norm_gain.reshape(1, -1),
        jnp.asarray(order, BF16),
        route,
    )
    pieces = kernel_call(
        functools.partial(expert_kernel, (heads, pools, rows_here)),
        [piece] * heads,
        args,
        [pltpu.VMEM((planes * parts * rows_here, width), F32)],
    )
    returned = []
    for step in range(heads):
        pairs = []
        for h in range(heads):
            for p in range(pools):
                to = h ^ step
                pairs.append((h * pools + p, (p * parts + to // pools) * pools + to % pools))
        returned.append(lax.ppermute(pieces[step], both, pairs))
    mixed = sum(value.astype(F32) for value in returned).astype(BF16)
    mixed = mixed.reshape(planes, rows_here, -1)
    total = mixed[0].astype(F32)
    for step in range(1, planes):
        total = total + send(mixed[step], "req", step).astype(F32)
    return total.astype(BF16)


def solution(mesh):
    return jax.shard_map(
        local,
        mesh=mesh,
        in_specs=(
            P(("group", "req"), "head"),
            P(("group", "req"), None, "head", None),
            P("head", ("group", "req", "pool"), None, None),
            P(("group", "req"), "pool", None),
            P(("group", "req"), "pool"),
            P(("group", "req", "pool")),
            P(("group", "req", "pool")),
            P(("group", "req", "head"), None),
            P(),
            P(("head", "pool"), None),
            P(("group", "req", "head"), None),
            P(("group", "req", "head"), None),
            P(("req", "head"), None, "pool", None),
            P(("req", "head"), "pool", None),
        ),
        out_specs=P(("group", "req", "head"), "pool"),
        check_vma=False,
    )
```

time: 160 us -> 78.2 us (0.49)
  waiting for transfers between devices: 77.9 us -> 20.6 us
  blocking collectives: 36 us -> 0 us
  starting transfers between devices: 7.32 us -> 36.4 us
  between operations: 13.6 us -> 0.25 us
  matrix products: 9.56 us -> 0 us
  Pallas kernels: 0 us -> 9.11 us
  other arithmetic: 4.95 us -> 2.49 us
    psum x1 -> x0, waiting for transfers between devices: 55.8 us -> none  [local(): lax.psum(partial_value.astype(jnp.bfloat16), ('head', 'pool'))]
    ppermute x1 -> x30, starting transfers between devices: 0.52 us -> 36.4 us  [the longest x26 28.9 us: send(): return lax.ppermute(value, axes, [(i, i ^ step) for i in range(size)])]
    all_to_all x1 -> x0, blocking collectives: 30.5 us -> none  [local(): lax.all_to_all(outgoing_rows, ('req', 'head'), split_axis=0, concat_axis=...]
    ppermute x1 -> x30, waiting for transfers between devices: 0.01 us -> 20.6 us  [the longest x26 16.2 us: send(): return lax.ppermute(value, axes, [(i, i ^ step) for i in range(size)])]
    all_to_all x1 -> x0, waiting for transfers between devices: 15.5 us -> none  [local(): lax.all_to_all(column_sum, ('req', 'head'), split_axis=0, concat_axis=0,...]
    dot_general x9 -> x0, matrix products: 9.56 us -> none  [the longest x1 2.38 us: local(): jnp.dot(activated, down_weight[0], preferred_element_type=jnp.float32)]
    pallas_call x0 -> x2, Pallas kernels: none -> 9.11 us  [kernel_call(): pl.pallas_call(body, out_shape=out_shape, in_specs=[pl.BlockSpec(memory_s...]
    all_to_all x1 -> x0, starting transfers between devices: 6.76 us -> none  [local(): lax.all_to_all(column_sum, ('req', 'head'), split_axis=0, concat_axis=0,...]
  transfers between devices with their start and end apart: 4 -> 30, of which waited for: 3 -> 12; matrix products, arithmetic and copies ran while one was open for 3% -> 12% of each run, Pallas kernels for 0% -> 5%
where the time goes in v1:
time: 78.2 us; the launch traced here: 77.8 us
  starting transfers between devices  36.4 us (47%)
  waiting for transfers between devices  20.6 us (26%)
  Pallas kernels  9.11 us (12%)
  local copies, waits for them, and re-layouts  8.99 us (11%)
  other arithmetic  2.49 us (3%)
    ppermute x26, starting transfers between devices, send(): return lax.ppermute(value, axes, [(i, i ^ step) for i in range(size)])  28.9 us
    ppermute x26, waiting for transfers between devices, send(): return lax.ppermute(value, axes, [(i, i ^ step) for i in range(size)])  16.2 us
    pallas_call x2, Pallas kernels, kernel_call(): pl.pallas_call(body, out_shape=out_shape, in_specs=[pl.BlockSpec(memory_s...  9.11 us
    ppermute x4, starting transfers between devices, local(): returned.append(lax.ppermute(pieces[step], both, pairs))  7.55 us
    ppermute x4, waiting for transfers between devices, local(): returned.append(lax.ppermute(pieces[step], both, pairs))  4.39 us
    unnamed x34, local copies, waits for them, and re-layouts  3.34 us
  transfers between devices with their start and end apart: 30, of which 12 were waited for; matrix products, arithmetic and copies ran while one was open for 12% of the time, Pallas kernels for 5%

profile of v1, /device:TPU:0, one launch (start us, length us, event | category | flops | bytes accessed | tf_op | source)
XLA Modules:
  0.0 77.8 jit_solution(14156475150703265952)
XLA Ops:
  2.1 2.6 %collective-permute-start.17 = (f32[12,16]{1,0:T(8,128)S(1)}, f32[12,16]{1,0:T(8,128)S(1)}, u32[]{:S(2)}, u32[]{:S(2)}) collective-permute-start(f32[12,16]{1,0:T(8,128)S(1)} %select_reduce_fusion), channel_id=1, source_target_pairs={{0,8},{8,0},{16,24},{24,16},{1,9},{9,1},{17,25},{25,17},{2,10},{10... | collective-permute-start | bytes 2312 | tf_op jit(solution)/shard_map/ppermute | solution.py:19
  4.7 2.6 %collective-permute-start.18 = (f32[12,16]{1,0:T(8,128)S(1)}, f32[12,16]{1,0:T(8,128)S(1)}, u32[]{:S(2)}, u32[]{:S(2)}) collective-permute-start(f32[12,16]{1,0:T(8,128)S(1)} %select_reduce_fusion), channel_id=1, source_target_pairs={{0,16},{8,24},{16,0},{24,8},{1,17},{9,25},{17,1},{25,9},{2,18},{10... | collective-permute-start | bytes 2312 | tf_op jit(solution)/shard_map/ppermute | solution.py:19
  9.3 3.5 %collective-permute-done.19 = f32[12,16]{1,0:T(8,128)S(1)} collective-permute-done((f32[12,16]{1,0:T(8,128)S(1)}, f32[12,16]{1,0:T(8,128)S(1)}, u32[]{:S(2)}, u32[]{:S(2)}) %collective-permute-start.19) | collective-permute-done | bytes 800 | tf_op jit(solution)/shard_map/ppermute | solution.py:19
  12.8 1.6 %collective-permute-start.20 = (f32[4,12,16]{2,1,0:T(8,128)S(1)}, f32[4,12,16]{2,1,0:T(8,128)S(1)}, u32[]{:S(2)}, u32[]{:S(2)}) collective-permute-start(f32[4,12,16]{2,1,0:T(8,128)S(1)} %get-tuple-element.43), channel_id=1, source_target_pairs={{0,2},{2,0},{4,6},{6,4},{1,3},{3,1},{5,7},{7,5},{8,10},{10,8},{12,... | collective-permute-start | bytes 9224 | tf_op jit(solution)/shard_map/ppermute | solution.py:19
  14.3 1.5 %collective-permute-start.21 = (f32[4,12,16]{2,1,0:T(8,128)S(1)}, f32[4,12,16]{2,1,0:T(8,128)S(1)}, u32[]{:S(2)}, u32[]{:S(2)}) collective-permute-start(f32[4,12,16]{2,1,0:T(8,128)S(1)} %get-tuple-element.43), channel_id=1, source_target_pairs={{0,4},{2,6},{4,0},{6,2},{1,5},{3,7},{5,1},{7,3},{8,12},{10,14},{12... | collective-permute-start | bytes 9224 | tf_op jit(solution)/shard_map/ppermute | solution.py:19
  16.7 1.4 %reshape.31.new_ref = bf16[96,256]{1,0:T(8,128)(2,1)} reshape(bf16[48,2,1,256]{3,1,2,0:T(2,128)(2,1)} %param.16) | data formatting | bytes 98304 | tf_op jit(solution)/shard_map/reshape | solution.py:219
  20.0 4.2 %shard_map.145 = (bf16[24,512]{1,0:T(8,128)(2,1)}, bf16[24,512]{1,0:T(8,128)(2,1)}, bf16[24,512]{1,0:T(8,128)(2,1)}, bf16[24,512]{1,0:T(8,128)(2,1)}, bf16[24,51...) custom-call(bf16[48,1024]{1,0:T(8,128)(2,1)} %q_ref.1, ...), custom_call_target="tpu_custom_call" | custom-call | tf_op jit(solution)/shard_map/pallas_call | solution.py:27
  24.3 1.4 %collective-permute-start.3 = (bf16[24,512]{1,0:T(8,128)(2,1)}, bf16[24,512]{1,0:T(8,128)(2,1)S(1)}, u32[]{:S(2)}, u32[]{:S(2)}) collective-permute-start(bf16[24,512]{1,0:T(8,128)(2,1)} %get-tuple-element.21), channel_id=1, source_target_pairs={{0,2},{1,3},{2,0},{3,1},{4,6},{5,7},{6,4},{7,5},{8,10},{9,11},{10,... | collective-permute-start | bytes 73736 | tf_op jit(solution)/shard_map/ppermute | solution.py:19
  26.3 1.4 %slice_bitcast_fusion.2 = (bf16[192,2048]{1,0:T(8,128)(2,1)}, bf16[192,2048]{1,0:T(8,128)(2,1)}) fusion(bf16[1,2,192,2048]{3,2,1,0:T(8,128)(2,1)S(1)} %copy-done), kind=kLoop, calls=%fused_computation.2 | loop fusion | bytes 3145728 | tf_op jit(solution)/shard_map/squeeze | solution.py:253
  27.7 1.4 %collective-permute-start.5 = (bf16[24,512]{1,0:T(8,128)(2,1)S(1)}, bf16[24,512]{1,0:T(8,128)(2,1)S(1)}, u32[]{:S(2)}, u32[]{:S(2)}) collective-permute-start(bf16[24,512]{1,0:T(8,128)(2,1)S(1)} %copy-done.15), channel_id=1, source_target_pairs={{0,4},{1,5},{2,6},{3,7},{4,0},{5,1},{6,2},{7,3},{8,12},{9,13},{10,... | collective-permute-start | bytes 73736 | tf_op jit(solution)/shard_map/ppermute | solution.py:19
  29.4 2.4 %collective-permute-start.7 = (bf16[24,512]{1,0:T(8,128)(2,1)S(1)}, bf16[24,512]{1,0:T(8,128)(2,1)S(1)}, u32[]{:S(2)}, u32[]{:S(2)}) collective-permute-start(bf16[24,512]{1,0:T(8,128)(2,1)S(1)} %copy-done.13), channel_id=1, source_target_pairs={{0,6},{1,7},{2,4},{3,5},{4,2},{5,3},{6,0},{7,1},{8,14},{9,15},{10,... | collective-permute-start | bytes 73736 | tf_op jit(solution)/shard_map/ppermute | solution.py:19
  32.7 1.4 %collective-permute-done.7 = bf16[24,512]{1,0:T(8,128)(2,1)S(1)} collective-permute-done((bf16[24,512]{1,0:T(8,128)(2,1)S(1)}, bf16[24,512]{1,0:T(8,128)(2,1)S(1)}, u32[]{:S(2)}, u32[]{:S(2)}) %collective-permute-start.7) | collective-permute-done | bytes 24608 | tf_op jit(solution)/shard_map/ppermute | solution.py:19
  34.1 1.8 %collective-permute-done.8 = bf16[24,512]{1,0:T(8,128)(2,1)S(1)} collective-permute-done((bf16[24,512]{1,0:T(8,128)(2,1)S(1)}, bf16[24,512]{1,0:T(8,128)(2,1)S(1)}, u32[]{:S(2)}, u32[]{:S(2)}) %collective-permute-start.8) | collective-permute-done | bytes 24608 | tf_op jit(solution)/shard_map/ppermute | solution.py:19
  36.8 3.6 %collective-permute-start.11 = (bf16[24,512]{1,0:T(8,128)(2,1)S(1)}, bf16[24,512]{1,0:T(8,128)(2,1)S(1)}, u32[]{:S(2)}, u32[]{:S(2)}) collective-permute-start(bf16[24,512]{1,0:T(8,128)(2,1)S(1)} %add_convert_fusion.2), channel_id=1, source_target_pairs={{0,24},{8,16},{16,8},{24,0},{1,25},{9,17},{17,9},{25,1},{2,26},{10... | collective-permute-start | bytes 73736 | tf_op jit(solution)/shard_map/ppermute | solution.py:19
  41.1 1.4 %collective-permute-done.11 = bf16[24,512]{1,0:T(8,128)(2,1)S(1)} collective-permute-done((bf16[24,512]{1,0:T(8,128)(2,1)S(1)}, bf16[24,512]{1,0:T(8,128)(2,1)S(1)}, u32[]{:S(2)}, u32[]{:S(2)}) %collective-permute-start.11) | collective-permute-done | bytes 24608 | tf_op jit(solution)/shard_map/ppermute | solution.py:19
  43.9 2.1 %collective-permute-start.14 = (bf16[4,24,512]{2,1,0:T(8,128)(2,1)S(1)}, bf16[4,24,512]{2,1,0:T(8,128)(2,1)S(1)}, u32[]{:S(2)}, u32[]{:S(2)}) collective-permute-start(bf16[4,24,512]{2,1,0:T(8,128)(2,1)S(1)} %pad_maximum_fusion.1.refs_0_), channel_id=1, source_target_pairs={{0,6},{2,4},{4,2},{6,0},{1,7},{3,5},{5,3},{7,1},{8,14},{10,12},{12... | collective-permute-start | bytes 294920 | tf_op jit(solution)/shard_map/ppermute | solution.py:19
  50.3 4.9 %shard_map.146 = (bf16[48,1024]{1,0:T(8,128)(2,1)}, bf16[48,1024]{1,0:T(8,128)(2,1)}, bf16[48,1024]{1,0:T(8,128)(2,1)}, bf16[48,1024]{1,0:T(8,128)(2,1)}) custom-call(bf16[4,24,512]{2,1,0:T(8,128)(2,1)} %copy-done.5, bf16[4,24,512]{2,1,0:T(8,128)(2,1)} %copy-done.6, bf16[4,24,512]{2,1,0:T(8,128)(2,1)} %copy-done.7, bf16[4,24,512]{2,1,0:T(8,128)(2,1)} %copy-done.8, ...), custom_call_target="tpu_custom_call" | custom-call | tf_op jit(solution)/shard_map/pallas_call | solution.py:27
  55.2 1.5 %collective-permute-start.23 = (bf16[48,1024]{1,0:T(8,128)(2,1)}, bf16[48,1024]{1,0:T(8,128)(2,1)S(1)}, u32[]{:S(2)}, u32[]{:S(2)}) collective-permute-start(bf16[48,1024]{1,0:T(8,128)(2,1)} %get-tuple-element.29), channel_id=1, source_target_pairs={{0,0},{1,4},{2,1},{3,5},{4,2},{5,6},{6,3},{7,7},{8,8},{9,12},{10,9... | collective-permute-start | bytes 294920 | tf_op jit(solution)/shard_map/ppermute | solution.py:274
  56.8 1.7 %collective-permute-start.24 = (bf16[48,1024]{1,0:T(8,128)(2,1)}, bf16[48,1024]{1,0:T(8,128)(2,1)S(1)}, u32[]{:S(2)}, u32[]{:S(2)}) collective-permute-start(bf16[48,1024]{1,0:T(8,128)(2,1)} %get-tuple-element.30), channel_id=1, source_target_pairs={{0,1},{1,5},{2,0},{3,4},{4,3},{5,7},{6,2},{7,6},{8,9},{9,13},{10,8... | collective-permute-start | bytes 294920 | tf_op jit(solution)/shard_map/ppermute | solution.py:274
  58.8 4.0 %collective-permute-start.26 = (bf16[48,1024]{1,0:T(8,128)(2,1)}, bf16[48,1024]{1,0:T(8,128)(2,1)S(1)}, u32[]{:S(2)}, u32[]{:S(2)}) collective-permute-start(bf16[48,1024]{1,0:T(8,128)(2,1)} %get-tuple-element.32), channel_id=1, source_target_pairs={{0,3},{1,7},{2,2},{3,6},{4,1},{5,5},{6,0},{7,4},{8,11},{9,15},{10,... | collective-permute-start | bytes 294920 | tf_op jit(solution)/shard_map/ppermute | solution.py:274
  63.3 3.9 %collective-permute-done.26 = bf16[48,1024]{1,0:T(8,128)(2,1)S(1)} collective-permute-done((bf16[48,1024]{1,0:T(8,128)(2,1)}, bf16[48,1024]{1,0:T(8,128)(2,1)S(1)}, u32[]{:S(2)}, u32[]{:S(2)}) %collective-permute-start.26) | collective-permute-done | bytes 98336 | tf_op jit(solution)/shard_map/ppermute | solution.py:274
  67.7 3.8 %collective-permute-start.28 = (bf16[12,1024]{1,0:T(8,128)(2,1)S(1)}, bf16[12,1024]{1,0:T(8,128)(2,1)S(1)}, u32[]{:S(2)}, u32[]{:S(2)}) collective-permute-start(bf16[12,1024]{1,0:T(8,128)(2,1)S(1)} %get-tuple-element.41), channel_id=1, source_target_pairs={{0,16},{8,24},{16,0},{24,8},{1,17},{9,25},{17,1},{25,9},{2,18},{10... | collective-permute-start | bytes 73736 | tf_op jit(solution)/shard_map/ppermute | solution.py:19
  71.7 2.0 %collective-permute-done.28 = bf16[12,1024]{1,0:T(8,128)(2,1)S(1)} collective-permute-done((bf16[12,1024]{1,0:T(8,128)(2,1)S(1)}, bf16[12,1024]{1,0:T(8,128)(2,1)S(1)}, u32[]{:S(2)}, u32[]{:S(2)}) %collective-permute-start.28) | collective-permute-done | bytes 24608 | tf_op jit(solution)/shard_map/ppermute | solution.py:19
  73.7 3.5 %collective-permute-done.29 = bf16[12,1024]{1,0:T(8,128)(2,1)S(1)} collective-permute-done((bf16[12,1024]{1,0:T(8,128)(2,1)S(1)}, bf16[12,1024]{1,0:T(8,128)(2,1)S(1)}, u32[]{:S(2)}, u32[]{:S(2)}) %collective-permute-start.29) | collective-permute-done | bytes 24608 | tf_op jit(solution)/shard_map/ppermute | solution.py:19
  (91 shorter events, 18.1 us)
Async XLA Ops:
  0.0 8.2 %collective-permute-start = (bf16[832,256]{1,0:T(8,128)(2,1)}, bf16[832,256]{1,0:T(8,128)(2,1)S(1)}, u32[]{:S(2)}, u32[]{:S(2)}) collective-permute-start(bf16[832,256]{1,0:T(8,128)(2,1)} %bitcast.35), channel_id=1, source_target_pairs={{0,1},{1,0},{2,3},{3,2},{4,5},{5,4},{6,7},{7,6},{8,9},{9,8},{10,11... | collective-permute-start | bytes 1277960 | tf_op jit(solution)/shard_map/ppermute | solution.py:19
  2.1 6.6 %collective-permute-start.17 = (f32[12,16]{1,0:T(8,128)S(1)}, f32[12,16]{1,0:T(8,128)S(1)}, u32[]{:S(2)}, u32[]{:S(2)}) collective-permute-start(f32[12,16]{1,0:T(8,128)S(1)} %select_reduce_fusion), channel_id=1, source_target_pairs={{0,8},{8,0},{16,24},{24,16},{1,9},{9,1},{17,25},{25,17},{2,10},{10... | collective-permute-start | bytes 2312 | tf_op jit(solution)/shard_map/ppermute | solution.py:19
  7.3 5.4 %collective-permute-start.19 = (f32[12,16]{1,0:T(8,128)S(1)}, f32[12,16]{1,0:T(8,128)S(1)}, u32[]{:S(2)}, u32[]{:S(2)}) collective-permute-start(f32[12,16]{1,0:T(8,128)S(1)} %select_reduce_fusion), channel_id=1, source_target_pairs={{0,24},{8,16},{16,8},{24,0},{1,25},{9,17},{17,9},{25,1},{2,26},{10... | collective-permute-start | bytes 2312 | tf_op jit(solution)/shard_map/ppermute | solution.py:19
  8.1 11.0 %collective-permute-start.1 = (s32[1,128]{1,0:T(1,128)S(1)}, s32[1,128]{1,0:T(1,128)S(1)}, u32[]{:S(2)}, u32[]{:S(2)}) collective-permute-start(s32[1,128]{1,0:T(1,128)S(1)} %pad_bitcast_fusion.own_ints_ref), channel_id=1, source_target_pairs={{0,1},{1,0},{2,3},{3,2},{4,5},{5,4},{6,7},{7,6},{8,9},{9,8},{10,11... | collective-permute-start | bytes 1544 | tf_op jit(solution)/shard_map/ppermute | solution.py:19
  8.2 37.8 %collective-permute-start.15 = (bf16[1,2,192,2048]{3,2,1,0:T(8,128)(2,1)}, bf16[1,2,192,2048]{3,2,1,0:T(8,128)(2,1)S(1)}, u32[]{:S(2)}, u32[]{:S(2)}) collective-permute-start(bf16[1,2,192,2048]{3,2,1,0:T(8,128)(2,1)} %param.27), channel_id=1, source_target_pairs={{0,1},{1,0},{2,3},{3,2},{4,5},{5,4},{6,7},{7,6},{8,9},{9,8},{10,11... | collective-permute-start | bytes 4718600 | tf_op jit(solution)/shard_map/ppermute | solution.py:19
  12.8 11.5 %collective-permute-start.20 = (f32[4,12,16]{2,1,0:T(8,128)S(1)}, f32[4,12,16]{2,1,0:T(8,128)S(1)}, u32[]{:S(2)}, u32[]{:S(2)}) collective-permute-start(f32[4,12,16]{2,1,0:T(8,128)S(1)} %get-tuple-element.43), channel_id=1, source_target_pairs={{0,2},{2,0},{4,6},{6,4},{1,3},{3,1},{5,7},{7,5},{8,10},{10,8},{12,... | collective-permute-start | bytes 9224 | tf_op jit(solution)/shard_map/ppermute | solution.py:19
  14.3 11.4 %collective-permute-start.21 = (f32[4,12,16]{2,1,0:T(8,128)S(1)}, f32[4,12,16]{2,1,0:T(8,128)S(1)}, u32[]{:S(2)}, u32[]{:S(2)}) collective-permute-start(f32[4,12,16]{2,1,0:T(8,128)S(1)} %get-tuple-element.43), channel_id=1, source_target_pairs={{0,4},{2,6},{4,0},{6,2},{1,5},{3,7},{5,1},{7,3},{8,12},{10,14},{12... | collective-permute-start | bytes 9224 | tf_op jit(solution)/shard_map/ppermute | solution.py:19
  18.8 8.8 %collective-permute-start.22 = (f32[4,12,16]{2,1,0:T(8,128)S(1)}, f32[4,12,16]{2,1,0:T(8,128)S(1)}, u32[]{:S(2)}, u32[]{:S(2)}) collective-permute-start(f32[4,12,16]{2,1,0:T(8,128)S(1)} %get-tuple-element.43), channel_id=1, source_target_pairs={{0,6},{2,4},{4,2},{6,0},{1,7},{3,5},{5,3},{7,1},{8,14},{10,12},{12... | collective-permute-start | bytes 9224 | tf_op jit(solution)/shard_map/ppermute | solution.py:19
  24.3 4.8 %collective-permute-start.2 = (bf16[24,512]{1,0:T(8,128)(2,1)}, bf16[24,512]{1,0:T(8,128)(2,1)S(1)}, u32[]{:S(2)}, u32[]{:S(2)}) collective-permute-start(bf16[24,512]{1,0:T(8,128)(2,1)} %get-tuple-element.20), channel_id=1, source_target_pairs={{0,1},{1,0},{2,3},{3,2},{4,5},{5,4},{6,7},{7,6},{8,9},{9,8},{10,11... | collective-permute-start | bytes 73736 | tf_op jit(solution)/shard_map/ppermute | solution.py:19
  24.3 5.0 %collective-permute-start.3 = (bf16[24,512]{1,0:T(8,128)(2,1)}, bf16[24,512]{1,0:T(8,128)(2,1)S(1)}, u32[]{:S(2)}, u32[]{:S(2)}) collective-permute-start(bf16[24,512]{1,0:T(8,128)(2,1)} %get-tuple-element.21), channel_id=1, source_target_pairs={{0,2},{1,3},{2,0},{3,1},{4,6},{5,7},{6,4},{7,5},{8,10},{9,11},{10,... | collective-permute-start | bytes 73736 | tf_op jit(solution)/shard_map/ppermute | solution.py:19
  25.7 6.0 %collective-permute-start.4 = (bf16[24,512]{1,0:T(8,128)(2,1)}, bf16[24,512]{1,0:T(8,128)(2,1)S(1)}, u32[]{:S(2)}, u32[]{:S(2)}) collective-permute-start(bf16[24,512]{1,0:T(8,128)(2,1)} %get-tuple-element.22), channel_id=1, source_target_pairs={{0,3},{1,2},{2,1},{3,0},{4,7},{5,6},{6,5},{7,4},{8,11},{9,10},{10,... | collective-permute-start | bytes 73736 | tf_op jit(solution)/shard_map/ppermute | solution.py:19
  32.3 17.2 %collective-permute-start.16 = (bf16[1,192,2048]{2,1,0:T(8,128)(2,1)S(1)}, bf16[1,192,2048]{2,1,0:T(8,128)(2,1)S(1)}, u32[]{:S(2)}, u32[]{:S(2)}) collective-permute-start(bf16[1,192,2048]{2,1,0:T(8,128)(2,1)S(1)} %copy-done.1), channel_id=1, source_target_pairs={{0,1},{1,0},{2,3},{3,2},{4,5},{5,4},{6,7},{7,6},{8,9},{9,8},{10,11... | collective-permute-start | bytes 2359304 | tf_op jit(solution)/shard_map/ppermute | solution.py:19
  35.9 5.2 %collective-permute-start.9 = (bf16[24,512]{1,0:T(8,128)(2,1)S(1)}, bf16[24,512]{1,0:T(8,128)(2,1)S(1)}, u32[]{:S(2)}, u32[]{:S(2)}) collective-permute-start(bf16[24,512]{1,0:T(8,128)(2,1)S(1)} %add_convert_fusion.2), channel_id=1, source_target_pairs={{0,8},{8,0},{16,24},{24,16},{1,9},{9,1},{17,25},{25,17},{2,10},{10... | collective-permute-start | bytes 73736 | tf_op jit(solution)/shard_map/ppermute | solution.py:19
  36.0 5.1 %collective-permute-start.10 = (bf16[24,512]{1,0:T(8,128)(2,1)S(1)}, bf16[24,512]{1,0:T(8,128)(2,1)S(1)}, u32[]{:S(2)}, u32[]{:S(2)}) collective-permute-start(bf16[24,512]{1,0:T(8,128)(2,1)S(1)} %add_convert_fusion.2), channel_id=1, source_target_pairs={{0,16},{8,24},{16,0},{24,8},{1,17},{9,25},{17,1},{25,9},{2,18},{10... | collective-permute-start | bytes 73736 | tf_op jit(solution)/shard_map/ppermute | solution.py:19
  36.8 5.7 %collective-permute-start.11 = (bf16[24,512]{1,0:T(8,128)(2,1)S(1)}, bf16[24,512]{1,0:T(8,128)(2,1)S(1)}, u32[]{:S(2)}, u32[]{:S(2)}) collective-permute-start(bf16[24,512]{1,0:T(8,128)(2,1)S(1)} %add_convert_fusion.2), channel_id=1, source_target_pairs={{0,24},{8,16},{16,8},{24,0},{1,25},{9,17},{17,9},{25,1},{2,26},{10... | collective-permute-start | bytes 73736 | tf_op jit(solution)/shard_map/ppermute | solution.py:19
  42.5 5.0 %collective-permute-start.12 = (bf16[4,24,512]{2,1,0:T(8,128)(2,1)S(1)}, bf16[4,24,512]{2,1,0:T(8,128)(2,1)S(1)}, u32[]{:S(2)}, u32[]{:S(2)}) collective-permute-start(bf16[4,24,512]{2,1,0:T(8,128)(2,1)S(1)} %pad_maximum_fusion.1.refs_0_), channel_id=1, source_target_pairs={{0,2},{2,0},{4,6},{6,4},{1,3},{3,1},{5,7},{7,5},{8,10},{10,8},{12,... | collective-permute-start | bytes 294920 | tf_op jit(solution)/shard_map/ppermute | solution.py:19
  43.1 5.0 %collective-permute-start.13 = (bf16[4,24,512]{2,1,0:T(8,128)(2,1)S(1)}, bf16[4,24,512]{2,1,0:T(8,128)(2,1)S(1)}, u32[]{:S(2)}, u32[]{:S(2)}) collective-permute-start(bf16[4,24,512]{2,1,0:T(8,128)(2,1)S(1)} %pad_maximum_fusion.1.refs_0_), channel_id=1, source_target_pairs={{0,4},{2,6},{4,0},{6,2},{1,5},{3,7},{5,1},{7,3},{8,12},{10,14},{12... | collective-permute-start | bytes 294920 | tf_op jit(solution)/shard_map/ppermute | solution.py:19
  43.9 5.5 %collective-permute-start.14 = (bf16[4,24,512]{2,1,0:T(8,128)(2,1)S(1)}, bf16[4,24,512]{2,1,0:T(8,128)(2,1)S(1)}, u32[]{:S(2)}, u32[]{:S(2)}) collective-permute-start(bf16[4,24,512]{2,1,0:T(8,128)(2,1)S(1)} %pad_maximum_fusion.1.refs_0_), channel_id=1, source_target_pairs={{0,6},{2,4},{4,2},{6,0},{1,7},{3,5},{5,3},{7,1},{8,14},{10,12},{12... | collective-permute-start | bytes 294920 | tf_op jit(solution)/shard_map/ppermute | solution.py:19
  55.2 7.6 %collective-permute-start.23 = (bf16[48,1024]{1,0:T(8,128)(2,1)}, bf16[48,1024]{1,0:T(8,128)(2,1)S(1)}, u32[]{:S(2)}, u32[]{:S(2)}) collective-permute-start(bf16[48,1024]{1,0:T(8,128)(2,1)} %get-tuple-element.29), channel_id=1, source_target_pairs={{0,0},{1,4},{2,1},{3,5},{4,2},{5,6},{6,3},{7,7},{8,8},{9,12},{10,9... | collective-permute-start | bytes 294920 | tf_op jit(solution)/shard_map/ppermute | solution.py:274
  56.8 6.0 %collective-permute-start.24 = (bf16[48,1024]{1,0:T(8,128)(2,1)}, bf16[48,1024]{1,0:T(8,128)(2,1)S(1)}, u32[]{:S(2)}, u32[]{:S(2)}) collective-permute-start(bf16[48,1024]{1,0:T(8,128)(2,1)} %get-tuple-element.30), channel_id=1, source_target_pairs={{0,1},{1,5},{2,0},{3,4},{4,3},{5,7},{6,2},{7,6},{8,9},{9,13},{10,8... | collective-permute-start | bytes 294920 | tf_op jit(solution)/shard_map/ppermute | solution.py:274
  58.5 4.8 %collective-permute-start.25 = (bf16[48,1024]{1,0:T(8,128)(2,1)}, bf16[48,1024]{1,0:T(8,128)(2,1)S(1)}, u32[]{:S(2)}, u32[]{:S(2)}) collective-permute-start(bf16[48,1024]{1,0:T(8,128)(2,1)} %get-tuple-element.31), channel_id=1, source_target_pairs={{0,2},{1,6},{2,3},{3,7},{4,0},{5,4},{6,1},{7,5},{8,10},{9,14},{10,... | collective-permute-start | bytes 294920 | tf_op jit(solution)/shard_map/ppermute | solution.py:274
  58.8 8.4 %collective-permute-start.26 = (bf16[48,1024]{1,0:T(8,128)(2,1)}, bf16[48,1024]{1,0:T(8,128)(2,1)S(1)}, u32[]{:S(2)}, u32[]{:S(2)}) collective-permute-start(bf16[48,1024]{1,0:T(8,128)(2,1)} %get-tuple-element.32), channel_id=1, source_target_pairs={{0,3},{1,7},{2,2},{3,6},{4,1},{5,5},{6,0},{7,4},{8,11},{9,15},{10,... | collective-permute-start | bytes 294920 | tf_op jit(solution)/shard_map/ppermute | solution.py:274
  67.7 6.1 %collective-permute-start.28 = (bf16[12,1024]{1,0:T(8,128)(2,1)S(1)}, bf16[12,1024]{1,0:T(8,128)(2,1)S(1)}, u32[]{:S(2)}, u32[]{:S(2)}) collective-permute-start(bf16[12,1024]{1,0:T(8,128)(2,1)S(1)} %get-tuple-element.41), channel_id=1, source_target_pairs={{0,16},{8,24},{16,0},{24,8},{1,17},{9,25},{17,1},{25,9},{2,18},{10... | collective-permute-start | bytes 73736 | tf_op jit(solution)/shard_map/ppermute | solution.py:19
  71.5 5.7 %collective-permute-start.29 = (bf16[12,1024]{1,0:T(8,128)(2,1)S(1)}, bf16[12,1024]{1,0:T(8,128)(2,1)S(1)}, u32[]{:S(2)}, u32[]{:S(2)}) collective-permute-start(bf16[12,1024]{1,0:T(8,128)(2,1)S(1)} %get-tuple-element.40), channel_id=1, source_target_pairs={{0,24},{8,16},{16,8},{24,0},{1,25},{9,17},{17,9},{25,1},{2,26},{10... | collective-permute-start | bytes 73736 | tf_op jit(solution)/shard_map/ppermute | solution.py:19
  (22 other events, 98.4 us)

commit v2 on v1

v2 whole, which is shorter than its diff:
```python
import functools

import jax
import jax.numpy as jnp
import numpy as np
from jax import lax
from jax.experimental import pallas as pl
from jax.experimental.pallas import tpu as pltpu
from jax.sharding import PartitionSpec as P

F32 = jnp.float32
BF16 = jnp.bfloat16
VMEM_LIMIT = 56 * 2**20
LANES = 128


def send(value, axes, step):
    size = lax.axis_size(axes)
    return lax.ppermute(value, axes, [(i, i ^ step) for i in range(size)])


def dot(a, b, contract=((1,), (0,))):
    return lax.dot_general(a, b, (contract, ((), ())), preferred_element_type=F32)


def kernel_call(body, out_shape, args, scratch=()):
    return pl.pallas_call(
        body,
        out_shape=out_shape,
        in_specs=[pl.BlockSpec(memory_space=pltpu.VMEM)] * len(args),
        out_specs=jax.tree.map(lambda _: pl.BlockSpec(memory_space=pltpu.VMEM), out_shape),
        scratch_shapes=list(scratch),
        compiler_params=pltpu.CompilerParams(vmem_limit_bytes=VMEM_LIMIT),
    )(*args)


def column(row, start, count):
    lane = lax.broadcasted_iota(jnp.int32, (count, row.shape[1]), 1)
    line = lax.broadcasted_iota(jnp.int32, (count, row.shape[1]), 0)
    return jnp.sum(jnp.where(lane == line + start, row, 0.0), axis=1, keepdims=True)


def place_kernel(sizes, residual_ref, choice_ref, route_ref, placed_ref):
    heads, pools, planes = sizes
    head = lax.axis_index("head")
    first = jnp.where(lax.axis_index("pool") == 0, 1.0, 0.0)
    rows_here, width = residual_ref.shape
    part = rows_here // pools
    total = heads * rows_here
    line = lax.broadcasted_iota(jnp.int32, (total, rows_here), 0)
    lane = lax.broadcasted_iota(jnp.int32, (total, rows_here), 1)
    own = None
    for p in range(pools):
        inside = line - (p * heads * part + head * part)
        one = (inside >= 0) & (inside < part) & (lane == inside + p * part)
        own = one if own is None else own | one
    spread = jnp.where(own, first, 0.0)
    placed_ref[:, :width] = dot(spread.astype(BF16), residual_ref[...]).astype(BF16)
    mixes = placed_ref.shape[1] - width
    target = lax.broadcasted_iota(jnp.int32, (total, mixes), 1)
    mix = jnp.zeros((total, mixes), F32)
    for k in range(choice_ref.shape[0]):
        expert = jnp.sum(spread * choice_ref[k : k + 1, :].astype(F32), axis=1, keepdims=True).astype(jnp.int32)
        weight = jnp.sum(spread * route_ref[k : k + 1, :], axis=1, keepdims=True)
        high = weight.astype(BF16).astype(F32)
        lanes = (expert % heads) * (mixes // heads) + expert // heads
        mix = mix + jnp.where(target == lanes, high, 0.0)
        mix = mix + jnp.where(target == lanes + planes, weight - high, 0.0)
    placed_ref[:, width:] = mix.astype(BF16)


def attend_kernel(sizes, q_ref, new_ref, own_ref, other_ref, own_ints_ref, other_ints_ref, placed_ref, order_ref, weight_ref, out_ref):
    requests, pages, moved, page, heads, pools, head_dim = sizes
    slots = own_ref.shape[0] // page
    here = lax.axis_index("pool")
    group = q_ref.shape[1] // head_dim // pools
    rows = requests // pools
    width = weight_ref.shape[1]
    columns = width // heads
    mixes = (placed_ref.shape[1] - width) // heads

    ints = [own_ints_ref[...].astype(F32), other_ints_ref[...].astype(F32)]
    live_from, live_count = [], []
    for q in range(2):
        row, across = ints[q], ints[1 - q]
        base = pages * requests
        length = column(row, base, requests)
        for j in range(pages):
            slot = column(row, j * requests, requests)
            source = slot + float(q * slots)
            for k in range(moved):
                leave = column(across, base + requests + k, 1)
                arrive = column(row, base + requests + moved + k, 1)
                source = jnp.where(slot == arrive, leave + float((1 - q) * slots), source)
            live_from.append((source * float(page)).astype(jnp.int32))
            live_count.append(jnp.clip(length - float(j * page), 0.0, float(page)).astype(jnp.int32))

    def cache_mask(offset, count):
        entry = lax.broadcasted_iota(jnp.int32, (requests, count), 1) + offset
        mask = None
        for start, amount in zip(live_from, live_count):
            apart = entry - start
            one = (apart >= 0) & (apart < amount)
            mask = one if mask is None else mask | one
        return mask

    count = own_ref.shape[0]
    fresh = new_ref.shape[0] // requests
    entry = lax.broadcasted_iota(jnp.int32, (requests, new_ref.shape[0]), 1)
    first = lax.broadcasted_iota(jnp.int32, (requests, new_ref.shape[0]), 0) * fresh
    masks = [cache_mask(0, count), cache_mask(count, count), (entry >= first) & (entry < first + fresh)]
    queries = jnp.concatenate(
        [
            q_ref[:, pl.ds(pl.multiple_of((here * group + g) * head_dim, LANES), head_dim)]
            for g in range(group)
        ],
        axis=0,
    )
    scale = head_dim ** (-0.5)
    scores = []
    for ref, mask in zip((own_ref, other_ref, new_ref), masks):
        score = dot(queries, ref[:, :head_dim], ((1,), (1,))) * scale
        bias = jnp.where(mask, 0.0, -jnp.inf)
        scores.append(score + jnp.concatenate([bias] * group, axis=0))
    largest = functools.reduce(
        jnp.maximum, [jnp.max(score, axis=1, keepdims=True) for score in scores]
    )
    total, value = 0.0, 0.0
    for ref, score in zip((own_ref, other_ref, new_ref), scores):
        weights = jnp.exp(score - largest)
        total = total + jnp.sum(weights, axis=1, keepdims=True)
        value = value + dot(weights.astype(BF16), ref[:, head_dim:])
    value = (value / total).astype(BF16)
    attended = jnp.concatenate(
        [value[g * requests : (g + 1) * requests] for g in range(group)], axis=1
    )
    attended = dot(order_ref[...], attended).astype(BF16)
    partial = dot(attended, weight_ref[...])
    placed = placed_ref[...].astype(F32)
    partial = partial + placed[:, :width]
    for h in range(heads):
        for p in range(pools):
            at = slice(p * rows, (p + 1) * rows)
            out_ref[h * pools + p, :, :columns] = partial[
                at, h * columns : (h + 1) * columns
            ].astype(BF16)
            out_ref[h * pools + p, :, columns:] = placed[
                at, width + h * mixes : width + (h + 1) * mixes
            ].astype(BF16)


def expert_kernel(sizes, blocks_ref, mix_ref, own_up_ref, other_up_ref, own_down_ref, other_down_ref, gain_ref, order_ref, out_ref):
    heads, planes = sizes
    head, plane = lax.axis_index("head"), lax.axis_index("req")
    columns = blocks_ref.shape[3]
    plane_rows = blocks_ref.shape[2]
    rows = planes * plane_rows
    width = heads * columns
    units = own_down_ref.shape[0]
    squares, projected = 0.0, 0.0
    for h in range(heads):
        at = slice(h * columns, (h + 1) * columns)
        block = blocks_ref[h].astype(F32).reshape(rows, columns)
        squares = squares + jnp.sum(block * block, axis=1, keepdims=True)
        block = (block * gain_ref[:, at]).astype(BF16)
        weights = jnp.concatenate(
            [own_up_ref[:units, at], other_up_ref[:units, at], own_up_ref[units:, at], other_up_ref[units:, at]],
            axis=0,
        )
        projected = projected + dot(block, weights, ((1,), (1,)))
    projected = projected * lax.rsqrt(squares / width + 1e-06)
    gate, up = projected[:, : 2 * units], projected[:, 2 * units :]
    mix = mix_ref[...].astype(F32).reshape(rows, mix_ref.shape[2])
    lane = lax.broadcasted_iota(jnp.int32, mix.shape, 1)
    route = jnp.sum(
        jnp.where((lane == plane) | (lane == plane + planes), mix, 0.0), axis=1, keepdims=True
    )
    activated = (gate / (1.0 + jnp.exp(-gate)) * up * route).astype(BF16)
    activated = dot(order_ref[...], activated).astype(BF16)
    down = jnp.concatenate([own_down_ref[...], other_down_ref[...]], axis=0)
    line = lax.broadcasted_iota(jnp.int32, (rows, columns), 0) - plane * plane_rows
    here = jnp.where(
        (line >= 0) & (line < plane_rows), blocks_ref[head].astype(F32).reshape(rows, columns), 0.0
    )
    here = dot(order_ref[...], here.astype(BF16))
    for h in range(heads):
        at = slice(h * columns, (h + 1) * columns)
        part = dot(activated, down[:, at]) + jnp.where(head == h, here, 0.0)
        for to in range(heads):
            lines = slice(to * rows // heads, (to + 1) * rows // heads)
            out_ref[to, :, at] = part[lines].astype(BF16)


def one_hot(rows):
    return jnp.asarray(np.eye(len(rows), dtype=np.float32)[np.asarray(rows)], BF16)


def exchange(value, axes):
    return lax.all_to_all(value, axes, split_axis=0, concat_axis=0, tiled=True)


def to_all(value, axes):
    return exchange(jnp.broadcast_to(value[None], (lax.axis_size(axes), *value.shape)), axes)


def local(
    queries,
    new_entries,
    cache_pages,
    page_table,
    cached_length,
    leave_slots,
    arrive_slots,
    residual,
    norm_gain,
    output_weight,
    expert_choice,
    route_weight,
    gate_up,
    down_weight,
):
    pools, heads, planes = lax.axis_size("pool"), lax.axis_size("head"), lax.axis_size("req")
    requests = queries.shape[0]
    slots, page, entry = cache_pages.shape[1:]
    moved = leave_slots.shape[0]
    pages = page_table.shape[2]
    rows_here, width = residual.shape
    part = rows_here // pools
    columns = width // heads
    mixes = 2 * planes + -2 * planes % LANES

    own_cache = cache_pages.reshape(slots * page, entry)
    other_cache = send(own_cache, "pool", 1)
    ints = jnp.concatenate(
        [page_table[:, 0, j] for j in range(pages)]
        + [cached_length.reshape(-1), leave_slots, arrive_slots]
    )
    ints = jnp.pad(ints, (0, -ints.shape[0] % LANES)).reshape(1, -1)
    other_ints = send(ints, "pool", 1)

    placed = kernel_call(
        functools.partial(place_kernel, (heads, pools, planes)),
        jax.ShapeDtypeStruct((requests, width + heads * mixes), BF16),
        (residual, expert_choice.T, route_weight.T),
    )
    order = [
        h * rows_here + p * part + i for p in range(pools) for h in range(heads) for i in range(part)
    ]
    args = (
        queries,
        new_entries.reshape(-1, entry),
        own_cache,
        other_cache,
        ints,
        other_ints,
        placed,
        one_hot(order),
        output_weight,
    )
    sizes = (requests, pages, moved, page, heads, pools, entry // 2)
    pieces = kernel_call(
        functools.partial(attend_kernel, sizes),
        jax.ShapeDtypeStruct((heads * pools, requests // pools, columns + mixes), BF16),
        args,
    )
    hidden = jnp.sum(exchange(pieces, ("head", "pool")).astype(F32), axis=0).astype(BF16)

    held = lax.optimization_barrier((gate_up, down_weight, other_cache))
    other_up = send(held[0].reshape(-1, width), "pool", 1)
    other_down = send(held[1].reshape(-1, width), "pool", 1)

    plane_blocks = to_all(hidden, "req")
    blocks = to_all(plane_blocks[:, :, :columns], "head")
    order = [
        (r * heads + h) * part + i for h in range(heads) for r in range(planes) for i in range(part)
    ]
    args = (
        blocks,
        plane_blocks[:, :, columns:],
        gate_up.reshape(-1, width),
        other_up,
        down_weight.reshape(-1, width),
        other_down,
        norm_gain.reshape(1, -1),
        one_hot(order),
    )
    pieces = kernel_call(
        functools.partial(expert_kernel, (heads, planes)),
        jax.ShapeDtypeStruct((heads, planes * part, width), BF16),
        args,
    )
    mixed = jnp.sum(exchange(pieces, "head").astype(F32), axis=0).astype(BF16)
    mixed = mixed.reshape(planes, part, pools, width // pools).transpose(0, 2, 1, 3)
    mixed = exchange(mixed.reshape(planes * pools, part, -1), ("req", "pool"))
    total = jnp.sum(mixed.reshape(planes, pools, part, -1).astype(F32), axis=0)
    return total.reshape(rows_here, -1).astype(BF16)


def solution(mesh):
    return jax.shard_map(
        local,
        mesh=mesh,
        in_specs=(
            P(("group", "req"), "head"),
            P(("group", "req"), None, "head", None),
            P("head", ("group", "req", "pool"), None, None),
            P(("group", "req"), "pool", None),
            P(("group", "req"), "pool"),
            P(("group", "req", "pool")),
            P(("group", "req", "pool")),
            P(("group", "req", "head"), None),
            P(),
            P(("head", "pool"), None),
            P(("group", "req", "head"), None),
            P(("group", "req", "head"), None),
            P(("req", "head"), None, "pool", None),
            P(("req", "head"), "pool", None),
        ),
        out_specs=P(("group", "req", "head"), "pool"),
        check_vma=False,
    )
```

time: 78.2 us -> 71.7 us (0.917)
  blocking collectives: 0 us -> 41.2 us
  starting transfers between devices: 36.4 us -> 4.8 us
  waiting for transfers between devices: 20.6 us -> 6.84 us
  local copies, waits for them, and re-layouts: 8.99 us -> 5.69 us
  Pallas kernels: 9.11 us -> 11.6 us
  other arithmetic: 2.49 us -> 0.91 us
    all_to_all x0 -> x4, blocking collectives: none -> 41.2 us  [exchange(): return lax.all_to_all(value, axes, split_axis=0, concat_axis=0, tiled=True)]
    ppermute x26 -> x4, starting transfers between devices: 28.9 us -> 1.34 us  [send(): return lax.ppermute(value, axes, [(i, i ^ step) for i in range(size)])]
    ppermute x26 -> x4, waiting for transfers between devices: 16.2 us -> 1.61 us  [send(): return lax.ppermute(value, axes, [(i, i ^ step) for i in range(size)])]
    ppermute x4 -> x0, starting transfers between devices: 7.55 us -> none  [local(): returned.append(lax.ppermute(pieces[step], both, pairs))]
    all_to_all x0 -> x1, waiting for transfers between devices: none -> 5.23 us  [exchange(): return lax.all_to_all(value, axes, split_axis=0, concat_axis=0, tiled=True)]
    ppermute x4 -> x0, waiting for transfers between devices: 4.39 us -> none  [local(): returned.append(lax.ppermute(pieces[step], both, pairs))]
    all_to_all x0 -> x1, starting transfers between devices: none -> 3.46 us  [exchange(): return lax.all_to_all(value, axes, split_axis=0, concat_axis=0, tiled=True)]
    squeeze x2 -> x0, local copies, waits for them, and re-layouts: 2.69 us -> none  [the longest x1 1.35 us: local(): gate_up[0, 1]]
  transfers between devices with their start and end apart: 30 -> 5, of which waited for: 12 -> 2; matrix products, arithmetic and copies ran while one was open for 12% -> 5% of each run, Pallas kernels for 5% -> 9%
where the time goes in v2:
time: 71.7 us; the launch traced here: 71.1 us
  blocking collectives  41.2 us (57%)
  Pallas kernels  11.6 us (16%)
  waiting for transfers between devices  6.84 us (10%)
  local copies, waits for them, and re-layouts  5.69 us (8%)
  starting transfers between devices  4.8 us (7%)
  other arithmetic  0.91 us (1%)
    all_to_all x4, blocking collectives, exchange(): return lax.all_to_all(value, axes, split_axis=0, concat_axis=0, tiled=True)  41.2 us
    pallas_call x3, Pallas kernels, kernel_call(): pl.pallas_call(body, out_shape=out_shape, in_specs=[pl.BlockSpec(memory_s...  11.6 us
    all_to_all x1, waiting for transfers between devices, exchange(): return lax.all_to_all(value, axes, split_axis=0, concat_axis=0, tiled=True)  5.23 us
    all_to_all x1, starting transfers between devices, exchange(): return lax.all_to_all(value, axes, split_axis=0, concat_axis=0, tiled=True)  3.46 us
    unnamed x12, local copies, waits for them, and re-layouts  2.13 us
    ppermute x4, waiting for transfers between devices, send(): return lax.ppermute(value, axes, [(i, i ^ step) for i in range(size)])  1.61 us
    reshape x1, local copies, waits for them, and re-layouts, local(): new_entries.reshape(-1, entry)  1.44 us
  transfers between devices with their start and end apart: 5, of which 2 were waited for; matrix products, arithmetic and copies ran while one was open for 5% of the time, Pallas kernels for 9%

profile of v2, /device:TPU:0, one launch (start us, length us, event | category | flops | bytes accessed | tf_op | source)
XLA Modules:
  0.0 71.1 jit_solution(17033868848722860843)
XLA Ops:
  0.0 0.5 collective-permute-start
  0.5 1.6 %collective-permute-done.other_ref = bf16[832,256]{1,0:T(8,128)(2,1)S(1)} collective-permute-done((bf16[832,256]{1,0:T(8,128)(2,1)}, bf16[832,256]{1,0:T(8,128)(2,1)S(1)}, u32[]{:S(2)}, u32[]{:S(2)}) %collective-permute-start) | collective-permute-done | bytes 426016 | tf_op jit(solution)/shard_map/ppermute | solution.py:19
  2.1 0.4 collective-permute-start.2
  2.4 0.8 %pad_add_fusion = s32[104]{0:T(128)S(1)} fusion(s32[4]{0:T(128)} %param.22, s32[4]{0:T(128)} %param.21, s32[48]{0:T(128)} %bitcast.29, s32[48]{0:T(128)} %bitcast.30), kind=kLoop, calls=%fused_computation | loop fusion | flops 312 | bytes 832 | tf_op jit(solution)/shard_map/concatenate | solution.py:234
  3.2 0.2 collective-permute-start.3
  3.4 0.3 collective-permute-start.1
  3.7 1.4 %reshape.40.new_ref = bf16[96,256]{1,0:T(8,128)(2,1)} reshape(bf16[48,2,1,256]{3,1,2,0:T(2,128)(2,1)} %param.17) | data formatting | bytes 98304 | tf_op jit(solution)/shard_map/reshape | solution.py:251
  5.2 2.1 %shard_map.154.placed_ref = bf16[48,2560]{1,0:T(8,128)(2,1)} custom-call(bf16[12,2048]{1,0:T(8,128)(2,1)} %residual_ref.1, s32[8,12]{1,0:T(8,128)} %bitcast.27, f32[8,12]{1,0:T(8,128)} %bitcast.28), custom_call_target="tpu_custom_call" | custom-call | tf_op jit(solution)/shard_map/pallas_call | solution.py:27
  7.2 0.6 copy-done.5
  7.8 4.3 %shard_map.155 = bf16[8,24,640]{2,1,0:T(8,128)(2,1)} custom-call(bf16[48,1024]{1,0:T(8,128)(2,1)} %q_ref.1, bf16[96,256]{1,0:T(8,128)(2,1)} %reshape.40.new_ref, bf16[832,256]{1,0:T(8,128)(2,1)} %bitcast.24, bf16[832,256]{1,0:T(8,128)(2,1)} %copy-done.3, s32[1,128]{1,0:T(1,128)} %copy-done.4, s32[1,128]{1,0:T(1,128)} %copy-done.5, ...), custom_call_target="tpu_custom_call" | custom-call | tf_op jit(solution)/shard_map/pallas_call | solution.py:27
  12.1 11.6 %all_to_all.25 = bf16[8,24,640]{2,1,0:T(8,128)(2,1)S(1)} all-to-all(bf16[8,24,640]{2,1,0:T(8,128)(2,1)} %shard_map.155), channel_id=1, replica_groups=mesh['group'=1,'req'=4,'head'=4,'pool'=2] {'head','pool'}, dimensions={0} | all-to-all | bytes 491520 | tf_op jit(solution)/shard_map/all_to_all | solution.py:199
  23.8 10.6 %all_to_all.26 = bf16[4,24,640]{2,1,0:T(8,128)(2,1)S(1)} all-to-all(bf16[4,24,640]{2,1,0:T(8,128)(2,1)S(1)} %broadcast_in_dim.4), channel_id=1, replica_groups=mesh['group'=1,'req'=4,'head'=4,'pool'=2] {'req'}, dimensions={0} | all-to-all | bytes 245760 | tf_op jit(solution)/shard_map/all_to_all | solution.py:199
  34.4 0.8 %broadcast_in_dim.5 = bf16[4,4,24,512]{3,2,1,0:T(8,128)(2,1)} broadcast(bf16[4,24,512]{2,1,0:T(8,128)(2,1)S(1)} %slice.8), dimensions={1,2,3} | broadcast | bytes 491520 | tf_op jit(solution)/shard_map/broadcast_in_dim | solution.py:203
  35.2 3.5 %all-to-all-start.2 = ((bf16[4,4,24,512]{3,2,1,0:T(8,128)(2,1)}), bf16[4,4,24,512]{3,2,1,0:T(8,128)(2,1)S(1)}, u32[]{:S(2)}, u32[]{:S(2)}) async-start(bf16[4,4,24,512]{3,2,1,0:T(8,128)(2,1)} %broadcast_in_dim.5), calls=%async_computation.2 | async-start | bytes 786432 | tf_op jit(solution)/shard_map/all_to_all | solution.py:199
  38.7 0.6 slice.9.mix_ref
  39.3 5.2 %all-to-all-done.2.blocks_ref = bf16[4,4,24,512]{3,2,1,0:T(8,128)(2,1)S(1)} async-done(((bf16[4,4,24,512]{3,2,1,0:T(8,128)(2,1)}), bf16[4,4,24,512]{3,2,1,0:T(8,128)(2,1)S(1)}, u32[]{:S(2)}, u32[]{:S(2)}) %all-to-all-start.2) | async-done | bytes 393248 | tf_op jit(solution)/shard_map/all_to_all | solution.py:199
  44.5 0.7 %copy-done.1 = bf16[4,4,24,512]{3,2,1,0:T(8,128)(2,1)} copy-done((bf16[4,4,24,512]{3,2,1,0:T(8,128)(2,1)}, bf16[4,4,24,512]{3,2,1,0:T(8,128)(2,1)S(1)}, u32[]{:S(2)}) %copy-start.1) | copy-done | bytes 393240
  45.2 0.3 copy-done.2
  45.5 0.5 copy-done
  46.1 5.2 %shard_map.156 = bf16[4,24,2048]{2,1,0:T(8,128)(2,1)} custom-call(bf16[4,4,24,512]{3,2,1,0:T(8,128)(2,1)} %copy-done.1, bf16[4,24,128]{2,1,0:T(8,128)(2,1)} %slice.9.mix_ref, bf16[384,2048]{1,0:T(8,128)(2,1)} %bitcast.18, bf16[384,2048]{1,0:T(8,128)(2,1)} %copy-done, bf16[192,2048]{1,0:T(8,128)(2,1)} %bitcast.20, bf16[192,2048]{1,0:T(8,128)(2,1)} %copy-done.2, ...), custom_call_target="tpu_custom_call" | custom-call | tf_op jit(solution)/shard_map/pallas_call | solution.py:27
  51.3 9.9 %all_to_all.27 = bf16[4,24,2048]{2,1,0:T(8,128)(2,1)S(1)} all-to-all(bf16[4,24,2048]{2,1,0:T(8,128)(2,1)} %shard_map.156), channel_id=1, replica_groups=mesh['group'=1,'req'=4,'head'=4,'pool'=2] {'head'}, dimensions={0} | all-to-all | bytes 786432 | tf_op jit(solution)/shard_map/all_to_all | solution.py:199
  61.2 0.1 reduce_sum.34
  61.3 9.2 %all_to_all.28 = bf16[8,6,1024]{2,1,0:T(8,128)(2,1)S(1)} all-to-all(bf16[8,6,1024]{2,1,0:T(8,128)(2,1)S(1)} %bitcast.22), channel_id=1, replica_groups=mesh['group'=1,'req'=4,'head'=4,'pool'=2] {'req','pool'}, dimensions={0} | all-to-all | bytes 196608 | tf_op jit(solution)/shard_map/all_to_all | solution.py:199
  70.5 0.6 convert_element_type.19
  (18 shorter events, 0.2 us)
Async XLA Ops:
  0.0 2.1 %collective-permute-start = (bf16[832,256]{1,0:T(8,128)(2,1)}, bf16[832,256]{1,0:T(8,128)(2,1)S(1)}, u32[]{:S(2)}, u32[]{:S(2)}) collective-permute-start(bf16[832,256]{1,0:T(8,128)(2,1)} %bitcast.23), channel_id=1, source_target_pairs={{0,1},{1,0},{2,3},{3,2},{4,5},{5,4},{6,7},{7,6},{8,9},{9,8},{10,11... | collective-permute-start | bytes 1277960 | tf_op jit(solution)/shard_map/ppermute | solution.py:19
  2.1 5.2 %copy-start.3 = (bf16[832,256]{1,0:T(8,128)(2,1)}, bf16[832,256]{1,0:T(8,128)(2,1)S(1)}, u32[]{:S(2)}) copy-start(bf16[832,256]{1,0:T(8,128)(2,1)S(1)} %collective-permute-done.other_ref) | copy-start | bytes 1277956
  2.1 42.4 %collective-permute-start.2 = (bf16[384,2048]{1,0:T(8,128)(2,1)}, bf16[384,2048]{1,0:T(8,128)(2,1)S(1)}, u32[]{:S(2)}, u32[]{:S(2)}) collective-permute-start(bf16[384,2048]{1,0:T(8,128)(2,1)} %bitcast.17), channel_id=1, source_target_pairs={{0,1},{1,0},{2,3},{3,2},{4,5},{5,4},{6,7},{7,6},{8,9},{9,8},{10,11... | collective-permute-start | bytes 4718600 | tf_op jit(solution)/shard_map/ppermute | solution.py:19
  3.2 41.3 %collective-permute-start.3 = (bf16[192,2048]{1,0:T(8,128)(2,1)}, bf16[192,2048]{1,0:T(8,128)(2,1)S(1)}, u32[]{:S(2)}, u32[]{:S(2)}) collective-permute-start(bf16[192,2048]{1,0:T(8,128)(2,1)} %bitcast.19), channel_id=1, source_target_pairs={{0,1},{1,0},{2,3},{3,2},{4,5},{5,4},{6,7},{7,6},{8,9},{9,8},{10,11... | collective-permute-start | bytes 2359304 | tf_op jit(solution)/shard_map/ppermute | solution.py:19
  3.4 3.8 %copy-start.4 = (s32[1,128]{1,0:T(1,128)}, s32[1,128]{1,0:T(1,128)S(1)}, u32[]{:S(2)}) copy-start(s32[1,128]{1,0:T(1,128)S(1)} %pad_bitcast_fusion.own_ints_ref) | copy-start | bytes 1540
  3.4 3.8 %collective-permute-start.1 = (s32[1,128]{1,0:T(1,128)S(1)}, s32[1,128]{1,0:T(1,128)S(1)}, u32[]{:S(2)}, u32[]{:S(2)}) collective-permute-start(s32[1,128]{1,0:T(1,128)S(1)} %pad_bitcast_fusion.own_ints_ref), channel_id=1, source_target_pairs={{0,1},{1,0},{2,3},{3,2},{4,5},{5,4},{6,7},{7,6},{8,9},{9,8},{10,11... | collective-permute-start | bytes 1544 | tf_op jit(solution)/shard_map/ppermute | solution.py:19
  7.2 0.6 copy-start.5
  35.2 9.3 %all-to-all-start.2 = ((bf16[4,4,24,512]{3,2,1,0:T(8,128)(2,1)}), bf16[4,4,24,512]{3,2,1,0:T(8,128)(2,1)S(1)}, u32[]{:S(2)}, u32[]{:S(2)}) async-start(bf16[4,4,24,512]{3,2,1,0:T(8,128)(2,1)} %broadcast_in_dim.5), calls=%async_computation.2 | async-start | bytes 786432 | tf_op jit(solution)/shard_map/all_to_all | solution.py:199
  44.5 0.7 %copy-start.1 = (bf16[4,4,24,512]{3,2,1,0:T(8,128)(2,1)}, bf16[4,4,24,512]{3,2,1,0:T(8,128)(2,1)S(1)}, u32[]{:S(2)}) copy-start(bf16[4,4,24,512]{3,2,1,0:T(8,128)(2,1)S(1)} %all-to-all-done.2.blocks_ref) | copy-start | bytes 1179652
  44.5 1.0 %copy-start.2 = (bf16[192,2048]{1,0:T(8,128)(2,1)}, bf16[192,2048]{1,0:T(8,128)(2,1)S(1)}, u32[]{:S(2)}) copy-start(bf16[192,2048]{1,0:T(8,128)(2,1)S(1)} %collective-permute-done.3.other_down_ref) | copy-start | bytes 2359300
  44.5 1.5 %copy-start = (bf16[384,2048]{1,0:T(8,128)(2,1)}, bf16[384,2048]{1,0:T(8,128)(2,1)S(1)}, u32[]{:S(2)}) copy-start(bf16[384,2048]{1,0:T(8,128)(2,1)S(1)} %collective-permute-done.2.other_up_ref) | copy-start | bytes 4718596

commit v3 on v2

--- a/solution.py
+++ b/solution.py
@@ -10,7 +10,7 @@
 
 F32 = jnp.float32
 BF16 = jnp.bfloat16
-VMEM_LIMIT = 56 * 2**20
+VMEM_LIMIT = 32 * 2**20
 LANES = 128
 
 
@@ -26,12 +26,12 @@
 def kernel_call(body, out_shape, args, scratch=()):
     return pl.pallas_call(
         body,
-        out_shape=out_shape,
+        out_shape=jax.tree.map(lambda out: pltpu.VMEM(out.shape, out.dtype), out_shape),
         in_specs=[pl.BlockSpec(memory_space=pltpu.VMEM)] * len(args),
         out_specs=jax.tree.map(lambda _: pl.BlockSpec(memory_space=pltpu.VMEM), out_shape),
         scratch_shapes=list(scratch),
         compiler_params=pltpu.CompilerParams(vmem_limit_bytes=VMEM_LIMIT),
-    )(*args)
+    )(*[pltpu.with_memory_space_constraint(arg, pltpu.VMEM) for arg in args])
 
 
 def column(row, start, count):
@@ -42,8 +42,8 @@
 
 def place_kernel(sizes, residual_ref, choice_ref, route_ref, placed_ref):
     heads, pools, planes = sizes
-    head = lax.axis_index("head")
-    first = jnp.where(lax.axis_index("pool") == 0, 1.0, 0.0)
+    head, pool = lax.axis_index("head"), lax.axis_index("pool")
+    first = jnp.where(pool == 0, 1.0, 0.0)
     rows_here, width = residual_ref.shape
     part = rows_here // pools
     total = heads * rows_here
@@ -52,11 +52,11 @@
     own = None
     for p in range(pools):
         inside = line - (p * heads * part + head * part)
-        one = (inside >= 0) & (inside < part) & (lane == inside + p * part)
+        one = (inside >= 0) & (inside < part) & (lane == inside + (pool ^ p) * part)
         own = one if own is None else own | one
     spread = jnp.where(own, first, 0.0)
-    placed_ref[:, :width] = dot(spread.astype(BF16), residual_ref[...]).astype(BF16)
     mixes = placed_ref.shape[1] - width
+    placed = dot(spread.astype(BF16), residual_ref[...])
     target = lax.broadcasted_iota(jnp.int32, (total, mixes), 1)
     mix = jnp.zeros((total, mixes), F32)
     for k in range(choice_ref.shape[0]):
@@ -66,10 +66,16 @@
         lanes = (expert % heads) * (mixes // heads) + expert // heads
         mix = mix + jnp.where(target == lanes, high, 0.0)
         mix = mix + jnp.where(target == lanes + planes, weight - high, 0.0)
-    placed_ref[:, width:] = mix.astype(BF16)
-
-
-def attend_kernel(sizes, q_ref, new_ref, own_ref, other_ref, own_ints_ref, other_ints_ref, placed_ref, order_ref, weight_ref, out_ref):
+    columns, share = width // heads, mixes // heads
+    for h in range(heads):
+        start = h * (columns + share)
+        placed_ref[:, start : start + columns] = placed[:, h * columns : (h + 1) * columns].astype(BF16)
+        placed_ref[:, start + columns : start + columns + share] = mix[
+            :, h * share : (h + 1) * share
+        ].astype(BF16)
+
+
+def attend_kernel(sizes, q_ref, new_ref, own_ref, other_ref, own_ints_ref, other_ints_ref, placed_ref, order_ref, weight_ref, own_out_ref, other_out_ref):
     requests, pages, moved, page, heads, pools, head_dim = sizes
     slots = own_ref.shape[0] // page
     here = lax.axis_index("pool")
@@ -136,31 +142,40 @@
     )
     attended = dot(order_ref[...], attended).astype(BF16)
     partial = dot(attended, weight_ref[...])
-    placed = placed_ref[...].astype(F32)
-    partial = partial + placed[:, :width]
     for h in range(heads):
-        for p in range(pools):
-            at = slice(p * rows, (p + 1) * rows)
-            out_ref[h * pools + p, :, :columns] = partial[
-                at, h * columns : (h + 1) * columns
-            ].astype(BF16)
-            out_ref[h * pools + p, :, columns:] = placed[
-                at, width + h * mixes : width + (h + 1) * mixes
-            ].astype(BF16)
-
-
-def expert_kernel(sizes, blocks_ref, mix_ref, own_up_ref, other_up_ref, own_down_ref, other_down_ref, gain_ref, order_ref, out_ref):
+        start = h * (columns + mixes)
+        at = slice(start, start + columns)
+        part = partial[:, h * columns : (h + 1) * columns] + placed_ref[:, at].astype(F32)
+        own_out_ref[:, at] = part[:rows]
+        other_out_ref[:, at] = part[rows:].astype(BF16)
+        at = slice(start + columns, start + columns + mixes)
+        part = placed_ref[:, at].astype(F32)
+        own_out_ref[:, at] = part[:rows]
+        other_out_ref[:, at] = part[rows:].astype(BF16)
+
+
+def split_kernel(own_ref, other_ref, *outs):
+    head = lax.axis_index("head")
+    columns = own_ref.shape[1] // len(outs)
+    for step, out in enumerate(outs):
+        at = pl.ds(pl.multiple_of((head ^ step) * columns, LANES), columns)
+        out[...] = (own_ref[:, at] + other_ref[:, at].astype(F32)).astype(out.dtype)
+
+
+def expert_kernel(sizes, *refs):
     heads, planes = sizes
+    blocks, refs = refs[:heads], refs[heads:]
+    own_up_ref, other_up_ref, own_down_ref, other_down_ref, gain_ref, order_ref = refs[:6]
+    outs = refs[6:]
     head, plane = lax.axis_index("head"), lax.axis_index("req")
-    columns = blocks_ref.shape[3]
-    plane_rows = blocks_ref.shape[2]
+    plane_rows, columns = blocks[1].shape[1:]
     rows = planes * plane_rows
     width = heads * columns
     units = own_down_ref.shape[0]
     squares, projected = 0.0, 0.0
-    for h in range(heads):
-        at = slice(h * columns, (h + 1) * columns)
-        block = blocks_ref[h].astype(F32).reshape(rows, columns)
+    for step in range(heads):
+        at = pl.ds(pl.multiple_of((head ^ step) * columns, LANES), columns)
+        block = blocks[step][:, :, :columns].astype(F32).reshape(rows, columns)
         squares = squares + jnp.sum(block * block, axis=1, keepdims=True)
         block = (block * gain_ref[:, at]).astype(BF16)
         weights = jnp.concatenate(
@@ -170,7 +185,8 @@
         projected = projected + dot(block, weights, ((1,), (1,)))
     projected = projected * lax.rsqrt(squares / width + 1e-06)
     gate, up = projected[:, : 2 * units], projected[:, 2 * units :]
-    mix = mix_ref[...].astype(F32).reshape(rows, mix_ref.shape[2])
+    mix = blocks[0][:, :, columns:].astype(F32)
+    mix = mix.reshape(rows, mix.shape[2])
     lane = lax.broadcasted_iota(jnp.int32, mix.shape, 1)
     route = jnp.sum(
         jnp.where((lane == plane) | (lane == plane + planes), mix, 0.0), axis=1, keepdims=True
@@ -178,29 +194,55 @@
     activated = (gate / (1.0 + jnp.exp(-gate)) * up * route).astype(BF16)
     activated = dot(order_ref[...], activated).astype(BF16)
     down = jnp.concatenate([own_down_ref[...], other_down_ref[...]], axis=0)
-    line = lax.broadcasted_iota(jnp.int32, (rows, columns), 0) - plane * plane_rows
-    here = jnp.where(
-        (line >= 0) & (line < plane_rows), blocks_ref[head].astype(F32).reshape(rows, columns), 0.0
-    )
-    here = dot(order_ref[...], here.astype(BF16))
+    line = lax.broadcasted_iota(jnp.int32, (rows, columns), 0)
+    own = blocks[0][:, :, :columns].astype(F32).reshape(rows, columns)
+    own = dot(order_ref[...], jnp.where(line < plane_rows, own, 0.0).astype(BF16))
+    count = rows // heads
     for h in range(heads):
         at = slice(h * columns, (h + 1) * columns)
-        part = dot(activated, down[:, at]) + jnp.where(head == h, here, 0.0)
-        for to in range(heads):
-            lines = slice(to * rows // heads, (to + 1) * rows // heads)
-            out_ref[to, :, at] = part[lines].astype(BF16)
-
-
-def one_hot(rows):
-    return jnp.asarray(np.eye(len(rows), dtype=np.float32)[np.asarray(rows)], BF16)
-
-
-def exchange(value, axes):
-    return lax.all_to_all(value, axes, split_axis=0, concat_axis=0, tiled=True)
-
-
-def to_all(value, axes):
-    return exchange(jnp.broadcast_to(value[None], (lax.axis_size(axes), *value.shape)), axes)
+        part = dot(activated, down[:, at]) + jnp.where(head == h, own, 0.0)
+        for step, out in enumerate(outs):
+            out[:, at] = part[step * count : (step + 1) * count].astype(out.dtype)
+
+
+def halve_kernel(*refs):
+    parts, (own_ref, other_ref) = refs[:-2], refs[-2:]
+    pool = lax.axis_index("pool")
+    columns = own_ref.shape[1]
+    for out, to in ((own_ref, pool), (other_ref, 1 - pool)):
+        at = pl.ds(pl.multiple_of(to * columns, LANES), columns)
+        out[...] = functools.reduce(
+            jnp.add, [part[:, at].astype(F32) for part in parts]
+        ).astype(BF16)
+
+
+def spread_kernel(own_ref, other_ref, order_ref, *outs):
+    pool = lax.axis_index("pool")
+    own, other = own_ref[...].astype(F32), other_ref[...].astype(F32)
+    both = jnp.concatenate([jnp.where(pool == 0, own, other), jnp.where(pool == 0, other, own)], axis=0)
+    both = both.astype(BF16)
+    columns = both.shape[1] // 2
+    value = dot(order_ref[0], both[:, :columns]) + dot(order_ref[1], both[:, columns:])
+    count = value.shape[0] // len(outs)
+    for step, out in enumerate(outs):
+        out[...] = value[step * count : (step + 1) * count].astype(BF16)
+
+
+def total_kernel(*refs):
+    parts, out_ref = refs[:-1], refs[-1]
+    total = functools.reduce(jnp.add, [part[...].astype(F32) for part in parts])
+    rows, columns = total.shape[0] // 2, total.shape[1]
+    out_ref[:, :columns] = total[:rows].astype(BF16)
+    out_ref[:, columns:] = total[rows:].astype(BF16)
+
+
+def one_hot(rows, count):
+    picked = np.asarray(rows)[..., None] == np.arange(count)
+    return jnp.asarray(picked.astype(np.float32), BF16)
+
+
+def shape(*dims, dtype=BF16):
+    return jax.ShapeDtypeStruct(dims, dtype)
 
 
 def local(
@@ -229,22 +271,24 @@
     columns = width // heads
     mixes = 2 * planes + -2 * planes % LANES
 
-    own_cache = cache_pages.reshape(slots * page, entry)
-    other_cache = send(own_cache, "pool", 1)
     ints = jnp.concatenate(
         [page_table[:, 0, j] for j in range(pages)]
         + [cached_length.reshape(-1), leave_slots, arrive_slots]
     )
     ints = jnp.pad(ints, (0, -ints.shape[0] % LANES)).reshape(1, -1)
+    own_cache = cache_pages.reshape(slots * page, entry)
+    other_cache = send(own_cache, "pool", 1)
     other_ints = send(ints, "pool", 1)
 
+    head, pool = lax.axis_index("head"), lax.axis_index("pool")
     placed = kernel_call(
         functools.partial(place_kernel, (heads, pools, planes)),
-        jax.ShapeDtypeStruct((requests, width + heads * mixes), BF16),
+        shape(requests, heads * (columns + mixes)),
         (residual, expert_choice.T, route_weight.T),
     )
     order = [
-        h * rows_here + p * part + i for p in range(pools) for h in range(heads) for i in range(part)
+        [h * rows_here + (here ^ p) * part + i for p in range(pools) for h in range(heads) for i in range(part)]
+        for here in range(pools)
     ]
     args = (
         queries,
@@ -254,46 +298,70 @@
         ints,
         other_ints,
         placed,
-        one_hot(order),
+        lax.dynamic_index_in_dim(one_hot(order, requests), pool, 0, False),
         output_weight,
     )
+    rows = requests // pools
     sizes = (requests, pages, moved, page, heads, pools, entry // 2)
-    pieces = kernel_call(
+    own, other = kernel_call(
         functools.partial(attend_kernel, sizes),
-        jax.ShapeDtypeStruct((heads * pools, requests // pools, columns + mixes), BF16),
+        [shape(rows, heads * (columns + mixes), dtype=F32), shape(rows, heads * (columns + mixes))],
         args,
     )
-    hidden = jnp.sum(exchange(pieces, ("head", "pool")).astype(F32), axis=0).astype(BF16)
-
-    held = lax.optimization_barrier((gate_up, down_weight, other_cache))
-    other_up = send(held[0].reshape(-1, width), "pool", 1)
-    other_down = send(held[1].reshape(-1, width), "pool", 1)
-
-    plane_blocks = to_all(hidden, "req")
-    blocks = to_all(plane_blocks[:, :, :columns], "head")
+    other = send(other, "pool", 1)
+
+    gate_up, down_weight = gate_up.reshape(-1, width), down_weight.reshape(-1, width)
+    held = lax.optimization_barrier((gate_up, down_weight, other))
+    other_up, other_down = send(held[0], "pool", 1), send(held[1], "pool", 1)
+
+    piece = shape(rows, columns + mixes)
+    pieces = kernel_call(split_kernel, [shape(rows, columns + mixes, dtype=F32)] + [piece] * (heads - 1), (own, other))
+    hidden = pieces[0]
+    for step in range(1, heads):
+        hidden = hidden + send(pieces[step], "head", step).astype(F32)
+    hidden = hidden.astype(BF16)
+
+    plane_blocks = jnp.stack([hidden] + [send(hidden, "req", step) for step in range(1, planes)])
+    sent = plane_blocks[:, :, :columns]
+    blocks = [plane_blocks] + [send(sent, "head", step) for step in range(1, heads)]
     order = [
-        (r * heads + h) * part + i for h in range(heads) for r in range(planes) for i in range(part)
+        [(r * heads + (here ^ h)) * part + i for h in range(heads) for r in range(planes) for i in range(part)]
+        for here in range(heads)
     ]
     args = (
-        blocks,
-        plane_blocks[:, :, columns:],
-        gate_up.reshape(-1, width),
+        *blocks,
+        gate_up,
         other_up,
-        down_weight.reshape(-1, width),
+        down_weight,
         other_down,
         norm_gain.reshape(1, -1),
-        one_hot(order),
-    )
+        lax.dynamic_index_in_dim(one_hot(order, planes * rows), head, 0, False),
+    )
+    piece = shape(planes * part, width)
     pieces = kernel_call(
         functools.partial(expert_kernel, (heads, planes)),
-        jax.ShapeDtypeStruct((heads, planes * part, width), BF16),
+        [shape(planes * part, width, dtype=F32)] + [piece] * (heads - 1),
         args,
     )
-    mixed = jnp.sum(exchange(pieces, "head").astype(F32), axis=0).astype(BF16)
-    mixed = mixed.reshape(planes, part, pools, width // pools).transpose(0, 2, 1, 3)
-    mixed = exchange(mixed.reshape(planes * pools, part, -1), ("req", "pool"))
-    total = jnp.sum(mixed.reshape(planes, pools, part, -1).astype(F32), axis=0)
-    return total.reshape(rows_here, -1).astype(BF16)
+    arrived = [pieces[0]] + [send(pieces[step], "head", step) for step in range(1, heads)]
+    own, other = kernel_call(halve_kernel, [shape(planes * part, width // pools)] * 2, arrived)
+    other = send(other, "pool", 1)
+    order = [
+        [
+            p * planes * part + r * part + i if half == at else -1
+            for r in range(planes)
+            for at in range(2)
+            for p in range(pools)
+            for i in range(part)
+        ]
+        for half in range(2)
+    ]
+    piece = shape(2 * rows_here, width // pools // 2)
+    pieces = kernel_call(
+        spread_kernel, [piece] * planes, (own, other, one_hot(order, pools * planes * part))
+    )
+    arrived = [pieces[0]] + [send(pieces[step], "req", step) for step in range(1, planes)]
+    return kernel_call(total_kernel, shape(rows_here, width // pools), arrived)
 
 
 def solution(mesh):

time: 71.7 us -> 58.7 us (0.82)
  blocking collectives: 41.2 us -> 0 us
  starting transfers between devices: 4.8 us -> 22.1 us
  waiting for transfers between devices: 6.84 us -> 20.7 us
  Pallas kernels: 11.6 us -> 5.75 us
  local copies, waits for them, and re-layouts: 5.69 us -> 8.61 us
    all_to_all x4 -> x0, blocking collectives: 41.2 us -> none  [exchange(): return lax.all_to_all(value, axes, split_axis=0, concat_axis=0, tiled=True)]
    ppermute x4 -> x21, starting transfers between devices: 1.34 us -> 22.1 us  [send(): return lax.ppermute(value, axes, [(i, i ^ step) for i in range(size)])]
    ppermute x4 -> x21, waiting for transfers between devices: 1.61 us -> 20.7 us  [send(): return lax.ppermute(value, axes, [(i, i ^ step) for i in range(size)])]
    pallas_call x3 -> x7, Pallas kernels: 11.6 us -> 5.75 us  [kernel_call(): pl.pallas_call(body, out_shape=jax.tree.map(lambda out: pltpu.VMEM(out.sh...]
    all_to_all x1 -> x0, waiting for transfers between devices: 5.23 us -> none  [exchange(): return lax.all_to_all(value, axes, split_axis=0, concat_axis=0, tiled=True)]
    unnamed x12 -> x19, local copies, waits for them, and re-layouts: 2.13 us -> 6.32 us
    all_to_all x1 -> x0, starting transfers between devices: 3.46 us -> none  [exchange(): return lax.all_to_all(value, axes, split_axis=0, concat_axis=0, tiled=True)]
    squeeze x0 -> x2, local copies, waits for them, and re-layouts: none -> 1.45 us  [the longest x1 0.74 us: local(): lax.dynamic_index_in_dim(one_hot(order, planes * rows), head, 0, False)]
  transfers between devices with their start and end apart: 5 -> 21, of which waited for: 2 -> 15; matrix products, arithmetic and copies ran while one was open for 5% -> 5% of each run, Pallas kernels for 9% -> 1%
where the time goes in v3:
time: 58.7 us; the launch traced here: 58.1 us
  starting transfers between devices  22.1 us (38%)
  waiting for transfers between devices  20.7 us (35%)
  local copies, waits for them, and re-layouts  8.61 us (15%)
  Pallas kernels  5.75 us (10%)
  other arithmetic  0.82 us (1%)
    ppermute x21, starting transfers between devices, send(): return lax.ppermute(value, axes, [(i, i ^ step) for i in range(size)])  22.1 us
    ppermute x21, waiting for transfers between devices, send(): return lax.ppermute(value, axes, [(i, i ^ step) for i in range(size)])  20.7 us
    unnamed x19, local copies, waits for them, and re-layouts  6.32 us
    pallas_call x7, Pallas kernels, kernel_call(): pl.pallas_call(body, out_shape=jax.tree.map(lambda out: pltpu.VMEM(out.sh...  5.75 us
  transfers between devices with their start and end apart: 21, of which 15 were waited for; matrix products, arithmetic and copies ran while one was open for 5% of the time, Pallas kernels for 1%

profile of v3, /device:TPU:0, one launch (start us, length us, event | category | flops | bytes accessed | tf_op | source)
XLA Modules:
  0.0 58.1 jit_solution(535664343922717037)
XLA Ops:
  5.6 1.6 %copy-done = bf16[512,2048]{1,0:T(8,128)(2,1)S(1)} copy-done((bf16[512,2048]{1,0:T(8,128)(2,1)S(1)}, bf16[512,2048]{1,0:T(8,128)(2,1)}, u32[]{:S(2)}) %copy-start) | copy-done | bytes 2097176
  7.2 1.0 %copy-done.2 = bf16[1,52,16,256]{3,2,1,0:T(8,128)(2,1)S(1)} copy-done((bf16[1,52,16,256]{3,2,1,0:T(8,128)(2,1)S(1)}, bf16[1,52,16,256]{3,2,1,0:T(8,128)(2,1)}, u32[]{:S(2)}) %copy-start.2) | copy-done | bytes 426008
  9.1 1.6 %shard_map.164 = (f32[24,2560]{1,0:T(8,128)S(1)}, bf16[24,2560]{1,0:T(8,128)(2,1)S(1)}) custom-call(bf16[48,1024]{1,0:T(8,128)(2,1)S(1)} %copy-done.3, bf16[96,256]{1,0:T(8,128)(2,1)S(1)} %reshape.21.new_ref, bf16[832,256]{1,0:T(8,128)(2,1)S(1)} %bitcast.23, bf16[832,256]{1,0:T(8,128)(2,1)S(1)} %collective-permute-done.other_ref, ...), custom_call_target="tpu_custom_call" | custom-call | tf_op jit(solution)/shard_map/pallas_call | solution.py:27
  11.2 1.0 %collective-permute-done.2.other_ref = bf16[24,2560]{1,0:T(8,128)(2,1)S(1)} collective-permute-done((bf16[24,2560]{1,0:T(8,128)(2,1)S(1)}, bf16[24,2560]{1,0:T(8,128)(2,1)S(1)}, u32[]{:S(2)}, u32[]{:S(2)}) %collective-permute-start.2) | collective-permute-done | bytes 122912 | tf_op jit(solution)/shard_map/ppermute | solution.py:19
  12.7 2.9 %collective-permute-start.3 = (bf16[24,640]{1,0:T(8,128)(2,1)S(1)}, bf16[24,640]{1,0:T(8,128)(2,1)S(1)}, u32[]{:S(2)}, u32[]{:S(2)}) collective-permute-start(bf16[24,640]{1,0:T(8,128)(2,1)S(1)} %get-tuple-element.26), channel_id=1, source_target_pairs={{0,2},{2,0},{4,6},{6,4},{1,3},{3,1},{5,7},{7,5},{8,10},{10,8},{12,... | collective-permute-start | bytes 92168 | tf_op jit(solution)/shard_map/ppermute | solution.py:19
  15.6 1.5 %collective-permute-start.4 = (bf16[24,640]{1,0:T(8,128)(2,1)S(1)}, bf16[24,640]{1,0:T(8,128)(2,1)S(1)}, u32[]{:S(2)}, u32[]{:S(2)}) collective-permute-start(bf16[24,640]{1,0:T(8,128)(2,1)S(1)} %get-tuple-element.27), channel_id=1, source_target_pairs={{0,4},{2,6},{4,0},{6,2},{1,5},{3,7},{5,1},{7,3},{8,12},{10,14},{12... | collective-permute-start | bytes 92168 | tf_op jit(solution)/shard_map/ppermute | solution.py:19
  17.5 2.0 %collective-permute-done.4 = bf16[24,640]{1,0:T(8,128)(2,1)S(1)} collective-permute-done((bf16[24,640]{1,0:T(8,128)(2,1)S(1)}, bf16[24,640]{1,0:T(8,128)(2,1)S(1)}, u32[]{:S(2)}, u32[]{:S(2)}) %collective-permute-start.4) | collective-permute-done | bytes 30752 | tf_op jit(solution)/shard_map/ppermute | solution.py:19
  19.5 2.4 %collective-permute-done.5 = bf16[24,640]{1,0:T(8,128)(2,1)S(1)} collective-permute-done((bf16[24,640]{1,0:T(8,128)(2,1)S(1)}, bf16[24,640]{1,0:T(8,128)(2,1)S(1)}, u32[]{:S(2)}, u32[]{:S(2)}) %collective-permute-start.5) | collective-permute-done | bytes 30752 | tf_op jit(solution)/shard_map/ppermute | solution.py:19
  22.0 3.7 %collective-permute-start.8 = (bf16[24,640]{1,0:T(8,128)(2,1)S(1)}, bf16[24,640]{1,0:T(8,128)(2,1)S(1)}, u32[]{:S(2)}, u32[]{:S(2)}) collective-permute-start(bf16[24,640]{1,0:T(8,128)(2,1)S(1)} %add_convert_fusion), channel_id=1, source_target_pairs={{0,24},{8,16},{16,8},{24,0},{1,25},{9,17},{17,9},{25,1},{2,26},{10... | collective-permute-start | bytes 92168 | tf_op jit(solution)/shard_map/ppermute | solution.py:19
  26.4 1.4 %collective-permute-done.8 = bf16[24,640]{1,0:T(8,128)(2,1)S(1)} collective-permute-done((bf16[24,640]{1,0:T(8,128)(2,1)S(1)}, bf16[24,640]{1,0:T(8,128)(2,1)S(1)}, u32[]{:S(2)}, u32[]{:S(2)}) %collective-permute-start.8) | collective-permute-done | bytes 30752 | tf_op jit(solution)/shard_map/ppermute | solution.py:19
  27.8 2.6 %collective-permute-done.7 = bf16[24,640]{1,0:T(8,128)(2,1)S(1)} collective-permute-done((bf16[24,640]{1,0:T(8,128)(2,1)S(1)}, bf16[24,640]{1,0:T(8,128)(2,1)S(1)}, u32[]{:S(2)}, u32[]{:S(2)}) %collective-permute-start.7) | collective-permute-done | bytes 30752 | tf_op jit(solution)/shard_map/ppermute | solution.py:19
  31.0 1.5 %collective-permute-start.10 = (bf16[4,24,512]{2,1,0:T(8,128)(2,1)S(1)}, bf16[4,24,512]{2,1,0:T(8,128)(2,1)S(1)}, u32[]{:S(2)}, u32[]{:S(2)}) collective-permute-start(bf16[4,24,512]{2,1,0:T(8,128)(2,1)S(1)} %slice.4), channel_id=1, source_target_pairs={{0,4},{2,6},{4,0},{6,2},{1,5},{3,7},{5,1},{7,3},{8,12},{10,14},{12... | collective-permute-start | bytes 294920 | tf_op jit(solution)/shard_map/ppermute | solution.py:19
  32.5 1.5 %collective-permute-start.9 = (bf16[4,24,512]{2,1,0:T(8,128)(2,1)S(1)}, bf16[4,24,512]{2,1,0:T(8,128)(2,1)S(1)}, u32[]{:S(2)}, u32[]{:S(2)}) collective-permute-start(bf16[4,24,512]{2,1,0:T(8,128)(2,1)S(1)} %slice.4), channel_id=1, source_target_pairs={{0,2},{2,0},{4,6},{6,4},{1,3},{3,1},{5,7},{7,5},{8,10},{10,8},{12,... | collective-permute-start | bytes 294920 | tf_op jit(solution)/shard_map/ppermute | solution.py:19
  34.8 1.4 %collective-permute-done.11.refs_3_ = bf16[4,24,512]{2,1,0:T(8,128)(2,1)S(1)} collective-permute-done((bf16[4,24,512]{2,1,0:T(8,128)(2,1)S(1)}, bf16[4,24,512]{2,1,0:T(8,128)(2,1)S(1)}, u32[]{:S(2)}, u32[]{:S(2)}) %collective-permute-start.11) | collective-permute-done | bytes 98336 | tf_op jit(solution)/shard_map/ppermute | solution.py:19
  37.2 3.4 %shard_map.166 = (f32[24,2048]{1,0:T(8,128)S(1)}, bf16[24,2048]{1,0:T(8,128)(2,1)S(1)}, bf16[24,2048]{1,0:T(8,128)(2,1)S(1)}, bf16[24,2048]{1,0:T(8,128)(2,1)S(1)}) custom-call(bf16[4,24,640]{2,1,0:T(8,128)(2,1)S(1)} %pad_maximum_fusion.refs_0_, bf16[4,24,512]{2,1,0:T(8,128)(2,1)S(1)} %collective-permute-done.9.refs_1_, ...), custom_call_target="tpu_custom_call" | custom-call | tf_op jit(solution)/shard_map/pallas_call | solution.py:27
  40.6 1.6 %collective-permute-start.14 = (bf16[24,2048]{1,0:T(8,128)(2,1)S(1)}, bf16[24,2048]{1,0:T(8,128)(2,1)S(1)}, u32[]{:S(2)}, u32[]{:S(2)}) collective-permute-start(bf16[24,2048]{1,0:T(8,128)(2,1)S(1)} %get-tuple-element.32), channel_id=1, source_target_pairs={{0,2},{2,0},{4,6},{6,4},{1,3},{3,1},{5,7},{7,5},{8,10},{10,8},{12,... | collective-permute-start | bytes 294920 | tf_op jit(solution)/shard_map/ppermute | solution.py:19
  42.6 1.5 %collective-permute-start.16 = (bf16[24,2048]{1,0:T(8,128)(2,1)S(1)}, bf16[24,2048]{1,0:T(8,128)(2,1)S(1)}, u32[]{:S(2)}, u32[]{:S(2)}) collective-permute-start(bf16[24,2048]{1,0:T(8,128)(2,1)S(1)} %get-tuple-element.34), channel_id=1, source_target_pairs={{0,6},{2,4},{4,2},{6,0},{1,7},{3,5},{5,3},{7,1},{8,14},{10,12},{12... | collective-permute-start | bytes 294920 | tf_op jit(solution)/shard_map/ppermute | solution.py:19
  44.1 1.1 %collective-permute-done.14.refs_1_ = bf16[24,2048]{1,0:T(8,128)(2,1)S(1)} collective-permute-done((bf16[24,2048]{1,0:T(8,128)(2,1)S(1)}, bf16[24,2048]{1,0:T(8,128)(2,1)S(1)}, u32[]{:S(2)}, u32[]{:S(2)}) %collective-permute-start.14) | collective-permute-done | bytes 98336 | tf_op jit(solution)/shard_map/ppermute | solution.py:19
  45.3 1.5 %collective-permute-done.15.refs_2_ = bf16[24,2048]{1,0:T(8,128)(2,1)S(1)} collective-permute-done((bf16[24,2048]{1,0:T(8,128)(2,1)S(1)}, bf16[24,2048]{1,0:T(8,128)(2,1)S(1)}, u32[]{:S(2)}, u32[]{:S(2)}) %collective-permute-start.15) | collective-permute-done | bytes 98336 | tf_op jit(solution)/shard_map/ppermute | solution.py:19
  46.8 1.4 %collective-permute-done.16.refs_3_ = bf16[24,2048]{1,0:T(8,128)(2,1)S(1)} collective-permute-done((bf16[24,2048]{1,0:T(8,128)(2,1)S(1)}, bf16[24,2048]{1,0:T(8,128)(2,1)S(1)}, u32[]{:S(2)}, u32[]{:S(2)}) %collective-permute-start.16) | collective-permute-done | bytes 98336 | tf_op jit(solution)/shard_map/ppermute | solution.py:19
  48.3 1.2 %collective-permute-done.17.other_ref = bf16[24,1024]{1,0:T(8,128)(2,1)S(1)} collective-permute-done((bf16[24,1024]{1,0:T(8,128)(2,1)S(1)}, bf16[24,1024]{1,0:T(8,128)(2,1)S(1)}, u32[]{:S(2)}, u32[]{:S(2)}) %collective-permute-start.17) | collective-permute-done | bytes 49184 | tf_op jit(solution)/shard_map/ppermute | solution.py:19
  49.8 2.1 %collective-permute-start.19 = (bf16[24,512]{1,0:T(8,128)(2,1)S(1)}, bf16[24,512]{1,0:T(8,128)(2,1)S(1)}, u32[]{:S(2)}, u32[]{:S(2)}) collective-permute-start(bf16[24,512]{1,0:T(8,128)(2,1)S(1)} %get-tuple-element.39), channel_id=1, source_target_pairs={{0,16},{8,24},{16,0},{24,8},{1,17},{9,25},{17,1},{25,9},{2,18},{10... | collective-permute-start | bytes 73736 | tf_op jit(solution)/shard_map/ppermute | solution.py:19
  51.9 2.3 %collective-permute-start.20 = (bf16[24,512]{1,0:T(8,128)(2,1)S(1)}, bf16[24,512]{1,0:T(8,128)(2,1)S(1)}, u32[]{:S(2)}, u32[]{:S(2)}) collective-permute-start(bf16[24,512]{1,0:T(8,128)(2,1)S(1)} %get-tuple-element.40), channel_id=1, source_target_pairs={{0,24},{8,16},{16,8},{24,0},{1,25},{9,17},{17,9},{25,1},{2,26},{10... | collective-permute-start | bytes 73736 | tf_op jit(solution)/shard_map/ppermute | solution.py:19
  54.6 2.9 %collective-permute-done.20.refs_3_ = bf16[24,512]{1,0:T(8,128)(2,1)S(1)} collective-permute-done((bf16[24,512]{1,0:T(8,128)(2,1)S(1)}, bf16[24,512]{1,0:T(8,128)(2,1)S(1)}, u32[]{:S(2)}, u32[]{:S(2)}) %collective-permute-start.20) | collective-permute-done | bytes 24608 | tf_op jit(solution)/shard_map/ppermute | solution.py:19
  (52 shorter events, 12.9 us)
Async XLA Ops:
  0.0 5.6 %collective-permute-start = (bf16[832,256]{1,0:T(8,128)(2,1)}, bf16[832,256]{1,0:T(8,128)(2,1)S(1)}, u32[]{:S(2)}, u32[]{:S(2)}) collective-permute-start(bf16[832,256]{1,0:T(8,128)(2,1)} %bitcast.22), channel_id=1, source_target_pairs={{0,1},{1,0},{2,3},{3,2},{4,5},{5,4},{6,7},{7,6},{8,9},{9,8},{10,11... | collective-permute-start | bytes 1277960 | tf_op jit(solution)/shard_map/ppermute | solution.py:19
  1.2 4.4 %collective-permute-start.1 = (s32[1,128]{1,0:T(1,128)S(1)}, s32[1,128]{1,0:T(1,128)S(1)}, u32[]{:S(2)}, u32[]{:S(2)}) collective-permute-start(s32[1,128]{1,0:T(1,128)S(1)} %pad_bitcast_fusion.own_ints_ref), channel_id=1, source_target_pairs={{0,1},{1,0},{2,3},{3,2},{4,5},{5,4},{6,7},{7,6},{8,9},{9,8},{10,11... | collective-permute-start | bytes 1544 | tf_op jit(solution)/shard_map/ppermute | solution.py:19
  5.1 32.1 %copy-start.6 = (f32[2048]{0:T(1024)S(1)}, f32[2048]{0:T(1024)}, u32[]{:S(2)}) copy-start(f32[2048]{0:T(1024)} %param.25) | copy-start | bytes 24580
  9.1 3.1 %copy-start.1 = (bf16[1,2,192,2048]{3,2,1,0:T(8,128)(2,1)S(1)}, bf16[1,2,192,2048]{3,2,1,0:T(8,128)(2,1)}, u32[]{:S(2)}) copy-start(bf16[1,2,192,2048]{3,2,1,0:T(8,128)(2,1)} %param.29) | copy-start | bytes 4718596
  10.7 1.5 %collective-permute-start.2 = (bf16[24,2560]{1,0:T(8,128)(2,1)S(1)}, bf16[24,2560]{1,0:T(8,128)(2,1)S(1)}, u32[]{:S(2)}, u32[]{:S(2)}) collective-permute-start(bf16[24,2560]{1,0:T(8,128)(2,1)S(1)} %get-tuple-element.24), channel_id=1, source_target_pairs={{0,1},{1,0},{2,3},{3,2},{4,5},{5,4},{6,7},{7,6},{8,9},{9,8},{10,11... | collective-permute-start | bytes 368648 | tf_op jit(solution)/shard_map/ppermute | solution.py:19
  12.2 25.0 %collective-permute-start.12 = (bf16[384,2048]{1,0:T(8,128)(2,1)S(1)}, bf16[384,2048]{1,0:T(8,128)(2,1)S(1)}, u32[]{:S(2)}, u32[]{:S(2)}) collective-permute-start(bf16[384,2048]{1,0:T(8,128)(2,1)S(1)} %bitcast.20), channel_id=1, source_target_pairs={{0,1},{1,0},{2,3},{3,2},{4,5},{5,4},{6,7},{7,6},{8,9},{9,8},{10,11... | collective-permute-start | bytes 4718600 | tf_op jit(solution)/shard_map/ppermute | solution.py:19
  12.5 24.6 %collective-permute-start.13 = (bf16[192,2048]{1,0:T(8,128)(2,1)}, bf16[192,2048]{1,0:T(8,128)(2,1)}, u32[]{:S(2)}, u32[]{:S(2)}) collective-permute-start(bf16[192,2048]{1,0:T(8,128)(2,1)} %bitcast.12.refs_6_), channel_id=1, source_target_pairs={{0,1},{1,0},{2,3},{3,2},{4,5},{5,4},{6,7},{7,6},{8,9},{9,8},{10,11... | collective-permute-start | bytes 2359304 | tf_op jit(solution)/shard_map/ppermute | solution.py:19
  12.7 4.8 %collective-permute-start.3 = (bf16[24,640]{1,0:T(8,128)(2,1)S(1)}, bf16[24,640]{1,0:T(8,128)(2,1)S(1)}, u32[]{:S(2)}, u32[]{:S(2)}) collective-permute-start(bf16[24,640]{1,0:T(8,128)(2,1)S(1)} %get-tuple-element.26), channel_id=1, source_target_pairs={{0,2},{2,0},{4,6},{6,4},{1,3},{3,1},{5,7},{7,5},{8,10},{10,8},{12,... | collective-permute-start | bytes 92168 | tf_op jit(solution)/shard_map/ppermute | solution.py:19
  15.6 3.9 %collective-permute-start.4 = (bf16[24,640]{1,0:T(8,128)(2,1)S(1)}, bf16[24,640]{1,0:T(8,128)(2,1)S(1)}, u32[]{:S(2)}, u32[]{:S(2)}) collective-permute-start(bf16[24,640]{1,0:T(8,128)(2,1)S(1)} %get-tuple-element.27), channel_id=1, source_target_pairs={{0,4},{2,6},{4,0},{6,2},{1,5},{3,7},{5,1},{7,3},{8,12},{10,14},{12... | collective-permute-start | bytes 92168 | tf_op jit(solution)/shard_map/ppermute | solution.py:19
  17.2 4.8 %collective-permute-start.5 = (bf16[24,640]{1,0:T(8,128)(2,1)S(1)}, bf16[24,640]{1,0:T(8,128)(2,1)S(1)}, u32[]{:S(2)}, u32[]{:S(2)}) collective-permute-start(bf16[24,640]{1,0:T(8,128)(2,1)S(1)} %get-tuple-element.28), channel_id=1, source_target_pairs={{0,6},{2,4},{4,2},{6,0},{1,7},{3,5},{5,3},{7,1},{8,14},{10,12},{12... | collective-permute-start | bytes 92168 | tf_op jit(solution)/shard_map/ppermute | solution.py:19
  22.0 5.9 %collective-permute-start.8 = (bf16[24,640]{1,0:T(8,128)(2,1)S(1)}, bf16[24,640]{1,0:T(8,128)(2,1)S(1)}, u32[]{:S(2)}, u32[]{:S(2)}) collective-permute-start(bf16[24,640]{1,0:T(8,128)(2,1)S(1)} %add_convert_fusion), channel_id=1, source_target_pairs={{0,24},{8,16},{16,8},{24,0},{1,25},{9,17},{17,9},{25,1},{2,26},{10... | collective-permute-start | bytes 92168 | tf_op jit(solution)/shard_map/ppermute | solution.py:19
  25.6 4.8 %collective-permute-start.7 = (bf16[24,640]{1,0:T(8,128)(2,1)S(1)}, bf16[24,640]{1,0:T(8,128)(2,1)S(1)}, u32[]{:S(2)}, u32[]{:S(2)}) collective-permute-start(bf16[24,640]{1,0:T(8,128)(2,1)S(1)} %add_convert_fusion), channel_id=1, source_target_pairs={{0,16},{8,24},{16,0},{24,8},{1,17},{9,25},{17,1},{25,9},{2,18},{10... | collective-permute-start | bytes 92168 | tf_op jit(solution)/shard_map/ppermute | solution.py:19
  25.6 4.8 %collective-permute-start.6 = (bf16[24,640]{1,0:T(8,128)(2,1)S(1)}, bf16[24,640]{1,0:T(8,128)(2,1)S(1)}, u32[]{:S(2)}, u32[]{:S(2)}) collective-permute-start(bf16[24,640]{1,0:T(8,128)(2,1)S(1)} %add_convert_fusion), channel_id=1, source_target_pairs={{0,8},{8,0},{16,24},{24,16},{1,9},{9,1},{17,25},{25,17},{2,10},{10... | collective-permute-start | bytes 92168 | tf_op jit(solution)/shard_map/ppermute | solution.py:19
  30.5 5.7 %collective-permute-start.11 = (bf16[4,24,512]{2,1,0:T(8,128)(2,1)S(1)}, bf16[4,24,512]{2,1,0:T(8,128)(2,1)S(1)}, u32[]{:S(2)}, u32[]{:S(2)}) collective-permute-start(bf16[4,24,512]{2,1,0:T(8,128)(2,1)S(1)} %slice.4), channel_id=1, source_target_pairs={{0,6},{2,4},{4,2},{6,0},{1,7},{3,5},{5,3},{7,1},{8,14},{10,12},{12... | collective-permute-start | bytes 294920 | tf_op jit(solution)/shard_map/ppermute | solution.py:19
  31.0 5.7 %collective-permute-start.10 = (bf16[4,24,512]{2,1,0:T(8,128)(2,1)S(1)}, bf16[4,24,512]{2,1,0:T(8,128)(2,1)S(1)}, u32[]{:S(2)}, u32[]{:S(2)}) collective-permute-start(bf16[4,24,512]{2,1,0:T(8,128)(2,1)S(1)} %slice.4), channel_id=1, source_target_pairs={{0,4},{2,6},{4,0},{6,2},{1,5},{3,7},{5,1},{7,3},{8,12},{10,14},{12... | collective-permute-start | bytes 294920 | tf_op jit(solution)/shard_map/ppermute | solution.py:19
  32.5 4.6 %collective-permute-start.9 = (bf16[4,24,512]{2,1,0:T(8,128)(2,1)S(1)}, bf16[4,24,512]{2,1,0:T(8,128)(2,1)S(1)}, u32[]{:S(2)}, u32[]{:S(2)}) collective-permute-start(bf16[4,24,512]{2,1,0:T(8,128)(2,1)S(1)} %slice.4), channel_id=1, source_target_pairs={{0,2},{2,0},{4,6},{6,4},{1,3},{3,1},{5,7},{7,5},{8,10},{10,8},{12,... | collective-permute-start | bytes 294920 | tf_op jit(solution)/shard_map/ppermute | solution.py:19
  37.2 12.4 %copy-start.5 = (bf16[2,96,48]{2,1,0:T(8,128)(2,1)S(1)}, bf16[2,96,48]{2,1,0:T(8,128)(2,1)}, u32[]{:S(2)}) copy-start(bf16[2,96,48]{2,1,0:T(8,128)(2,1)} %constant.28.clone.order_ref) | copy-start | bytes 55300
  40.6 4.7 %collective-permute-start.14 = (bf16[24,2048]{1,0:T(8,128)(2,1)S(1)}, bf16[24,2048]{1,0:T(8,128)(2,1)S(1)}, u32[]{:S(2)}, u32[]{:S(2)}) collective-permute-start(bf16[24,2048]{1,0:T(8,128)(2,1)S(1)} %get-tuple-element.32), channel_id=1, source_target_pairs={{0,2},{2,0},{4,6},{6,4},{1,3},{3,1},{5,7},{7,5},{8,10},{10,8},{12,... | collective-permute-start | bytes 294920 | tf_op jit(solution)/shard_map/ppermute | solution.py:19
  42.1 4.6 %collective-permute-start.15 = (bf16[24,2048]{1,0:T(8,128)(2,1)S(1)}, bf16[24,2048]{1,0:T(8,128)(2,1)S(1)}, u32[]{:S(2)}, u32[]{:S(2)}) collective-permute-start(bf16[24,2048]{1,0:T(8,128)(2,1)S(1)} %get-tuple-element.33), channel_id=1, source_target_pairs={{0,4},{2,6},{4,0},{6,2},{1,5},{3,7},{5,1},{7,3},{8,12},{10,14},{12... | collective-permute-start | bytes 294920 | tf_op jit(solution)/shard_map/ppermute | solution.py:19
  42.6 5.5 %collective-permute-start.16 = (bf16[24,2048]{1,0:T(8,128)(2,1)S(1)}, bf16[24,2048]{1,0:T(8,128)(2,1)S(1)}, u32[]{:S(2)}, u32[]{:S(2)}) collective-permute-start(bf16[24,2048]{1,0:T(8,128)(2,1)S(1)} %get-tuple-element.34), channel_id=1, source_target_pairs={{0,6},{2,4},{4,2},{6,0},{1,7},{3,5},{5,3},{7,1},{8,14},{10,12},{12... | collective-permute-start | bytes 294920 | tf_op jit(solution)/shard_map/ppermute | solution.py:19
  48.2 1.3 %collective-permute-start.17 = (bf16[24,1024]{1,0:T(8,128)(2,1)S(1)}, bf16[24,1024]{1,0:T(8,128)(2,1)S(1)}, u32[]{:S(2)}, u32[]{:S(2)}) collective-permute-start(bf16[24,1024]{1,0:T(8,128)(2,1)S(1)} %get-tuple-element.36), channel_id=1, source_target_pairs={{0,1},{1,0},{2,3},{3,2},{4,5},{5,4},{6,7},{7,6},{8,9},{9,8},{10,11... | collective-permute-start | bytes 147464 | tf_op jit(solution)/shard_map/ppermute | solution.py:19
  49.7 4.5 %collective-permute-start.18 = (bf16[24,512]{1,0:T(8,128)(2,1)S(1)}, bf16[24,512]{1,0:T(8,128)(2,1)S(1)}, u32[]{:S(2)}, u32[]{:S(2)}) collective-permute-start(bf16[24,512]{1,0:T(8,128)(2,1)S(1)} %get-tuple-element.38), channel_id=1, source_target_pairs={{0,8},{8,0},{16,24},{24,16},{1,9},{9,1},{17,25},{25,17},{2,10},{10... | collective-permute-start | bytes 73736 | tf_op jit(solution)/shard_map/ppermute | solution.py:19
  49.8 4.8 %collective-permute-start.19 = (bf16[24,512]{1,0:T(8,128)(2,1)S(1)}, bf16[24,512]{1,0:T(8,128)(2,1)S(1)}, u32[]{:S(2)}, u32[]{:S(2)}) collective-permute-start(bf16[24,512]{1,0:T(8,128)(2,1)S(1)} %get-tuple-element.39), channel_id=1, source_target_pairs={{0,16},{8,24},{16,0},{24,8},{1,17},{9,25},{17,1},{25,9},{2,18},{10... | collective-permute-start | bytes 73736 | tf_op jit(solution)/shard_map/ppermute | solution.py:19
  51.9 5.6 %collective-permute-start.20 = (bf16[24,512]{1,0:T(8,128)(2,1)S(1)}, bf16[24,512]{1,0:T(8,128)(2,1)S(1)}, u32[]{:S(2)}, u32[]{:S(2)}) collective-permute-start(bf16[24,512]{1,0:T(8,128)(2,1)S(1)} %get-tuple-element.40), channel_id=1, source_target_pairs={{0,24},{8,16},{16,8},{24,0},{1,25},{9,17},{17,9},{25,1},{2,26},{10... | collective-permute-start | bytes 73736 | tf_op jit(solution)/shard_map/ppermute | solution.py:19
  (6 other events, 5.7 us)

commit v4 on v3

--- a/solution.py
+++ b/solution.py
@@ -23,15 +23,20 @@
     return lax.dot_general(a, b, (contract, ((), ())), preferred_element_type=F32)
 
 
-def kernel_call(body, out_shape, args, scratch=()):
+def kernel_call(body, out_shape, args, scratch=(), outside=()):
     return pl.pallas_call(
         body,
         out_shape=jax.tree.map(lambda out: pltpu.VMEM(out.shape, out.dtype), out_shape),
-        in_specs=[pl.BlockSpec(memory_space=pltpu.VMEM)] * len(args),
+        in_specs=[pl.BlockSpec(memory_space=pl.ANY)] * len(outside)
+        + [pl.BlockSpec(memory_space=pltpu.VMEM)] * len(args),
         out_specs=jax.tree.map(lambda _: pl.BlockSpec(memory_space=pltpu.VMEM), out_shape),
         scratch_shapes=list(scratch),
         compiler_params=pltpu.CompilerParams(vmem_limit_bytes=VMEM_LIMIT),
-    )(*[pltpu.with_memory_space_constraint(arg, pltpu.VMEM) for arg in args])
+    )(*outside, *args)
+
+
+def held(*args):
+    return [pltpu.with_memory_space_constraint(arg, pltpu.VMEM) for arg in args]
 
 
 def column(row, start, count):
@@ -40,9 +45,19 @@
     return jnp.sum(jnp.where(lane == line + start, row, 0.0), axis=1, keepdims=True)
 
 
-def place_kernel(sizes, residual_ref, choice_ref, route_ref, placed_ref):
-    heads, pools, planes = sizes
+def place_kernel(sizes, *refs):
+    heads, pools, planes, count = sizes
+    sources, refs = refs[:count], refs[count:]
+    residual_ref, choice_ref, route_ref, placed_ref = refs[:4]
+    targets, semaphores = refs[4 : 4 + count], refs[-1]
     head, pool = lax.axis_index("head"), lax.axis_index("pool")
+    picked = {count - 2: pool, count - 1: head}
+    copies = []
+    for i in range(count):
+        source = sources[i].at[picked[i]] if i in picked else sources[i]
+        copies.append(pltpu.make_async_copy(source, targets[i], semaphores.at[i]))
+    for copy in copies:
+        copy.start()
     first = jnp.where(pool == 0, 1.0, 0.0)
     rows_here, width = residual_ref.shape
     part = rows_here // pools
@@ -73,6 +88,8 @@
         placed_ref[:, start + columns : start + columns + share] = mix[
             :, h * share : (h + 1) * share
         ].astype(BF16)
+    for copy in copies:
+        copy.wait()
 
 
 def attend_kernel(sizes, q_ref, new_ref, own_ref, other_ref, own_ints_ref, other_ints_ref, placed_ref, order_ref, weight_ref, own_out_ref, other_out_ref):
@@ -162,45 +179,54 @@
         out[...] = (own_ref[:, at] + other_ref[:, at].astype(F32)).astype(out.dtype)
 
 
-def expert_kernel(sizes, *refs):
-    heads, planes = sizes
-    blocks, refs = refs[:heads], refs[heads:]
-    own_up_ref, other_up_ref, own_down_ref, other_down_ref, gain_ref, order_ref = refs[:6]
-    outs = refs[6:]
-    head, plane = lax.axis_index("head"), lax.axis_index("req")
-    plane_rows, columns = blocks[1].shape[1:]
+def project_kernel(step, planes, block_ref, own_up_ref, other_up_ref, gain_ref, *refs):
+    head = lax.axis_index("head")
+    plane_rows = block_ref.shape[1]
     rows = planes * plane_rows
-    width = heads * columns
-    units = own_down_ref.shape[0]
-    squares, projected = 0.0, 0.0
-    for step in range(heads):
-        at = pl.ds(pl.multiple_of((head ^ step) * columns, LANES), columns)
-        block = blocks[step][:, :, :columns].astype(F32).reshape(rows, columns)
-        squares = squares + jnp.sum(block * block, axis=1, keepdims=True)
-        block = (block * gain_ref[:, at]).astype(BF16)
-        weights = jnp.concatenate(
-            [own_up_ref[:units, at], other_up_ref[:units, at], own_up_ref[units:, at], other_up_ref[units:, at]],
-            axis=0,
-        )
-        projected = projected + dot(block, weights, ((1,), (1,)))
-    projected = projected * lax.rsqrt(squares / width + 1e-06)
-    gate, up = projected[:, : 2 * units], projected[:, 2 * units :]
-    mix = blocks[0][:, :, columns:].astype(F32)
+    columns = gain_ref.shape[1] // lax.axis_size("head")
+    units = own_up_ref.shape[0] // 2
+    at = pl.ds(pl.multiple_of((head ^ step) * columns, LANES), columns)
+    block = block_ref[:, :, :columns].astype(F32).reshape(rows, columns)
+    scaled = (block * gain_ref[:, at]).astype(BF16)
+    weights = jnp.concatenate(
+        [own_up_ref[:units, at], other_up_ref[:units, at], own_up_ref[units:, at], other_up_ref[units:, at]],
+        axis=0,
+    )
+    projected = dot(scaled, weights, ((1,), (1,)))
+    squares = jnp.sum(block * block, axis=1, keepdims=True)
+    if step:
+        before_ref, before_squares_ref, projected_ref, squares_ref = refs
+        projected_ref[...] = before_ref[...] + projected
+        squares_ref[...] = before_squares_ref[...] + squares
+        return
+    order_ref, projected_ref, squares_ref, route_ref, own_ref = refs
+    projected_ref[...] = projected
+    squares_ref[...] = squares
+    plane = lax.axis_index("req")
+    mix = block_ref[:, :, columns:].astype(F32)
     mix = mix.reshape(rows, mix.shape[2])
     lane = lax.broadcasted_iota(jnp.int32, mix.shape, 1)
-    route = jnp.sum(
+    route_ref[...] = jnp.sum(
         jnp.where((lane == plane) | (lane == plane + planes), mix, 0.0), axis=1, keepdims=True
     )
-    activated = (gate / (1.0 + jnp.exp(-gate)) * up * route).astype(BF16)
+    line = lax.broadcasted_iota(jnp.int32, (rows, columns), 0)
+    own_ref[...] = dot(order_ref[...], jnp.where(line < plane_rows, block, 0.0).astype(BF16))
+
+
+def expert_kernel(projected_ref, squares_ref, route_ref, own_ref, own_down_ref, other_down_ref, order_ref, *outs):
+    heads = len(outs)
+    head = lax.axis_index("head")
+    rows, columns = own_ref.shape
+    units = own_down_ref.shape[0]
+    projected = projected_ref[...] * lax.rsqrt(squares_ref[...] / (heads * columns) + 1e-06)
+    gate, up = projected[:, : 2 * units], projected[:, 2 * units :]
+    activated = (gate / (1.0 + jnp.exp(-gate)) * up * route_ref[...]).astype(BF16)
     activated = dot(order_ref[...], activated).astype(BF16)
     down = jnp.concatenate([own_down_ref[...], other_down_ref[...]], axis=0)
-    line = lax.broadcasted_iota(jnp.int32, (rows, columns), 0)
-    own = blocks[0][:, :, :columns].astype(F32).reshape(rows, columns)
-    own = dot(order_ref[...], jnp.where(line < plane_rows, own, 0.0).astype(BF16))
     count = rows // heads
     for h in range(heads):
         at = slice(h * columns, (h + 1) * columns)
-        part = dot(activated, down[:, at]) + jnp.where(head == h, own, 0.0)
+        part = dot(activated, down[:, at]) + jnp.where(head == h, own_ref[...], 0.0)
         for step, out in enumerate(outs):
             out[:, at] = part[step * count : (step + 1) * count].astype(out.dtype)
 
@@ -280,73 +306,19 @@
     other_cache = send(own_cache, "pool", 1)
     other_ints = send(ints, "pool", 1)
 
-    head, pool = lax.axis_index("head"), lax.axis_index("pool")
-    placed = kernel_call(
-        functools.partial(place_kernel, (heads, pools, planes)),
-        shape(requests, heads * (columns + mixes)),
-        (residual, expert_choice.T, route_weight.T),
-    )
-    order = [
+    gate_up, down_weight = gate_up.reshape(-1, width), down_weight.reshape(-1, width)
+    other_up, other_down = send(gate_up, "pool", 1), send(down_weight, "pool", 1)
+
+    rows = requests // pools
+    pool_order = [
         [h * rows_here + (here ^ p) * part + i for p in range(pools) for h in range(heads) for i in range(part)]
         for here in range(pools)
     ]
-    args = (
-        queries,
-        new_entries.reshape(-1, entry),
-        own_cache,
-        other_cache,
-        ints,
-        other_ints,
-        placed,
-        lax.dynamic_index_in_dim(one_hot(order, requests), pool, 0, False),
-        output_weight,
-    )
-    rows = requests // pools
-    sizes = (requests, pages, moved, page, heads, pools, entry // 2)
-    own, other = kernel_call(
-        functools.partial(attend_kernel, sizes),
-        [shape(rows, heads * (columns + mixes), dtype=F32), shape(rows, heads * (columns + mixes))],
-        args,
-    )
-    other = send(other, "pool", 1)
-
-    gate_up, down_weight = gate_up.reshape(-1, width), down_weight.reshape(-1, width)
-    held = lax.optimization_barrier((gate_up, down_weight, other))
-    other_up, other_down = send(held[0], "pool", 1), send(held[1], "pool", 1)
-
-    piece = shape(rows, columns + mixes)
-    pieces = kernel_call(split_kernel, [shape(rows, columns + mixes, dtype=F32)] + [piece] * (heads - 1), (own, other))
-    hidden = pieces[0]
-    for step in range(1, heads):
-        hidden = hidden + send(pieces[step], "head", step).astype(F32)
-    hidden = hidden.astype(BF16)
-
-    plane_blocks = jnp.stack([hidden] + [send(hidden, "req", step) for step in range(1, planes)])
-    sent = plane_blocks[:, :, :columns]
-    blocks = [plane_blocks] + [send(sent, "head", step) for step in range(1, heads)]
-    order = [
+    head_order = [
         [(r * heads + (here ^ h)) * part + i for h in range(heads) for r in range(planes) for i in range(part)]
         for here in range(heads)
     ]
-    args = (
-        *blocks,
-        gate_up,
-        other_up,
-        down_weight,
-        other_down,
-        norm_gain.reshape(1, -1),
-        lax.dynamic_index_in_dim(one_hot(order, planes * rows), head, 0, False),
-    )
-    piece = shape(planes * part, width)
-    pieces = kernel_call(
-        functools.partial(expert_kernel, (heads, planes)),
-        [shape(planes * part, width, dtype=F32)] + [piece] * (heads - 1),
-        args,
-    )
-    arrived = [pieces[0]] + [send(pieces[step], "head", step) for step in range(1, heads)]
-    own, other = kernel_call(halve_kernel, [shape(planes * part, width // pools)] * 2, arrived)
-    other = send(other, "pool", 1)
-    order = [
+    plane_order = [
         [
             p * planes * part + r * part + i if half == at else -1
             for r in range(planes)
@@ -356,12 +328,83 @@
         ]
         for half in range(2)
     ]
+    outside = (
+        own_cache,
+        queries,
+        output_weight,
+        one_hot(plane_order, pools * planes * part),
+        one_hot(pool_order, requests),
+        one_hot(head_order, planes * rows),
+    )
+    copied = [shape(*array.shape[i // 4 :], dtype=array.dtype) for i, array in enumerate(outside)]
+    placed, held_cache, held_queries, held_weight, plane_order, pool_order, head_order = kernel_call(
+        functools.partial(place_kernel, (heads, pools, planes, len(outside))),
+        [shape(requests, heads * (columns + mixes))] + copied,
+        (residual, expert_choice.T, route_weight.T),
+        [pltpu.SemaphoreType.DMA((len(outside),))],
+        outside,
+    )
+    args = held(
+        held_queries,
+        new_entries.reshape(-1, entry),
+        held_cache,
+        other_cache,
+        ints,
+        other_ints,
+        placed,
+        pool_order,
+        held_weight,
+    )
+    sizes = (requests, pages, moved, page, heads, pools, entry // 2)
+    own, other = kernel_call(
+        functools.partial(attend_kernel, sizes),
+        [shape(rows, heads * (columns + mixes), dtype=F32), shape(rows, heads * (columns + mixes))],
+        args,
+    )
+    other = send(other, "pool", 1)
+    other, other_up, other_down = lax.optimization_barrier((other, other_up, other_down))
+    piece = shape(rows, columns + mixes)
+    pieces = kernel_call(
+        split_kernel,
+        [shape(rows, columns + mixes, dtype=F32)] + [piece] * (heads - 1),
+        held(own, other),
+    )
+    hidden = pieces[0]
+    for step in range(1, heads):
+        hidden = hidden + send(pieces[step], "head", step).astype(F32)
+    hidden = hidden.astype(BF16)
+
+    plane_blocks = jnp.stack([hidden] + [send(hidden, "req", step) for step in range(1, planes)])
+    sent = plane_blocks[:, :, :columns]
+    weights = held(gate_up, other_up, norm_gain.reshape(1, -1))
+    total = planes * rows
+    sums = [shape(total, 2 * gate_up.shape[0], dtype=F32), shape(total, 1, dtype=F32)]
+    *state, route, own = kernel_call(
+        functools.partial(project_kernel, 0, planes),
+        sums + [shape(total, 1, dtype=F32), shape(total, columns, dtype=F32)],
+        held(plane_blocks, *weights, head_order),
+    )
+    for step in range(1, heads):
+        state = kernel_call(
+            functools.partial(project_kernel, step, planes),
+            sums,
+            held(send(sent, "head", step), *weights, *state),
+        )
+    piece = shape(planes * part, width)
+    pieces = kernel_call(
+        expert_kernel,
+        [shape(planes * part, width, dtype=F32)] + [piece] * (heads - 1),
+        held(*state, route, own, down_weight, other_down, head_order),
+    )
+    arrived = [pieces[0]] + [send(pieces[step], "head", step) for step in range(1, heads)]
+    own, other = kernel_call(
+        halve_kernel, [shape(planes * part, width // pools)] * 2, held(*arrived)
+    )
+    other = send(other, "pool", 1)
     piece = shape(2 * rows_here, width // pools // 2)
-    pieces = kernel_call(
-        spread_kernel, [piece] * planes, (own, other, one_hot(order, pools * planes * part))
-    )
+    pieces = kernel_call(spread_kernel, [piece] * planes, held(own, other, plane_order))
     arrived = [pieces[0]] + [send(pieces[step], "req", step) for step in range(1, planes)]
-    return kernel_call(total_kernel, shape(rows_here, width // pools), arrived)
+    return kernel_call(total_kernel, shape(rows_here, width // pools), held(*arrived))
 
 
 def solution(mesh):

time: 58.7 us -> 61.2 us (1.043)
  waiting for transfers between devices: 20.7 us -> 22.6 us
  local copies, waits for them, and re-layouts: 8.61 us -> 9.59 us
    unnamed x19 -> x25, local copies, waits for them, and re-layouts: 6.32 us -> 8.76 us
    ppermute x21, waiting for transfers between devices: 20.7 us -> 22.6 us  [send(): return lax.ppermute(value, axes, [(i, i ^ step) for i in range(size)])]
    squeeze x2 -> x0, local copies, waits for them, and re-layouts: 1.45 us -> none  [the longest x1 0.74 us: local(): lax.dynamic_index_in_dim(one_hot(order, planes * rows), head, 0, False)]
    pallas_call x7 -> x11, Pallas kernels: 5.75 us -> 5.28 us  [kernel_call(): pl.pallas_call(body, out_shape=jax.tree.map(lambda out: pltpu.VMEM(out.sh...]
  transfers between devices with their start and end apart: 21 -> 21, of which waited for: 15 -> 15; matrix products, arithmetic and copies ran while one was open for 5% -> 3% of each run, Pallas kernels for 1% -> 6%
where the time goes in v4:
time: 61.2 us; the launch traced here: 60.7 us
  waiting for transfers between devices  22.6 us (37%)
  starting transfers between devices  22.2 us (36%)
  local copies, waits for them, and re-layouts  9.59 us (16%)
  Pallas kernels  5.28 us (9%)
  other arithmetic  0.82 us (1%)
    ppermute x21, waiting for transfers between devices, send(): return lax.ppermute(value, axes, [(i, i ^ step) for i in range(size)])  22.6 us
    ppermute x21, starting transfers between devices, send(): return lax.ppermute(value, axes, [(i, i ^ step) for i in range(size)])  22.2 us
    unnamed x25, local copies, waits for them, and re-layouts  8.76 us
    pallas_call x11, Pallas kernels, kernel_call(): pl.pallas_call(body, out_shape=jax.tree.map(lambda out: pltpu.VMEM(out.sh...  5.28 us
  transfers between devices with their start and end apart: 21, of which 15 were waited for; matrix products, arithmetic and copies ran while one was open for 3% of the time, Pallas kernels for 6%

profile of v4, /device:TPU:0, one launch (start us, length us, event | category | flops | bytes accessed | tf_op | source)
XLA Modules:
  0.0 60.7 jit_solution(13198221324953057859)
XLA Ops:
  2.7 1.6 %copy-done.1 = bf16[512,2048]{1,0:T(8,128)(2,1)S(1)} copy-done((bf16[512,2048]{1,0:T(8,128)(2,1)S(1)}, bf16[512,2048]{1,0:T(8,128)(2,1)}, u32[]{:S(2)}) %copy-start.1) | copy-done | bytes 2097176
  4.3 1.0 %copy-done.3 = bf16[1,52,16,256]{3,2,1,0:T(8,128)(2,1)S(1)} copy-done((bf16[1,52,16,256]{3,2,1,0:T(8,128)(2,1)S(1)}, bf16[1,52,16,256]{3,2,1,0:T(8,128)(2,1)}, u32[]{:S(2)}) %copy-start.3) | copy-done | bytes 426008
  5.3 0.9 %copy-done.5 = bf16[48,1024]{1,0:T(8,128)(2,1)S(1)} copy-done((bf16[48,1024]{1,0:T(8,128)(2,1)S(1)}, bf16[48,1024]{1,0:T(8,128)(2,1)}, u32[]{:S(2)}) %copy-start.5) | copy-done | bytes 98328
  10.8 1.2 %shard_map.163 = (bf16[48,2560]{1,0:T(8,128)(2,1)S(1)}, bf16[832,256]{1,0:T(8,128)(2,1)S(1)}, bf16[48,1024]{1,0:T(8,128)(2,1)S(1)}, bf16[512,2048]{1,0:T(8,128)(...) custom-call(bf16[832,256]{1,0:T(8,128)(2,1)S(1)} %bitcast.24, ...), custom_call_target="tpu_custom_call" | custom-call | tf_op jit(solution)/shard_map/pallas_call | solution.py:27
  12.0 1.6 %shard_map.164 = (f32[24,2560]{1,0:T(8,128)S(1)}, bf16[24,2560]{1,0:T(8,128)(2,1)S(1)}) custom-call(bf16[48,1024]{1,0:T(8,128)(2,1)S(1)} %get-tuple-element.41.q_ref, bf16[96,256]{1,0:T(8,128)(2,1)S(1)} %reshape.22.new_ref, bf16[832,256]{1,0:T(8,128)(2,1)S(1)} %get-tuple-element.42.own_ref, bf16[832,256]{1,0:T(8,128)(2,1)S(1)} %collective-permute-done.other_ref, ...), custom_call_target="tpu_custom_call" | custom-call | tf_op jit(solution)/shard_map/pallas_call | solution.py:27
  14.1 1.0 %collective-permute-done.2.other_ref = bf16[24,2560]{1,0:T(8,128)(2,1)S(1)} collective-permute-done((bf16[24,2560]{1,0:T(8,128)(2,1)S(1)}, bf16[24,2560]{1,0:T(8,128)(2,1)S(1)}, u32[]{:S(2)}, u32[]{:S(2)}) %collective-permute-start.2) | collective-permute-done | bytes 122912 | tf_op jit(solution)/shard_map/ppermute | solution.py:19
  15.1 2.9 %collective-permute-start.5 = (bf16[24,640]{1,0:T(8,128)(2,1)S(1)}, bf16[24,640]{1,0:T(8,128)(2,1)S(1)}, u32[]{:S(2)}, u32[]{:S(2)}) collective-permute-start(bf16[24,640]{1,0:T(8,128)(2,1)S(1)} %get-tuple-element.50), channel_id=1, source_target_pairs={{0,2},{2,0},{4,6},{6,4},{1,3},{3,1},{5,7},{7,5},{8,10},{10,8},{12,... | collective-permute-start | bytes 92168 | tf_op jit(solution)/shard_map/ppermute | solution.py:19
  18.1 1.5 %collective-permute-start.6 = (bf16[24,640]{1,0:T(8,128)(2,1)S(1)}, bf16[24,640]{1,0:T(8,128)(2,1)S(1)}, u32[]{:S(2)}, u32[]{:S(2)}) collective-permute-start(bf16[24,640]{1,0:T(8,128)(2,1)S(1)} %get-tuple-element.51), channel_id=1, source_target_pairs={{0,4},{2,6},{4,0},{6,2},{1,5},{3,7},{5,1},{7,3},{8,12},{10,14},{12... | collective-permute-start | bytes 92168 | tf_op jit(solution)/shard_map/ppermute | solution.py:19
  19.9 2.0 %collective-permute-done.6 = bf16[24,640]{1,0:T(8,128)(2,1)S(1)} collective-permute-done((bf16[24,640]{1,0:T(8,128)(2,1)S(1)}, bf16[24,640]{1,0:T(8,128)(2,1)S(1)}, u32[]{:S(2)}, u32[]{:S(2)}) %collective-permute-start.6) | collective-permute-done | bytes 30752 | tf_op jit(solution)/shard_map/ppermute | solution.py:19
  21.9 2.4 %collective-permute-done.7 = bf16[24,640]{1,0:T(8,128)(2,1)S(1)} collective-permute-done((bf16[24,640]{1,0:T(8,128)(2,1)S(1)}, bf16[24,640]{1,0:T(8,128)(2,1)S(1)}, u32[]{:S(2)}, u32[]{:S(2)}) %collective-permute-start.7) | collective-permute-done | bytes 30752 | tf_op jit(solution)/shard_map/ppermute | solution.py:19
  24.4 2.6 %collective-permute-start.9 = (bf16[24,640]{1,0:T(8,128)(2,1)S(1)}, bf16[24,640]{1,0:T(8,128)(2,1)S(1)}, u32[]{:S(2)}, u32[]{:S(2)}) collective-permute-start(bf16[24,640]{1,0:T(8,128)(2,1)S(1)} %add_convert_fusion), channel_id=1, source_target_pairs={{0,16},{8,24},{16,0},{24,8},{1,17},{9,25},{17,1},{25,9},{2,18},{10... | collective-permute-start | bytes 92168 | tf_op jit(solution)/shard_map/ppermute | solution.py:19
  27.0 1.3 %collective-permute-start.10 = (bf16[24,640]{1,0:T(8,128)(2,1)S(1)}, bf16[24,640]{1,0:T(8,128)(2,1)S(1)}, u32[]{:S(2)}, u32[]{:S(2)}) collective-permute-start(bf16[24,640]{1,0:T(8,128)(2,1)S(1)} %add_convert_fusion), channel_id=1, source_target_pairs={{0,24},{8,16},{16,8},{24,0},{1,25},{9,17},{17,9},{25,1},{2,26},{10... | collective-permute-start | bytes 92168 | tf_op jit(solution)/shard_map/ppermute | solution.py:19
  28.6 0.9 %collective-permute-done.9 = bf16[24,640]{1,0:T(8,128)(2,1)S(1)} collective-permute-done((bf16[24,640]{1,0:T(8,128)(2,1)S(1)}, bf16[24,640]{1,0:T(8,128)(2,1)S(1)}, u32[]{:S(2)}, u32[]{:S(2)}) %collective-permute-start.9) | collective-permute-done | bytes 30752 | tf_op jit(solution)/shard_map/ppermute | solution.py:19
  29.5 3.2 %collective-permute-done.10 = bf16[24,640]{1,0:T(8,128)(2,1)S(1)} collective-permute-done((bf16[24,640]{1,0:T(8,128)(2,1)S(1)}, bf16[24,640]{1,0:T(8,128)(2,1)S(1)}, u32[]{:S(2)}, u32[]{:S(2)}) %collective-permute-start.10) | collective-permute-done | bytes 30752 | tf_op jit(solution)/shard_map/ppermute | solution.py:19
  33.9 2.4 %collective-permute-start.11 = (bf16[4,24,512]{2,1,0:T(8,128)(2,1)S(1)}, bf16[4,24,512]{2,1,0:T(8,128)(2,1)S(1)}, u32[]{:S(2)}, u32[]{:S(2)}) collective-permute-start(bf16[4,24,512]{2,1,0:T(8,128)(2,1)S(1)} %slice.4), channel_id=1, source_target_pairs={{0,6},{2,4},{4,2},{6,0},{1,7},{3,5},{5,3},{7,1},{8,14},{10,12},{12... | collective-permute-start | bytes 294920 | tf_op jit(solution)/shard_map/ppermute | solution.py:19
  38.4 1.0 %collective-permute-done.11.block_ref = bf16[4,24,512]{2,1,0:T(8,128)(2,1)S(1)} collective-permute-done((bf16[4,24,512]{2,1,0:T(8,128)(2,1)S(1)}, bf16[4,24,512]{2,1,0:T(8,128)(2,1)S(1)}, u32[]{:S(2)}, u32[]{:S(2)}) %collective-permute-start.11) | collective-permute-done | bytes 98336 | tf_op jit(solution)/shard_map/ppermute | solution.py:19
  40.5 1.6 %collective-permute-start.14 = (bf16[24,2048]{1,0:T(8,128)(2,1)S(1)}, bf16[24,2048]{1,0:T(8,128)(2,1)S(1)}, u32[]{:S(2)}, u32[]{:S(2)}) collective-permute-start(bf16[24,2048]{1,0:T(8,128)(2,1)S(1)} %get-tuple-element.67), channel_id=1, source_target_pairs={{0,2},{2,0},{4,6},{6,4},{1,3},{3,1},{5,7},{7,5},{8,10},{10,8},{12,... | collective-permute-start | bytes 294920 | tf_op jit(solution)/shard_map/ppermute | solution.py:19
  42.1 2.3 %collective-permute-start.15 = (bf16[24,2048]{1,0:T(8,128)(2,1)S(1)}, bf16[24,2048]{1,0:T(8,128)(2,1)S(1)}, u32[]{:S(2)}, u32[]{:S(2)}) collective-permute-start(bf16[24,2048]{1,0:T(8,128)(2,1)S(1)} %get-tuple-element.68), channel_id=1, source_target_pairs={{0,4},{2,6},{4,0},{6,2},{1,5},{3,7},{5,1},{7,3},{8,12},{10,14},{12... | collective-permute-start | bytes 294920 | tf_op jit(solution)/shard_map/ppermute | solution.py:19
  45.2 1.8 %collective-permute-done.15.refs_2_ = bf16[24,2048]{1,0:T(8,128)(2,1)S(1)} collective-permute-done((bf16[24,2048]{1,0:T(8,128)(2,1)S(1)}, bf16[24,2048]{1,0:T(8,128)(2,1)S(1)}, u32[]{:S(2)}, u32[]{:S(2)}) %collective-permute-start.15) | collective-permute-done | bytes 98336 | tf_op jit(solution)/shard_map/ppermute | solution.py:19
  47.0 2.9 %collective-permute-done.16.refs_3_ = bf16[24,2048]{1,0:T(8,128)(2,1)S(1)} collective-permute-done((bf16[24,2048]{1,0:T(8,128)(2,1)S(1)}, bf16[24,2048]{1,0:T(8,128)(2,1)S(1)}, u32[]{:S(2)}, u32[]{:S(2)}) %collective-permute-start.16) | collective-permute-done | bytes 98336 | tf_op jit(solution)/shard_map/ppermute | solution.py:19
  50.0 1.2 %collective-permute-done.17.other_ref = bf16[24,1024]{1,0:T(8,128)(2,1)S(1)} collective-permute-done((bf16[24,1024]{1,0:T(8,128)(2,1)S(1)}, bf16[24,1024]{1,0:T(8,128)(2,1)S(1)}, u32[]{:S(2)}, u32[]{:S(2)}) %collective-permute-start.17) | collective-permute-done | bytes 49184 | tf_op jit(solution)/shard_map/ppermute | solution.py:19
  51.5 2.9 %collective-permute-start.19 = (bf16[24,512]{1,0:T(8,128)(2,1)S(1)}, bf16[24,512]{1,0:T(8,128)(2,1)S(1)}, u32[]{:S(2)}, u32[]{:S(2)}) collective-permute-start(bf16[24,512]{1,0:T(8,128)(2,1)S(1)} %get-tuple-element.75), channel_id=1, source_target_pairs={{0,16},{8,24},{16,0},{24,8},{1,17},{9,25},{17,1},{25,9},{2,18},{10... | collective-permute-start | bytes 73736 | tf_op jit(solution)/shard_map/ppermute | solution.py:19
  54.4 1.5 %collective-permute-start.20 = (bf16[24,512]{1,0:T(8,128)(2,1)S(1)}, bf16[24,512]{1,0:T(8,128)(2,1)S(1)}, u32[]{:S(2)}, u32[]{:S(2)}) collective-permute-start(bf16[24,512]{1,0:T(8,128)(2,1)S(1)} %get-tuple-element.76), channel_id=1, source_target_pairs={{0,24},{8,16},{16,8},{24,0},{1,25},{9,17},{17,9},{25,1},{2,26},{10... | collective-permute-start | bytes 73736 | tf_op jit(solution)/shard_map/ppermute | solution.py:19
  56.3 3.7 %collective-permute-done.20.refs_3_ = bf16[24,512]{1,0:T(8,128)(2,1)S(1)} collective-permute-done((bf16[24,512]{1,0:T(8,128)(2,1)S(1)}, bf16[24,512]{1,0:T(8,128)(2,1)S(1)}, u32[]{:S(2)}, u32[]{:S(2)}) %collective-permute-start.20) | collective-permute-done | bytes 24608 | tf_op jit(solution)/shard_map/ppermute | solution.py:19
  (60 shorter events, 14.9 us)
Async XLA Ops:
  0.0 15.1 %collective-permute-start.3 = (bf16[384,2048]{1,0:T(8,128)(2,1)}, bf16[384,2048]{1,0:T(8,128)(2,1)S(1)}, u32[]{:S(2)}, u32[]{:S(2)}) collective-permute-start(bf16[384,2048]{1,0:T(8,128)(2,1)} %bitcast.16), channel_id=1, source_target_pairs={{0,1},{1,0},{2,3},{3,2},{4,5},{5,4},{6,7},{7,6},{8,9},{9,8},{10,11... | collective-permute-start | bytes 4718600 | tf_op jit(solution)/shard_map/ppermute | solution.py:19
  0.5 14.7 %collective-permute-start.4 = (bf16[192,2048]{1,0:T(8,128)(2,1)}, bf16[192,2048]{1,0:T(8,128)(2,1)S(1)}, u32[]{:S(2)}, u32[]{:S(2)}) collective-permute-start(bf16[192,2048]{1,0:T(8,128)(2,1)} %bitcast.21), channel_id=1, source_target_pairs={{0,1},{1,0},{2,3},{3,2},{4,5},{5,4},{6,7},{7,6},{8,9},{9,8},{10,11... | collective-permute-start | bytes 2359304 | tf_op jit(solution)/shard_map/ppermute | solution.py:19
  0.5 11.5 %collective-permute-start = (bf16[832,256]{1,0:T(8,128)(2,1)}, bf16[832,256]{1,0:T(8,128)(2,1)S(1)}, u32[]{:S(2)}, u32[]{:S(2)}) collective-permute-start(bf16[832,256]{1,0:T(8,128)(2,1)} %bitcast.23), channel_id=1, source_target_pairs={{0,1},{1,0},{2,3},{3,2},{4,5},{5,4},{6,7},{7,6},{8,9},{9,8},{10,11... | collective-permute-start | bytes 1277960 | tf_op jit(solution)/shard_map/ppermute | solution.py:19
  1.8 10.2 %collective-permute-start.1 = (s32[1,128]{1,0:T(1,128)S(1)}, s32[1,128]{1,0:T(1,128)S(1)}, u32[]{:S(2)}, u32[]{:S(2)}) collective-permute-start(s32[1,128]{1,0:T(1,128)S(1)} %pad_bitcast_fusion.own_ints_ref), channel_id=1, source_target_pairs={{0,1},{1,0},{2,3},{3,2},{4,5},{5,4},{6,7},{7,6},{8,9},{9,8},{10,11... | collective-permute-start | bytes 1544 | tf_op jit(solution)/shard_map/ppermute | solution.py:19
  2.7 1.6 %copy-start.1 = (bf16[512,2048]{1,0:T(8,128)(2,1)S(1)}, bf16[512,2048]{1,0:T(8,128)(2,1)}, u32[]{:S(2)}) copy-start(bf16[512,2048]{1,0:T(8,128)(2,1)} %refs_2_.1) | copy-start | bytes 6291460
  12.0 24.3 %copy-start = (bf16[1,2,192,2048]{3,2,1,0:T(8,128)(2,1)S(1)}, bf16[1,2,192,2048]{3,2,1,0:T(8,128)(2,1)}, u32[]{:S(2)}) copy-start(bf16[1,2,192,2048]{3,2,1,0:T(8,128)(2,1)} %param.29) | copy-start | bytes 4718596
  12.0 24.3 %copy-start.4 = (f32[2048]{0:T(1024)S(1)}, f32[2048]{0:T(1024)}, u32[]{:S(2)}) copy-start(f32[2048]{0:T(1024)} %param.25) | copy-start | bytes 24580
  13.6 1.5 %collective-permute-start.2 = (bf16[24,2560]{1,0:T(8,128)(2,1)S(1)}, bf16[24,2560]{1,0:T(8,128)(2,1)S(1)}, u32[]{:S(2)}, u32[]{:S(2)}) collective-permute-start(bf16[24,2560]{1,0:T(8,128)(2,1)S(1)} %get-tuple-element.47), channel_id=1, source_target_pairs={{0,1},{1,0},{2,3},{3,2},{4,5},{5,4},{6,7},{7,6},{8,9},{9,8},{10,11... | collective-permute-start | bytes 368648 | tf_op jit(solution)/shard_map/ppermute | solution.py:19
  15.1 4.8 %collective-permute-start.5 = (bf16[24,640]{1,0:T(8,128)(2,1)S(1)}, bf16[24,640]{1,0:T(8,128)(2,1)S(1)}, u32[]{:S(2)}, u32[]{:S(2)}) collective-permute-start(bf16[24,640]{1,0:T(8,128)(2,1)S(1)} %get-tuple-element.50), channel_id=1, source_target_pairs={{0,2},{2,0},{4,6},{6,4},{1,3},{3,1},{5,7},{7,5},{8,10},{10,8},{12,... | collective-permute-start | bytes 92168 | tf_op jit(solution)/shard_map/ppermute | solution.py:19
  18.1 3.9 %collective-permute-start.6 = (bf16[24,640]{1,0:T(8,128)(2,1)S(1)}, bf16[24,640]{1,0:T(8,128)(2,1)S(1)}, u32[]{:S(2)}, u32[]{:S(2)}) collective-permute-start(bf16[24,640]{1,0:T(8,128)(2,1)S(1)} %get-tuple-element.51), channel_id=1, source_target_pairs={{0,4},{2,6},{4,0},{6,2},{1,5},{3,7},{5,1},{7,3},{8,12},{10,14},{12... | collective-permute-start | bytes 92168 | tf_op jit(solution)/shard_map/ppermute | solution.py:19
  19.6 4.8 %collective-permute-start.7 = (bf16[24,640]{1,0:T(8,128)(2,1)S(1)}, bf16[24,640]{1,0:T(8,128)(2,1)S(1)}, u32[]{:S(2)}, u32[]{:S(2)}) collective-permute-start(bf16[24,640]{1,0:T(8,128)(2,1)S(1)} %get-tuple-element.52), channel_id=1, source_target_pairs={{0,6},{2,4},{4,2},{6,0},{1,7},{3,5},{5,3},{7,1},{8,14},{10,12},{12... | collective-permute-start | bytes 92168 | tf_op jit(solution)/shard_map/ppermute | solution.py:19
  24.4 5.2 %collective-permute-start.9 = (bf16[24,640]{1,0:T(8,128)(2,1)S(1)}, bf16[24,640]{1,0:T(8,128)(2,1)S(1)}, u32[]{:S(2)}, u32[]{:S(2)}) collective-permute-start(bf16[24,640]{1,0:T(8,128)(2,1)S(1)} %add_convert_fusion), channel_id=1, source_target_pairs={{0,16},{8,24},{16,0},{24,8},{1,17},{9,25},{17,1},{25,9},{2,18},{10... | collective-permute-start | bytes 92168 | tf_op jit(solution)/shard_map/ppermute | solution.py:19
  27.0 5.7 %collective-permute-start.10 = (bf16[24,640]{1,0:T(8,128)(2,1)S(1)}, bf16[24,640]{1,0:T(8,128)(2,1)S(1)}, u32[]{:S(2)}, u32[]{:S(2)}) collective-permute-start(bf16[24,640]{1,0:T(8,128)(2,1)S(1)} %add_convert_fusion), channel_id=1, source_target_pairs={{0,24},{8,16},{16,8},{24,0},{1,25},{9,17},{17,9},{25,1},{2,26},{10... | collective-permute-start | bytes 92168 | tf_op jit(solution)/shard_map/ppermute | solution.py:19
  28.4 4.3 %collective-permute-start.8 = (bf16[24,640]{1,0:T(8,128)(2,1)S(1)}, bf16[24,640]{1,0:T(8,128)(2,1)S(1)}, u32[]{:S(2)}, u32[]{:S(2)}) collective-permute-start(bf16[24,640]{1,0:T(8,128)(2,1)S(1)} %add_convert_fusion), channel_id=1, source_target_pairs={{0,8},{8,0},{16,24},{24,16},{1,9},{9,1},{17,25},{25,17},{2,10},{10... | collective-permute-start | bytes 92168 | tf_op jit(solution)/shard_map/ppermute | solution.py:19
  32.8 4.7 %collective-permute-start.13 = (bf16[4,24,512]{2,1,0:T(8,128)(2,1)S(1)}, bf16[4,24,512]{2,1,0:T(8,128)(2,1)S(1)}, u32[]{:S(2)}, u32[]{:S(2)}) collective-permute-start(bf16[4,24,512]{2,1,0:T(8,128)(2,1)S(1)} %slice.4), channel_id=1, source_target_pairs={{0,2},{2,0},{4,6},{6,4},{1,3},{3,1},{5,7},{7,5},{8,10},{10,8},{12,... | collective-permute-start | bytes 294920 | tf_op jit(solution)/shard_map/ppermute | solution.py:19
  33.4 4.6 %collective-permute-start.12 = (bf16[4,24,512]{2,1,0:T(8,128)(2,1)S(1)}, bf16[4,24,512]{2,1,0:T(8,128)(2,1)S(1)}, u32[]{:S(2)}, u32[]{:S(2)}) collective-permute-start(bf16[4,24,512]{2,1,0:T(8,128)(2,1)S(1)} %slice.4), channel_id=1, source_target_pairs={{0,4},{2,6},{4,0},{6,2},{1,5},{3,7},{5,1},{7,3},{8,12},{10,14},{12... | collective-permute-start | bytes 294920 | tf_op jit(solution)/shard_map/ppermute | solution.py:19
  33.9 5.5 %collective-permute-start.11 = (bf16[4,24,512]{2,1,0:T(8,128)(2,1)S(1)}, bf16[4,24,512]{2,1,0:T(8,128)(2,1)S(1)}, u32[]{:S(2)}, u32[]{:S(2)}) collective-permute-start(bf16[4,24,512]{2,1,0:T(8,128)(2,1)S(1)} %slice.4), channel_id=1, source_target_pairs={{0,6},{2,4},{4,2},{6,0},{1,7},{3,5},{5,3},{7,1},{8,14},{10,12},{12... | collective-permute-start | bytes 294920 | tf_op jit(solution)/shard_map/ppermute | solution.py:19
  40.5 4.7 %collective-permute-start.14 = (bf16[24,2048]{1,0:T(8,128)(2,1)S(1)}, bf16[24,2048]{1,0:T(8,128)(2,1)S(1)}, u32[]{:S(2)}, u32[]{:S(2)}) collective-permute-start(bf16[24,2048]{1,0:T(8,128)(2,1)S(1)} %get-tuple-element.67), channel_id=1, source_target_pairs={{0,2},{2,0},{4,6},{6,4},{1,3},{3,1},{5,7},{7,5},{8,10},{10,8},{12,... | collective-permute-start | bytes 294920 | tf_op jit(solution)/shard_map/ppermute | solution.py:19
  42.1 4.9 %collective-permute-start.15 = (bf16[24,2048]{1,0:T(8,128)(2,1)S(1)}, bf16[24,2048]{1,0:T(8,128)(2,1)S(1)}, u32[]{:S(2)}, u32[]{:S(2)}) collective-permute-start(bf16[24,2048]{1,0:T(8,128)(2,1)S(1)} %get-tuple-element.68), channel_id=1, source_target_pairs={{0,4},{2,6},{4,0},{6,2},{1,5},{3,7},{5,1},{7,3},{8,12},{10,14},{12... | collective-permute-start | bytes 294920 | tf_op jit(solution)/shard_map/ppermute | solution.py:19
  44.4 5.5 %collective-permute-start.16 = (bf16[24,2048]{1,0:T(8,128)(2,1)S(1)}, bf16[24,2048]{1,0:T(8,128)(2,1)S(1)}, u32[]{:S(2)}, u32[]{:S(2)}) collective-permute-start(bf16[24,2048]{1,0:T(8,128)(2,1)S(1)} %get-tuple-element.69), channel_id=1, source_target_pairs={{0,6},{2,4},{4,2},{6,0},{1,7},{3,5},{5,3},{7,1},{8,14},{10,12},{12... | collective-permute-start | bytes 294920 | tf_op jit(solution)/shard_map/ppermute | solution.py:19
  49.9 1.3 %collective-permute-start.17 = (bf16[24,1024]{1,0:T(8,128)(2,1)S(1)}, bf16[24,1024]{1,0:T(8,128)(2,1)S(1)}, u32[]{:S(2)}, u32[]{:S(2)}) collective-permute-start(bf16[24,1024]{1,0:T(8,128)(2,1)S(1)} %get-tuple-element.71), channel_id=1, source_target_pairs={{0,1},{1,0},{2,3},{3,2},{4,5},{5,4},{6,7},{7,6},{8,9},{9,8},{10,11... | collective-permute-start | bytes 147464 | tf_op jit(solution)/shard_map/ppermute | solution.py:19
  51.4 4.5 %collective-permute-start.18 = (bf16[24,512]{1,0:T(8,128)(2,1)S(1)}, bf16[24,512]{1,0:T(8,128)(2,1)S(1)}, u32[]{:S(2)}, u32[]{:S(2)}) collective-permute-start(bf16[24,512]{1,0:T(8,128)(2,1)S(1)} %get-tuple-element.74), channel_id=1, source_target_pairs={{0,8},{8,0},{16,24},{24,16},{1,9},{9,1},{17,25},{25,17},{2,10},{10... | collective-permute-start | bytes 73736 | tf_op jit(solution)/shard_map/ppermute | solution.py:19
  51.5 4.8 %collective-permute-start.19 = (bf16[24,512]{1,0:T(8,128)(2,1)S(1)}, bf16[24,512]{1,0:T(8,128)(2,1)S(1)}, u32[]{:S(2)}, u32[]{:S(2)}) collective-permute-start(bf16[24,512]{1,0:T(8,128)(2,1)S(1)} %get-tuple-element.75), channel_id=1, source_target_pairs={{0,16},{8,24},{16,0},{24,8},{1,17},{9,25},{17,1},{25,9},{2,18},{10... | collective-permute-start | bytes 73736 | tf_op jit(solution)/shard_map/ppermute | solution.py:19
  54.4 5.6 %collective-permute-start.20 = (bf16[24,512]{1,0:T(8,128)(2,1)S(1)}, bf16[24,512]{1,0:T(8,128)(2,1)S(1)}, u32[]{:S(2)}, u32[]{:S(2)}) collective-permute-start(bf16[24,512]{1,0:T(8,128)(2,1)S(1)} %get-tuple-element.76), channel_id=1, source_target_pairs={{0,24},{8,16},{16,8},{24,0},{1,25},{9,17},{17,9},{25,1},{2,26},{10... | collective-permute-start | bytes 73736 | tf_op jit(solution)/shard_map/ppermute | solution.py:19
  (9 other events, 8.0 us)

commit v5 on v4

--- a/solution.py
+++ b/solution.py
@@ -27,12 +27,12 @@
     return pl.pallas_call(
         body,
         out_shape=jax.tree.map(lambda out: pltpu.VMEM(out.shape, out.dtype), out_shape),
-        in_specs=[pl.BlockSpec(memory_space=pl.ANY)] * len(outside)
+        in_specs=[pl.BlockSpec(memory_space=pltpu.HBM)] * len(outside)
         + [pl.BlockSpec(memory_space=pltpu.VMEM)] * len(args),
         out_specs=jax.tree.map(lambda _: pl.BlockSpec(memory_space=pltpu.VMEM), out_shape),
         scratch_shapes=list(scratch),
         compiler_params=pltpu.CompilerParams(vmem_limit_bytes=VMEM_LIMIT),
-    )(*outside, *args)
+    )(*[pltpu.with_memory_space_constraint(arg, pltpu.HBM) for arg in outside], *args)
 
 
 def held(*args):
@@ -179,6 +179,13 @@
         out[...] = (own_ref[:, at] + other_ref[:, at].astype(F32)).astype(out.dtype)
 
 
+def stack_kernel(*refs):
+    parts, (all_ref, first_ref) = refs[:-2], refs[-2:]
+    for step, part in enumerate(reversed(parts)):
+        all_ref[step] = part[...]
+        first_ref[step] = part[:, : first_ref.shape[2]]
+
+
 def project_kernel(step, planes, block_ref, own_up_ref, other_up_ref, gain_ref, *refs):
     head = lax.axis_index("head")
     plane_rows = block_ref.shape[1]
@@ -340,7 +347,10 @@
     placed, held_cache, held_queries, held_weight, plane_order, pool_order, head_order = kernel_call(
         functools.partial(place_kernel, (heads, pools, planes, len(outside))),
         [shape(requests, heads * (columns + mixes))] + copied,
-        (residual, expert_choice.T, route_weight.T),
+        [
+            pltpu.with_memory_space_constraint(arg, pltpu.HBM)
+            for arg in (residual, expert_choice.T, route_weight.T)
+        ],
         [pltpu.SemaphoreType.DMA((len(outside),))],
         outside,
     )
@@ -370,12 +380,16 @@
         held(own, other),
     )
     hidden = pieces[0]
-    for step in range(1, heads):
+    for step in reversed(range(1, heads)):
         hidden = hidden + send(pieces[step], "head", step).astype(F32)
     hidden = hidden.astype(BF16)
 
-    plane_blocks = jnp.stack([hidden] + [send(hidden, "req", step) for step in range(1, planes)])
-    sent = plane_blocks[:, :, :columns]
+    arrived = [send(hidden, "req", step) for step in reversed(range(1, planes))] + [hidden]
+    plane_blocks, sent = kernel_call(
+        stack_kernel,
+        [shape(planes, rows, columns + mixes), shape(planes, rows, columns)],
+        held(*arrived),
+    )
     weights = held(gate_up, other_up, norm_gain.reshape(1, -1))
     total = planes * rows
     sums = [shape(total, 2 * gate_up.shape[0], dtype=F32), shape(total, 1, dtype=F32)]
@@ -384,7 +398,7 @@
         sums + [shape(total, 1, dtype=F32), shape(total, columns, dtype=F32)],
         held(plane_blocks, *weights, head_order),
     )
-    for step in range(1, heads):
+    for step in reversed(range(1, heads)):
         state = kernel_call(
             functools.partial(project_kernel, step, planes),
             sums,
@@ -396,14 +410,14 @@
         [shape(planes * part, width, dtype=F32)] + [piece] * (heads - 1),
         held(*state, route, own, down_weight, other_down, head_order),
     )
-    arrived = [pieces[0]] + [send(pieces[step], "head", step) for step in range(1, heads)]
+    arrived = [send(pieces[step], "head", step) for step in reversed(range(1, heads))] + [pieces[0]]
     own, other = kernel_call(
         halve_kernel, [shape(planes * part, width // pools)] * 2, held(*arrived)
     )
     other = send(other, "pool", 1)
     piece = shape(2 * rows_here, width // pools // 2)
     pieces = kernel_call(spread_kernel, [piece] * planes, held(own, other, plane_order))
-    arrived = [pieces[0]] + [send(pieces[step], "req", step) for step in range(1, planes)]
+    arrived = [send(pieces[step], "req", step) for step in reversed(range(1, planes))] + [pieces[0]]
     return kernel_call(total_kernel, shape(rows_here, width // pools), held(*arrived))
 
 

time: 61.2 us -> 51 us (0.83)
  local copies, waits for them, and re-layouts: 9.59 us -> 2.18 us
  waiting for transfers between devices: 22.6 us -> 18.8 us
  Pallas kernels: 5.28 us -> 6.83 us
    unnamed x25 -> x7, local copies, waits for them, and re-layouts: 8.76 us -> 1.35 us
    ppermute x21, waiting for transfers between devices: 22.6 us -> 18.8 us  [send(): return lax.ppermute(value, axes, [(i, i ^ step) for i in range(size)])]
    pallas_call x11 -> x12, Pallas kernels: 5.28 us -> 6.83 us  [kernel_call(): pl.pallas_call(body, out_shape=jax.tree.map(lambda out: pltpu.VMEM(out.sh...]
  transfers between devices with their start and end apart: 21 -> 21, of which waited for: 15 -> 15; matrix products, arithmetic and copies ran while one was open for 3% -> 3% of each run, Pallas kernels for 6% -> 11%
where the time goes in v5:
time: 51 us; the launch traced here: 50.7 us
  starting transfers between devices  21.9 us (43%)
  waiting for transfers between devices  18.8 us (37%)
  Pallas kernels  6.83 us (13%)
  local copies, waits for them, and re-layouts  2.18 us (4%)
  other arithmetic  0.8 us (2%)
    ppermute x21, starting transfers between devices, send(): return lax.ppermute(value, axes, [(i, i ^ step) for i in range(size)])  21.9 us
    ppermute x21, waiting for transfers between devices, send(): return lax.ppermute(value, axes, [(i, i ^ step) for i in range(size)])  18.8 us
    pallas_call x12, Pallas kernels, kernel_call(): pl.pallas_call(body, out_shape=jax.tree.map(lambda out: pltpu.VMEM(out.sh...  6.83 us
    unnamed x7, local copies, waits for them, and re-layouts  1.35 us
  transfers between devices with their start and end apart: 21, of which 15 were waited for; matrix products, arithmetic and copies ran while one was open for 3% of the time, Pallas kernels for 11%

profile of v5, /device:TPU:0, one launch (start us, length us, event | category | flops | bytes accessed | tf_op | source)
XLA Modules:
  0.0 50.7 jit_solution(17132939235071706291)
XLA Ops:
  1.0 0.8 %pad_add_fusion = s32[104]{0:T(128)S(1)} fusion(s32[4]{0:T(128)} %param.23, s32[4]{0:T(128)} %param.22, s32[48]{0:T(128)} %bitcast.27, s32[48]{0:T(128)} %bitcast.28), kind=kLoop, calls=%fused_computation.1 | loop fusion | flops 312 | bytes 832 | tf_op jit(solution)/shard_map/concatenate | solution.py:307
  1.8 0.8 %reshape.22.new_ref = bf16[96,256]{1,0:T(8,128)(2,1)S(1)} reshape(bf16[48,2,1,256]{3,1,2,0:T(2,128)(2,1)} %param.18) | data formatting | bytes 98304 | tf_op jit(solution)/shard_map/reshape | solution.py:359
  2.7 2.7 %shard_map.163 = (bf16[48,2560]{1,0:T(8,128)(2,1)S(1)}, bf16[832,256]{1,0:T(8,128)(2,1)S(1)}, bf16[48,1024]{1,0:T(8,128)(2,1)S(1)}, bf16[512,2048]{1,0:T(8,128)(...) custom-call(bf16[832,256]{1,0:T(8,128)(2,1)} %bitcast.24, ...), custom_call_target="tpu_custom_call" | custom-call | tf_op jit(solution)/shard_map/pallas_call | solution.py:27
  5.4 1.6 %shard_map.164 = (f32[24,2560]{1,0:T(8,128)S(1)}, bf16[24,2560]{1,0:T(8,128)(2,1)S(1)}) custom-call(bf16[48,1024]{1,0:T(8,128)(2,1)S(1)} %get-tuple-element.43.q_ref, bf16[96,256]{1,0:T(8,128)(2,1)S(1)} %reshape.22.new_ref, bf16[832,256]{1,0:T(8,128)(2,1)S(1)} %get-tuple-element.44.own_ref, bf16[832,256]{1,0:T(8,128)(2,1)S(1)} %collective-permute-done.other_ref, ...), custom_call_target="tpu_custom_call" | custom-call | tf_op jit(solution)/shard_map/pallas_call | solution.py:27
  7.5 1.0 %collective-permute-done.2.other_ref = bf16[24,2560]{1,0:T(8,128)(2,1)S(1)} collective-permute-done((bf16[24,2560]{1,0:T(8,128)(2,1)S(1)}, bf16[24,2560]{1,0:T(8,128)(2,1)S(1)}, u32[]{:S(2)}, u32[]{:S(2)}) %collective-permute-start.2) | collective-permute-done | bytes 122912 | tf_op jit(solution)/shard_map/ppermute | solution.py:19
  8.5 3.9 %collective-permute-start.5 = (bf16[24,640]{1,0:T(8,128)(2,1)S(1)}, bf16[24,640]{1,0:T(8,128)(2,1)S(1)}, u32[]{:S(2)}, u32[]{:S(2)}) collective-permute-start(bf16[24,640]{1,0:T(8,128)(2,1)S(1)} %get-tuple-element.52), channel_id=1, source_target_pairs={{0,6},{2,4},{4,2},{6,0},{1,7},{3,5},{5,3},{7,1},{8,14},{10,12},{12... | collective-permute-start | bytes 92168 | tf_op jit(solution)/shard_map/ppermute | solution.py:19
  13.1 1.2 %collective-permute-done.5 = bf16[24,640]{1,0:T(8,128)(2,1)S(1)} collective-permute-done((bf16[24,640]{1,0:T(8,128)(2,1)S(1)}, bf16[24,640]{1,0:T(8,128)(2,1)S(1)}, u32[]{:S(2)}, u32[]{:S(2)}) %collective-permute-start.5) | collective-permute-done | bytes 30752 | tf_op jit(solution)/shard_map/ppermute | solution.py:19
  14.3 2.0 %collective-permute-done.6 = bf16[24,640]{1,0:T(8,128)(2,1)S(1)} collective-permute-done((bf16[24,640]{1,0:T(8,128)(2,1)S(1)}, bf16[24,640]{1,0:T(8,128)(2,1)S(1)}, u32[]{:S(2)}, u32[]{:S(2)}) %collective-permute-start.6) | collective-permute-done | bytes 30752 | tf_op jit(solution)/shard_map/ppermute | solution.py:19
  16.8 1.6 %collective-permute-start.10 = (bf16[24,640]{1,0:T(8,128)(2,1)S(1)}, bf16[24,640]{1,0:T(8,128)(2,1)S(1)}, u32[]{:S(2)}, u32[]{:S(2)}) collective-permute-start(bf16[24,640]{1,0:T(8,128)(2,1)S(1)} %add_convert_fusion.refs_3_), channel_id=1, source_target_pairs={{0,8},{8,0},{16,24},{24,16},{1,9},{9,1},{17,25},{25,17},{2,10},{10... | collective-permute-start | bytes 92168 | tf_op jit(solution)/shard_map/ppermute | solution.py:19
  18.5 2.5 %collective-permute-start.8 = (bf16[24,640]{1,0:T(8,128)(2,1)S(1)}, bf16[24,640]{1,0:T(8,128)(2,1)S(1)}, u32[]{:S(2)}, u32[]{:S(2)}) collective-permute-start(bf16[24,640]{1,0:T(8,128)(2,1)S(1)} %add_convert_fusion.refs_3_), channel_id=1, source_target_pairs={{0,24},{8,16},{16,8},{24,0},{1,25},{9,17},{17,9},{25,1},{2,26},{10... | collective-permute-start | bytes 92168 | tf_op jit(solution)/shard_map/ppermute | solution.py:19
  21.1 3.1 %collective-permute-done.8.refs_0_ = bf16[24,640]{1,0:T(8,128)(2,1)S(1)} collective-permute-done((bf16[24,640]{1,0:T(8,128)(2,1)S(1)}, bf16[24,640]{1,0:T(8,128)(2,1)S(1)}, u32[]{:S(2)}, u32[]{:S(2)}) %collective-permute-start.8) | collective-permute-done | bytes 30752 | tf_op jit(solution)/shard_map/ppermute | solution.py:19
  24.2 1.9 %collective-permute-done.9.refs_1_ = bf16[24,640]{1,0:T(8,128)(2,1)S(1)} collective-permute-done((bf16[24,640]{1,0:T(8,128)(2,1)S(1)}, bf16[24,640]{1,0:T(8,128)(2,1)S(1)}, u32[]{:S(2)}, u32[]{:S(2)}) %collective-permute-start.9) | collective-permute-done | bytes 30752 | tf_op jit(solution)/shard_map/ppermute | solution.py:19
  26.1 1.6 %collective-permute-start.13 = (bf16[4,24,512]{2,1,0:T(8,128)(2,1)S(1)}, bf16[4,24,512]{2,1,0:T(8,128)(2,1)S(1)}, u32[]{:S(2)}, u32[]{:S(2)}) collective-permute-start(bf16[4,24,512]{2,1,0:T(8,128)(2,1)S(1)} %get-tuple-element.55), channel_id=1, source_target_pairs={{0,6},{2,4},{4,2},{6,0},{1,7},{3,5},{5,3},{7,1},{8,14},{10,12},{12... | collective-permute-start | bytes 294920 | tf_op jit(solution)/shard_map/ppermute | solution.py:19
  28.2 1.5 %collective-permute-start.11 = (bf16[4,24,512]{2,1,0:T(8,128)(2,1)S(1)}, bf16[4,24,512]{2,1,0:T(8,128)(2,1)S(1)}, u32[]{:S(2)}, u32[]{:S(2)}) collective-permute-start(bf16[4,24,512]{2,1,0:T(8,128)(2,1)S(1)} %get-tuple-element.55), channel_id=1, source_target_pairs={{0,2},{2,0},{4,6},{6,4},{1,3},{3,1},{5,7},{7,5},{8,10},{10,8},{12,... | collective-permute-start | bytes 294920 | tf_op jit(solution)/shard_map/ppermute | solution.py:19
  30.1 1.6 %collective-permute-done.13.block_ref = bf16[4,24,512]{2,1,0:T(8,128)(2,1)S(1)} collective-permute-done((bf16[4,24,512]{2,1,0:T(8,128)(2,1)S(1)}, bf16[4,24,512]{2,1,0:T(8,128)(2,1)S(1)}, u32[]{:S(2)}, u32[]{:S(2)}) %collective-permute-start.13) | collective-permute-done | bytes 98336 | tf_op jit(solution)/shard_map/ppermute | solution.py:19
  34.9 1.6 %collective-permute-start.14 = (bf16[24,2048]{1,0:T(8,128)(2,1)S(1)}, bf16[24,2048]{1,0:T(8,128)(2,1)S(1)}, u32[]{:S(2)}, u32[]{:S(2)}) collective-permute-start(bf16[24,2048]{1,0:T(8,128)(2,1)S(1)} %get-tuple-element.70), channel_id=1, source_target_pairs={{0,6},{2,4},{4,2},{6,0},{1,7},{3,5},{5,3},{7,1},{8,14},{10,12},{12... | collective-permute-start | bytes 294920 | tf_op jit(solution)/shard_map/ppermute | solution.py:19
  36.5 1.0 %collective-permute-start.15 = (bf16[24,2048]{1,0:T(8,128)(2,1)S(1)}, bf16[24,2048]{1,0:T(8,128)(2,1)S(1)}, u32[]{:S(2)}, u32[]{:S(2)}) collective-permute-start(bf16[24,2048]{1,0:T(8,128)(2,1)S(1)} %get-tuple-element.71), channel_id=1, source_target_pairs={{0,4},{2,6},{4,0},{6,2},{1,5},{3,7},{5,1},{7,3},{8,12},{10,14},{12... | collective-permute-start | bytes 294920 | tf_op jit(solution)/shard_map/ppermute | solution.py:19
  37.5 1.0 %collective-permute-start.16 = (bf16[24,2048]{1,0:T(8,128)(2,1)S(1)}, bf16[24,2048]{1,0:T(8,128)(2,1)S(1)}, u32[]{:S(2)}, u32[]{:S(2)}) collective-permute-start(bf16[24,2048]{1,0:T(8,128)(2,1)S(1)} %get-tuple-element.72), channel_id=1, source_target_pairs={{0,2},{2,0},{4,6},{6,4},{1,3},{3,1},{5,7},{7,5},{8,10},{10,8},{12,... | collective-permute-start | bytes 294920 | tf_op jit(solution)/shard_map/ppermute | solution.py:19
  38.5 2.1 %collective-permute-done.14.refs_0_ = bf16[24,2048]{1,0:T(8,128)(2,1)S(1)} collective-permute-done((bf16[24,2048]{1,0:T(8,128)(2,1)S(1)}, bf16[24,2048]{1,0:T(8,128)(2,1)S(1)}, u32[]{:S(2)}, u32[]{:S(2)}) %collective-permute-start.14) | collective-permute-done | bytes 98336 | tf_op jit(solution)/shard_map/ppermute | solution.py:19
  40.5 1.0 %collective-permute-done.15.refs_1_ = bf16[24,2048]{1,0:T(8,128)(2,1)S(1)} collective-permute-done((bf16[24,2048]{1,0:T(8,128)(2,1)S(1)}, bf16[24,2048]{1,0:T(8,128)(2,1)S(1)}, u32[]{:S(2)}, u32[]{:S(2)}) %collective-permute-start.15) | collective-permute-done | bytes 98336 | tf_op jit(solution)/shard_map/ppermute | solution.py:19
  42.2 1.2 %collective-permute-done.17.other_ref = bf16[24,1024]{1,0:T(8,128)(2,1)S(1)} collective-permute-done((bf16[24,1024]{1,0:T(8,128)(2,1)S(1)}, bf16[24,1024]{1,0:T(8,128)(2,1)S(1)}, u32[]{:S(2)}, u32[]{:S(2)}) %collective-permute-start.17) | collective-permute-done | bytes 49184 | tf_op jit(solution)/shard_map/ppermute | solution.py:19
  43.6 1.3 %collective-permute-start.18 = (bf16[24,512]{1,0:T(8,128)(2,1)S(1)}, bf16[24,512]{1,0:T(8,128)(2,1)S(1)}, u32[]{:S(2)}, u32[]{:S(2)}) collective-permute-start(bf16[24,512]{1,0:T(8,128)(2,1)S(1)} %get-tuple-element.77), channel_id=1, source_target_pairs={{0,24},{8,16},{16,8},{24,0},{1,25},{9,17},{17,9},{25,1},{2,26},{10... | collective-permute-start | bytes 73736 | tf_op jit(solution)/shard_map/ppermute | solution.py:19
  45.6 2.5 %collective-permute-start.20 = (bf16[24,512]{1,0:T(8,128)(2,1)S(1)}, bf16[24,512]{1,0:T(8,128)(2,1)S(1)}, u32[]{:S(2)}, u32[]{:S(2)}) collective-permute-start(bf16[24,512]{1,0:T(8,128)(2,1)S(1)} %get-tuple-element.79), channel_id=1, source_target_pairs={{0,8},{8,0},{16,24},{24,16},{1,9},{9,1},{17,25},{25,17},{2,10},{10... | collective-permute-start | bytes 73736 | tf_op jit(solution)/shard_map/ppermute | solution.py:19
  48.1 1.2 %collective-permute-done.18.refs_0_ = bf16[24,512]{1,0:T(8,128)(2,1)S(1)} collective-permute-done((bf16[24,512]{1,0:T(8,128)(2,1)S(1)}, bf16[24,512]{1,0:T(8,128)(2,1)S(1)}, u32[]{:S(2)}, u32[]{:S(2)}) %collective-permute-start.18) | collective-permute-done | bytes 24608 | tf_op jit(solution)/shard_map/ppermute | solution.py:19
  (41 shorter events, 9.9 us)
Async XLA Ops:
  0.0 8.5 %collective-permute-start.3 = (bf16[384,2048]{1,0:T(8,128)(2,1)}, bf16[384,2048]{1,0:T(8,128)(2,1)S(1)}, u32[]{:S(2)}, u32[]{:S(2)}) collective-permute-start(bf16[384,2048]{1,0:T(8,128)(2,1)} %bitcast.12), channel_id=1, source_target_pairs={{0,1},{1,0},{2,3},{3,2},{4,5},{5,4},{6,7},{7,6},{8,9},{9,8},{10,11... | collective-permute-start | bytes 4718600 | tf_op jit(solution)/shard_map/ppermute | solution.py:19
  0.5 8.1 %collective-permute-start.4 = (bf16[192,2048]{1,0:T(8,128)(2,1)}, bf16[192,2048]{1,0:T(8,128)(2,1)S(1)}, u32[]{:S(2)}, u32[]{:S(2)}) collective-permute-start(bf16[192,2048]{1,0:T(8,128)(2,1)} %bitcast.17), channel_id=1, source_target_pairs={{0,1},{1,0},{2,3},{3,2},{4,5},{5,4},{6,7},{7,6},{8,9},{9,8},{10,11... | collective-permute-start | bytes 2359304 | tf_op jit(solution)/shard_map/ppermute | solution.py:19
  0.5 4.9 %collective-permute-start = (bf16[832,256]{1,0:T(8,128)(2,1)}, bf16[832,256]{1,0:T(8,128)(2,1)S(1)}, u32[]{:S(2)}, u32[]{:S(2)}) collective-permute-start(bf16[832,256]{1,0:T(8,128)(2,1)} %bitcast.23), channel_id=1, source_target_pairs={{0,1},{1,0},{2,3},{3,2},{4,5},{5,4},{6,7},{7,6},{8,9},{9,8},{10,11... | collective-permute-start | bytes 1277960 | tf_op jit(solution)/shard_map/ppermute | solution.py:19
  1.8 3.7 %collective-permute-start.1 = (s32[1,128]{1,0:T(1,128)S(1)}, s32[1,128]{1,0:T(1,128)S(1)}, u32[]{:S(2)}, u32[]{:S(2)}) collective-permute-start(s32[1,128]{1,0:T(1,128)S(1)} %pad_bitcast_fusion.own_ints_ref), channel_id=1, source_target_pairs={{0,1},{1,0},{2,3},{3,2},{4,5},{5,4},{6,7},{7,6},{8,9},{9,8},{10,11... | collective-permute-start | bytes 1544 | tf_op jit(solution)/shard_map/ppermute | solution.py:19
  5.4 24.3 %copy-start = (bf16[1,2,192,2048]{3,2,1,0:T(8,128)(2,1)S(1)}, bf16[1,2,192,2048]{3,2,1,0:T(8,128)(2,1)}, u32[]{:S(2)}) copy-start(bf16[1,2,192,2048]{3,2,1,0:T(8,128)(2,1)} %param.29) | copy-start | bytes 4718596
  5.4 24.2 %copy-start.2 = (f32[2048]{0:T(1024)S(1)}, f32[2048]{0:T(1024)}, u32[]{:S(2)}) copy-start(f32[2048]{0:T(1024)} %param.25) | copy-start | bytes 24580
  7.0 1.5 %collective-permute-start.2 = (bf16[24,2560]{1,0:T(8,128)(2,1)S(1)}, bf16[24,2560]{1,0:T(8,128)(2,1)S(1)}, u32[]{:S(2)}, u32[]{:S(2)}) collective-permute-start(bf16[24,2560]{1,0:T(8,128)(2,1)S(1)} %get-tuple-element.49), channel_id=1, source_target_pairs={{0,1},{1,0},{2,3},{3,2},{4,5},{5,4},{6,7},{7,6},{8,9},{9,8},{10,11... | collective-permute-start | bytes 368648 | tf_op jit(solution)/shard_map/ppermute | solution.py:19
  8.5 5.7 %collective-permute-start.5 = (bf16[24,640]{1,0:T(8,128)(2,1)S(1)}, bf16[24,640]{1,0:T(8,128)(2,1)S(1)}, u32[]{:S(2)}, u32[]{:S(2)}) collective-permute-start(bf16[24,640]{1,0:T(8,128)(2,1)S(1)} %get-tuple-element.52), channel_id=1, source_target_pairs={{0,6},{2,4},{4,2},{6,0},{1,7},{3,5},{5,3},{7,1},{8,14},{10,12},{12... | collective-permute-start | bytes 92168 | tf_op jit(solution)/shard_map/ppermute | solution.py:19
  12.4 3.9 %collective-permute-start.6 = (bf16[24,640]{1,0:T(8,128)(2,1)S(1)}, bf16[24,640]{1,0:T(8,128)(2,1)S(1)}, u32[]{:S(2)}, u32[]{:S(2)}) collective-permute-start(bf16[24,640]{1,0:T(8,128)(2,1)S(1)} %get-tuple-element.53), channel_id=1, source_target_pairs={{0,4},{2,6},{4,0},{6,2},{1,5},{3,7},{5,1},{7,3},{8,12},{10,14},{12... | collective-permute-start | bytes 92168 | tf_op jit(solution)/shard_map/ppermute | solution.py:19
  12.9 3.9 %collective-permute-start.7 = (bf16[24,640]{1,0:T(8,128)(2,1)S(1)}, bf16[24,640]{1,0:T(8,128)(2,1)S(1)}, u32[]{:S(2)}, u32[]{:S(2)}) collective-permute-start(bf16[24,640]{1,0:T(8,128)(2,1)S(1)} %get-tuple-element.54), channel_id=1, source_target_pairs={{0,2},{2,0},{4,6},{6,4},{1,3},{3,1},{5,7},{7,5},{8,10},{10,8},{12,... | collective-permute-start | bytes 92168 | tf_op jit(solution)/shard_map/ppermute | solution.py:19
  16.8 4.2 %collective-permute-start.10 = (bf16[24,640]{1,0:T(8,128)(2,1)S(1)}, bf16[24,640]{1,0:T(8,128)(2,1)S(1)}, u32[]{:S(2)}, u32[]{:S(2)}) collective-permute-start(bf16[24,640]{1,0:T(8,128)(2,1)S(1)} %add_convert_fusion.refs_3_), channel_id=1, source_target_pairs={{0,8},{8,0},{16,24},{24,16},{1,9},{9,1},{17,25},{25,17},{2,10},{10... | collective-permute-start | bytes 92168 | tf_op jit(solution)/shard_map/ppermute | solution.py:19
  18.5 5.7 %collective-permute-start.8 = (bf16[24,640]{1,0:T(8,128)(2,1)S(1)}, bf16[24,640]{1,0:T(8,128)(2,1)S(1)}, u32[]{:S(2)}, u32[]{:S(2)}) collective-permute-start(bf16[24,640]{1,0:T(8,128)(2,1)S(1)} %add_convert_fusion.refs_3_), channel_id=1, source_target_pairs={{0,24},{8,16},{16,8},{24,0},{1,25},{9,17},{17,9},{25,1},{2,26},{10... | collective-permute-start | bytes 92168 | tf_op jit(solution)/shard_map/ppermute | solution.py:19
  20.9 5.1 %collective-permute-start.9 = (bf16[24,640]{1,0:T(8,128)(2,1)S(1)}, bf16[24,640]{1,0:T(8,128)(2,1)S(1)}, u32[]{:S(2)}, u32[]{:S(2)}) collective-permute-start(bf16[24,640]{1,0:T(8,128)(2,1)S(1)} %add_convert_fusion.refs_3_), channel_id=1, source_target_pairs={{0,16},{8,24},{16,0},{24,8},{1,17},{9,25},{17,1},{25,9},{2,18},{10... | collective-permute-start | bytes 92168 | tf_op jit(solution)/shard_map/ppermute | solution.py:19
  26.1 5.6 %collective-permute-start.13 = (bf16[4,24,512]{2,1,0:T(8,128)(2,1)S(1)}, bf16[4,24,512]{2,1,0:T(8,128)(2,1)S(1)}, u32[]{:S(2)}, u32[]{:S(2)}) collective-permute-start(bf16[4,24,512]{2,1,0:T(8,128)(2,1)S(1)} %get-tuple-element.55), channel_id=1, source_target_pairs={{0,6},{2,4},{4,2},{6,0},{1,7},{3,5},{5,3},{7,1},{8,14},{10,12},{12... | collective-permute-start | bytes 294920 | tf_op jit(solution)/shard_map/ppermute | solution.py:19
  27.6 5.1 %collective-permute-start.12 = (bf16[4,24,512]{2,1,0:T(8,128)(2,1)S(1)}, bf16[4,24,512]{2,1,0:T(8,128)(2,1)S(1)}, u32[]{:S(2)}, u32[]{:S(2)}) collective-permute-start(bf16[4,24,512]{2,1,0:T(8,128)(2,1)S(1)} %get-tuple-element.55), channel_id=1, source_target_pairs={{0,4},{2,6},{4,0},{6,2},{1,5},{3,7},{5,1},{7,3},{8,12},{10,14},{12... | collective-permute-start | bytes 294920 | tf_op jit(solution)/shard_map/ppermute | solution.py:19
  28.2 5.0 %collective-permute-start.11 = (bf16[4,24,512]{2,1,0:T(8,128)(2,1)S(1)}, bf16[4,24,512]{2,1,0:T(8,128)(2,1)S(1)}, u32[]{:S(2)}, u32[]{:S(2)}) collective-permute-start(bf16[4,24,512]{2,1,0:T(8,128)(2,1)S(1)} %get-tuple-element.55), channel_id=1, source_target_pairs={{0,2},{2,0},{4,6},{6,4},{1,3},{3,1},{5,7},{7,5},{8,10},{10,8},{12,... | collective-permute-start | bytes 294920 | tf_op jit(solution)/shard_map/ppermute | solution.py:19
  33.1 1.1 %copy-start.1 = (bf16[1,192,2048]{2,1,0:T(8,128)(2,1)S(1)}, bf16[1,192,2048]{2,1,0:T(8,128)(2,1)}, u32[]{:S(2)}) copy-start(bf16[1,192,2048]{2,1,0:T(8,128)(2,1)} %param.30) | copy-start | bytes 2359300
  34.9 5.6 %collective-permute-start.14 = (bf16[24,2048]{1,0:T(8,128)(2,1)S(1)}, bf16[24,2048]{1,0:T(8,128)(2,1)S(1)}, u32[]{:S(2)}, u32[]{:S(2)}) collective-permute-start(bf16[24,2048]{1,0:T(8,128)(2,1)S(1)} %get-tuple-element.70), channel_id=1, source_target_pairs={{0,6},{2,4},{4,2},{6,0},{1,7},{3,5},{5,3},{7,1},{8,14},{10,12},{12... | collective-permute-start | bytes 294920 | tf_op jit(solution)/shard_map/ppermute | solution.py:19
  36.5 5.1 %collective-permute-start.15 = (bf16[24,2048]{1,0:T(8,128)(2,1)S(1)}, bf16[24,2048]{1,0:T(8,128)(2,1)S(1)}, u32[]{:S(2)}, u32[]{:S(2)}) collective-permute-start(bf16[24,2048]{1,0:T(8,128)(2,1)S(1)} %get-tuple-element.71), channel_id=1, source_target_pairs={{0,4},{2,6},{4,0},{6,2},{1,5},{3,7},{5,1},{7,3},{8,12},{10,14},{12... | collective-permute-start | bytes 294920 | tf_op jit(solution)/shard_map/ppermute | solution.py:19
  37.5 4.6 %collective-permute-start.16 = (bf16[24,2048]{1,0:T(8,128)(2,1)S(1)}, bf16[24,2048]{1,0:T(8,128)(2,1)S(1)}, u32[]{:S(2)}, u32[]{:S(2)}) collective-permute-start(bf16[24,2048]{1,0:T(8,128)(2,1)S(1)} %get-tuple-element.72), channel_id=1, source_target_pairs={{0,2},{2,0},{4,6},{6,4},{1,3},{3,1},{5,7},{7,5},{8,10},{10,8},{12,... | collective-permute-start | bytes 294920 | tf_op jit(solution)/shard_map/ppermute | solution.py:19
  42.1 1.3 %collective-permute-start.17 = (bf16[24,1024]{1,0:T(8,128)(2,1)S(1)}, bf16[24,1024]{1,0:T(8,128)(2,1)S(1)}, u32[]{:S(2)}, u32[]{:S(2)}) collective-permute-start(bf16[24,1024]{1,0:T(8,128)(2,1)S(1)} %get-tuple-element.75), channel_id=1, source_target_pairs={{0,1},{1,0},{2,3},{3,2},{4,5},{5,4},{6,7},{7,6},{8,9},{9,8},{10,11... | collective-permute-start | bytes 147464 | tf_op jit(solution)/shard_map/ppermute | solution.py:19
  43.6 5.7 %collective-permute-start.18 = (bf16[24,512]{1,0:T(8,128)(2,1)S(1)}, bf16[24,512]{1,0:T(8,128)(2,1)S(1)}, u32[]{:S(2)}, u32[]{:S(2)}) collective-permute-start(bf16[24,512]{1,0:T(8,128)(2,1)S(1)} %get-tuple-element.77), channel_id=1, source_target_pairs={{0,24},{8,16},{16,8},{24,0},{1,25},{9,17},{17,9},{25,1},{2,26},{10... | collective-permute-start | bytes 73736 | tf_op jit(solution)/shard_map/ppermute | solution.py:19
  44.9 5.0 %collective-permute-start.19 = (bf16[24,512]{1,0:T(8,128)(2,1)S(1)}, bf16[24,512]{1,0:T(8,128)(2,1)S(1)}, u32[]{:S(2)}, u32[]{:S(2)}) collective-permute-start(bf16[24,512]{1,0:T(8,128)(2,1)S(1)} %get-tuple-element.78), channel_id=1, source_target_pairs={{0,16},{8,24},{16,0},{24,8},{1,17},{9,25},{17,1},{25,9},{2,18},{10... | collective-permute-start | bytes 73736 | tf_op jit(solution)/shard_map/ppermute | solution.py:19
  45.6 4.4 %collective-permute-start.20 = (bf16[24,512]{1,0:T(8,128)(2,1)S(1)}, bf16[24,512]{1,0:T(8,128)(2,1)S(1)}, u32[]{:S(2)}, u32[]{:S(2)}) collective-permute-start(bf16[24,512]{1,0:T(8,128)(2,1)S(1)} %get-tuple-element.79), channel_id=1, source_target_pairs={{0,8},{8,0},{16,24},{24,16},{1,9},{9,1},{17,25},{25,17},{2,10},{10... | collective-permute-start | bytes 73736 | tf_op jit(solution)/shard_map/ppermute | solution.py:19

commit v6 on v5

--- a/solution.py
+++ b/solution.py
@@ -17,6 +17,18 @@
 def send(value, axes, step):
     size = lax.axis_size(axes)
     return lax.ppermute(value, axes, [(i, i ^ step) for i in range(size)])
+
+
+def cross(value, axis, step):
+    size, pools = lax.axis_size(axis), lax.axis_size("pool")
+    pairs = [
+        (i * pools + p, (i ^ step) * pools + (p ^ (step & 1))) for i in range(size) for p in range(pools)
+    ]
+    return lax.ppermute(value, (axis, "pool"), pairs)
+
+
+def taken():
+    return lax.axis_index("pool") ^ (lax.axis_index("head") & 1) ^ (lax.axis_index("req") & 1)
 
 
 def dot(a, b, contract=((1,), (0,))):
@@ -47,18 +59,20 @@
 
 def place_kernel(sizes, *refs):
     heads, pools, planes, count = sizes
-    sources, refs = refs[:count], refs[count:]
-    residual_ref, choice_ref, route_ref, placed_ref = refs[:4]
-    targets, semaphores = refs[4 : 4 + count], refs[-1]
-    head, pool = lax.axis_index("head"), lax.axis_index("pool")
-    picked = {count - 2: pool, count - 1: head}
+    sources, placed_ref, targets = refs[:count], refs[count], refs[count + 1 : -1]
+    residual_ref, choice_ref, route_ref = targets[-3:]
+    semaphores = refs[-1]
+    head, mine = lax.axis_index("head"), taken()
+    first = jnp.where(lax.axis_index("pool") == 0, 1.0, 0.0)
+    picked = {count - 5: mine, count - 4: head}
     copies = []
     for i in range(count):
         source = sources[i].at[picked[i]] if i in picked else sources[i]
         copies.append(pltpu.make_async_copy(source, targets[i], semaphores.at[i]))
-    for copy in copies:
+    for copy in reversed(copies):
         copy.start()
-    first = jnp.where(pool == 0, 1.0, 0.0)
+    for copy in copies[-3:]:
+        copy.wait()
     rows_here, width = residual_ref.shape
     part = rows_here // pools
     total = heads * rows_here
@@ -67,7 +81,7 @@
     own = None
     for p in range(pools):
         inside = line - (p * heads * part + head * part)
-        one = (inside >= 0) & (inside < part) & (lane == inside + (pool ^ p) * part)
+        one = (inside >= 0) & (inside < part) & (lane == inside + (mine ^ p) * part)
         own = one if own is None else own | one
     spread = jnp.where(own, first, 0.0)
     mixes = placed_ref.shape[1] - width
@@ -88,7 +102,7 @@
         placed_ref[:, start + columns : start + columns + share] = mix[
             :, h * share : (h + 1) * share
         ].astype(BF16)
-    for copy in copies:
+    for copy in copies[:-3]:
         copy.wait()
 
 
@@ -179,6 +193,12 @@
         out[...] = (own_ref[:, at] + other_ref[:, at].astype(F32)).astype(out.dtype)
 
 
+def sum_kernel(count, *refs):
+    total = functools.reduce(jnp.add, [part[...].astype(F32) for part in refs[:count]])
+    for out in refs[count:]:
+        out[...] = total.astype(BF16)
+
+
 def stack_kernel(*refs):
     parts, (all_ref, first_ref) = refs[:-2], refs[-2:]
     for step, part in enumerate(reversed(parts)):
@@ -206,7 +226,7 @@
         projected_ref[...] = before_ref[...] + projected
         squares_ref[...] = before_squares_ref[...] + squares
         return
-    order_ref, projected_ref, squares_ref, route_ref, own_ref = refs
+    order_ref, _, projected_ref, squares_ref, route_ref, own_ref = refs
     projected_ref[...] = projected
     squares_ref[...] = squares
     plane = lax.axis_index("req")
@@ -250,9 +270,9 @@
 
 
 def spread_kernel(own_ref, other_ref, order_ref, *outs):
-    pool = lax.axis_index("pool")
+    mine = taken()
     own, other = own_ref[...].astype(F32), other_ref[...].astype(F32)
-    both = jnp.concatenate([jnp.where(pool == 0, own, other), jnp.where(pool == 0, other, own)], axis=0)
+    both = jnp.concatenate([jnp.where(mine == 0, own, other), jnp.where(mine == 0, other, own)], axis=0)
     both = both.astype(BF16)
     columns = both.shape[1] // 2
     value = dot(order_ref[0], both[:, :columns]) + dot(order_ref[1], both[:, columns:])
@@ -342,16 +362,19 @@
         one_hot(plane_order, pools * planes * part),
         one_hot(pool_order, requests),
         one_hot(head_order, planes * rows),
-    )
-    copied = [shape(*array.shape[i // 4 :], dtype=array.dtype) for i, array in enumerate(outside)]
+        residual,
+        expert_choice.T,
+        route_weight.T,
+    )
+    copied = [
+        shape(*array.shape[i // 4 :], dtype=array.dtype) for i, array in enumerate(outside[:-3])
+    ]
     placed, held_cache, held_queries, held_weight, plane_order, pool_order, head_order = kernel_call(
         functools.partial(place_kernel, (heads, pools, planes, len(outside))),
         [shape(requests, heads * (columns + mixes))] + copied,
-        [
-            pltpu.with_memory_space_constraint(arg, pltpu.HBM)
-            for arg in (residual, expert_choice.T, route_weight.T)
-        ],
-        [pltpu.SemaphoreType.DMA((len(outside),))],
+        (),
+        [pltpu.VMEM(array.shape, array.dtype) for array in outside[-3:]]
+        + [pltpu.SemaphoreType.DMA((len(outside),))],
         outside,
     )
     args = held(
@@ -379,12 +402,12 @@
         [shape(rows, columns + mixes, dtype=F32)] + [piece] * (heads - 1),
         held(own, other),
     )
-    hidden = pieces[0]
-    for step in reversed(range(1, heads)):
-        hidden = hidden + send(pieces[step], "head", step).astype(F32)
-    hidden = hidden.astype(BF16)
-
-    arrived = [send(hidden, "req", step) for step in reversed(range(1, planes))] + [hidden]
+    arrived = [cross(pieces[step], "head", step) for step in reversed(range(1, heads))] + [pieces[0]]
+    hidden = kernel_call(
+        functools.partial(sum_kernel, heads), [piece] * planes, held(*arrived)
+    )
+
+    arrived = [cross(hidden[step], "req", step) for step in reversed(range(1, planes))] + [hidden[0]]
     plane_blocks, sent = kernel_call(
         stack_kernel,
         [shape(planes, rows, columns + mixes), shape(planes, rows, columns)],
@@ -396,13 +419,13 @@
     *state, route, own = kernel_call(
         functools.partial(project_kernel, 0, planes),
         sums + [shape(total, 1, dtype=F32), shape(total, columns, dtype=F32)],
-        held(plane_blocks, *weights, head_order),
+        held(plane_blocks, *weights, head_order, down_weight),
     )
     for step in reversed(range(1, heads)):
         state = kernel_call(
             functools.partial(project_kernel, step, planes),
             sums,
-            held(send(sent, "head", step), *weights, *state),
+            held(cross(sent, "head", step), *weights, *state),
         )
     piece = shape(planes * part, width)
     pieces = kernel_call(
@@ -410,7 +433,7 @@
         [shape(planes * part, width, dtype=F32)] + [piece] * (heads - 1),
         held(*state, route, own, down_weight, other_down, head_order),
     )
-    arrived = [send(pieces[step], "head", step) for step in reversed(range(1, heads))] + [pieces[0]]
+    arrived = [cross(pieces[step], "head", step) for step in reversed(range(1, heads))] + [pieces[0]]
     own, other = kernel_call(
         halve_kernel, [shape(planes * part, width // pools)] * 2, held(*arrived)
     )

time: 51 us -> 51.8 us (1.016)
  waiting for transfers between devices: 18.8 us -> 23 us
  starting transfers between devices: 21.9 us -> 20.2 us
  Pallas kernels: 6.83 us -> 6.04 us
  local copies, waits for them, and re-layouts: 2.18 us -> 1.46 us
    ppermute x0 -> x12, waiting for transfers between devices: none -> 17 us  [cross(): return lax.ppermute(value, (axis, 'pool'), pairs)]
    ppermute x21 -> x9, starting transfers between devices: 21.9 us -> 6.13 us  [send(): return lax.ppermute(value, axes, [(i, i ^ step) for i in range(size)])]
    ppermute x0 -> x12, starting transfers between devices: none -> 14.1 us  [cross(): return lax.ppermute(value, (axis, 'pool'), pairs)]
    ppermute x21 -> x9, waiting for transfers between devices: 18.8 us -> 5.93 us  [send(): return lax.ppermute(value, axes, [(i, i ^ step) for i in range(size)])]
    pallas_call x12 -> x13, Pallas kernels: 6.83 us -> 6.04 us  [kernel_call(): pl.pallas_call(body, out_shape=jax.tree.map(lambda out: pltpu.VMEM(out.sh...]
    unnamed x7, local copies, waits for them, and re-layouts: 1.35 us -> 0.64 us
  transfers between devices with their start and end apart: 21 -> 21, of which waited for: 15 -> 13; matrix products, arithmetic and copies ran while one was open for 3% -> 3% of each run, Pallas kernels for 11% -> 9%
where the time goes in v6:
time: 51.8 us; the launch traced here: 51.6 us
  waiting for transfers between devices  23 us (44%)
  starting transfers between devices  20.2 us (39%)
  Pallas kernels  6.04 us (12%)
  local copies, waits for them, and re-layouts  1.46 us (3%)
  other arithmetic  0.78 us (2%)
    ppermute x12, waiting for transfers between devices, cross(): return lax.ppermute(value, (axis, 'pool'), pairs)  17 us
    ppermute x12, starting transfers between devices, cross(): return lax.ppermute(value, (axis, 'pool'), pairs)  14.1 us
    ppermute x9, starting transfers between devices, send(): return lax.ppermute(value, axes, [(i, i ^ step) for i in range(size)])  6.13 us
    pallas_call x13, Pallas kernels, kernel_call(): pl.pallas_call(body, out_shape=jax.tree.map(lambda out: pltpu.VMEM(out.sh...  6.04 us
    ppermute x9, waiting for transfers between devices, send(): return lax.ppermute(value, axes, [(i, i ^ step) for i in range(size)])  5.93 us
  transfers between devices with their start and end apart: 21, of which 13 were waited for; matrix products, arithmetic and copies ran while one was open for 3% of the time, Pallas kernels for 9%

profile of v6, /device:TPU:0, one launch (start us, length us, event | category | flops | bytes accessed | tf_op | source)
XLA Modules:
  0.0 51.6 jit_solution(13500415367766636974)
XLA Ops:
  1.8 0.8 %reshape.22.new_ref = bf16[96,256]{1,0:T(8,128)(2,1)S(1)} reshape(bf16[48,2,1,256]{3,1,2,0:T(2,128)(2,1)} %param.18) | data formatting | bytes 98304 | tf_op jit(solution)/shard_map/reshape | solution.py:382
  2.7 1.9 %shard_map.163 = (bf16[48,2560]{1,0:T(8,128)(2,1)S(1)}, bf16[832,256]{1,0:T(8,128)(2,1)S(1)}, bf16[48,1024]{1,0:T(8,128)(2,1)S(1)}, bf16[512,2048]{1,0:T(8,128)(...) custom-call(bf16[832,256]{1,0:T(8,128)(2,1)} %bitcast.25, ...), custom_call_target="tpu_custom_call" | custom-call | tf_op jit(solution)/shard_map/pallas_call | solution.py:39
  5.4 1.6 %shard_map.164 = (f32[24,2560]{1,0:T(8,128)S(1)}, bf16[24,2560]{1,0:T(8,128)(2,1)S(1)}) custom-call(bf16[48,1024]{1,0:T(8,128)(2,1)S(1)} %get-tuple-element.47.q_ref, bf16[96,256]{1,0:T(8,128)(2,1)S(1)} %reshape.22.new_ref, bf16[832,256]{1,0:T(8,128)(2,1)S(1)} %get-tuple-element.48.own_ref, bf16[832,256]{1,0:T(8,128)(2,1)S(1)} %collective-permute-done.other_ref, ...), custom_call_target="tpu_custom_call" | custom-call | tf_op jit(solution)/shard_map/pallas_call | solution.py:39
  7.5 1.0 %collective-permute-done.2.other_ref = bf16[24,2560]{1,0:T(8,128)(2,1)S(1)} collective-permute-done((bf16[24,2560]{1,0:T(8,128)(2,1)S(1)}, bf16[24,2560]{1,0:T(8,128)(2,1)S(1)}, u32[]{:S(2)}, u32[]{:S(2)}) %collective-permute-start.2) | collective-permute-done | bytes 122912 | tf_op jit(solution)/shard_map/ppermute | solution.py:19
  8.5 3.6 %collective-permute-start.5 = (bf16[24,640]{1,0:T(8,128)(2,1)S(1)}, bf16[24,640]{1,0:T(8,128)(2,1)S(1)}, u32[]{:S(2)}, u32[]{:S(2)}) collective-permute-start(bf16[24,640]{1,0:T(8,128)(2,1)S(1)} %get-tuple-element.55), channel_id=1, source_target_pairs={{0,7},{1,6},{2,5},{3,4},{4,3},{5,2},{6,1},{7,0},{8,15},{9,14},{10,... | collective-permute-start | bytes 92168 | tf_op jit(solution)/shard_map/ppermute | solution.py:27
  12.6 1.1 %collective-permute-done.5.refs_0_ = bf16[24,640]{1,0:T(8,128)(2,1)S(1)} collective-permute-done((bf16[24,640]{1,0:T(8,128)(2,1)S(1)}, bf16[24,640]{1,0:T(8,128)(2,1)S(1)}, u32[]{:S(2)}, u32[]{:S(2)}) %collective-permute-start.5) | collective-permute-done | bytes 30752 | tf_op jit(solution)/shard_map/ppermute | solution.py:27
  13.7 2.3 %collective-permute-done.6.refs_1_ = bf16[24,640]{1,0:T(8,128)(2,1)S(1)} collective-permute-done((bf16[24,640]{1,0:T(8,128)(2,1)S(1)}, bf16[24,640]{1,0:T(8,128)(2,1)S(1)}, u32[]{:S(2)}, u32[]{:S(2)}) %collective-permute-start.6) | collective-permute-done | bytes 30752 | tf_op jit(solution)/shard_map/ppermute | solution.py:27
  16.0 1.4 %collective-permute-start.10 = (bf16[24,640]{1,0:T(8,128)(2,1)S(1)}, bf16[24,640]{1,0:T(8,128)(2,1)S(1)}, u32[]{:S(2)}, u32[]{:S(2)}) collective-permute-start(bf16[24,640]{1,0:T(8,128)(2,1)S(1)} %get-tuple-element.61), channel_id=1, source_target_pairs={{0,9},{1,8},{8,1},{9,0},{16,25},{17,24},{24,17},{25,16},{2,11},{3,... | collective-permute-start | bytes 92168 | tf_op jit(solution)/shard_map/ppermute | solution.py:27
  17.4 2.5 %collective-permute-start.8 = (bf16[24,640]{1,0:T(8,128)(2,1)S(1)}, bf16[24,640]{1,0:T(8,128)(2,1)S(1)}, u32[]{:S(2)}, u32[]{:S(2)}) collective-permute-start(bf16[24,640]{1,0:T(8,128)(2,1)S(1)} %get-tuple-element.59), channel_id=1, source_target_pairs={{0,25},{1,24},{8,17},{9,16},{16,9},{17,8},{24,1},{25,0},{2,27},{3,... | collective-permute-start | bytes 92168 | tf_op jit(solution)/shard_map/ppermute | solution.py:27
  20.0 2.5 %collective-permute-done.8.refs_0_ = bf16[24,640]{1,0:T(8,128)(2,1)S(1)} collective-permute-done((bf16[24,640]{1,0:T(8,128)(2,1)S(1)}, bf16[24,640]{1,0:T(8,128)(2,1)S(1)}, u32[]{:S(2)}, u32[]{:S(2)}) %collective-permute-start.8) | collective-permute-done | bytes 30752 | tf_op jit(solution)/shard_map/ppermute | solution.py:27
  22.5 2.5 %collective-permute-done.9.refs_1_ = bf16[24,640]{1,0:T(8,128)(2,1)S(1)} collective-permute-done((bf16[24,640]{1,0:T(8,128)(2,1)S(1)}, bf16[24,640]{1,0:T(8,128)(2,1)S(1)}, u32[]{:S(2)}, u32[]{:S(2)}) %collective-permute-start.9) | collective-permute-done | bytes 30752 | tf_op jit(solution)/shard_map/ppermute | solution.py:27
  25.1 1.6 %collective-permute-start.12 = (bf16[4,24,512]{2,1,0:T(8,128)(2,1)S(1)}, bf16[4,24,512]{2,1,0:T(8,128)(2,1)S(1)}, u32[]{:S(2)}, u32[]{:S(2)}) collective-permute-start(bf16[4,24,512]{2,1,0:T(8,128)(2,1)S(1)} %get-tuple-element.63), channel_id=1, source_target_pairs={{0,4},{1,5},{2,6},{3,7},{4,0},{5,1},{6,2},{7,3},{8,12},{9,13},{10,... | collective-permute-start | bytes 294920 | tf_op jit(solution)/shard_map/ppermute | solution.py:27
  26.7 1.3 %collective-permute-start.11 = (bf16[4,24,512]{2,1,0:T(8,128)(2,1)S(1)}, bf16[4,24,512]{2,1,0:T(8,128)(2,1)S(1)}, u32[]{:S(2)}, u32[]{:S(2)}) collective-permute-start(bf16[4,24,512]{2,1,0:T(8,128)(2,1)S(1)} %get-tuple-element.63), channel_id=1, source_target_pairs={{0,3},{1,2},{2,1},{3,0},{4,7},{5,6},{6,5},{7,4},{8,11},{9,10},{10,... | collective-permute-start | bytes 294920 | tf_op jit(solution)/shard_map/ppermute | solution.py:27
  28.5 1.9 %collective-permute-done.13.block_ref = bf16[4,24,512]{2,1,0:T(8,128)(2,1)S(1)} collective-permute-done((bf16[4,24,512]{2,1,0:T(8,128)(2,1)S(1)}, bf16[4,24,512]{2,1,0:T(8,128)(2,1)S(1)}, u32[]{:S(2)}, u32[]{:S(2)}) %collective-permute-start.13) | collective-permute-done | bytes 98336 | tf_op jit(solution)/shard_map/ppermute | solution.py:27
  30.7 1.6 %collective-permute-done.12.block_ref = bf16[4,24,512]{2,1,0:T(8,128)(2,1)S(1)} collective-permute-done((bf16[4,24,512]{2,1,0:T(8,128)(2,1)S(1)}, bf16[4,24,512]{2,1,0:T(8,128)(2,1)S(1)}, u32[]{:S(2)}, u32[]{:S(2)}) %collective-permute-start.12) | collective-permute-done | bytes 98336 | tf_op jit(solution)/shard_map/ppermute | solution.py:27
  33.8 1.2 %collective-permute-start.14 = (bf16[24,2048]{1,0:T(8,128)(2,1)S(1)}, bf16[24,2048]{1,0:T(8,128)(2,1)S(1)}, u32[]{:S(2)}, u32[]{:S(2)}) collective-permute-start(bf16[24,2048]{1,0:T(8,128)(2,1)S(1)} %get-tuple-element.78), channel_id=1, source_target_pairs={{0,7},{1,6},{2,5},{3,4},{4,3},{5,2},{6,1},{7,0},{8,15},{9,14},{10,... | collective-permute-start | bytes 294920 | tf_op jit(solution)/shard_map/ppermute | solution.py:27
  35.0 1.4 %collective-permute-start.15 = (bf16[24,2048]{1,0:T(8,128)(2,1)S(1)}, bf16[24,2048]{1,0:T(8,128)(2,1)S(1)}, u32[]{:S(2)}, u32[]{:S(2)}) collective-permute-start(bf16[24,2048]{1,0:T(8,128)(2,1)S(1)} %get-tuple-element.79), channel_id=1, source_target_pairs={{0,4},{1,5},{2,6},{3,7},{4,0},{5,1},{6,2},{7,3},{8,12},{9,13},{10,... | collective-permute-start | bytes 294920 | tf_op jit(solution)/shard_map/ppermute | solution.py:27
  36.8 2.8 %collective-permute-done.14.refs_0_ = bf16[24,2048]{1,0:T(8,128)(2,1)S(1)} collective-permute-done((bf16[24,2048]{1,0:T(8,128)(2,1)S(1)}, bf16[24,2048]{1,0:T(8,128)(2,1)S(1)}, u32[]{:S(2)}, u32[]{:S(2)}) %collective-permute-start.14) | collective-permute-done | bytes 98336 | tf_op jit(solution)/shard_map/ppermute | solution.py:27
  39.6 2.4 %collective-permute-done.15.refs_1_ = bf16[24,2048]{1,0:T(8,128)(2,1)S(1)} collective-permute-done((bf16[24,2048]{1,0:T(8,128)(2,1)S(1)}, bf16[24,2048]{1,0:T(8,128)(2,1)S(1)}, u32[]{:S(2)}, u32[]{:S(2)}) %collective-permute-start.15) | collective-permute-done | bytes 98336 | tf_op jit(solution)/shard_map/ppermute | solution.py:27
  42.2 1.1 %collective-permute-done.17.other_ref = bf16[24,1024]{1,0:T(8,128)(2,1)S(1)} collective-permute-done((bf16[24,1024]{1,0:T(8,128)(2,1)S(1)}, bf16[24,1024]{1,0:T(8,128)(2,1)S(1)}, u32[]{:S(2)}, u32[]{:S(2)}) %collective-permute-start.17) | collective-permute-done | bytes 49184 | tf_op jit(solution)/shard_map/ppermute | solution.py:19
  43.5 2.7 %collective-permute-start.18 = (bf16[24,512]{1,0:T(8,128)(2,1)S(1)}, bf16[24,512]{1,0:T(8,128)(2,1)S(1)}, u32[]{:S(2)}, u32[]{:S(2)}) collective-permute-start(bf16[24,512]{1,0:T(8,128)(2,1)S(1)} %get-tuple-element.85), channel_id=1, source_target_pairs={{0,24},{8,16},{16,8},{24,0},{1,25},{9,17},{17,9},{25,1},{2,26},{10... | collective-permute-start | bytes 73736 | tf_op jit(solution)/shard_map/ppermute | solution.py:19
  46.2 1.7 %collective-permute-start.20 = (bf16[24,512]{1,0:T(8,128)(2,1)S(1)}, bf16[24,512]{1,0:T(8,128)(2,1)S(1)}, u32[]{:S(2)}, u32[]{:S(2)}) collective-permute-start(bf16[24,512]{1,0:T(8,128)(2,1)S(1)} %get-tuple-element.87), channel_id=1, source_target_pairs={{0,8},{8,0},{16,24},{24,16},{1,9},{9,1},{17,25},{25,17},{2,10},{10... | collective-permute-start | bytes 73736 | tf_op jit(solution)/shard_map/ppermute | solution.py:19
  47.9 1.3 %collective-permute-done.18.refs_0_ = bf16[24,512]{1,0:T(8,128)(2,1)S(1)} collective-permute-done((bf16[24,512]{1,0:T(8,128)(2,1)S(1)}, bf16[24,512]{1,0:T(8,128)(2,1)S(1)}, u32[]{:S(2)}, u32[]{:S(2)}) %collective-permute-start.18) | collective-permute-done | bytes 24608 | tf_op jit(solution)/shard_map/ppermute | solution.py:19
  49.2 1.7 %collective-permute-done.19.refs_1_ = bf16[24,512]{1,0:T(8,128)(2,1)S(1)} collective-permute-done((bf16[24,512]{1,0:T(8,128)(2,1)S(1)}, bf16[24,512]{1,0:T(8,128)(2,1)S(1)}, u32[]{:S(2)}, u32[]{:S(2)}) %collective-permute-start.19) | collective-permute-done | bytes 24608 | tf_op jit(solution)/shard_map/ppermute | solution.py:19
  (41 shorter events, 7.6 us)
Async XLA Ops:
  0.0 8.4 %collective-permute-start.3 = (bf16[384,2048]{1,0:T(8,128)(2,1)}, bf16[384,2048]{1,0:T(8,128)(2,1)S(1)}, u32[]{:S(2)}, u32[]{:S(2)}) collective-permute-start(bf16[384,2048]{1,0:T(8,128)(2,1)} %bitcast.12), channel_id=1, source_target_pairs={{0,1},{1,0},{2,3},{3,2},{4,5},{5,4},{6,7},{7,6},{8,9},{9,8},{10,11... | collective-permute-start | bytes 4718600 | tf_op jit(solution)/shard_map/ppermute | solution.py:19
  0.5 8.0 %collective-permute-start.4 = (bf16[192,2048]{1,0:T(8,128)(2,1)}, bf16[192,2048]{1,0:T(8,128)(2,1)S(1)}, u32[]{:S(2)}, u32[]{:S(2)}) collective-permute-start(bf16[192,2048]{1,0:T(8,128)(2,1)} %bitcast.17), channel_id=1, source_target_pairs={{0,1},{1,0},{2,3},{3,2},{4,5},{5,4},{6,7},{7,6},{8,9},{9,8},{10,11... | collective-permute-start | bytes 2359304 | tf_op jit(solution)/shard_map/ppermute | solution.py:19
  0.5 4.9 %collective-permute-start = (bf16[832,256]{1,0:T(8,128)(2,1)}, bf16[832,256]{1,0:T(8,128)(2,1)S(1)}, u32[]{:S(2)}, u32[]{:S(2)}) collective-permute-start(bf16[832,256]{1,0:T(8,128)(2,1)} %bitcast.24), channel_id=1, source_target_pairs={{0,1},{1,0},{2,3},{3,2},{4,5},{5,4},{6,7},{7,6},{8,9},{9,8},{10,11... | collective-permute-start | bytes 1277960 | tf_op jit(solution)/shard_map/ppermute | solution.py:19
  1.8 2.9 %collective-permute-start.1 = (s32[1,128]{1,0:T(1,128)S(1)}, s32[1,128]{1,0:T(1,128)S(1)}, u32[]{:S(2)}, u32[]{:S(2)}) collective-permute-start(s32[1,128]{1,0:T(1,128)S(1)} %pad_bitcast_fusion.own_ints_ref), channel_id=1, source_target_pairs={{0,1},{1,0},{2,3},{3,2},{4,5},{5,4},{6,7},{7,6},{8,9},{9,8},{10,11... | collective-permute-start | bytes 1544 | tf_op jit(solution)/shard_map/ppermute | solution.py:19
  4.6 23.5 %copy-start = (bf16[1,2,192,2048]{3,2,1,0:T(8,128)(2,1)S(1)}, bf16[1,2,192,2048]{3,2,1,0:T(8,128)(2,1)}, u32[]{:S(2)}) copy-start(bf16[1,2,192,2048]{3,2,1,0:T(8,128)(2,1)} %param.29) | copy-start | bytes 4718596
  4.6 23.5 %copy-start.1 = (bf16[1,192,2048]{2,1,0:T(8,128)(2,1)S(1)}, bf16[1,192,2048]{2,1,0:T(8,128)(2,1)}, u32[]{:S(2)}) copy-start(bf16[1,192,2048]{2,1,0:T(8,128)(2,1)} %param.30) | copy-start | bytes 2359300
  4.6 23.5 %copy-start.2 = (f32[2048]{0:T(1024)S(1)}, f32[2048]{0:T(1024)}, u32[]{:S(2)}) copy-start(f32[2048]{0:T(1024)} %param.25) | copy-start | bytes 24580
  7.0 1.4 %collective-permute-start.2 = (bf16[24,2560]{1,0:T(8,128)(2,1)S(1)}, bf16[24,2560]{1,0:T(8,128)(2,1)S(1)}, u32[]{:S(2)}, u32[]{:S(2)}) collective-permute-start(bf16[24,2560]{1,0:T(8,128)(2,1)S(1)} %get-tuple-element.53), channel_id=1, source_target_pairs={{0,1},{1,0},{2,3},{3,2},{4,5},{5,4},{6,7},{7,6},{8,9},{9,8},{10,11... | collective-permute-start | bytes 368648 | tf_op jit(solution)/shard_map/ppermute | solution.py:19
  8.5 5.2 %collective-permute-start.5 = (bf16[24,640]{1,0:T(8,128)(2,1)S(1)}, bf16[24,640]{1,0:T(8,128)(2,1)S(1)}, u32[]{:S(2)}, u32[]{:S(2)}) collective-permute-start(bf16[24,640]{1,0:T(8,128)(2,1)S(1)} %get-tuple-element.55), channel_id=1, source_target_pairs={{0,7},{1,6},{2,5},{3,4},{4,3},{5,2},{6,1},{7,0},{8,15},{9,14},{10,... | collective-permute-start | bytes 92168 | tf_op jit(solution)/shard_map/ppermute | solution.py:27
  12.1 3.9 %collective-permute-start.6 = (bf16[24,640]{1,0:T(8,128)(2,1)S(1)}, bf16[24,640]{1,0:T(8,128)(2,1)S(1)}, u32[]{:S(2)}, u32[]{:S(2)}) collective-permute-start(bf16[24,640]{1,0:T(8,128)(2,1)S(1)} %get-tuple-element.56), channel_id=1, source_target_pairs={{0,4},{1,5},{2,6},{3,7},{4,0},{5,1},{6,2},{7,3},{8,12},{9,13},{10,... | collective-permute-start | bytes 92168 | tf_op jit(solution)/shard_map/ppermute | solution.py:27
  12.6 3.4 %collective-permute-start.7 = (bf16[24,640]{1,0:T(8,128)(2,1)S(1)}, bf16[24,640]{1,0:T(8,128)(2,1)S(1)}, u32[]{:S(2)}, u32[]{:S(2)}) collective-permute-start(bf16[24,640]{1,0:T(8,128)(2,1)S(1)} %get-tuple-element.57), channel_id=1, source_target_pairs={{0,3},{1,2},{2,1},{3,0},{4,7},{5,6},{6,5},{7,4},{8,11},{9,10},{10,... | collective-permute-start | bytes 92168 | tf_op jit(solution)/shard_map/ppermute | solution.py:27
  16.0 4.0 %collective-permute-start.10 = (bf16[24,640]{1,0:T(8,128)(2,1)S(1)}, bf16[24,640]{1,0:T(8,128)(2,1)S(1)}, u32[]{:S(2)}, u32[]{:S(2)}) collective-permute-start(bf16[24,640]{1,0:T(8,128)(2,1)S(1)} %get-tuple-element.61), channel_id=1, source_target_pairs={{0,9},{1,8},{8,1},{9,0},{16,25},{17,24},{24,17},{25,16},{2,11},{3,... | collective-permute-start | bytes 92168 | tf_op jit(solution)/shard_map/ppermute | solution.py:27
  17.4 5.1 %collective-permute-start.8 = (bf16[24,640]{1,0:T(8,128)(2,1)S(1)}, bf16[24,640]{1,0:T(8,128)(2,1)S(1)}, u32[]{:S(2)}, u32[]{:S(2)}) collective-permute-start(bf16[24,640]{1,0:T(8,128)(2,1)S(1)} %get-tuple-element.59), channel_id=1, source_target_pairs={{0,25},{1,24},{8,17},{9,16},{16,9},{17,8},{24,1},{25,0},{2,27},{3,... | collective-permute-start | bytes 92168 | tf_op jit(solution)/shard_map/ppermute | solution.py:27
  19.9 5.1 %collective-permute-start.9 = (bf16[24,640]{1,0:T(8,128)(2,1)S(1)}, bf16[24,640]{1,0:T(8,128)(2,1)S(1)}, u32[]{:S(2)}, u32[]{:S(2)}) collective-permute-start(bf16[24,640]{1,0:T(8,128)(2,1)S(1)} %get-tuple-element.60), channel_id=1, source_target_pairs={{0,16},{1,17},{8,24},{9,25},{16,0},{17,1},{24,8},{25,9},{2,18},{3,... | collective-permute-start | bytes 92168 | tf_op jit(solution)/shard_map/ppermute | solution.py:27
  25.0 5.3 %collective-permute-start.13 = (bf16[4,24,512]{2,1,0:T(8,128)(2,1)S(1)}, bf16[4,24,512]{2,1,0:T(8,128)(2,1)S(1)}, u32[]{:S(2)}, u32[]{:S(2)}) collective-permute-start(bf16[4,24,512]{2,1,0:T(8,128)(2,1)S(1)} %get-tuple-element.63), channel_id=1, source_target_pairs={{0,7},{1,6},{2,5},{3,4},{4,3},{5,2},{6,1},{7,0},{8,15},{9,14},{10,... | collective-permute-start | bytes 294920 | tf_op jit(solution)/shard_map/ppermute | solution.py:27
  25.1 7.2 %collective-permute-start.12 = (bf16[4,24,512]{2,1,0:T(8,128)(2,1)S(1)}, bf16[4,24,512]{2,1,0:T(8,128)(2,1)S(1)}, u32[]{:S(2)}, u32[]{:S(2)}) collective-permute-start(bf16[4,24,512]{2,1,0:T(8,128)(2,1)S(1)} %get-tuple-element.63), channel_id=1, source_target_pairs={{0,4},{1,5},{2,6},{3,7},{4,0},{5,1},{6,2},{7,3},{8,12},{9,13},{10,... | collective-permute-start | bytes 294920 | tf_op jit(solution)/shard_map/ppermute | solution.py:27
  26.7 6.0 %collective-permute-start.11 = (bf16[4,24,512]{2,1,0:T(8,128)(2,1)S(1)}, bf16[4,24,512]{2,1,0:T(8,128)(2,1)S(1)}, u32[]{:S(2)}, u32[]{:S(2)}) collective-permute-start(bf16[4,24,512]{2,1,0:T(8,128)(2,1)S(1)} %get-tuple-element.63), channel_id=1, source_target_pairs={{0,3},{1,2},{2,1},{3,0},{4,7},{5,6},{6,5},{7,4},{8,11},{9,10},{10,... | collective-permute-start | bytes 294920 | tf_op jit(solution)/shard_map/ppermute | solution.py:27
  33.8 5.8 %collective-permute-start.14 = (bf16[24,2048]{1,0:T(8,128)(2,1)S(1)}, bf16[24,2048]{1,0:T(8,128)(2,1)S(1)}, u32[]{:S(2)}, u32[]{:S(2)}) collective-permute-start(bf16[24,2048]{1,0:T(8,128)(2,1)S(1)} %get-tuple-element.78), channel_id=1, source_target_pairs={{0,7},{1,6},{2,5},{3,4},{4,3},{5,2},{6,1},{7,0},{8,15},{9,14},{10,... | collective-permute-start | bytes 294920 | tf_op jit(solution)/shard_map/ppermute | solution.py:27
  35.0 6.9 %collective-permute-start.15 = (bf16[24,2048]{1,0:T(8,128)(2,1)S(1)}, bf16[24,2048]{1,0:T(8,128)(2,1)S(1)}, u32[]{:S(2)}, u32[]{:S(2)}) collective-permute-start(bf16[24,2048]{1,0:T(8,128)(2,1)S(1)} %get-tuple-element.79), channel_id=1, source_target_pairs={{0,4},{1,5},{2,6},{3,7},{4,0},{5,1},{6,2},{7,3},{8,12},{9,13},{10,... | collective-permute-start | bytes 294920 | tf_op jit(solution)/shard_map/ppermute | solution.py:27
  36.4 5.5 %collective-permute-start.16 = (bf16[24,2048]{1,0:T(8,128)(2,1)S(1)}, bf16[24,2048]{1,0:T(8,128)(2,1)S(1)}, u32[]{:S(2)}, u32[]{:S(2)}) collective-permute-start(bf16[24,2048]{1,0:T(8,128)(2,1)S(1)} %get-tuple-element.80), channel_id=1, source_target_pairs={{0,3},{1,2},{2,1},{3,0},{4,7},{5,6},{6,5},{7,4},{8,11},{9,10},{10,... | collective-permute-start | bytes 294920 | tf_op jit(solution)/shard_map/ppermute | solution.py:27
  42.0 1.3 %collective-permute-start.17 = (bf16[24,1024]{1,0:T(8,128)(2,1)S(1)}, bf16[24,1024]{1,0:T(8,128)(2,1)S(1)}, u32[]{:S(2)}, u32[]{:S(2)}) collective-permute-start(bf16[24,1024]{1,0:T(8,128)(2,1)S(1)} %get-tuple-element.83), channel_id=1, source_target_pairs={{0,1},{1,0},{2,3},{3,2},{4,5},{5,4},{6,7},{7,6},{8,9},{9,8},{10,11... | collective-permute-start | bytes 147464 | tf_op jit(solution)/shard_map/ppermute | solution.py:19
  43.5 5.7 %collective-permute-start.18 = (bf16[24,512]{1,0:T(8,128)(2,1)S(1)}, bf16[24,512]{1,0:T(8,128)(2,1)S(1)}, u32[]{:S(2)}, u32[]{:S(2)}) collective-permute-start(bf16[24,512]{1,0:T(8,128)(2,1)S(1)} %get-tuple-element.85), channel_id=1, source_target_pairs={{0,24},{8,16},{16,8},{24,0},{1,25},{9,17},{17,9},{25,1},{2,26},{10... | collective-permute-start | bytes 73736 | tf_op jit(solution)/shard_map/ppermute | solution.py:19
  46.2 4.7 %collective-permute-start.19 = (bf16[24,512]{1,0:T(8,128)(2,1)S(1)}, bf16[24,512]{1,0:T(8,128)(2,1)S(1)}, u32[]{:S(2)}, u32[]{:S(2)}) collective-permute-start(bf16[24,512]{1,0:T(8,128)(2,1)S(1)} %get-tuple-element.86), channel_id=1, source_target_pairs={{0,16},{8,24},{16,0},{24,8},{1,17},{9,25},{17,1},{25,9},{2,18},{10... | collective-permute-start | bytes 73736 | tf_op jit(solution)/shard_map/ppermute | solution.py:19
  46.2 4.7 %collective-permute-start.20 = (bf16[24,512]{1,0:T(8,128)(2,1)S(1)}, bf16[24,512]{1,0:T(8,128)(2,1)S(1)}, u32[]{:S(2)}, u32[]{:S(2)}) collective-permute-start(bf16[24,512]{1,0:T(8,128)(2,1)S(1)} %get-tuple-element.87), channel_id=1, source_target_pairs={{0,8},{8,0},{16,24},{24,16},{1,9},{9,1},{17,25},{25,17},{2,10},{10... | collective-permute-start | bytes 73736 | tf_op jit(solution)/shard_map/ppermute | solution.py:19

commit v7 on v6

--- a/solution.py
+++ b/solution.py
@@ -17,18 +17,6 @@
 def send(value, axes, step):
     size = lax.axis_size(axes)
     return lax.ppermute(value, axes, [(i, i ^ step) for i in range(size)])
-
-
-def cross(value, axis, step):
-    size, pools = lax.axis_size(axis), lax.axis_size("pool")
-    pairs = [
-        (i * pools + p, (i ^ step) * pools + (p ^ (step & 1))) for i in range(size) for p in range(pools)
-    ]
-    return lax.ppermute(value, (axis, "pool"), pairs)
-
-
-def taken():
-    return lax.axis_index("pool") ^ (lax.axis_index("head") & 1) ^ (lax.axis_index("req") & 1)
 
 
 def dot(a, b, contract=((1,), (0,))):
@@ -59,20 +47,26 @@
 
 def place_kernel(sizes, *refs):
     heads, pools, planes, count = sizes
-    sources, placed_ref, targets = refs[:count], refs[count], refs[count + 1 : -1]
-    residual_ref, choice_ref, route_ref = targets[-3:]
+    sources, (placed_ref, tables_ref), targets = refs[:count], refs[count : count + 2], refs[count + 2 : -1]
+    small = targets[6:]
+    residual_ref, choice_ref, route_ref = small[:3]
     semaphores = refs[-1]
-    head, mine = lax.axis_index("head"), taken()
-    first = jnp.where(lax.axis_index("pool") == 0, 1.0, 0.0)
-    picked = {count - 5: mine, count - 4: head}
+    head, mine = lax.axis_index("head"), lax.axis_index("pool")
+    first = jnp.where(mine == 0, 1.0, 0.0)
+    picked = {4: mine, 5: head}
     copies = []
     for i in range(count):
         source = sources[i].at[picked[i]] if i in picked else sources[i]
         copies.append(pltpu.make_async_copy(source, targets[i], semaphores.at[i]))
     for copy in reversed(copies):
         copy.start()
-    for copy in copies[-3:]:
+    for copy in copies[6:]:
         copy.wait()
+    tables_ref[...] = jnp.zeros_like(tables_ref)
+    line = 0
+    for ref in small[3:]:
+        tables_ref[line : line + ref.shape[0], : ref.shape[1]] = ref[...]
+        line += ref.shape[0]
     rows_here, width = residual_ref.shape
     part = rows_here // pools
     total = heads * rows_here
@@ -102,7 +96,7 @@
         placed_ref[:, start + columns : start + columns + share] = mix[
             :, h * share : (h + 1) * share
         ].astype(BF16)
-    for copy in copies[:-3]:
+    for copy in copies[:6]:
         copy.wait()
 
 
@@ -120,14 +114,13 @@
     live_from, live_count = [], []
     for q in range(2):
         row, across = ints[q], ints[1 - q]
-        base = pages * requests
-        length = column(row, base, requests)
+        length = column(row[pages : pages + 1], 0, requests)
         for j in range(pages):
-            slot = column(row, j * requests, requests)
+            slot = column(row[j : j + 1], 0, requests)
             source = slot + float(q * slots)
             for k in range(moved):
-                leave = column(across, base + requests + k, 1)
-                arrive = column(row, base + requests + moved + k, 1)
+                leave = column(across[pages + 1 : pages + 2], k, 1)
+                arrive = column(row[pages + 2 : pages + 3], k, 1)
                 source = jnp.where(slot == arrive, leave + float((1 - q) * slots), source)
             live_from.append((source * float(page)).astype(jnp.int32))
             live_count.append(jnp.clip(length - float(j * page), 0.0, float(page)).astype(jnp.int32))
@@ -193,6 +186,15 @@
         out[...] = (own_ref[:, at] + other_ref[:, at].astype(F32)).astype(out.dtype)
 
 
+def add_kernel(total_ref, part_ref, out_ref):
+    out_ref[...] = total_ref[...] + part_ref[...].astype(F32)
+
+
+def mark_kernel(part_ref, *refs):
+    out_ref = refs[-1]
+    out_ref[...] = part_ref[: out_ref.shape[0], : out_ref.shape[1]]
+
+
 def sum_kernel(count, *refs):
     total = functools.reduce(jnp.add, [part[...].astype(F32) for part in refs[:count]])
     for out in refs[count:]:
@@ -200,7 +202,7 @@
 
 
 def stack_kernel(*refs):
-    parts, (all_ref, first_ref) = refs[:-2], refs[-2:]
+    parts, (all_ref, first_ref) = refs[1:-2], refs[-2:]
     for step, part in enumerate(reversed(parts)):
         all_ref[step] = part[...]
         first_ref[step] = part[:, : first_ref.shape[2]]
@@ -270,7 +272,7 @@
 
 
 def spread_kernel(own_ref, other_ref, order_ref, *outs):
-    mine = taken()
+    mine = lax.axis_index("pool")
     own, other = own_ref[...].astype(F32), other_ref[...].astype(F32)
     both = jnp.concatenate([jnp.where(mine == 0, own, other), jnp.where(mine == 0, other, own)], axis=0)
     both = both.astype(BF16)
@@ -324,17 +326,10 @@
     columns = width // heads
     mixes = 2 * planes + -2 * planes % LANES
 
-    ints = jnp.concatenate(
-        [page_table[:, 0, j] for j in range(pages)]
-        + [cached_length.reshape(-1), leave_slots, arrive_slots]
-    )
-    ints = jnp.pad(ints, (0, -ints.shape[0] % LANES)).reshape(1, -1)
     own_cache = cache_pages.reshape(slots * page, entry)
     other_cache = send(own_cache, "pool", 1)
-    other_ints = send(ints, "pool", 1)
 
     gate_up, down_weight = gate_up.reshape(-1, width), down_weight.reshape(-1, width)
-    other_up, other_down = send(gate_up, "pool", 1), send(down_weight, "pool", 1)
 
     rows = requests // pools
     pool_order = [
@@ -365,18 +360,26 @@
         residual,
         expert_choice.T,
         route_weight.T,
+        page_table.transpose(1, 2, 0).reshape(pages, requests),
+        cached_length.reshape(1, requests),
+        leave_slots.reshape(1, moved),
+        arrive_slots.reshape(1, moved),
     )
     copied = [
-        shape(*array.shape[i // 4 :], dtype=array.dtype) for i, array in enumerate(outside[:-3])
+        shape(*array.shape[i // 4 :], dtype=array.dtype) for i, array in enumerate(outside[:6])
     ]
-    placed, held_cache, held_queries, held_weight, plane_order, pool_order, head_order = kernel_call(
+    tables = shape(
+        pages + 3 + -(pages + 3) % 8, requests + -requests % LANES, dtype=jnp.int32
+    )
+    placed, ints, held_cache, held_queries, held_weight, plane_order, pool_order, head_order = kernel_call(
         functools.partial(place_kernel, (heads, pools, planes, len(outside))),
-        [shape(requests, heads * (columns + mixes))] + copied,
+        [shape(requests, heads * (columns + mixes)), tables] + copied,
         (),
-        [pltpu.VMEM(array.shape, array.dtype) for array in outside[-3:]]
+        [pltpu.VMEM(array.shape, array.dtype) for array in outside[6:]]
         + [pltpu.SemaphoreType.DMA((len(outside),))],
         outside,
     )
+    other_ints = send(ints, "pool", 1)
     args = held(
         held_queries,
         new_entries.reshape(-1, entry),
@@ -395,23 +398,35 @@
         args,
     )
     other = send(other, "pool", 1)
-    other, other_up, other_down = lax.optimization_barrier((other, other_up, other_down))
+    ready = lax.optimization_barrier((gate_up, down_weight, other))
+    other_up, other_down = send(ready[0], "pool", 1), send(ready[1], "pool", 1)
     piece = shape(rows, columns + mixes)
     pieces = kernel_call(
         split_kernel,
         [shape(rows, columns + mixes, dtype=F32)] + [piece] * (heads - 1),
         held(own, other),
     )
-    arrived = [cross(pieces[step], "head", step) for step in reversed(range(1, heads))] + [pieces[0]]
+    total = pieces[0]
+    for step in reversed(range(2, heads)):
+        total = kernel_call(
+            add_kernel,
+            shape(rows, columns + mixes, dtype=F32),
+            held(total, send(pieces[step], "head", step)),
+        )
     hidden = kernel_call(
-        functools.partial(sum_kernel, heads), [piece] * planes, held(*arrived)
-    )
-
-    arrived = [cross(hidden[step], "req", step) for step in reversed(range(1, planes))] + [hidden[0]]
+        functools.partial(sum_kernel, 2),
+        [piece] * planes,
+        held(send(pieces[1], "head", 1), total),
+    )
+
+    arrived = [send(hidden[step], "req", step) for step in reversed(range(1, planes))] + [hidden[0]]
+    marks = []
+    for part_arrived in arrived[:-2]:
+        marks = [kernel_call(mark_kernel, shape(16, LANES), held(part_arrived, *marks))]
     plane_blocks, sent = kernel_call(
         stack_kernel,
         [shape(planes, rows, columns + mixes), shape(planes, rows, columns)],
-        held(*arrived),
+        held(*marks, *arrived),
     )
     weights = held(gate_up, other_up, norm_gain.reshape(1, -1))
     total = planes * rows
@@ -425,7 +440,7 @@
         state = kernel_call(
             functools.partial(project_kernel, step, planes),
             sums,
-            held(cross(sent, "head", step), *weights, *state),
+            held(send(sent, "head", step), *weights, *state),
         )
     piece = shape(planes * part, width)
     pieces = kernel_call(
@@ -433,7 +448,7 @@
         [shape(planes * part, width, dtype=F32)] + [piece] * (heads - 1),
         held(*state, route, own, down_weight, other_down, head_order),
     )
-    arrived = [cross(pieces[step], "head", step) for step in reversed(range(1, heads))] + [pieces[0]]
+    arrived = [send(pieces[step], "head", step) for step in reversed(range(1, heads))] + [pieces[0]]
     own, other = kernel_call(
         halve_kernel, [shape(planes * part, width // pools)] * 2, held(*arrived)
     )

time: 51.8 us -> 53.5 us (1.033)
  local copies, waits for them, and re-layouts: 1.46 us -> 6.69 us
  waiting for transfers between devices: 23 us -> 18.3 us
  starting transfers between devices: 20.2 us -> 22.1 us
  other arithmetic: 0.78 us -> 0 us
    ppermute x12 -> x0, waiting for transfers between devices: 17 us -> none  [cross(): return lax.ppermute(value, (axis, 'pool'), pairs)]
    ppermute x9 -> x21, starting transfers between devices: 6.13 us -> 22.1 us  [send(): return lax.ppermute(value, axes, [(i, i ^ step) for i in range(size)])]
    ppermute x12 -> x0, starting transfers between devices: 14.1 us -> none  [cross(): return lax.ppermute(value, (axis, 'pool'), pairs)]
    ppermute x9 -> x21, waiting for transfers between devices: 5.93 us -> 18.3 us  [send(): return lax.ppermute(value, axes, [(i, i ^ step) for i in range(size)])]
    unnamed x7 -> x19, local copies, waits for them, and re-layouts: 0.64 us -> 5.71 us
    concatenate x1 -> x0, other arithmetic: 0.78 us -> none  [local(): jnp.concatenate([page_table[:, 0, j] for j in range(pages)] + [cached_len...]
    pallas_call x13 -> x17, Pallas kernels: 6.04 us -> 6.13 us  [kernel_call(): pl.pallas_call(body, out_shape=jax.tree.map(lambda out: pltpu.VMEM(out.sh...]
  transfers between devices with their start and end apart: 21 -> 21, of which waited for: 13 -> 15; matrix products, arithmetic and copies ran while one was open for 3% -> 2% of each run, Pallas kernels for 9% -> 7%
where the time goes in v7:
time: 53.5 us; the launch traced here: 53.3 us
  starting transfers between devices  22.1 us (41%)
  waiting for transfers between devices  18.3 us (34%)
  local copies, waits for them, and re-layouts  6.69 us (13%)
  Pallas kernels  6.13 us (11%)
    ppermute x21, starting transfers between devices, send(): return lax.ppermute(value, axes, [(i, i ^ step) for i in range(size)])  22.1 us
    ppermute x21, waiting for transfers between devices, send(): return lax.ppermute(value, axes, [(i, i ^ step) for i in range(size)])  18.3 us
    pallas_call x17, Pallas kernels, kernel_call(): pl.pallas_call(body, out_shape=jax.tree.map(lambda out: pltpu.VMEM(out.sh...  6.13 us
    unnamed x19, local copies, waits for them, and re-layouts  5.71 us
  transfers between devices with their start and end apart: 21, of which 15 were waited for; matrix products, arithmetic and copies ran while one was open for 2% of the time, Pallas kernels for 7%

profile of v7, /device:TPU:0, one launch (start us, length us, event | category | flops | bytes accessed | tf_op | source)
XLA Modules:
  0.0 53.3 jit_solution(7507994925105223485)
XLA Ops:
  0.5 2.0 %shard_map.163 = (bf16[48,2560]{1,0:T(8,128)(2,1)S(1)}, s32[8,128]{1,0:T(8,128)S(1)}, bf16[832,256]{1,0:T(8,128)(2,1)S(1)}, bf16[48,1024]{1,0:T(8,128)(2,1)S(1)}...) custom-call(bf16[832,256]{1,0:T(8,128)(2,1)} %bitcast.25, ...), custom_call_target="tpu_custom_call" | custom-call | tf_op jit(solution)/shard_map/pallas_call | solution.py:27
  2.4 1.3 %copy-done.2 = bf16[512,2048]{1,0:T(8,128)(2,1)} copy-done((bf16[512,2048]{1,0:T(8,128)(2,1)}, bf16[512,2048]{1,0:T(8,128)(2,1)S(1)}, u32[]{:S(2)}) %copy-start.2) | copy-done | bytes 2097176
  5.1 1.0 %reshape.28.new_ref = bf16[96,256]{1,0:T(8,128)(2,1)S(1)} reshape(bf16[48,2,1,256]{3,1,2,0:T(2,128)(2,1)} %param.18) | data formatting | bytes 98304 | tf_op jit(solution)/shard_map/reshape | solution.py:385
  6.2 1.6 %copy-done.3 = bf16[512,2048]{1,0:T(8,128)(2,1)S(1)} copy-done((bf16[512,2048]{1,0:T(8,128)(2,1)S(1)}, bf16[512,2048]{1,0:T(8,128)(2,1)}, u32[]{:S(2)}) %copy-start.3) | copy-done | bytes 2097176
  7.8 0.9 %copy-done.6 = bf16[48,1024]{1,0:T(8,128)(2,1)S(1)} copy-done((bf16[48,1024]{1,0:T(8,128)(2,1)S(1)}, bf16[48,1024]{1,0:T(8,128)(2,1)}, u32[]{:S(2)}) %copy-start.6) | copy-done | bytes 98328
  8.7 1.6 %shard_map.164 = (f32[24,2560]{1,0:T(8,128)S(1)}, bf16[24,2560]{1,0:T(8,128)(2,1)S(1)}) custom-call(bf16[48,1024]{1,0:T(8,128)(2,1)S(1)} %copy-done.6, bf16[96,256]{1,0:T(8,128)(2,1)S(1)} %reshape.28.new_ref, bf16[832,256]{1,0:T(8,128)(2,1)S(1)} %get-tuple-element.48.own_ref, bf16[832,256]{1,0:T(8,128)(2,1)S(1)} %collective-permute-done.other_ref, ...), custom_call_target="tpu_custom_call" | custom-call | tf_op jit(solution)/shard_map/pallas_call | solution.py:27
  10.7 1.0 %collective-permute-done.2.other_ref = bf16[24,2560]{1,0:T(8,128)(2,1)S(1)} collective-permute-done((bf16[24,2560]{1,0:T(8,128)(2,1)S(1)}, bf16[24,2560]{1,0:T(8,128)(2,1)S(1)}, u32[]{:S(2)}, u32[]{:S(2)}) %collective-permute-start.2) | collective-permute-done | bytes 122912 | tf_op jit(solution)/shard_map/ppermute | solution.py:19
  12.3 3.8 %collective-permute-start.4 = (bf16[24,640]{1,0:T(8,128)(2,1)S(1)}, bf16[24,640]{1,0:T(8,128)(2,1)S(1)}, u32[]{:S(2)}, u32[]{:S(2)}) collective-permute-start(bf16[24,640]{1,0:T(8,128)(2,1)S(1)} %get-tuple-element.57), channel_id=1, source_target_pairs={{0,6},{2,4},{4,2},{6,0},{1,7},{3,5},{5,3},{7,1},{8,14},{10,12},{12... | collective-permute-start | bytes 92168 | tf_op jit(solution)/shard_map/ppermute | solution.py:19
  16.8 1.2 %collective-permute-done.4.part_ref = bf16[24,640]{1,0:T(8,128)(2,1)S(1)} collective-permute-done((bf16[24,640]{1,0:T(8,128)(2,1)S(1)}, bf16[24,640]{1,0:T(8,128)(2,1)S(1)}, u32[]{:S(2)}, u32[]{:S(2)}) %collective-permute-start.4) | collective-permute-done | bytes 30752 | tf_op jit(solution)/shard_map/ppermute | solution.py:19
  18.0 2.0 %collective-permute-done.5.part_ref = bf16[24,640]{1,0:T(8,128)(2,1)S(1)} collective-permute-done((bf16[24,640]{1,0:T(8,128)(2,1)S(1)}, bf16[24,640]{1,0:T(8,128)(2,1)S(1)}, u32[]{:S(2)}, u32[]{:S(2)}) %collective-permute-start.5) | collective-permute-done | bytes 30752 | tf_op jit(solution)/shard_map/ppermute | solution.py:19
  20.5 3.7 %collective-permute-start.7 = (bf16[24,640]{1,0:T(8,128)(2,1)S(1)}, bf16[24,640]{1,0:T(8,128)(2,1)S(1)}, u32[]{:S(2)}, u32[]{:S(2)}) collective-permute-start(bf16[24,640]{1,0:T(8,128)(2,1)S(1)} %get-tuple-element.60), channel_id=1, source_target_pairs={{0,24},{8,16},{16,8},{24,0},{1,25},{9,17},{17,9},{25,1},{2,26},{10... | collective-permute-start | bytes 92168 | tf_op jit(solution)/shard_map/ppermute | solution.py:19
  25.0 1.4 %collective-permute-done.7.part_ref.refs_1_ = bf16[24,640]{1,0:T(8,128)(2,1)S(1)} collective-permute-done((bf16[24,640]{1,0:T(8,128)(2,1)S(1)}, bf16[24,640]{1,0:T(8,128)(2,1)S(1)}, u32[]{:S(2)}, u32[]{:S(2)}) %collective-permute-start.7) | collective-permute-done | bytes 30752 | tf_op jit(solution)/shard_map/ppermute | solution.py:19
  26.4 2.6 %collective-permute-done.6.part_ref.refs_2_ = bf16[24,640]{1,0:T(8,128)(2,1)S(1)} collective-permute-done((bf16[24,640]{1,0:T(8,128)(2,1)S(1)}, bf16[24,640]{1,0:T(8,128)(2,1)S(1)}, u32[]{:S(2)}, u32[]{:S(2)}) %collective-permute-start.6) | collective-permute-done | bytes 30752 | tf_op jit(solution)/shard_map/ppermute | solution.py:19
  29.0 1.6 %collective-permute-start.12 = (bf16[4,24,512]{2,1,0:T(8,128)(2,1)S(1)}, bf16[4,24,512]{2,1,0:T(8,128)(2,1)S(1)}, u32[]{:S(2)}, u32[]{:S(2)}) collective-permute-start(bf16[4,24,512]{2,1,0:T(8,128)(2,1)S(1)} %get-tuple-element.63), channel_id=1, source_target_pairs={{0,6},{2,4},{4,2},{6,0},{1,7},{3,5},{5,3},{7,1},{8,14},{10,12},{12... | collective-permute-start | bytes 294920 | tf_op jit(solution)/shard_map/ppermute | solution.py:19
  31.1 1.5 %collective-permute-start.9 = (bf16[4,24,512]{2,1,0:T(8,128)(2,1)S(1)}, bf16[4,24,512]{2,1,0:T(8,128)(2,1)S(1)}, u32[]{:S(2)}, u32[]{:S(2)}) collective-permute-start(bf16[4,24,512]{2,1,0:T(8,128)(2,1)S(1)} %get-tuple-element.63), channel_id=1, source_target_pairs={{0,2},{2,0},{4,6},{6,4},{1,3},{3,1},{5,7},{7,5},{8,10},{10,8},{12,... | collective-permute-start | bytes 294920 | tf_op jit(solution)/shard_map/ppermute | solution.py:19
  33.0 1.6 %collective-permute-done.12.block_ref = bf16[4,24,512]{2,1,0:T(8,128)(2,1)S(1)} collective-permute-done((bf16[4,24,512]{2,1,0:T(8,128)(2,1)S(1)}, bf16[4,24,512]{2,1,0:T(8,128)(2,1)S(1)}, u32[]{:S(2)}, u32[]{:S(2)}) %collective-permute-start.12) | collective-permute-done | bytes 98336 | tf_op jit(solution)/shard_map/ppermute | solution.py:19
  37.1 2.6 %collective-permute-start.14 = (bf16[24,2048]{1,0:T(8,128)(2,1)S(1)}, bf16[24,2048]{1,0:T(8,128)(2,1)S(1)}, u32[]{:S(2)}, u32[]{:S(2)}) collective-permute-start(bf16[24,2048]{1,0:T(8,128)(2,1)S(1)} %get-tuple-element.78), channel_id=1, source_target_pairs={{0,6},{2,4},{4,2},{6,0},{1,7},{3,5},{5,3},{7,1},{8,14},{10,12},{12... | collective-permute-start | bytes 294920 | tf_op jit(solution)/shard_map/ppermute | solution.py:19
  39.8 0.9 %collective-permute-start.16 = (bf16[24,2048]{1,0:T(8,128)(2,1)S(1)}, bf16[24,2048]{1,0:T(8,128)(2,1)S(1)}, u32[]{:S(2)}, u32[]{:S(2)}) collective-permute-start(bf16[24,2048]{1,0:T(8,128)(2,1)S(1)} %get-tuple-element.80), channel_id=1, source_target_pairs={{0,2},{2,0},{4,6},{6,4},{1,3},{3,1},{5,7},{7,5},{8,10},{10,8},{12,... | collective-permute-start | bytes 294920 | tf_op jit(solution)/shard_map/ppermute | solution.py:19
  40.7 2.0 %collective-permute-done.14.refs_0_ = bf16[24,2048]{1,0:T(8,128)(2,1)S(1)} collective-permute-done((bf16[24,2048]{1,0:T(8,128)(2,1)S(1)}, bf16[24,2048]{1,0:T(8,128)(2,1)S(1)}, u32[]{:S(2)}, u32[]{:S(2)}) %collective-permute-start.14) | collective-permute-done | bytes 98336 | tf_op jit(solution)/shard_map/ppermute | solution.py:19
  42.7 1.7 %collective-permute-done.15.refs_1_ = bf16[24,2048]{1,0:T(8,128)(2,1)S(1)} collective-permute-done((bf16[24,2048]{1,0:T(8,128)(2,1)S(1)}, bf16[24,2048]{1,0:T(8,128)(2,1)S(1)}, u32[]{:S(2)}, u32[]{:S(2)}) %collective-permute-start.15) | collective-permute-done | bytes 98336 | tf_op jit(solution)/shard_map/ppermute | solution.py:19
  44.6 1.2 %collective-permute-done.17.other_ref = bf16[24,1024]{1,0:T(8,128)(2,1)S(1)} collective-permute-done((bf16[24,1024]{1,0:T(8,128)(2,1)S(1)}, bf16[24,1024]{1,0:T(8,128)(2,1)S(1)}, u32[]{:S(2)}, u32[]{:S(2)}) %collective-permute-start.17) | collective-permute-done | bytes 49184 | tf_op jit(solution)/shard_map/ppermute | solution.py:19
  46.0 1.7 %collective-permute-start.18 = (bf16[24,512]{1,0:T(8,128)(2,1)S(1)}, bf16[24,512]{1,0:T(8,128)(2,1)S(1)}, u32[]{:S(2)}, u32[]{:S(2)}) collective-permute-start(bf16[24,512]{1,0:T(8,128)(2,1)S(1)} %get-tuple-element.85), channel_id=1, source_target_pairs={{0,24},{8,16},{16,8},{24,0},{1,25},{9,17},{17,9},{25,1},{2,26},{10... | collective-permute-start | bytes 73736 | tf_op jit(solution)/shard_map/ppermute | solution.py:19
  48.6 1.8 %collective-permute-start.20 = (bf16[24,512]{1,0:T(8,128)(2,1)S(1)}, bf16[24,512]{1,0:T(8,128)(2,1)S(1)}, u32[]{:S(2)}, u32[]{:S(2)}) collective-permute-start(bf16[24,512]{1,0:T(8,128)(2,1)S(1)} %get-tuple-element.87), channel_id=1, source_target_pairs={{0,8},{8,0},{16,24},{24,16},{1,9},{9,1},{17,25},{25,17},{2,10},{10... | collective-permute-start | bytes 73736 | tf_op jit(solution)/shard_map/ppermute | solution.py:19
  50.4 1.3 %collective-permute-done.18.refs_0_ = bf16[24,512]{1,0:T(8,128)(2,1)S(1)} collective-permute-done((bf16[24,512]{1,0:T(8,128)(2,1)S(1)}, bf16[24,512]{1,0:T(8,128)(2,1)S(1)}, u32[]{:S(2)}, u32[]{:S(2)}) %collective-permute-start.18) | collective-permute-done | bytes 24608 | tf_op jit(solution)/shard_map/ppermute | solution.py:19
  (55 shorter events, 11.2 us)
Async XLA Ops:
  0.0 6.2 %collective-permute-start = (bf16[832,256]{1,0:T(8,128)(2,1)}, bf16[832,256]{1,0:T(8,128)(2,1)S(1)}, u32[]{:S(2)}, u32[]{:S(2)}) collective-permute-start(bf16[832,256]{1,0:T(8,128)(2,1)} %bitcast.24), channel_id=1, source_target_pairs={{0,1},{1,0},{2,3},{3,2},{4,5},{5,4},{6,7},{7,6},{8,9},{9,8},{10,11... | collective-permute-start | bytes 1277960 | tf_op jit(solution)/shard_map/ppermute | solution.py:19
  5.0 7.1 %copy-start.1 = (bf16[1,192,2048]{2,1,0:T(8,128)(2,1)S(1)}, bf16[1,192,2048]{2,1,0:T(8,128)(2,1)}, u32[]{:S(2)}) copy-start(bf16[1,192,2048]{2,1,0:T(8,128)(2,1)} %param.30) | copy-start | bytes 2359300
  5.0 1.2 %collective-permute-start.1 = (s32[8,128]{1,0:T(8,128)S(1)}, s32[8,128]{1,0:T(8,128)S(1)}, u32[]{:S(2)}, u32[]{:S(2)}) collective-permute-start(s32[8,128]{1,0:T(8,128)S(1)} %get-tuple-element.49.own_ints_ref), channel_id=1, source_target_pairs={{0,1},{1,0},{2,3},{3,2},{4,5},{5,4},{6,7},{7,6},{8,9},{9,8},{10,11... | collective-permute-start | bytes 12296 | tf_op jit(solution)/shard_map/ppermute | solution.py:19
  8.7 23.9 %copy-start.4 = (f32[2048]{0:T(1024)S(1)}, f32[2048]{0:T(1024)}, u32[]{:S(2)}) copy-start(f32[2048]{0:T(1024)} %param.25) | copy-start | bytes 24580
  10.3 1.4 %collective-permute-start.2 = (bf16[24,2560]{1,0:T(8,128)(2,1)S(1)}, bf16[24,2560]{1,0:T(8,128)(2,1)S(1)}, u32[]{:S(2)}, u32[]{:S(2)}) collective-permute-start(bf16[24,2560]{1,0:T(8,128)(2,1)S(1)} %get-tuple-element.54), channel_id=1, source_target_pairs={{0,1},{1,0},{2,3},{3,2},{4,5},{5,4},{6,7},{7,6},{8,9},{9,8},{10,11... | collective-permute-start | bytes 368648 | tf_op jit(solution)/shard_map/ppermute | solution.py:19
  11.7 20.9 %collective-permute-start.10 = (bf16[384,2048]{1,0:T(8,128)(2,1)S(1)}, bf16[384,2048]{1,0:T(8,128)(2,1)S(1)}, u32[]{:S(2)}, u32[]{:S(2)}) collective-permute-start(bf16[384,2048]{1,0:T(8,128)(2,1)S(1)} %bitcast.12), channel_id=1, source_target_pairs={{0,1},{1,0},{2,3},{3,2},{4,5},{5,4},{6,7},{7,6},{8,9},{9,8},{10,11... | collective-permute-start | bytes 4718600 | tf_op jit(solution)/shard_map/ppermute | solution.py:19
  12.1 24.4 %collective-permute-start.13 = (bf16[192,2048]{1,0:T(8,128)(2,1)S(1)}, bf16[192,2048]{1,0:T(8,128)(2,1)S(1)}, u32[]{:S(2)}, u32[]{:S(2)}) collective-permute-start(bf16[192,2048]{1,0:T(8,128)(2,1)S(1)} %bitcast.17), channel_id=1, source_target_pairs={{0,1},{1,0},{2,3},{3,2},{4,5},{5,4},{6,7},{7,6},{8,9},{9,8},{10,11... | collective-permute-start | bytes 2359304 | tf_op jit(solution)/shard_map/ppermute | solution.py:19
  12.3 5.7 %collective-permute-start.4 = (bf16[24,640]{1,0:T(8,128)(2,1)S(1)}, bf16[24,640]{1,0:T(8,128)(2,1)S(1)}, u32[]{:S(2)}, u32[]{:S(2)}) collective-permute-start(bf16[24,640]{1,0:T(8,128)(2,1)S(1)} %get-tuple-element.57), channel_id=1, source_target_pairs={{0,6},{2,4},{4,2},{6,0},{1,7},{3,5},{5,3},{7,1},{8,14},{10,12},{12... | collective-permute-start | bytes 92168 | tf_op jit(solution)/shard_map/ppermute | solution.py:19
  16.1 3.9 %collective-permute-start.5 = (bf16[24,640]{1,0:T(8,128)(2,1)S(1)}, bf16[24,640]{1,0:T(8,128)(2,1)S(1)}, u32[]{:S(2)}, u32[]{:S(2)}) collective-permute-start(bf16[24,640]{1,0:T(8,128)(2,1)S(1)} %get-tuple-element.58), channel_id=1, source_target_pairs={{0,4},{2,6},{4,0},{6,2},{1,5},{3,7},{5,1},{7,3},{8,12},{10,14},{12... | collective-permute-start | bytes 92168 | tf_op jit(solution)/shard_map/ppermute | solution.py:19
  16.6 3.9 %collective-permute-start.3 = (bf16[24,640]{1,0:T(8,128)(2,1)S(1)}, bf16[24,640]{1,0:T(8,128)(2,1)S(1)}, u32[]{:S(2)}, u32[]{:S(2)}) collective-permute-start(bf16[24,640]{1,0:T(8,128)(2,1)S(1)} %get-tuple-element.55), channel_id=1, source_target_pairs={{0,2},{2,0},{4,6},{6,4},{1,3},{3,1},{5,7},{7,5},{8,10},{10,8},{12,... | collective-permute-start | bytes 92168 | tf_op jit(solution)/shard_map/ppermute | solution.py:19
  20.5 5.9 %collective-permute-start.7 = (bf16[24,640]{1,0:T(8,128)(2,1)S(1)}, bf16[24,640]{1,0:T(8,128)(2,1)S(1)}, u32[]{:S(2)}, u32[]{:S(2)}) collective-permute-start(bf16[24,640]{1,0:T(8,128)(2,1)S(1)} %get-tuple-element.60), channel_id=1, source_target_pairs={{0,24},{8,16},{16,8},{24,0},{1,25},{9,17},{17,9},{25,1},{2,26},{10... | collective-permute-start | bytes 92168 | tf_op jit(solution)/shard_map/ppermute | solution.py:19
  24.2 4.8 %collective-permute-start.6 = (bf16[24,640]{1,0:T(8,128)(2,1)S(1)}, bf16[24,640]{1,0:T(8,128)(2,1)S(1)}, u32[]{:S(2)}, u32[]{:S(2)}) collective-permute-start(bf16[24,640]{1,0:T(8,128)(2,1)S(1)} %get-tuple-element.59), channel_id=1, source_target_pairs={{0,16},{8,24},{16,0},{24,8},{1,17},{9,25},{17,1},{25,9},{2,18},{10... | collective-permute-start | bytes 92168 | tf_op jit(solution)/shard_map/ppermute | solution.py:19
  24.2 4.8 %collective-permute-start.8 = (bf16[24,640]{1,0:T(8,128)(2,1)S(1)}, bf16[24,640]{1,0:T(8,128)(2,1)S(1)}, u32[]{:S(2)}, u32[]{:S(2)}) collective-permute-start(bf16[24,640]{1,0:T(8,128)(2,1)S(1)} %get-tuple-element.61), channel_id=1, source_target_pairs={{0,8},{8,0},{16,24},{24,16},{1,9},{9,1},{17,25},{25,17},{2,10},{10... | collective-permute-start | bytes 92168 | tf_op jit(solution)/shard_map/ppermute | solution.py:19
  29.0 5.6 %collective-permute-start.12 = (bf16[4,24,512]{2,1,0:T(8,128)(2,1)S(1)}, bf16[4,24,512]{2,1,0:T(8,128)(2,1)S(1)}, u32[]{:S(2)}, u32[]{:S(2)}) collective-permute-start(bf16[4,24,512]{2,1,0:T(8,128)(2,1)S(1)} %get-tuple-element.63), channel_id=1, source_target_pairs={{0,6},{2,4},{4,2},{6,0},{1,7},{3,5},{5,3},{7,1},{8,14},{10,12},{12... | collective-permute-start | bytes 294920 | tf_op jit(solution)/shard_map/ppermute | solution.py:19
  30.6 5.1 %collective-permute-start.11 = (bf16[4,24,512]{2,1,0:T(8,128)(2,1)S(1)}, bf16[4,24,512]{2,1,0:T(8,128)(2,1)S(1)}, u32[]{:S(2)}, u32[]{:S(2)}) collective-permute-start(bf16[4,24,512]{2,1,0:T(8,128)(2,1)S(1)} %get-tuple-element.63), channel_id=1, source_target_pairs={{0,4},{2,6},{4,0},{6,2},{1,5},{3,7},{5,1},{7,3},{8,12},{10,14},{12... | collective-permute-start | bytes 294920 | tf_op jit(solution)/shard_map/ppermute | solution.py:19
  31.1 5.0 %collective-permute-start.9 = (bf16[4,24,512]{2,1,0:T(8,128)(2,1)S(1)}, bf16[4,24,512]{2,1,0:T(8,128)(2,1)S(1)}, u32[]{:S(2)}, u32[]{:S(2)}) collective-permute-start(bf16[4,24,512]{2,1,0:T(8,128)(2,1)S(1)} %get-tuple-element.63), channel_id=1, source_target_pairs={{0,2},{2,0},{4,6},{6,4},{1,3},{3,1},{5,7},{7,5},{8,10},{10,8},{12,... | collective-permute-start | bytes 294920 | tf_op jit(solution)/shard_map/ppermute | solution.py:19
  36.4 9.3 %copy-start.8 = (bf16[2,96,48]{2,1,0:T(8,128)(2,1)S(1)}, bf16[2,96,48]{2,1,0:T(8,128)(2,1)}, u32[]{:S(2)}) copy-start(bf16[2,96,48]{2,1,0:T(8,128)(2,1)} %copy-done.7) | copy-start | bytes 55300
  37.1 5.6 %collective-permute-start.14 = (bf16[24,2048]{1,0:T(8,128)(2,1)S(1)}, bf16[24,2048]{1,0:T(8,128)(2,1)S(1)}, u32[]{:S(2)}, u32[]{:S(2)}) collective-permute-start(bf16[24,2048]{1,0:T(8,128)(2,1)S(1)} %get-tuple-element.78), channel_id=1, source_target_pairs={{0,6},{2,4},{4,2},{6,0},{1,7},{3,5},{5,3},{7,1},{8,14},{10,12},{12... | collective-permute-start | bytes 294920 | tf_op jit(solution)/shard_map/ppermute | solution.py:19
  39.8 4.6 %collective-permute-start.15 = (bf16[24,2048]{1,0:T(8,128)(2,1)S(1)}, bf16[24,2048]{1,0:T(8,128)(2,1)S(1)}, u32[]{:S(2)}, u32[]{:S(2)}) collective-permute-start(bf16[24,2048]{1,0:T(8,128)(2,1)S(1)} %get-tuple-element.79), channel_id=1, source_target_pairs={{0,4},{2,6},{4,0},{6,2},{1,5},{3,7},{5,1},{7,3},{8,12},{10,14},{12... | collective-permute-start | bytes 294920 | tf_op jit(solution)/shard_map/ppermute | solution.py:19
  39.8 4.6 %collective-permute-start.16 = (bf16[24,2048]{1,0:T(8,128)(2,1)S(1)}, bf16[24,2048]{1,0:T(8,128)(2,1)S(1)}, u32[]{:S(2)}, u32[]{:S(2)}) collective-permute-start(bf16[24,2048]{1,0:T(8,128)(2,1)S(1)} %get-tuple-element.80), channel_id=1, source_target_pairs={{0,2},{2,0},{4,6},{6,4},{1,3},{3,1},{5,7},{7,5},{8,10},{10,8},{12,... | collective-permute-start | bytes 294920 | tf_op jit(solution)/shard_map/ppermute | solution.py:19
  44.5 1.3 %collective-permute-start.17 = (bf16[24,1024]{1,0:T(8,128)(2,1)S(1)}, bf16[24,1024]{1,0:T(8,128)(2,1)S(1)}, u32[]{:S(2)}, u32[]{:S(2)}) collective-permute-start(bf16[24,1024]{1,0:T(8,128)(2,1)S(1)} %get-tuple-element.83), channel_id=1, source_target_pairs={{0,1},{1,0},{2,3},{3,2},{4,5},{5,4},{6,7},{7,6},{8,9},{9,8},{10,11... | collective-permute-start | bytes 147464 | tf_op jit(solution)/shard_map/ppermute | solution.py:19
  46.0 5.7 %collective-permute-start.18 = (bf16[24,512]{1,0:T(8,128)(2,1)S(1)}, bf16[24,512]{1,0:T(8,128)(2,1)S(1)}, u32[]{:S(2)}, u32[]{:S(2)}) collective-permute-start(bf16[24,512]{1,0:T(8,128)(2,1)S(1)} %get-tuple-element.85), channel_id=1, source_target_pairs={{0,24},{8,16},{16,8},{24,0},{1,25},{9,17},{17,9},{25,1},{2,26},{10... | collective-permute-start | bytes 73736 | tf_op jit(solution)/shard_map/ppermute | solution.py:19
  47.7 4.8 %collective-permute-start.19 = (bf16[24,512]{1,0:T(8,128)(2,1)S(1)}, bf16[24,512]{1,0:T(8,128)(2,1)S(1)}, u32[]{:S(2)}, u32[]{:S(2)}) collective-permute-start(bf16[24,512]{1,0:T(8,128)(2,1)S(1)} %get-tuple-element.86), channel_id=1, source_target_pairs={{0,16},{8,24},{16,0},{24,8},{1,17},{9,25},{17,1},{25,9},{2,18},{10... | collective-permute-start | bytes 73736 | tf_op jit(solution)/shard_map/ppermute | solution.py:19
  48.6 4.1 %collective-permute-start.20 = (bf16[24,512]{1,0:T(8,128)(2,1)S(1)}, bf16[24,512]{1,0:T(8,128)(2,1)S(1)}, u32[]{:S(2)}, u32[]{:S(2)}) collective-permute-start(bf16[24,512]{1,0:T(8,128)(2,1)S(1)} %get-tuple-element.87), channel_id=1, source_target_pairs={{0,8},{8,0},{16,24},{24,16},{1,9},{9,1},{17,25},{25,17},{2,10},{10... | collective-permute-start | bytes 73736 | tf_op jit(solution)/shard_map/ppermute | solution.py:19
  (6 other events, 11.8 us)

commit v8 on v7

--- a/solution.py
+++ b/solution.py
@@ -47,9 +47,8 @@
 
 def place_kernel(sizes, *refs):
     heads, pools, planes, count = sizes
-    sources, (placed_ref, tables_ref), targets = refs[:count], refs[count : count + 2], refs[count + 2 : -1]
-    small = targets[6:]
-    residual_ref, choice_ref, route_ref = small[:3]
+    sources, placed_ref, targets = refs[:count], refs[count], refs[count + 1 : -1]
+    residual_ref, choice_ref, route_ref = targets[6:]
     semaphores = refs[-1]
     head, mine = lax.axis_index("head"), lax.axis_index("pool")
     first = jnp.where(mine == 0, 1.0, 0.0)
@@ -62,11 +61,6 @@
         copy.start()
     for copy in copies[6:]:
         copy.wait()
-    tables_ref[...] = jnp.zeros_like(tables_ref)
-    line = 0
-    for ref in small[3:]:
-        tables_ref[line : line + ref.shape[0], : ref.shape[1]] = ref[...]
-        line += ref.shape[0]
     rows_here, width = residual_ref.shape
     part = rows_here // pools
     total = heads * rows_here
@@ -114,13 +108,14 @@
     live_from, live_count = [], []
     for q in range(2):
         row, across = ints[q], ints[1 - q]
-        length = column(row[pages : pages + 1], 0, requests)
+        base = pages * requests
+        length = column(row, base, requests)
         for j in range(pages):
-            slot = column(row[j : j + 1], 0, requests)
+            slot = column(row, j * requests, requests)
             source = slot + float(q * slots)
             for k in range(moved):
-                leave = column(across[pages + 1 : pages + 2], k, 1)
-                arrive = column(row[pages + 2 : pages + 3], k, 1)
+                leave = column(across, base + requests + k, 1)
+                arrive = column(row, base + requests + moved + k, 1)
                 source = jnp.where(slot == arrive, leave + float((1 - q) * slots), source)
             live_from.append((source * float(page)).astype(jnp.int32))
             live_count.append(jnp.clip(length - float(j * page), 0.0, float(page)).astype(jnp.int32))
@@ -328,6 +323,12 @@
 
     own_cache = cache_pages.reshape(slots * page, entry)
     other_cache = send(own_cache, "pool", 1)
+    ints = jnp.concatenate(
+        [page_table[:, 0, j] for j in range(pages)]
+        + [cached_length.reshape(-1), leave_slots, arrive_slots]
+    )
+    ints = jnp.pad(ints, (0, -ints.shape[0] % LANES)).reshape(1, -1)
+    other_ints = send(ints, "pool", 1)
 
     gate_up, down_weight = gate_up.reshape(-1, width), down_weight.reshape(-1, width)
 
@@ -360,26 +361,18 @@
         residual,
         expert_choice.T,
         route_weight.T,
-        page_table.transpose(1, 2, 0).reshape(pages, requests),
-        cached_length.reshape(1, requests),
-        leave_slots.reshape(1, moved),
-        arrive_slots.reshape(1, moved),
     )
     copied = [
         shape(*array.shape[i // 4 :], dtype=array.dtype) for i, array in enumerate(outside[:6])
     ]
-    tables = shape(
-        pages + 3 + -(pages + 3) % 8, requests + -requests % LANES, dtype=jnp.int32
-    )
-    placed, ints, held_cache, held_queries, held_weight, plane_order, pool_order, head_order = kernel_call(
+    placed, held_cache, held_queries, held_weight, plane_order, pool_order, head_order = kernel_call(
         functools.partial(place_kernel, (heads, pools, planes, len(outside))),
-        [shape(requests, heads * (columns + mixes)), tables] + copied,
+        [shape(requests, heads * (columns + mixes))] + copied,
         (),
         [pltpu.VMEM(array.shape, array.dtype) for array in outside[6:]]
         + [pltpu.SemaphoreType.DMA((len(outside),))],
         outside,
     )
-    other_ints = send(ints, "pool", 1)
     args = held(
         held_queries,
         new_entries.reshape(-1, entry),

time: 53.5 us -> 49 us (0.916)
  local copies, waits for them, and re-layouts: 6.69 us -> 1.46 us
  other arithmetic: 0 us -> 0.78 us
    unnamed x19 -> x7, local copies, waits for them, and re-layouts: 5.71 us -> 0.64 us
    concatenate x0 -> x1, other arithmetic: none -> 0.78 us  [local(): jnp.concatenate([page_table[:, 0, j] for j in range(pages)] + [cached_len...]
  transfers between devices with their start and end apart: 21 -> 21, of which waited for: 15 -> 14; matrix products, arithmetic and copies ran while one was open for 2% -> 3% of each run, Pallas kernels for 7% -> 7%
where the time goes in v8:
time: 49 us; the launch traced here: 48.8 us
  starting transfers between devices  22.2 us (45%)
  waiting for transfers between devices  18.2 us (37%)
  Pallas kernels  6.05 us (12%)
  local copies, waits for them, and re-layouts  1.46 us (3%)
  other arithmetic  0.78 us (2%)
    ppermute x21, starting transfers between devices, send(): return lax.ppermute(value, axes, [(i, i ^ step) for i in range(size)])  22.2 us
    ppermute x21, waiting for transfers between devices, send(): return lax.ppermute(value, axes, [(i, i ^ step) for i in range(size)])  18.2 us
    pallas_call x17, Pallas kernels, kernel_call(): pl.pallas_call(body, out_shape=jax.tree.map(lambda out: pltpu.VMEM(out.sh...  6.05 us
  transfers between devices with their start and end apart: 21, of which 14 were waited for; matrix products, arithmetic and copies ran while one was open for 3% of the time, Pallas kernels for 7%

profile of v8, /device:TPU:0, one launch (start us, length us, event | category | flops | bytes accessed | tf_op | source)
XLA Modules:
  0.0 48.8 jit_solution(12013702837399913370)
XLA Ops:
  1.3 0.8 %reshape.22.new_ref = bf16[96,256]{1,0:T(8,128)(2,1)S(1)} reshape(bf16[48,2,1,256]{3,1,2,0:T(2,128)(2,1)} %param.18) | data formatting | bytes 98304 | tf_op jit(solution)/shard_map/reshape | solution.py:378
  2.2 1.9 %shard_map.163 = (bf16[48,2560]{1,0:T(8,128)(2,1)S(1)}, bf16[832,256]{1,0:T(8,128)(2,1)S(1)}, bf16[48,1024]{1,0:T(8,128)(2,1)S(1)}, bf16[512,2048]{1,0:T(8,128)(...) custom-call(bf16[832,256]{1,0:T(8,128)(2,1)} %bitcast.25, ...), custom_call_target="tpu_custom_call" | custom-call | tf_op jit(solution)/shard_map/pallas_call | solution.py:27
  4.1 1.6 %shard_map.164 = (f32[24,2560]{1,0:T(8,128)S(1)}, bf16[24,2560]{1,0:T(8,128)(2,1)S(1)}) custom-call(bf16[48,1024]{1,0:T(8,128)(2,1)S(1)} %get-tuple-element.46.q_ref, bf16[96,256]{1,0:T(8,128)(2,1)S(1)} %reshape.22.new_ref, bf16[832,256]{1,0:T(8,128)(2,1)S(1)} %get-tuple-element.47.own_ref, bf16[832,256]{1,0:T(8,128)(2,1)S(1)} %collective-permute-done.other_ref, ...), custom_call_target="tpu_custom_call" | custom-call | tf_op jit(solution)/shard_map/pallas_call | solution.py:27
  6.2 1.0 %collective-permute-done.2.other_ref = bf16[24,2560]{1,0:T(8,128)(2,1)S(1)} collective-permute-done((bf16[24,2560]{1,0:T(8,128)(2,1)S(1)}, bf16[24,2560]{1,0:T(8,128)(2,1)S(1)}, u32[]{:S(2)}, u32[]{:S(2)}) %collective-permute-start.2) | collective-permute-done | bytes 122912 | tf_op jit(solution)/shard_map/ppermute | solution.py:19
  7.7 3.9 %collective-permute-start.4 = (bf16[24,640]{1,0:T(8,128)(2,1)S(1)}, bf16[24,640]{1,0:T(8,128)(2,1)S(1)}, u32[]{:S(2)}, u32[]{:S(2)}) collective-permute-start(bf16[24,640]{1,0:T(8,128)(2,1)S(1)} %get-tuple-element.55), channel_id=1, source_target_pairs={{0,6},{2,4},{4,2},{6,0},{1,7},{3,5},{5,3},{7,1},{8,14},{10,12},{12... | collective-permute-start | bytes 92168 | tf_op jit(solution)/shard_map/ppermute | solution.py:19
  12.2 1.2 %collective-permute-done.4.part_ref = bf16[24,640]{1,0:T(8,128)(2,1)S(1)} collective-permute-done((bf16[24,640]{1,0:T(8,128)(2,1)S(1)}, bf16[24,640]{1,0:T(8,128)(2,1)S(1)}, u32[]{:S(2)}, u32[]{:S(2)}) %collective-permute-start.4) | collective-permute-done | bytes 30752 | tf_op jit(solution)/shard_map/ppermute | solution.py:19
  13.5 2.0 %collective-permute-done.5.part_ref = bf16[24,640]{1,0:T(8,128)(2,1)S(1)} collective-permute-done((bf16[24,640]{1,0:T(8,128)(2,1)S(1)}, bf16[24,640]{1,0:T(8,128)(2,1)S(1)}, u32[]{:S(2)}, u32[]{:S(2)}) %collective-permute-start.5) | collective-permute-done | bytes 30752 | tf_op jit(solution)/shard_map/ppermute | solution.py:19
  16.0 3.7 %collective-permute-start.7 = (bf16[24,640]{1,0:T(8,128)(2,1)S(1)}, bf16[24,640]{1,0:T(8,128)(2,1)S(1)}, u32[]{:S(2)}, u32[]{:S(2)}) collective-permute-start(bf16[24,640]{1,0:T(8,128)(2,1)S(1)} %get-tuple-element.58), channel_id=1, source_target_pairs={{0,24},{8,16},{16,8},{24,0},{1,25},{9,17},{17,9},{25,1},{2,26},{10... | collective-permute-start | bytes 92168 | tf_op jit(solution)/shard_map/ppermute | solution.py:19
  19.7 0.8 %collective-permute-start.8 = (bf16[24,640]{1,0:T(8,128)(2,1)S(1)}, bf16[24,640]{1,0:T(8,128)(2,1)S(1)}, u32[]{:S(2)}, u32[]{:S(2)}) collective-permute-start(bf16[24,640]{1,0:T(8,128)(2,1)S(1)} %get-tuple-element.59), channel_id=1, source_target_pairs={{0,8},{8,0},{16,24},{24,16},{1,9},{9,1},{17,25},{25,17},{2,10},{10... | collective-permute-start | bytes 92168 | tf_op jit(solution)/shard_map/ppermute | solution.py:19
  20.5 1.4 %collective-permute-done.7.part_ref.refs_1_ = bf16[24,640]{1,0:T(8,128)(2,1)S(1)} collective-permute-done((bf16[24,640]{1,0:T(8,128)(2,1)S(1)}, bf16[24,640]{1,0:T(8,128)(2,1)S(1)}, u32[]{:S(2)}, u32[]{:S(2)}) %collective-permute-start.7) | collective-permute-done | bytes 30752 | tf_op jit(solution)/shard_map/ppermute | solution.py:19
  21.9 2.6 %collective-permute-done.6.part_ref.refs_2_ = bf16[24,640]{1,0:T(8,128)(2,1)S(1)} collective-permute-done((bf16[24,640]{1,0:T(8,128)(2,1)S(1)}, bf16[24,640]{1,0:T(8,128)(2,1)S(1)}, u32[]{:S(2)}, u32[]{:S(2)}) %collective-permute-start.6) | collective-permute-done | bytes 30752 | tf_op jit(solution)/shard_map/ppermute | solution.py:19
  24.5 1.6 %collective-permute-start.12 = (bf16[4,24,512]{2,1,0:T(8,128)(2,1)S(1)}, bf16[4,24,512]{2,1,0:T(8,128)(2,1)S(1)}, u32[]{:S(2)}, u32[]{:S(2)}) collective-permute-start(bf16[4,24,512]{2,1,0:T(8,128)(2,1)S(1)} %get-tuple-element.61), channel_id=1, source_target_pairs={{0,6},{2,4},{4,2},{6,0},{1,7},{3,5},{5,3},{7,1},{8,14},{10,12},{12... | collective-permute-start | bytes 294920 | tf_op jit(solution)/shard_map/ppermute | solution.py:19
  26.6 1.5 %collective-permute-start.9 = (bf16[4,24,512]{2,1,0:T(8,128)(2,1)S(1)}, bf16[4,24,512]{2,1,0:T(8,128)(2,1)S(1)}, u32[]{:S(2)}, u32[]{:S(2)}) collective-permute-start(bf16[4,24,512]{2,1,0:T(8,128)(2,1)S(1)} %get-tuple-element.61), channel_id=1, source_target_pairs={{0,2},{2,0},{4,6},{6,4},{1,3},{3,1},{5,7},{7,5},{8,10},{10,8},{12,... | collective-permute-start | bytes 294920 | tf_op jit(solution)/shard_map/ppermute | solution.py:19
  28.5 1.6 %collective-permute-done.12.block_ref = bf16[4,24,512]{2,1,0:T(8,128)(2,1)S(1)} collective-permute-done((bf16[4,24,512]{2,1,0:T(8,128)(2,1)S(1)}, bf16[4,24,512]{2,1,0:T(8,128)(2,1)S(1)}, u32[]{:S(2)}, u32[]{:S(2)}) %collective-permute-start.12) | collective-permute-done | bytes 98336 | tf_op jit(solution)/shard_map/ppermute | solution.py:19
  32.6 2.6 %collective-permute-start.14 = (bf16[24,2048]{1,0:T(8,128)(2,1)S(1)}, bf16[24,2048]{1,0:T(8,128)(2,1)S(1)}, u32[]{:S(2)}, u32[]{:S(2)}) collective-permute-start(bf16[24,2048]{1,0:T(8,128)(2,1)S(1)} %get-tuple-element.76), channel_id=1, source_target_pairs={{0,6},{2,4},{4,2},{6,0},{1,7},{3,5},{5,3},{7,1},{8,14},{10,12},{12... | collective-permute-start | bytes 294920 | tf_op jit(solution)/shard_map/ppermute | solution.py:19
  35.3 0.9 %collective-permute-start.16 = (bf16[24,2048]{1,0:T(8,128)(2,1)S(1)}, bf16[24,2048]{1,0:T(8,128)(2,1)S(1)}, u32[]{:S(2)}, u32[]{:S(2)}) collective-permute-start(bf16[24,2048]{1,0:T(8,128)(2,1)S(1)} %get-tuple-element.78), channel_id=1, source_target_pairs={{0,2},{2,0},{4,6},{6,4},{1,3},{3,1},{5,7},{7,5},{8,10},{10,8},{12,... | collective-permute-start | bytes 294920 | tf_op jit(solution)/shard_map/ppermute | solution.py:19
  36.2 2.0 %collective-permute-done.14.refs_0_ = bf16[24,2048]{1,0:T(8,128)(2,1)S(1)} collective-permute-done((bf16[24,2048]{1,0:T(8,128)(2,1)S(1)}, bf16[24,2048]{1,0:T(8,128)(2,1)S(1)}, u32[]{:S(2)}, u32[]{:S(2)}) %collective-permute-start.14) | collective-permute-done | bytes 98336 | tf_op jit(solution)/shard_map/ppermute | solution.py:19
  38.2 1.6 %collective-permute-done.15.refs_1_ = bf16[24,2048]{1,0:T(8,128)(2,1)S(1)} collective-permute-done((bf16[24,2048]{1,0:T(8,128)(2,1)S(1)}, bf16[24,2048]{1,0:T(8,128)(2,1)S(1)}, u32[]{:S(2)}, u32[]{:S(2)}) %collective-permute-start.15) | collective-permute-done | bytes 98336 | tf_op jit(solution)/shard_map/ppermute | solution.py:19
  40.0 1.2 %collective-permute-done.17.other_ref = bf16[24,1024]{1,0:T(8,128)(2,1)S(1)} collective-permute-done((bf16[24,1024]{1,0:T(8,128)(2,1)S(1)}, bf16[24,1024]{1,0:T(8,128)(2,1)S(1)}, u32[]{:S(2)}, u32[]{:S(2)}) %collective-permute-start.17) | collective-permute-done | bytes 49184 | tf_op jit(solution)/shard_map/ppermute | solution.py:19
  41.4 1.8 %collective-permute-start.18 = (bf16[24,512]{1,0:T(8,128)(2,1)S(1)}, bf16[24,512]{1,0:T(8,128)(2,1)S(1)}, u32[]{:S(2)}, u32[]{:S(2)}) collective-permute-start(bf16[24,512]{1,0:T(8,128)(2,1)S(1)} %get-tuple-element.83), channel_id=1, source_target_pairs={{0,24},{8,16},{16,8},{24,0},{1,25},{9,17},{17,9},{25,1},{2,26},{10... | collective-permute-start | bytes 73736 | tf_op jit(solution)/shard_map/ppermute | solution.py:19
  43.2 0.9 %collective-permute-start.19 = (bf16[24,512]{1,0:T(8,128)(2,1)S(1)}, bf16[24,512]{1,0:T(8,128)(2,1)S(1)}, u32[]{:S(2)}, u32[]{:S(2)}) collective-permute-start(bf16[24,512]{1,0:T(8,128)(2,1)S(1)} %get-tuple-element.84), channel_id=1, source_target_pairs={{0,16},{8,24},{16,0},{24,8},{1,17},{9,25},{17,1},{25,9},{2,18},{10... | collective-permute-start | bytes 73736 | tf_op jit(solution)/shard_map/ppermute | solution.py:19
  44.1 1.8 %collective-permute-start.20 = (bf16[24,512]{1,0:T(8,128)(2,1)S(1)}, bf16[24,512]{1,0:T(8,128)(2,1)S(1)}, u32[]{:S(2)}, u32[]{:S(2)}) collective-permute-start(bf16[24,512]{1,0:T(8,128)(2,1)S(1)} %get-tuple-element.85), channel_id=1, source_target_pairs={{0,8},{8,0},{16,24},{24,16},{1,9},{9,1},{17,25},{25,17},{2,10},{10... | collective-permute-start | bytes 73736 | tf_op jit(solution)/shard_map/ppermute | solution.py:19
  45.9 1.3 %collective-permute-done.18.refs_0_ = bf16[24,512]{1,0:T(8,128)(2,1)S(1)} collective-permute-done((bf16[24,512]{1,0:T(8,128)(2,1)S(1)}, bf16[24,512]{1,0:T(8,128)(2,1)S(1)}, u32[]{:S(2)}, u32[]{:S(2)}) %collective-permute-start.18) | collective-permute-done | bytes 24608 | tf_op jit(solution)/shard_map/ppermute | solution.py:19
  47.2 0.8 %collective-permute-done.19.refs_1_ = bf16[24,512]{1,0:T(8,128)(2,1)S(1)} collective-permute-done((bf16[24,512]{1,0:T(8,128)(2,1)S(1)}, bf16[24,512]{1,0:T(8,128)(2,1)S(1)}, u32[]{:S(2)}, u32[]{:S(2)}) %collective-permute-start.19) | collective-permute-done | bytes 24608 | tf_op jit(solution)/shard_map/ppermute | solution.py:19
  (45 shorter events, 8.2 us)
Async XLA Ops:
  0.0 4.1 %collective-permute-start = (bf16[832,256]{1,0:T(8,128)(2,1)}, bf16[832,256]{1,0:T(8,128)(2,1)S(1)}, u32[]{:S(2)}, u32[]{:S(2)}) collective-permute-start(bf16[832,256]{1,0:T(8,128)(2,1)} %bitcast.24), channel_id=1, source_target_pairs={{0,1},{1,0},{2,3},{3,2},{4,5},{5,4},{6,7},{7,6},{8,9},{9,8},{10,11... | collective-permute-start | bytes 1277960 | tf_op jit(solution)/shard_map/ppermute | solution.py:19
  1.2 2.8 %collective-permute-start.1 = (s32[1,128]{1,0:T(1,128)S(1)}, s32[1,128]{1,0:T(1,128)S(1)}, u32[]{:S(2)}, u32[]{:S(2)}) collective-permute-start(s32[1,128]{1,0:T(1,128)S(1)} %pad_bitcast_fusion.own_ints_ref), channel_id=1, source_target_pairs={{0,1},{1,0},{2,3},{3,2},{4,5},{5,4},{6,7},{7,6},{8,9},{9,8},{10,11... | collective-permute-start | bytes 1544 | tf_op jit(solution)/shard_map/ppermute | solution.py:19
  4.1 3.1 %copy-start = (bf16[1,2,192,2048]{3,2,1,0:T(8,128)(2,1)S(1)}, bf16[1,2,192,2048]{3,2,1,0:T(8,128)(2,1)}, u32[]{:S(2)}) copy-start(bf16[1,2,192,2048]{3,2,1,0:T(8,128)(2,1)} %param.29) | copy-start | bytes 4718596
  4.1 3.5 %copy-start.1 = (bf16[1,192,2048]{2,1,0:T(8,128)(2,1)S(1)}, bf16[1,192,2048]{2,1,0:T(8,128)(2,1)}, u32[]{:S(2)}) copy-start(bf16[1,192,2048]{2,1,0:T(8,128)(2,1)} %param.30) | copy-start | bytes 2359300
  4.1 24.0 %copy-start.2 = (f32[2048]{0:T(1024)S(1)}, f32[2048]{0:T(1024)}, u32[]{:S(2)}) copy-start(f32[2048]{0:T(1024)} %param.25) | copy-start | bytes 24580
  5.7 1.5 %collective-permute-start.2 = (bf16[24,2560]{1,0:T(8,128)(2,1)S(1)}, bf16[24,2560]{1,0:T(8,128)(2,1)S(1)}, u32[]{:S(2)}, u32[]{:S(2)}) collective-permute-start(bf16[24,2560]{1,0:T(8,128)(2,1)S(1)} %get-tuple-element.52), channel_id=1, source_target_pairs={{0,1},{1,0},{2,3},{3,2},{4,5},{5,4},{6,7},{7,6},{8,9},{9,8},{10,11... | collective-permute-start | bytes 368648 | tf_op jit(solution)/shard_map/ppermute | solution.py:19
  7.2 20.9 %collective-permute-start.10 = (bf16[384,2048]{1,0:T(8,128)(2,1)S(1)}, bf16[384,2048]{1,0:T(8,128)(2,1)S(1)}, u32[]{:S(2)}, u32[]{:S(2)}) collective-permute-start(bf16[384,2048]{1,0:T(8,128)(2,1)S(1)} %bitcast.12), channel_id=1, source_target_pairs={{0,1},{1,0},{2,3},{3,2},{4,5},{5,4},{6,7},{7,6},{8,9},{9,8},{10,11... | collective-permute-start | bytes 4718600 | tf_op jit(solution)/shard_map/ppermute | solution.py:19
  7.6 24.4 %collective-permute-start.13 = (bf16[192,2048]{1,0:T(8,128)(2,1)S(1)}, bf16[192,2048]{1,0:T(8,128)(2,1)S(1)}, u32[]{:S(2)}, u32[]{:S(2)}) collective-permute-start(bf16[192,2048]{1,0:T(8,128)(2,1)S(1)} %bitcast.17), channel_id=1, source_target_pairs={{0,1},{1,0},{2,3},{3,2},{4,5},{5,4},{6,7},{7,6},{8,9},{9,8},{10,11... | collective-permute-start | bytes 2359304 | tf_op jit(solution)/shard_map/ppermute | solution.py:19
  7.7 5.7 %collective-permute-start.4 = (bf16[24,640]{1,0:T(8,128)(2,1)S(1)}, bf16[24,640]{1,0:T(8,128)(2,1)S(1)}, u32[]{:S(2)}, u32[]{:S(2)}) collective-permute-start(bf16[24,640]{1,0:T(8,128)(2,1)S(1)} %get-tuple-element.55), channel_id=1, source_target_pairs={{0,6},{2,4},{4,2},{6,0},{1,7},{3,5},{5,3},{7,1},{8,14},{10,12},{12... | collective-permute-start | bytes 92168 | tf_op jit(solution)/shard_map/ppermute | solution.py:19
  11.6 3.9 %collective-permute-start.5 = (bf16[24,640]{1,0:T(8,128)(2,1)S(1)}, bf16[24,640]{1,0:T(8,128)(2,1)S(1)}, u32[]{:S(2)}, u32[]{:S(2)}) collective-permute-start(bf16[24,640]{1,0:T(8,128)(2,1)S(1)} %get-tuple-element.56), channel_id=1, source_target_pairs={{0,4},{2,6},{4,0},{6,2},{1,5},{3,7},{5,1},{7,3},{8,12},{10,14},{12... | collective-permute-start | bytes 92168 | tf_op jit(solution)/shard_map/ppermute | solution.py:19
  12.1 3.9 %collective-permute-start.3 = (bf16[24,640]{1,0:T(8,128)(2,1)S(1)}, bf16[24,640]{1,0:T(8,128)(2,1)S(1)}, u32[]{:S(2)}, u32[]{:S(2)}) collective-permute-start(bf16[24,640]{1,0:T(8,128)(2,1)S(1)} %get-tuple-element.53), channel_id=1, source_target_pairs={{0,2},{2,0},{4,6},{6,4},{1,3},{3,1},{5,7},{7,5},{8,10},{10,8},{12,... | collective-permute-start | bytes 92168 | tf_op jit(solution)/shard_map/ppermute | solution.py:19
  16.0 5.9 %collective-permute-start.7 = (bf16[24,640]{1,0:T(8,128)(2,1)S(1)}, bf16[24,640]{1,0:T(8,128)(2,1)S(1)}, u32[]{:S(2)}, u32[]{:S(2)}) collective-permute-start(bf16[24,640]{1,0:T(8,128)(2,1)S(1)} %get-tuple-element.58), channel_id=1, source_target_pairs={{0,24},{8,16},{16,8},{24,0},{1,25},{9,17},{17,9},{25,1},{2,26},{10... | collective-permute-start | bytes 92168 | tf_op jit(solution)/shard_map/ppermute | solution.py:19
  19.7 4.8 %collective-permute-start.6 = (bf16[24,640]{1,0:T(8,128)(2,1)S(1)}, bf16[24,640]{1,0:T(8,128)(2,1)S(1)}, u32[]{:S(2)}, u32[]{:S(2)}) collective-permute-start(bf16[24,640]{1,0:T(8,128)(2,1)S(1)} %get-tuple-element.57), channel_id=1, source_target_pairs={{0,16},{8,24},{16,0},{24,8},{1,17},{9,25},{17,1},{25,9},{2,18},{10... | collective-permute-start | bytes 92168 | tf_op jit(solution)/shard_map/ppermute | solution.py:19
  19.7 4.8 %collective-permute-start.8 = (bf16[24,640]{1,0:T(8,128)(2,1)S(1)}, bf16[24,640]{1,0:T(8,128)(2,1)S(1)}, u32[]{:S(2)}, u32[]{:S(2)}) collective-permute-start(bf16[24,640]{1,0:T(8,128)(2,1)S(1)} %get-tuple-element.59), channel_id=1, source_target_pairs={{0,8},{8,0},{16,24},{24,16},{1,9},{9,1},{17,25},{25,17},{2,10},{10... | collective-permute-start | bytes 92168 | tf_op jit(solution)/shard_map/ppermute | solution.py:19
  24.5 5.6 %collective-permute-start.12 = (bf16[4,24,512]{2,1,0:T(8,128)(2,1)S(1)}, bf16[4,24,512]{2,1,0:T(8,128)(2,1)S(1)}, u32[]{:S(2)}, u32[]{:S(2)}) collective-permute-start(bf16[4,24,512]{2,1,0:T(8,128)(2,1)S(1)} %get-tuple-element.61), channel_id=1, source_target_pairs={{0,6},{2,4},{4,2},{6,0},{1,7},{3,5},{5,3},{7,1},{8,14},{10,12},{12... | collective-permute-start | bytes 294920 | tf_op jit(solution)/shard_map/ppermute | solution.py:19
  26.1 5.1 %collective-permute-start.11 = (bf16[4,24,512]{2,1,0:T(8,128)(2,1)S(1)}, bf16[4,24,512]{2,1,0:T(8,128)(2,1)S(1)}, u32[]{:S(2)}, u32[]{:S(2)}) collective-permute-start(bf16[4,24,512]{2,1,0:T(8,128)(2,1)S(1)} %get-tuple-element.61), channel_id=1, source_target_pairs={{0,4},{2,6},{4,0},{6,2},{1,5},{3,7},{5,1},{7,3},{8,12},{10,14},{12... | collective-permute-start | bytes 294920 | tf_op jit(solution)/shard_map/ppermute | solution.py:19
  26.6 5.0 %collective-permute-start.9 = (bf16[4,24,512]{2,1,0:T(8,128)(2,1)S(1)}, bf16[4,24,512]{2,1,0:T(8,128)(2,1)S(1)}, u32[]{:S(2)}, u32[]{:S(2)}) collective-permute-start(bf16[4,24,512]{2,1,0:T(8,128)(2,1)S(1)} %get-tuple-element.61), channel_id=1, source_target_pairs={{0,2},{2,0},{4,6},{6,4},{1,3},{3,1},{5,7},{7,5},{8,10},{10,8},{12,... | collective-permute-start | bytes 294920 | tf_op jit(solution)/shard_map/ppermute | solution.py:19
  32.6 5.6 %collective-permute-start.14 = (bf16[24,2048]{1,0:T(8,128)(2,1)S(1)}, bf16[24,2048]{1,0:T(8,128)(2,1)S(1)}, u32[]{:S(2)}, u32[]{:S(2)}) collective-permute-start(bf16[24,2048]{1,0:T(8,128)(2,1)S(1)} %get-tuple-element.76), channel_id=1, source_target_pairs={{0,6},{2,4},{4,2},{6,0},{1,7},{3,5},{5,3},{7,1},{8,14},{10,12},{12... | collective-permute-start | bytes 294920 | tf_op jit(solution)/shard_map/ppermute | solution.py:19
  35.2 4.6 %collective-permute-start.15 = (bf16[24,2048]{1,0:T(8,128)(2,1)S(1)}, bf16[24,2048]{1,0:T(8,128)(2,1)S(1)}, u32[]{:S(2)}, u32[]{:S(2)}) collective-permute-start(bf16[24,2048]{1,0:T(8,128)(2,1)S(1)} %get-tuple-element.77), channel_id=1, source_target_pairs={{0,4},{2,6},{4,0},{6,2},{1,5},{3,7},{5,1},{7,3},{8,12},{10,14},{12... | collective-permute-start | bytes 294920 | tf_op jit(solution)/shard_map/ppermute | solution.py:19
  35.3 4.6 %collective-permute-start.16 = (bf16[24,2048]{1,0:T(8,128)(2,1)S(1)}, bf16[24,2048]{1,0:T(8,128)(2,1)S(1)}, u32[]{:S(2)}, u32[]{:S(2)}) collective-permute-start(bf16[24,2048]{1,0:T(8,128)(2,1)S(1)} %get-tuple-element.78), channel_id=1, source_target_pairs={{0,2},{2,0},{4,6},{6,4},{1,3},{3,1},{5,7},{7,5},{8,10},{10,8},{12,... | collective-permute-start | bytes 294920 | tf_op jit(solution)/shard_map/ppermute | solution.py:19
  39.9 1.3 %collective-permute-start.17 = (bf16[24,1024]{1,0:T(8,128)(2,1)S(1)}, bf16[24,1024]{1,0:T(8,128)(2,1)S(1)}, u32[]{:S(2)}, u32[]{:S(2)}) collective-permute-start(bf16[24,1024]{1,0:T(8,128)(2,1)S(1)} %get-tuple-element.81), channel_id=1, source_target_pairs={{0,1},{1,0},{2,3},{3,2},{4,5},{5,4},{6,7},{7,6},{8,9},{9,8},{10,11... | collective-permute-start | bytes 147464 | tf_op jit(solution)/shard_map/ppermute | solution.py:19
  41.4 5.8 %collective-permute-start.18 = (bf16[24,512]{1,0:T(8,128)(2,1)S(1)}, bf16[24,512]{1,0:T(8,128)(2,1)S(1)}, u32[]{:S(2)}, u32[]{:S(2)}) collective-permute-start(bf16[24,512]{1,0:T(8,128)(2,1)S(1)} %get-tuple-element.83), channel_id=1, source_target_pairs={{0,24},{8,16},{16,8},{24,0},{1,25},{9,17},{17,9},{25,1},{2,26},{10... | collective-permute-start | bytes 73736 | tf_op jit(solution)/shard_map/ppermute | solution.py:19
  43.2 4.8 %collective-permute-start.19 = (bf16[24,512]{1,0:T(8,128)(2,1)S(1)}, bf16[24,512]{1,0:T(8,128)(2,1)S(1)}, u32[]{:S(2)}, u32[]{:S(2)}) collective-permute-start(bf16[24,512]{1,0:T(8,128)(2,1)S(1)} %get-tuple-element.84), channel_id=1, source_target_pairs={{0,16},{8,24},{16,0},{24,8},{1,17},{9,25},{17,1},{25,9},{2,18},{10... | collective-permute-start | bytes 73736 | tf_op jit(solution)/shard_map/ppermute | solution.py:19
  44.1 4.1 %collective-permute-start.20 = (bf16[24,512]{1,0:T(8,128)(2,1)S(1)}, bf16[24,512]{1,0:T(8,128)(2,1)S(1)}, u32[]{:S(2)}, u32[]{:S(2)}) collective-permute-start(bf16[24,512]{1,0:T(8,128)(2,1)S(1)} %get-tuple-element.85), channel_id=1, source_target_pairs={{0,8},{8,0},{16,24},{24,16},{1,9},{9,1},{17,25},{25,17},{2,10},{10... | collective-permute-start | bytes 73736 | tf_op jit(solution)/shard_map/ppermute | solution.py:19

commit v9 on v8

--- a/solution.py
+++ b/solution.py
@@ -48,18 +48,18 @@
 def place_kernel(sizes, *refs):
     heads, pools, planes, count = sizes
     sources, placed_ref, targets = refs[:count], refs[count], refs[count + 1 : -1]
-    residual_ref, choice_ref, route_ref = targets[6:]
+    residual_ref, choice_ref, route_ref = targets[7:]
     semaphores = refs[-1]
     head, mine = lax.axis_index("head"), lax.axis_index("pool")
     first = jnp.where(mine == 0, 1.0, 0.0)
-    picked = {4: mine, 5: head}
+    picked = {5: mine, 6: head}
     copies = []
     for i in range(count):
         source = sources[i].at[picked[i]] if i in picked else sources[i]
         copies.append(pltpu.make_async_copy(source, targets[i], semaphores.at[i]))
     for copy in reversed(copies):
         copy.start()
-    for copy in copies[6:]:
+    for copy in copies[7:]:
         copy.wait()
     rows_here, width = residual_ref.shape
     part = rows_here // pools
@@ -90,7 +90,7 @@
         placed_ref[:, start + columns : start + columns + share] = mix[
             :, h * share : (h + 1) * share
         ].astype(BF16)
-    for copy in copies[:6]:
+    for copy in copies[:7]:
         copy.wait()
 
 
@@ -130,9 +130,10 @@
         return mask
 
     count = own_ref.shape[0]
-    fresh = new_ref.shape[0] // requests
-    entry = lax.broadcasted_iota(jnp.int32, (requests, new_ref.shape[0]), 1)
-    first = lax.broadcasted_iota(jnp.int32, (requests, new_ref.shape[0]), 0) * fresh
+    fresh = new_ref.shape[1]
+    entry = lax.broadcasted_iota(jnp.int32, (requests, requests * fresh), 1)
+    first = lax.broadcasted_iota(jnp.int32, (requests, requests * fresh), 0) * fresh
+    newest = new_ref[...].astype(F32).reshape(requests * fresh, new_ref.shape[2]).astype(BF16)
     masks = [cache_mask(0, count), cache_mask(count, count), (entry >= first) & (entry < first + fresh)]
     queries = jnp.concatenate(
         [
@@ -143,7 +144,7 @@
     )
     scale = head_dim ** (-0.5)
     scores = []
-    for ref, mask in zip((own_ref, other_ref, new_ref), masks):
+    for ref, mask in zip((own_ref, other_ref, newest), masks):
         score = dot(queries, ref[:, :head_dim], ((1,), (1,))) * scale
         bias = jnp.where(mask, 0.0, -jnp.inf)
         scores.append(score + jnp.concatenate([bias] * group, axis=0))
@@ -151,7 +152,7 @@
         jnp.maximum, [jnp.max(score, axis=1, keepdims=True) for score in scores]
     )
     total, value = 0.0, 0.0
-    for ref, score in zip((own_ref, other_ref, new_ref), scores):
+    for ref, score in zip((own_ref, other_ref, newest), scores):
         weights = jnp.exp(score - largest)
         total = total + jnp.sum(weights, axis=1, keepdims=True)
         value = value + dot(weights.astype(BF16), ref[:, head_dim:])
@@ -355,6 +356,7 @@
         own_cache,
         queries,
         output_weight,
+        new_entries.reshape(requests, -1, entry),
         one_hot(plane_order, pools * planes * part),
         one_hot(pool_order, requests),
         one_hot(head_order, planes * rows),
@@ -363,19 +365,19 @@
         route_weight.T,
     )
     copied = [
-        shape(*array.shape[i // 4 :], dtype=array.dtype) for i, array in enumerate(outside[:6])
+        shape(*array.shape[i // 5 :], dtype=array.dtype) for i, array in enumerate(outside[:7])
     ]
-    placed, held_cache, held_queries, held_weight, plane_order, pool_order, head_order = kernel_call(
+    placed, held_cache, held_queries, held_weight, held_entries, plane_order, pool_order, head_order = kernel_call(
         functools.partial(place_kernel, (heads, pools, planes, len(outside))),
         [shape(requests, heads * (columns + mixes))] + copied,
         (),
-        [pltpu.VMEM(array.shape, array.dtype) for array in outside[6:]]
+        [pltpu.VMEM(array.shape, array.dtype) for array in outside[7:]]
         + [pltpu.SemaphoreType.DMA((len(outside),))],
         outside,
     )
     args = held(
         held_queries,
-        new_entries.reshape(-1, entry),
+        held_entries,
         held_cache,
         other_cache,
         ints,

time: 49 us -> 48.2 us (0.984)
  local copies, waits for them, and re-layouts: 1.46 us -> 0.64 us
    reshape x1 -> x0, local copies, waits for them, and re-layouts: 0.82 us -> none  [local(): new_entries.reshape(-1, entry)]
  transfers between devices with their start and end apart: 21 -> 21, of which waited for: 14 -> 15; matrix products, arithmetic and copies ran while one was open for 3% -> 2% of each run, Pallas kernels for 7% -> 7%
where the time goes in v9:
time: 48.2 us; the launch traced here: 48 us
  starting transfers between devices  22.2 us (46%)
  waiting for transfers between devices  18.2 us (38%)
  Pallas kernels  6.09 us (13%)
  other arithmetic  0.78 us (2%)
  local copies, waits for them, and re-layouts  0.64 us (1%)
    ppermute x21, starting transfers between devices, send(): return lax.ppermute(value, axes, [(i, i ^ step) for i in range(size)])  22.2 us
    ppermute x21, waiting for transfers between devices, send(): return lax.ppermute(value, axes, [(i, i ^ step) for i in range(size)])  18.2 us
    pallas_call x17, Pallas kernels, kernel_call(): pl.pallas_call(body, out_shape=jax.tree.map(lambda out: pltpu.VMEM(out.sh...  6.09 us
  transfers between devices with their start and end apart: 21, of which 15 were waited for; matrix products, arithmetic and copies ran while one was open for 2% of the time, Pallas kernels for 7%

profile of v9, /device:TPU:0, one launch (start us, length us, event | category | flops | bytes accessed | tf_op | source)
XLA Modules:
  0.0 48.0 jit_solution(5923964111397813783)
XLA Ops:
  0.5 0.8 %pad_add_fusion = s32[104]{0:T(128)S(1)} fusion(s32[4]{0:T(128)} %param.23, s32[4]{0:T(128)} %param.22, s32[48]{0:T(128)} %bitcast.28, s32[48]{0:T(128)} %bitcast.29), kind=kLoop, calls=%fused_computation | loop fusion | flops 312 | bytes 832 | tf_op jit(solution)/shard_map/concatenate | solution.py:327
  1.3 1.9 %shard_map.163 = (bf16[48,2560]{1,0:T(8,128)(2,1)S(1)}, bf16[832,256]{1,0:T(8,128)(2,1)S(1)}, bf16[48,1024]{1,0:T(8,128)(2,1)S(1)}, bf16[512,2048]{1,0:T(8,128)(...) custom-call(bf16[832,256]{1,0:T(8,128)(2,1)} %bitcast.24, ...), custom_call_target="tpu_custom_call" | custom-call | tf_op jit(solution)/shard_map/pallas_call | solution.py:27
  3.3 1.6 %shard_map.164 = (f32[24,2560]{1,0:T(8,128)S(1)}, bf16[24,2560]{1,0:T(8,128)(2,1)S(1)}) custom-call(bf16[48,1024]{1,0:T(8,128)(2,1)S(1)} %get-tuple-element.47.q_ref, bf16[48,2,256]{2,1,0:T(2,128)(2,1)S(1)} %get-tuple-element.48.new_ref, bf16[832,256]{1,0:T(8,128)(2,1)S(1)} %get-tuple-element.49.own_ref, ...), custom_call_target="tpu_custom_call" | custom-call | tf_op jit(solution)/shard_map/pallas_call | solution.py:27
  5.4 1.0 %collective-permute-done.2.other_ref = bf16[24,2560]{1,0:T(8,128)(2,1)S(1)} collective-permute-done((bf16[24,2560]{1,0:T(8,128)(2,1)S(1)}, bf16[24,2560]{1,0:T(8,128)(2,1)S(1)}, u32[]{:S(2)}, u32[]{:S(2)}) %collective-permute-start.2) | collective-permute-done | bytes 122912 | tf_op jit(solution)/shard_map/ppermute | solution.py:19
  6.9 3.9 %collective-permute-start.4 = (bf16[24,640]{1,0:T(8,128)(2,1)S(1)}, bf16[24,640]{1,0:T(8,128)(2,1)S(1)}, u32[]{:S(2)}, u32[]{:S(2)}) collective-permute-start(bf16[24,640]{1,0:T(8,128)(2,1)S(1)} %get-tuple-element.57), channel_id=1, source_target_pairs={{0,6},{2,4},{4,2},{6,0},{1,7},{3,5},{5,3},{7,1},{8,14},{10,12},{12... | collective-permute-start | bytes 92168 | tf_op jit(solution)/shard_map/ppermute | solution.py:19
  11.5 1.2 %collective-permute-done.4.part_ref = bf16[24,640]{1,0:T(8,128)(2,1)S(1)} collective-permute-done((bf16[24,640]{1,0:T(8,128)(2,1)S(1)}, bf16[24,640]{1,0:T(8,128)(2,1)S(1)}, u32[]{:S(2)}, u32[]{:S(2)}) %collective-permute-start.4) | collective-permute-done | bytes 30752 | tf_op jit(solution)/shard_map/ppermute | solution.py:19
  12.7 2.0 %collective-permute-done.5.part_ref = bf16[24,640]{1,0:T(8,128)(2,1)S(1)} collective-permute-done((bf16[24,640]{1,0:T(8,128)(2,1)S(1)}, bf16[24,640]{1,0:T(8,128)(2,1)S(1)}, u32[]{:S(2)}, u32[]{:S(2)}) %collective-permute-start.5) | collective-permute-done | bytes 30752 | tf_op jit(solution)/shard_map/ppermute | solution.py:19
  15.2 3.7 %collective-permute-start.7 = (bf16[24,640]{1,0:T(8,128)(2,1)S(1)}, bf16[24,640]{1,0:T(8,128)(2,1)S(1)}, u32[]{:S(2)}, u32[]{:S(2)}) collective-permute-start(bf16[24,640]{1,0:T(8,128)(2,1)S(1)} %get-tuple-element.60), channel_id=1, source_target_pairs={{0,24},{8,16},{16,8},{24,0},{1,25},{9,17},{17,9},{25,1},{2,26},{10... | collective-permute-start | bytes 92168 | tf_op jit(solution)/shard_map/ppermute | solution.py:19
  18.9 0.8 %collective-permute-start.8 = (bf16[24,640]{1,0:T(8,128)(2,1)S(1)}, bf16[24,640]{1,0:T(8,128)(2,1)S(1)}, u32[]{:S(2)}, u32[]{:S(2)}) collective-permute-start(bf16[24,640]{1,0:T(8,128)(2,1)S(1)} %get-tuple-element.61), channel_id=1, source_target_pairs={{0,8},{8,0},{16,24},{24,16},{1,9},{9,1},{17,25},{25,17},{2,10},{10... | collective-permute-start | bytes 92168 | tf_op jit(solution)/shard_map/ppermute | solution.py:19
  19.7 1.4 %collective-permute-done.7.part_ref.refs_1_ = bf16[24,640]{1,0:T(8,128)(2,1)S(1)} collective-permute-done((bf16[24,640]{1,0:T(8,128)(2,1)S(1)}, bf16[24,640]{1,0:T(8,128)(2,1)S(1)}, u32[]{:S(2)}, u32[]{:S(2)}) %collective-permute-start.7) | collective-permute-done | bytes 30752 | tf_op jit(solution)/shard_map/ppermute | solution.py:19
  21.1 2.6 %collective-permute-done.6.part_ref.refs_2_ = bf16[24,640]{1,0:T(8,128)(2,1)S(1)} collective-permute-done((bf16[24,640]{1,0:T(8,128)(2,1)S(1)}, bf16[24,640]{1,0:T(8,128)(2,1)S(1)}, u32[]{:S(2)}, u32[]{:S(2)}) %collective-permute-start.6) | collective-permute-done | bytes 30752 | tf_op jit(solution)/shard_map/ppermute | solution.py:19
  23.7 1.6 %collective-permute-start.12 = (bf16[4,24,512]{2,1,0:T(8,128)(2,1)S(1)}, bf16[4,24,512]{2,1,0:T(8,128)(2,1)S(1)}, u32[]{:S(2)}, u32[]{:S(2)}) collective-permute-start(bf16[4,24,512]{2,1,0:T(8,128)(2,1)S(1)} %get-tuple-element.63), channel_id=1, source_target_pairs={{0,6},{2,4},{4,2},{6,0},{1,7},{3,5},{5,3},{7,1},{8,14},{10,12},{12... | collective-permute-start | bytes 294920 | tf_op jit(solution)/shard_map/ppermute | solution.py:19
  25.8 1.5 %collective-permute-start.9 = (bf16[4,24,512]{2,1,0:T(8,128)(2,1)S(1)}, bf16[4,24,512]{2,1,0:T(8,128)(2,1)S(1)}, u32[]{:S(2)}, u32[]{:S(2)}) collective-permute-start(bf16[4,24,512]{2,1,0:T(8,128)(2,1)S(1)} %get-tuple-element.63), channel_id=1, source_target_pairs={{0,2},{2,0},{4,6},{6,4},{1,3},{3,1},{5,7},{7,5},{8,10},{10,8},{12,... | collective-permute-start | bytes 294920 | tf_op jit(solution)/shard_map/ppermute | solution.py:19
  27.7 1.6 %collective-permute-done.12.block_ref = bf16[4,24,512]{2,1,0:T(8,128)(2,1)S(1)} collective-permute-done((bf16[4,24,512]{2,1,0:T(8,128)(2,1)S(1)}, bf16[4,24,512]{2,1,0:T(8,128)(2,1)S(1)}, u32[]{:S(2)}, u32[]{:S(2)}) %collective-permute-start.12) | collective-permute-done | bytes 98336 | tf_op jit(solution)/shard_map/ppermute | solution.py:19
  31.8 2.6 %collective-permute-start.14 = (bf16[24,2048]{1,0:T(8,128)(2,1)S(1)}, bf16[24,2048]{1,0:T(8,128)(2,1)S(1)}, u32[]{:S(2)}, u32[]{:S(2)}) collective-permute-start(bf16[24,2048]{1,0:T(8,128)(2,1)S(1)} %get-tuple-element.78), channel_id=1, source_target_pairs={{0,6},{2,4},{4,2},{6,0},{1,7},{3,5},{5,3},{7,1},{8,14},{10,12},{12... | collective-permute-start | bytes 294920 | tf_op jit(solution)/shard_map/ppermute | solution.py:19
  34.5 0.9 %collective-permute-start.16 = (bf16[24,2048]{1,0:T(8,128)(2,1)S(1)}, bf16[24,2048]{1,0:T(8,128)(2,1)S(1)}, u32[]{:S(2)}, u32[]{:S(2)}) collective-permute-start(bf16[24,2048]{1,0:T(8,128)(2,1)S(1)} %get-tuple-element.80), channel_id=1, source_target_pairs={{0,2},{2,0},{4,6},{6,4},{1,3},{3,1},{5,7},{7,5},{8,10},{10,8},{12,... | collective-permute-start | bytes 294920 | tf_op jit(solution)/shard_map/ppermute | solution.py:19
  35.4 2.0 %collective-permute-done.14.refs_0_ = bf16[24,2048]{1,0:T(8,128)(2,1)S(1)} collective-permute-done((bf16[24,2048]{1,0:T(8,128)(2,1)S(1)}, bf16[24,2048]{1,0:T(8,128)(2,1)S(1)}, u32[]{:S(2)}, u32[]{:S(2)}) %collective-permute-start.14) | collective-permute-done | bytes 98336 | tf_op jit(solution)/shard_map/ppermute | solution.py:19
  37.4 1.6 %collective-permute-done.15.refs_1_ = bf16[24,2048]{1,0:T(8,128)(2,1)S(1)} collective-permute-done((bf16[24,2048]{1,0:T(8,128)(2,1)S(1)}, bf16[24,2048]{1,0:T(8,128)(2,1)S(1)}, u32[]{:S(2)}, u32[]{:S(2)}) %collective-permute-start.15) | collective-permute-done | bytes 98336 | tf_op jit(solution)/shard_map/ppermute | solution.py:19
  39.2 1.2 %collective-permute-done.17.other_ref = bf16[24,1024]{1,0:T(8,128)(2,1)S(1)} collective-permute-done((bf16[24,1024]{1,0:T(8,128)(2,1)S(1)}, bf16[24,1024]{1,0:T(8,128)(2,1)S(1)}, u32[]{:S(2)}, u32[]{:S(2)}) %collective-permute-start.17) | collective-permute-done | bytes 49184 | tf_op jit(solution)/shard_map/ppermute | solution.py:19
  40.6 1.8 %collective-permute-start.18 = (bf16[24,512]{1,0:T(8,128)(2,1)S(1)}, bf16[24,512]{1,0:T(8,128)(2,1)S(1)}, u32[]{:S(2)}, u32[]{:S(2)}) collective-permute-start(bf16[24,512]{1,0:T(8,128)(2,1)S(1)} %get-tuple-element.85), channel_id=1, source_target_pairs={{0,24},{8,16},{16,8},{24,0},{1,25},{9,17},{17,9},{25,1},{2,26},{10... | collective-permute-start | bytes 73736 | tf_op jit(solution)/shard_map/ppermute | solution.py:19
  42.4 0.9 %collective-permute-start.19 = (bf16[24,512]{1,0:T(8,128)(2,1)S(1)}, bf16[24,512]{1,0:T(8,128)(2,1)S(1)}, u32[]{:S(2)}, u32[]{:S(2)}) collective-permute-start(bf16[24,512]{1,0:T(8,128)(2,1)S(1)} %get-tuple-element.86), channel_id=1, source_target_pairs={{0,16},{8,24},{16,0},{24,8},{1,17},{9,25},{17,1},{25,9},{2,18},{10... | collective-permute-start | bytes 73736 | tf_op jit(solution)/shard_map/ppermute | solution.py:19
  43.3 1.8 %collective-permute-start.20 = (bf16[24,512]{1,0:T(8,128)(2,1)S(1)}, bf16[24,512]{1,0:T(8,128)(2,1)S(1)}, u32[]{:S(2)}, u32[]{:S(2)}) collective-permute-start(bf16[24,512]{1,0:T(8,128)(2,1)S(1)} %get-tuple-element.87), channel_id=1, source_target_pairs={{0,8},{8,0},{16,24},{24,16},{1,9},{9,1},{17,25},{25,17},{2,10},{10... | collective-permute-start | bytes 73736 | tf_op jit(solution)/shard_map/ppermute | solution.py:19
  45.1 1.3 %collective-permute-done.18.refs_0_ = bf16[24,512]{1,0:T(8,128)(2,1)S(1)} collective-permute-done((bf16[24,512]{1,0:T(8,128)(2,1)S(1)}, bf16[24,512]{1,0:T(8,128)(2,1)S(1)}, u32[]{:S(2)}, u32[]{:S(2)}) %collective-permute-start.18) | collective-permute-done | bytes 24608 | tf_op jit(solution)/shard_map/ppermute | solution.py:19
  46.4 0.8 %collective-permute-done.19.refs_1_ = bf16[24,512]{1,0:T(8,128)(2,1)S(1)} collective-permute-done((bf16[24,512]{1,0:T(8,128)(2,1)S(1)}, bf16[24,512]{1,0:T(8,128)(2,1)S(1)}, u32[]{:S(2)}, u32[]{:S(2)}) %collective-permute-start.19) | collective-permute-done | bytes 24608 | tf_op jit(solution)/shard_map/ppermute | solution.py:19
  (44 shorter events, 7.4 us)
Async XLA Ops:
  0.0 3.3 %collective-permute-start = (bf16[832,256]{1,0:T(8,128)(2,1)}, bf16[832,256]{1,0:T(8,128)(2,1)S(1)}, u32[]{:S(2)}, u32[]{:S(2)}) collective-permute-start(bf16[832,256]{1,0:T(8,128)(2,1)} %bitcast.23), channel_id=1, source_target_pairs={{0,1},{1,0},{2,3},{3,2},{4,5},{5,4},{6,7},{7,6},{8,9},{9,8},{10,11... | collective-permute-start | bytes 1277960 | tf_op jit(solution)/shard_map/ppermute | solution.py:19
  1.2 2.0 %collective-permute-start.1 = (s32[1,128]{1,0:T(1,128)S(1)}, s32[1,128]{1,0:T(1,128)S(1)}, u32[]{:S(2)}, u32[]{:S(2)}) collective-permute-start(s32[1,128]{1,0:T(1,128)S(1)} %pad_bitcast_fusion.own_ints_ref), channel_id=1, source_target_pairs={{0,1},{1,0},{2,3},{3,2},{4,5},{5,4},{6,7},{7,6},{8,9},{9,8},{10,11... | collective-permute-start | bytes 1544 | tf_op jit(solution)/shard_map/ppermute | solution.py:19
  3.3 3.1 %copy-start = (bf16[1,2,192,2048]{3,2,1,0:T(8,128)(2,1)S(1)}, bf16[1,2,192,2048]{3,2,1,0:T(8,128)(2,1)}, u32[]{:S(2)}) copy-start(bf16[1,2,192,2048]{3,2,1,0:T(8,128)(2,1)} %param.29) | copy-start | bytes 4718596
  3.3 3.5 %copy-start.1 = (bf16[1,192,2048]{2,1,0:T(8,128)(2,1)S(1)}, bf16[1,192,2048]{2,1,0:T(8,128)(2,1)}, u32[]{:S(2)}) copy-start(bf16[1,192,2048]{2,1,0:T(8,128)(2,1)} %param.30) | copy-start | bytes 2359300
  3.3 24.0 %copy-start.2 = (f32[2048]{0:T(1024)S(1)}, f32[2048]{0:T(1024)}, u32[]{:S(2)}) copy-start(f32[2048]{0:T(1024)} %param.25) | copy-start | bytes 24580
  4.9 1.5 %collective-permute-start.2 = (bf16[24,2560]{1,0:T(8,128)(2,1)S(1)}, bf16[24,2560]{1,0:T(8,128)(2,1)S(1)}, u32[]{:S(2)}, u32[]{:S(2)}) collective-permute-start(bf16[24,2560]{1,0:T(8,128)(2,1)S(1)} %get-tuple-element.54), channel_id=1, source_target_pairs={{0,1},{1,0},{2,3},{3,2},{4,5},{5,4},{6,7},{7,6},{8,9},{9,8},{10,11... | collective-permute-start | bytes 368648 | tf_op jit(solution)/shard_map/ppermute | solution.py:19
  6.4 20.9 %collective-permute-start.10 = (bf16[384,2048]{1,0:T(8,128)(2,1)S(1)}, bf16[384,2048]{1,0:T(8,128)(2,1)S(1)}, u32[]{:S(2)}, u32[]{:S(2)}) collective-permute-start(bf16[384,2048]{1,0:T(8,128)(2,1)S(1)} %bitcast.11), channel_id=1, source_target_pairs={{0,1},{1,0},{2,3},{3,2},{4,5},{5,4},{6,7},{7,6},{8,9},{9,8},{10,11... | collective-permute-start | bytes 4718600 | tf_op jit(solution)/shard_map/ppermute | solution.py:19
  6.8 24.4 %collective-permute-start.13 = (bf16[192,2048]{1,0:T(8,128)(2,1)S(1)}, bf16[192,2048]{1,0:T(8,128)(2,1)S(1)}, u32[]{:S(2)}, u32[]{:S(2)}) collective-permute-start(bf16[192,2048]{1,0:T(8,128)(2,1)S(1)} %bitcast.16), channel_id=1, source_target_pairs={{0,1},{1,0},{2,3},{3,2},{4,5},{5,4},{6,7},{7,6},{8,9},{9,8},{10,11... | collective-permute-start | bytes 2359304 | tf_op jit(solution)/shard_map/ppermute | solution.py:19
  6.9 5.7 %collective-permute-start.4 = (bf16[24,640]{1,0:T(8,128)(2,1)S(1)}, bf16[24,640]{1,0:T(8,128)(2,1)S(1)}, u32[]{:S(2)}, u32[]{:S(2)}) collective-permute-start(bf16[24,640]{1,0:T(8,128)(2,1)S(1)} %get-tuple-element.57), channel_id=1, source_target_pairs={{0,6},{2,4},{4,2},{6,0},{1,7},{3,5},{5,3},{7,1},{8,14},{10,12},{12... | collective-permute-start | bytes 92168 | tf_op jit(solution)/shard_map/ppermute | solution.py:19
  10.8 3.9 %collective-permute-start.5 = (bf16[24,640]{1,0:T(8,128)(2,1)S(1)}, bf16[24,640]{1,0:T(8,128)(2,1)S(1)}, u32[]{:S(2)}, u32[]{:S(2)}) collective-permute-start(bf16[24,640]{1,0:T(8,128)(2,1)S(1)} %get-tuple-element.58), channel_id=1, source_target_pairs={{0,4},{2,6},{4,0},{6,2},{1,5},{3,7},{5,1},{7,3},{8,12},{10,14},{12... | collective-permute-start | bytes 92168 | tf_op jit(solution)/shard_map/ppermute | solution.py:19
  11.3 3.9 %collective-permute-start.3 = (bf16[24,640]{1,0:T(8,128)(2,1)S(1)}, bf16[24,640]{1,0:T(8,128)(2,1)S(1)}, u32[]{:S(2)}, u32[]{:S(2)}) collective-permute-start(bf16[24,640]{1,0:T(8,128)(2,1)S(1)} %get-tuple-element.55), channel_id=1, source_target_pairs={{0,2},{2,0},{4,6},{6,4},{1,3},{3,1},{5,7},{7,5},{8,10},{10,8},{12,... | collective-permute-start | bytes 92168 | tf_op jit(solution)/shard_map/ppermute | solution.py:19
  15.2 5.9 %collective-permute-start.7 = (bf16[24,640]{1,0:T(8,128)(2,1)S(1)}, bf16[24,640]{1,0:T(8,128)(2,1)S(1)}, u32[]{:S(2)}, u32[]{:S(2)}) collective-permute-start(bf16[24,640]{1,0:T(8,128)(2,1)S(1)} %get-tuple-element.60), channel_id=1, source_target_pairs={{0,24},{8,16},{16,8},{24,0},{1,25},{9,17},{17,9},{25,1},{2,26},{10... | collective-permute-start | bytes 92168 | tf_op jit(solution)/shard_map/ppermute | solution.py:19
  18.9 4.8 %collective-permute-start.6 = (bf16[24,640]{1,0:T(8,128)(2,1)S(1)}, bf16[24,640]{1,0:T(8,128)(2,1)S(1)}, u32[]{:S(2)}, u32[]{:S(2)}) collective-permute-start(bf16[24,640]{1,0:T(8,128)(2,1)S(1)} %get-tuple-element.59), channel_id=1, source_target_pairs={{0,16},{8,24},{16,0},{24,8},{1,17},{9,25},{17,1},{25,9},{2,18},{10... | collective-permute-start | bytes 92168 | tf_op jit(solution)/shard_map/ppermute | solution.py:19
  18.9 4.8 %collective-permute-start.8 = (bf16[24,640]{1,0:T(8,128)(2,1)S(1)}, bf16[24,640]{1,0:T(8,128)(2,1)S(1)}, u32[]{:S(2)}, u32[]{:S(2)}) collective-permute-start(bf16[24,640]{1,0:T(8,128)(2,1)S(1)} %get-tuple-element.61), channel_id=1, source_target_pairs={{0,8},{8,0},{16,24},{24,16},{1,9},{9,1},{17,25},{25,17},{2,10},{10... | collective-permute-start | bytes 92168 | tf_op jit(solution)/shard_map/ppermute | solution.py:19
  23.7 5.6 %collective-permute-start.12 = (bf16[4,24,512]{2,1,0:T(8,128)(2,1)S(1)}, bf16[4,24,512]{2,1,0:T(8,128)(2,1)S(1)}, u32[]{:S(2)}, u32[]{:S(2)}) collective-permute-start(bf16[4,24,512]{2,1,0:T(8,128)(2,1)S(1)} %get-tuple-element.63), channel_id=1, source_target_pairs={{0,6},{2,4},{4,2},{6,0},{1,7},{3,5},{5,3},{7,1},{8,14},{10,12},{12... | collective-permute-start | bytes 294920 | tf_op jit(solution)/shard_map/ppermute | solution.py:19
  25.3 5.1 %collective-permute-start.11 = (bf16[4,24,512]{2,1,0:T(8,128)(2,1)S(1)}, bf16[4,24,512]{2,1,0:T(8,128)(2,1)S(1)}, u32[]{:S(2)}, u32[]{:S(2)}) collective-permute-start(bf16[4,24,512]{2,1,0:T(8,128)(2,1)S(1)} %get-tuple-element.63), channel_id=1, source_target_pairs={{0,4},{2,6},{4,0},{6,2},{1,5},{3,7},{5,1},{7,3},{8,12},{10,14},{12... | collective-permute-start | bytes 294920 | tf_op jit(solution)/shard_map/ppermute | solution.py:19
  25.8 5.0 %collective-permute-start.9 = (bf16[4,24,512]{2,1,0:T(8,128)(2,1)S(1)}, bf16[4,24,512]{2,1,0:T(8,128)(2,1)S(1)}, u32[]{:S(2)}, u32[]{:S(2)}) collective-permute-start(bf16[4,24,512]{2,1,0:T(8,128)(2,1)S(1)} %get-tuple-element.63), channel_id=1, source_target_pairs={{0,2},{2,0},{4,6},{6,4},{1,3},{3,1},{5,7},{7,5},{8,10},{10,8},{12,... | collective-permute-start | bytes 294920 | tf_op jit(solution)/shard_map/ppermute | solution.py:19
  31.8 5.6 %collective-permute-start.14 = (bf16[24,2048]{1,0:T(8,128)(2,1)S(1)}, bf16[24,2048]{1,0:T(8,128)(2,1)S(1)}, u32[]{:S(2)}, u32[]{:S(2)}) collective-permute-start(bf16[24,2048]{1,0:T(8,128)(2,1)S(1)} %get-tuple-element.78), channel_id=1, source_target_pairs={{0,6},{2,4},{4,2},{6,0},{1,7},{3,5},{5,3},{7,1},{8,14},{10,12},{12... | collective-permute-start | bytes 294920 | tf_op jit(solution)/shard_map/ppermute | solution.py:19
  34.4 4.6 %collective-permute-start.15 = (bf16[24,2048]{1,0:T(8,128)(2,1)S(1)}, bf16[24,2048]{1,0:T(8,128)(2,1)S(1)}, u32[]{:S(2)}, u32[]{:S(2)}) collective-permute-start(bf16[24,2048]{1,0:T(8,128)(2,1)S(1)} %get-tuple-element.79), channel_id=1, source_target_pairs={{0,4},{2,6},{4,0},{6,2},{1,5},{3,7},{5,1},{7,3},{8,12},{10,14},{12... | collective-permute-start | bytes 294920 | tf_op jit(solution)/shard_map/ppermute | solution.py:19
  34.5 4.6 %collective-permute-start.16 = (bf16[24,2048]{1,0:T(8,128)(2,1)S(1)}, bf16[24,2048]{1,0:T(8,128)(2,1)S(1)}, u32[]{:S(2)}, u32[]{:S(2)}) collective-permute-start(bf16[24,2048]{1,0:T(8,128)(2,1)S(1)} %get-tuple-element.80), channel_id=1, source_target_pairs={{0,2},{2,0},{4,6},{6,4},{1,3},{3,1},{5,7},{7,5},{8,10},{10,8},{12,... | collective-permute-start | bytes 294920 | tf_op jit(solution)/shard_map/ppermute | solution.py:19
  39.2 1.3 %collective-permute-start.17 = (bf16[24,1024]{1,0:T(8,128)(2,1)S(1)}, bf16[24,1024]{1,0:T(8,128)(2,1)S(1)}, u32[]{:S(2)}, u32[]{:S(2)}) collective-permute-start(bf16[24,1024]{1,0:T(8,128)(2,1)S(1)} %get-tuple-element.83), channel_id=1, source_target_pairs={{0,1},{1,0},{2,3},{3,2},{4,5},{5,4},{6,7},{7,6},{8,9},{9,8},{10,11... | collective-permute-start | bytes 147464 | tf_op jit(solution)/shard_map/ppermute | solution.py:19
  40.6 5.8 %collective-permute-start.18 = (bf16[24,512]{1,0:T(8,128)(2,1)S(1)}, bf16[24,512]{1,0:T(8,128)(2,1)S(1)}, u32[]{:S(2)}, u32[]{:S(2)}) collective-permute-start(bf16[24,512]{1,0:T(8,128)(2,1)S(1)} %get-tuple-element.85), channel_id=1, source_target_pairs={{0,24},{8,16},{16,8},{24,0},{1,25},{9,17},{17,9},{25,1},{2,26},{10... | collective-permute-start | bytes 73736 | tf_op jit(solution)/shard_map/ppermute | solution.py:19
  42.4 4.8 %collective-permute-start.19 = (bf16[24,512]{1,0:T(8,128)(2,1)S(1)}, bf16[24,512]{1,0:T(8,128)(2,1)S(1)}, u32[]{:S(2)}, u32[]{:S(2)}) collective-permute-start(bf16[24,512]{1,0:T(8,128)(2,1)S(1)} %get-tuple-element.86), channel_id=1, source_target_pairs={{0,16},{8,24},{16,0},{24,8},{1,17},{9,25},{17,1},{25,9},{2,18},{10... | collective-permute-start | bytes 73736 | tf_op jit(solution)/shard_map/ppermute | solution.py:19
  43.3 4.1 %collective-permute-start.20 = (bf16[24,512]{1,0:T(8,128)(2,1)S(1)}, bf16[24,512]{1,0:T(8,128)(2,1)S(1)}, u32[]{:S(2)}, u32[]{:S(2)}) collective-permute-start(bf16[24,512]{1,0:T(8,128)(2,1)S(1)} %get-tuple-element.87), channel_id=1, source_target_pairs={{0,8},{8,0},{16,24},{24,16},{1,9},{9,1},{17,25},{25,17},{2,10},{10... | collective-permute-start | bytes 73736 | tf_op jit(solution)/shard_map/ppermute | solution.py:19

commit v10 on v9

--- a/solution.py
+++ b/solution.py
@@ -17,6 +17,16 @@
 def send(value, axes, step):
     size = lax.axis_size(axes)
     return lax.ppermute(value, axes, [(i, i ^ step) for i in range(size)])
+
+
+def give(value, source):
+    return lax.ppermute(value, "pool", [(source, 1 - source)])
+
+
+def send_last(value, axis, step):
+    size, pools = lax.axis_size(axis), lax.axis_size("pool")
+    pairs = [(i * pools + pools - 1, (i ^ step) * pools + pools - 1) for i in range(size)]
+    return lax.ppermute(value, (axis, "pool"), pairs)
 
 
 def dot(a, b, contract=((1,), (0,))):
@@ -69,7 +79,7 @@
     own = None
     for p in range(pools):
         inside = line - (p * heads * part + head * part)
-        one = (inside >= 0) & (inside < part) & (lane == inside + (mine ^ p) * part)
+        one = (inside >= 0) & (inside < part) & (lane == inside + p * part)
         own = one if own is None else own | one
     spread = jnp.where(own, first, 0.0)
     mixes = placed_ref.shape[1] - width
@@ -99,7 +109,6 @@
     slots = own_ref.shape[0] // page
     here = lax.axis_index("pool")
     group = q_ref.shape[1] // head_dim // pools
-    rows = requests // pools
     width = weight_ref.shape[1]
     columns = width // heads
     mixes = (placed_ref.shape[1] - width) // heads
@@ -166,12 +175,12 @@
         start = h * (columns + mixes)
         at = slice(start, start + columns)
         part = partial[:, h * columns : (h + 1) * columns] + placed_ref[:, at].astype(F32)
-        own_out_ref[:, at] = part[:rows]
-        other_out_ref[:, at] = part[rows:].astype(BF16)
+        own_out_ref[:, at] = part
+        other_out_ref[:, at] = part.astype(BF16)
         at = slice(start + columns, start + columns + mixes)
         part = placed_ref[:, at].astype(F32)
-        own_out_ref[:, at] = part[:rows]
-        other_out_ref[:, at] = part[rows:].astype(BF16)
+        own_out_ref[:, at] = part
+        other_out_ref[:, at] = part.astype(BF16)
 
 
 def split_kernel(own_ref, other_ref, *outs):
@@ -198,10 +207,19 @@
 
 
 def stack_kernel(*refs):
-    parts, (all_ref, first_ref) = refs[1:-2], refs[-2:]
+    parts, (mine_ref, other_ref) = refs[1:-2], refs[-2:]
+    rows = mine_ref.shape[1]
     for step, part in enumerate(reversed(parts)):
-        all_ref[step] = part[...]
-        first_ref[step] = part[:, : first_ref.shape[2]]
+        block = part[...].astype(F32)
+        other_ref[step] = block[:rows].astype(BF16)
+        mine_ref[step] = block[rows:].astype(BF16)
+
+
+def choose_kernel(mine_ref, given_ref, all_ref, first_ref):
+    last = lax.axis_index("pool") == 1
+    block = jnp.where(last, mine_ref[...].astype(F32), given_ref[...].astype(F32)).astype(BF16)
+    all_ref[...] = block
+    first_ref[...] = block[:, :, : first_ref.shape[2]]
 
 
 def project_kernel(step, planes, block_ref, own_up_ref, other_up_ref, gain_ref, *refs):
@@ -335,9 +353,8 @@
 
     rows = requests // pools
     pool_order = [
-        [h * rows_here + (here ^ p) * part + i for p in range(pools) for h in range(heads) for i in range(part)]
-        for here in range(pools)
-    ]
+        [h * rows_here + p * part + i for p in range(pools) for h in range(heads) for i in range(part)]
+    ] * pools
     head_order = [
         [(r * heads + (here ^ h)) * part + i for h in range(heads) for r in range(planes) for i in range(part)]
         for here in range(heads)
@@ -389,39 +406,42 @@
     sizes = (requests, pages, moved, page, heads, pools, entry // 2)
     own, other = kernel_call(
         functools.partial(attend_kernel, sizes),
-        [shape(rows, heads * (columns + mixes), dtype=F32), shape(rows, heads * (columns + mixes))],
+        [
+            shape(requests, heads * (columns + mixes), dtype=F32),
+            shape(requests, heads * (columns + mixes)),
+        ],
         args,
     )
-    other = send(other, "pool", 1)
+    other = give(other, 0)
     ready = lax.optimization_barrier((gate_up, down_weight, other))
     other_up, other_down = send(ready[0], "pool", 1), send(ready[1], "pool", 1)
-    piece = shape(rows, columns + mixes)
+    piece = shape(requests, columns + mixes)
     pieces = kernel_call(
         split_kernel,
-        [shape(rows, columns + mixes, dtype=F32)] + [piece] * (heads - 1),
+        [shape(requests, columns + mixes, dtype=F32)] + [piece] * (heads - 1),
         held(own, other),
     )
     total = pieces[0]
     for step in reversed(range(2, heads)):
         total = kernel_call(
             add_kernel,
-            shape(rows, columns + mixes, dtype=F32),
-            held(total, send(pieces[step], "head", step)),
+            shape(requests, columns + mixes, dtype=F32),
+            held(total, send_last(pieces[step], "head", step)),
         )
     hidden = kernel_call(
         functools.partial(sum_kernel, 2),
         [piece] * planes,
-        held(send(pieces[1], "head", 1), total),
-    )
-
-    arrived = [send(hidden[step], "req", step) for step in reversed(range(1, planes))] + [hidden[0]]
+        held(send_last(pieces[1], "head", 1), total),
+    )
+
+    arrived = [send_last(hidden[step], "req", step) for step in reversed(range(1, planes))] + [hidden[0]]
     marks = []
     for part_arrived in arrived[:-2]:
         marks = [kernel_call(mark_kernel, shape(16, LANES), held(part_arrived, *marks))]
+    piece = shape(planes, rows, columns + mixes)
+    mine, given = kernel_call(stack_kernel, [piece] * 2, held(*marks, *arrived))
     plane_blocks, sent = kernel_call(
-        stack_kernel,
-        [shape(planes, rows, columns + mixes), shape(planes, rows, columns)],
-        held(*marks, *arrived),
+        choose_kernel, [piece, shape(planes, rows, columns)], held(mine, give(given, 1))
     )
     weights = held(gate_up, other_up, norm_gain.reshape(1, -1))
     total = planes * rows

time: 48.2 us -> 62.7 us (1.30)
  waiting for transfers between devices: 18.2 us -> 34.2 us
  starting transfers between devices: 22.2 us -> 20.4 us
    ppermute x0 -> x8, waiting for transfers between devices: none -> 22.5 us  [the longest x2 22.4 us: give(): return lax.ppermute(value, 'pool', [(source, 1 - source)])]
    ppermute x21 -> x14, starting transfers between devices: 22.2 us -> 12.7 us  [send(): return lax.ppermute(value, axes, [(i, i ^ step) for i in range(size)])]
    ppermute x0 -> x8, starting transfers between devices: none -> 7.66 us  [the longest x6 3.99 us: send_last(): return lax.ppermute(value, (axis, 'pool'), pairs)]
    ppermute x21 -> x14, waiting for transfers between devices: 18.2 us -> 11.7 us  [send(): return lax.ppermute(value, axes, [(i, i ^ step) for i in range(size)])]
    pallas_call x17 -> x18, Pallas kernels: 6.09 us -> 6.18 us  [kernel_call(): pl.pallas_call(body, out_shape=jax.tree.map(lambda out: pltpu.VMEM(out.sh...]
  transfers between devices with their start and end apart: 21 -> 22, of which waited for: 15 -> 9; matrix products, arithmetic and copies ran while one was open for 2% -> 1% of each run, Pallas kernels for 7% -> 6%
where the time goes in v10:
time: 62.7 us; the launch traced here: 62.4 us
  waiting for transfers between devices  34.2 us (55%)
  starting transfers between devices  20.4 us (33%)
  Pallas kernels  6.18 us (10%)
  other arithmetic  0.78 us (1%)
  local copies, waits for them, and re-layouts  0.64 us (1%)
    ppermute x2, waiting for transfers between devices, give(): return lax.ppermute(value, 'pool', [(source, 1 - source)])  22.4 us
    ppermute x14, starting transfers between devices, send(): return lax.ppermute(value, axes, [(i, i ^ step) for i in range(size)])  12.7 us
    ppermute x14, waiting for transfers between devices, send(): return lax.ppermute(value, axes, [(i, i ^ step) for i in range(size)])  11.7 us
    pallas_call x18, Pallas kernels, kernel_call(): pl.pallas_call(body, out_shape=jax.tree.map(lambda out: pltpu.VMEM(out.sh...  6.18 us
    ppermute x6, starting transfers between devices, send_last(): return lax.ppermute(value, (axis, 'pool'), pairs)  3.99 us
    ppermute x2, starting transfers between devices, give(): return lax.ppermute(value, 'pool', [(source, 1 - source)])  3.67 us
  transfers between devices with their start and end apart: 22, of which 9 were waited for; matrix products, arithmetic and copies ran while one was open for 1% of the time, Pallas kernels for 6%

profile of v10, /device:TPU:0, one launch (start us, length us, event | category | flops | bytes accessed | tf_op | source)
XLA Modules:
  0.0 62.4 jit_solution(8086810819254010589)
XLA Ops:
  0.5 0.8 %pad_add_fusion = s32[104]{0:T(128)S(1)} fusion(s32[4]{0:T(128)} %param.23, s32[4]{0:T(128)} %param.22, s32[48]{0:T(128)} %bitcast.28, s32[48]{0:T(128)} %bitcast.29), kind=kLoop, calls=%fused_computation | loop fusion | flops 312 | bytes 832 | tf_op jit(solution)/shard_map/concatenate | solution.py:345
  1.3 1.9 %shard_map.163 = (bf16[48,2560]{1,0:T(8,128)(2,1)S(1)}, bf16[832,256]{1,0:T(8,128)(2,1)S(1)}, bf16[48,1024]{1,0:T(8,128)(2,1)S(1)}, bf16[512,2048]{1,0:T(8,128)(...) custom-call(bf16[832,256]{1,0:T(8,128)(2,1)} %bitcast.24, ...), custom_call_target="tpu_custom_call" | custom-call | tf_op jit(solution)/shard_map/pallas_call | solution.py:37
  3.3 1.6 %shard_map.164 = (f32[48,2560]{1,0:T(8,128)S(1)}, bf16[48,2560]{1,0:T(8,128)(2,1)S(1)}) custom-call(bf16[48,1024]{1,0:T(8,128)(2,1)S(1)} %get-tuple-element.49.q_ref, bf16[48,2,256]{2,1,0:T(2,128)(2,1)S(1)} %get-tuple-element.50.new_ref, bf16[832,256]{1,0:T(8,128)(2,1)S(1)} %get-tuple-element.51.own_ref, ...), custom_call_target="tpu_custom_call" | custom-call | tf_op jit(solution)/shard_map/pallas_call | solution.py:37
  4.9 2.4 %collective-permute-start.2 = (bf16[48,2560]{1,0:T(8,128)(2,1)S(1)}, bf16[48,2560]{1,0:T(8,128)(2,1)S(1)}, u32[]{:S(2)}, u32[]{:S(2)}) collective-permute-start(bf16[48,2560]{1,0:T(8,128)(2,1)S(1)} %get-tuple-element.56), channel_id=1, source_target_pairs={{0,1},{2,3},{4,5},{6,7},{8,9},{10,11},{12,13},{14,15},{16,17},{18,... | collective-permute-start | bytes 737288 | tf_op jit(solution)/shard_map/ppermute | solution.py:23
  7.3 1.1 %collective-permute-done.2.other_ref = bf16[48,2560]{1,0:T(8,128)(2,1)S(1)} collective-permute-done((bf16[48,2560]{1,0:T(8,128)(2,1)S(1)}, bf16[48,2560]{1,0:T(8,128)(2,1)S(1)}, u32[]{:S(2)}, u32[]{:S(2)}) %collective-permute-start.2) | collective-permute-done | bytes 245792 | tf_op jit(solution)/shard_map/ppermute | solution.py:23
  9.0 0.7 %collective-permute-start.4 = (bf16[48,640]{1,0:T(8,128)(2,1)S(1)}, bf16[48,640]{1,0:T(8,128)(2,1)S(1)}, u32[]{:S(2)}, u32[]{:S(2)}) collective-permute-start(bf16[48,640]{1,0:T(8,128)(2,1)S(1)} %get-tuple-element.59), channel_id=1, source_target_pairs={{1,7},{3,5},{5,3},{7,1},{9,15},{11,13},{13,11},{15,9},{17,23},{19,... | collective-permute-start | bytes 184328 | tf_op jit(solution)/shard_map/ppermute | solution.py:29
  9.6 0.7 %collective-permute-start.5 = (bf16[48,640]{1,0:T(8,128)(2,1)S(1)}, bf16[48,640]{1,0:T(8,128)(2,1)S(1)}, u32[]{:S(2)}, u32[]{:S(2)}) collective-permute-start(bf16[48,640]{1,0:T(8,128)(2,1)S(1)} %get-tuple-element.60), channel_id=1, source_target_pairs={{1,5},{3,7},{5,1},{7,3},{9,13},{11,15},{13,9},{15,11},{17,21},{19,... | collective-permute-start | bytes 184328 | tf_op jit(solution)/shard_map/ppermute | solution.py:29
  11.1 0.7 %collective-permute-start.7 = (bf16[48,640]{1,0:T(8,128)(2,1)S(1)}, bf16[48,640]{1,0:T(8,128)(2,1)S(1)}, u32[]{:S(2)}, u32[]{:S(2)}) collective-permute-start(bf16[48,640]{1,0:T(8,128)(2,1)S(1)} %get-tuple-element.62), channel_id=1, source_target_pairs={{1,25},{9,17},{17,9},{25,1},{3,27},{11,19},{19,11},{27,3},{5,29},{... | collective-permute-start | bytes 184328 | tf_op jit(solution)/shard_map/ppermute | solution.py:29
  13.2 1.3 %collective-permute-start.9 = (bf16[4,24,640]{2,1,0:T(8,128)(2,1)S(1)}, bf16[4,24,640]{2,1,0:T(8,128)(2,1)S(1)}, u32[]{:S(2)}, u32[]{:S(2)}) collective-permute-start(bf16[4,24,640]{2,1,0:T(8,128)(2,1)S(1)} %get-tuple-element.66), channel_id=1, source_target_pairs={{1,0},{3,2},{5,4},{7,6},{9,8},{11,10},{13,12},{15,14},{17,16},{19,... | collective-permute-start | bytes 368648 | tf_op jit(solution)/shard_map/ppermute | solution.py:23
  14.5 21.3 %collective-permute-done.9.given_ref = bf16[4,24,640]{2,1,0:T(8,128)(2,1)S(1)} collective-permute-done((bf16[4,24,640]{2,1,0:T(8,128)(2,1)S(1)}, bf16[4,24,640]{2,1,0:T(8,128)(2,1)S(1)}, u32[]{:S(2)}, u32[]{:S(2)}) %collective-permute-start.9) | collective-permute-done | bytes 122912 | tf_op jit(solution)/shard_map/ppermute | solution.py:23
  35.9 1.6 %collective-permute-start.13 = (bf16[4,24,512]{2,1,0:T(8,128)(2,1)S(1)}, bf16[4,24,512]{2,1,0:T(8,128)(2,1)S(1)}, u32[]{:S(2)}, u32[]{:S(2)}) collective-permute-start(bf16[4,24,512]{2,1,0:T(8,128)(2,1)S(1)} %get-tuple-element.67), channel_id=1, source_target_pairs={{0,6},{2,4},{4,2},{6,0},{1,7},{3,5},{5,3},{7,1},{8,14},{10,12},{12... | collective-permute-start | bytes 294920 | tf_op jit(solution)/shard_map/ppermute | solution.py:19
  37.9 1.5 %collective-permute-start.10 = (bf16[4,24,512]{2,1,0:T(8,128)(2,1)S(1)}, bf16[4,24,512]{2,1,0:T(8,128)(2,1)S(1)}, u32[]{:S(2)}, u32[]{:S(2)}) collective-permute-start(bf16[4,24,512]{2,1,0:T(8,128)(2,1)S(1)} %get-tuple-element.67), channel_id=1, source_target_pairs={{0,2},{2,0},{4,6},{6,4},{1,3},{3,1},{5,7},{7,5},{8,10},{10,8},{12,... | collective-permute-start | bytes 294920 | tf_op jit(solution)/shard_map/ppermute | solution.py:19
  39.9 2.5 %collective-permute-done.13.block_ref = bf16[4,24,512]{2,1,0:T(8,128)(2,1)S(1)} collective-permute-done((bf16[4,24,512]{2,1,0:T(8,128)(2,1)S(1)}, bf16[4,24,512]{2,1,0:T(8,128)(2,1)S(1)}, u32[]{:S(2)}, u32[]{:S(2)}) %collective-permute-start.13) | collective-permute-done | bytes 98336 | tf_op jit(solution)/shard_map/ppermute | solution.py:19
  42.7 1.1 %collective-permute-done.12.block_ref = bf16[4,24,512]{2,1,0:T(8,128)(2,1)S(1)} collective-permute-done((bf16[4,24,512]{2,1,0:T(8,128)(2,1)S(1)}, bf16[4,24,512]{2,1,0:T(8,128)(2,1)S(1)}, u32[]{:S(2)}, u32[]{:S(2)}) %collective-permute-start.12) | collective-permute-done | bytes 98336 | tf_op jit(solution)/shard_map/ppermute | solution.py:19
  44.6 0.7 %shard_map.177 = (f32[24,2048]{1,0:T(8,128)S(1)}, bf16[24,2048]{1,0:T(8,128)(2,1)S(1)}, bf16[24,2048]{1,0:T(8,128)(2,1)S(1)}, bf16[24,2048]{1,0:T(8,128)(2,1)S(1)}) custom-call(f32[96,768]{1,0:T(8,128)S(1)} %get-tuple-element.77.projected_ref, f32[96,1]{1,0:T(8,128)S(1)} %get-tuple-element.78.squares_ref, f32[96,1]{1,0:T(8,128)S(1)} %get-tuple-element.79.route_ref, ...), custom_call_target="tpu_custom_call" | custom-call | tf_op jit(solution)/shard_map/pallas_call | solution.py:37
  45.3 1.6 %collective-permute-start.15 = (bf16[24,2048]{1,0:T(8,128)(2,1)S(1)}, bf16[24,2048]{1,0:T(8,128)(2,1)S(1)}, u32[]{:S(2)}, u32[]{:S(2)}) collective-permute-start(bf16[24,2048]{1,0:T(8,128)(2,1)S(1)} %get-tuple-element.82), channel_id=1, source_target_pairs={{0,6},{2,4},{4,2},{6,0},{1,7},{3,5},{5,3},{7,1},{8,14},{10,12},{12... | collective-permute-start | bytes 294920 | tf_op jit(solution)/shard_map/ppermute | solution.py:19
  47.3 1.5 %collective-permute-start.17 = (bf16[24,2048]{1,0:T(8,128)(2,1)S(1)}, bf16[24,2048]{1,0:T(8,128)(2,1)S(1)}, u32[]{:S(2)}, u32[]{:S(2)}) collective-permute-start(bf16[24,2048]{1,0:T(8,128)(2,1)S(1)} %get-tuple-element.84), channel_id=1, source_target_pairs={{0,2},{2,0},{4,6},{6,4},{1,3},{3,1},{5,7},{7,5},{8,10},{10,8},{12,... | collective-permute-start | bytes 294920 | tf_op jit(solution)/shard_map/ppermute | solution.py:19
  48.8 2.8 %collective-permute-done.15.refs_0_ = bf16[24,2048]{1,0:T(8,128)(2,1)S(1)} collective-permute-done((bf16[24,2048]{1,0:T(8,128)(2,1)S(1)}, bf16[24,2048]{1,0:T(8,128)(2,1)S(1)}, u32[]{:S(2)}, u32[]{:S(2)}) %collective-permute-start.15) | collective-permute-done | bytes 98336 | tf_op jit(solution)/shard_map/ppermute | solution.py:19
  51.6 1.4 %collective-permute-done.16.refs_1_ = bf16[24,2048]{1,0:T(8,128)(2,1)S(1)} collective-permute-done((bf16[24,2048]{1,0:T(8,128)(2,1)S(1)}, bf16[24,2048]{1,0:T(8,128)(2,1)S(1)}, u32[]{:S(2)}, u32[]{:S(2)}) %collective-permute-start.16) | collective-permute-done | bytes 98336 | tf_op jit(solution)/shard_map/ppermute | solution.py:19
  53.2 1.2 %collective-permute-done.18.other_ref = bf16[24,1024]{1,0:T(8,128)(2,1)S(1)} collective-permute-done((bf16[24,1024]{1,0:T(8,128)(2,1)S(1)}, bf16[24,1024]{1,0:T(8,128)(2,1)S(1)}, u32[]{:S(2)}, u32[]{:S(2)}) %collective-permute-start.18) | collective-permute-done | bytes 49184 | tf_op jit(solution)/shard_map/ppermute | solution.py:19
  54.6 2.4 %collective-permute-start.19 = (bf16[24,512]{1,0:T(8,128)(2,1)S(1)}, bf16[24,512]{1,0:T(8,128)(2,1)S(1)}, u32[]{:S(2)}, u32[]{:S(2)}) collective-permute-start(bf16[24,512]{1,0:T(8,128)(2,1)S(1)} %get-tuple-element.89), channel_id=1, source_target_pairs={{0,24},{8,16},{16,8},{24,0},{1,25},{9,17},{17,9},{25,1},{2,26},{10... | collective-permute-start | bytes 73736 | tf_op jit(solution)/shard_map/ppermute | solution.py:19
  57.4 1.7 %collective-permute-start.21 = (bf16[24,512]{1,0:T(8,128)(2,1)S(1)}, bf16[24,512]{1,0:T(8,128)(2,1)S(1)}, u32[]{:S(2)}, u32[]{:S(2)}) collective-permute-start(bf16[24,512]{1,0:T(8,128)(2,1)S(1)} %get-tuple-element.91), channel_id=1, source_target_pairs={{0,8},{8,0},{16,24},{24,16},{1,9},{9,1},{17,25},{25,17},{2,10},{10... | collective-permute-start | bytes 73736 | tf_op jit(solution)/shard_map/ppermute | solution.py:19
  59.1 1.3 %collective-permute-done.19.refs_0_ = bf16[24,512]{1,0:T(8,128)(2,1)S(1)} collective-permute-done((bf16[24,512]{1,0:T(8,128)(2,1)S(1)}, bf16[24,512]{1,0:T(8,128)(2,1)S(1)}, u32[]{:S(2)}, u32[]{:S(2)}) %collective-permute-start.19) | collective-permute-done | bytes 24608 | tf_op jit(solution)/shard_map/ppermute | solution.py:19
  60.4 1.4 %collective-permute-done.20.refs_1_ = bf16[24,512]{1,0:T(8,128)(2,1)S(1)} collective-permute-done((bf16[24,512]{1,0:T(8,128)(2,1)S(1)}, bf16[24,512]{1,0:T(8,128)(2,1)S(1)}, u32[]{:S(2)}, u32[]{:S(2)}) %collective-permute-start.20) | collective-permute-done | bytes 24608 | tf_op jit(solution)/shard_map/ppermute | solution.py:19
  (47 shorter events, 7.2 us)
Async XLA Ops:
  0.0 3.3 %collective-permute-start = (bf16[832,256]{1,0:T(8,128)(2,1)}, bf16[832,256]{1,0:T(8,128)(2,1)S(1)}, u32[]{:S(2)}, u32[]{:S(2)}) collective-permute-start(bf16[832,256]{1,0:T(8,128)(2,1)} %bitcast.23), channel_id=1, source_target_pairs={{0,1},{1,0},{2,3},{3,2},{4,5},{5,4},{6,7},{7,6},{8,9},{9,8},{10,11... | collective-permute-start | bytes 1277960 | tf_op jit(solution)/shard_map/ppermute | solution.py:19
  1.2 2.0 %collective-permute-start.1 = (s32[1,128]{1,0:T(1,128)S(1)}, s32[1,128]{1,0:T(1,128)S(1)}, u32[]{:S(2)}, u32[]{:S(2)}) collective-permute-start(s32[1,128]{1,0:T(1,128)S(1)} %pad_bitcast_fusion.own_ints_ref), channel_id=1, source_target_pairs={{0,1},{1,0},{2,3},{3,2},{4,5},{5,4},{6,7},{7,6},{8,9},{9,8},{10,11... | collective-permute-start | bytes 1544 | tf_op jit(solution)/shard_map/ppermute | solution.py:19
  3.3 5.5 %copy-start.1 = (bf16[1,192,2048]{2,1,0:T(8,128)(2,1)S(1)}, bf16[1,192,2048]{2,1,0:T(8,128)(2,1)}, u32[]{:S(2)}) copy-start(bf16[1,192,2048]{2,1,0:T(8,128)(2,1)} %param.30) | copy-start | bytes 2359300
  3.3 36.1 %copy-start.2 = (f32[2048]{0:T(1024)S(1)}, f32[2048]{0:T(1024)}, u32[]{:S(2)}) copy-start(f32[2048]{0:T(1024)} %param.25) | copy-start | bytes 24580
  4.9 3.5 %collective-permute-start.2 = (bf16[48,2560]{1,0:T(8,128)(2,1)S(1)}, bf16[48,2560]{1,0:T(8,128)(2,1)S(1)}, u32[]{:S(2)}, u32[]{:S(2)}) collective-permute-start(bf16[48,2560]{1,0:T(8,128)(2,1)S(1)} %get-tuple-element.56), channel_id=1, source_target_pairs={{0,1},{2,3},{4,5},{6,7},{8,9},{10,11},{12,13},{14,15},{16,17},{18,... | collective-permute-start | bytes 737288 | tf_op jit(solution)/shard_map/ppermute | solution.py:23
  8.4 31.0 %collective-permute-start.11 = (bf16[384,2048]{1,0:T(8,128)(2,1)S(1)}, bf16[384,2048]{1,0:T(8,128)(2,1)S(1)}, u32[]{:S(2)}, u32[]{:S(2)}) collective-permute-start(bf16[384,2048]{1,0:T(8,128)(2,1)S(1)} %bitcast.11), channel_id=1, source_target_pairs={{0,1},{1,0},{2,3},{3,2},{4,5},{5,4},{6,7},{7,6},{8,9},{9,8},{10,11... | collective-permute-start | bytes 4718600 | tf_op jit(solution)/shard_map/ppermute | solution.py:19
  8.8 35.8 %collective-permute-start.14 = (bf16[192,2048]{1,0:T(8,128)(2,1)S(1)}, bf16[192,2048]{1,0:T(8,128)(2,1)S(1)}, u32[]{:S(2)}, u32[]{:S(2)}) collective-permute-start(bf16[192,2048]{1,0:T(8,128)(2,1)S(1)} %bitcast.16), channel_id=1, source_target_pairs={{0,1},{1,0},{2,3},{3,2},{4,5},{5,4},{6,7},{7,6},{8,9},{9,8},{10,11... | collective-permute-start | bytes 2359304 | tf_op jit(solution)/shard_map/ppermute | solution.py:19
  9.0 2.0 %collective-permute-start.4 = (bf16[48,640]{1,0:T(8,128)(2,1)S(1)}, bf16[48,640]{1,0:T(8,128)(2,1)S(1)}, u32[]{:S(2)}, u32[]{:S(2)}) collective-permute-start(bf16[48,640]{1,0:T(8,128)(2,1)S(1)} %get-tuple-element.59), channel_id=1, source_target_pairs={{1,7},{3,5},{5,3},{7,1},{9,15},{11,13},{13,11},{15,9},{17,23},{19,... | collective-permute-start | bytes 184328 | tf_op jit(solution)/shard_map/ppermute | solution.py:29
  9.6 1.4 %collective-permute-start.5 = (bf16[48,640]{1,0:T(8,128)(2,1)S(1)}, bf16[48,640]{1,0:T(8,128)(2,1)S(1)}, u32[]{:S(2)}, u32[]{:S(2)}) collective-permute-start(bf16[48,640]{1,0:T(8,128)(2,1)S(1)} %get-tuple-element.60), channel_id=1, source_target_pairs={{1,5},{3,7},{5,1},{7,3},{9,13},{11,15},{13,9},{15,11},{17,21},{19,... | collective-permute-start | bytes 184328 | tf_op jit(solution)/shard_map/ppermute | solution.py:29
  10.3 0.7 %collective-permute-start.3 = (bf16[48,640]{1,0:T(8,128)(2,1)S(1)}, bf16[48,640]{1,0:T(8,128)(2,1)S(1)}, u32[]{:S(2)}, u32[]{:S(2)}) collective-permute-start(bf16[48,640]{1,0:T(8,128)(2,1)S(1)} %get-tuple-element.57), channel_id=1, source_target_pairs={{1,3},{3,1},{5,7},{7,5},{9,11},{11,9},{13,15},{15,13},{17,19},{19,... | collective-permute-start | bytes 184328 | tf_op jit(solution)/shard_map/ppermute | solution.py:29
  11.1 2.0 %collective-permute-start.7 = (bf16[48,640]{1,0:T(8,128)(2,1)S(1)}, bf16[48,640]{1,0:T(8,128)(2,1)S(1)}, u32[]{:S(2)}, u32[]{:S(2)}) collective-permute-start(bf16[48,640]{1,0:T(8,128)(2,1)S(1)} %get-tuple-element.62), channel_id=1, source_target_pairs={{1,25},{9,17},{17,9},{25,1},{3,27},{11,19},{19,11},{27,3},{5,29},{... | collective-permute-start | bytes 184328 | tf_op jit(solution)/shard_map/ppermute | solution.py:29
  11.8 1.4 %collective-permute-start.6 = (bf16[48,640]{1,0:T(8,128)(2,1)S(1)}, bf16[48,640]{1,0:T(8,128)(2,1)S(1)}, u32[]{:S(2)}, u32[]{:S(2)}) collective-permute-start(bf16[48,640]{1,0:T(8,128)(2,1)S(1)} %get-tuple-element.61), channel_id=1, source_target_pairs={{1,17},{9,25},{17,1},{25,9},{3,19},{11,27},{19,3},{27,11},{5,21},{... | collective-permute-start | bytes 184328 | tf_op jit(solution)/shard_map/ppermute | solution.py:29
  12.4 0.7 %collective-permute-start.8 = (bf16[48,640]{1,0:T(8,128)(2,1)S(1)}, bf16[48,640]{1,0:T(8,128)(2,1)S(1)}, u32[]{:S(2)}, u32[]{:S(2)}) collective-permute-start(bf16[48,640]{1,0:T(8,128)(2,1)S(1)} %get-tuple-element.63), channel_id=1, source_target_pairs={{1,9},{9,1},{17,25},{25,17},{3,11},{11,3},{19,27},{27,19},{5,13},{... | collective-permute-start | bytes 184328 | tf_op jit(solution)/shard_map/ppermute | solution.py:29
  13.2 22.6 %collective-permute-start.9 = (bf16[4,24,640]{2,1,0:T(8,128)(2,1)S(1)}, bf16[4,24,640]{2,1,0:T(8,128)(2,1)S(1)}, u32[]{:S(2)}, u32[]{:S(2)}) collective-permute-start(bf16[4,24,640]{2,1,0:T(8,128)(2,1)S(1)} %get-tuple-element.66), channel_id=1, source_target_pairs={{1,0},{3,2},{5,4},{7,6},{9,8},{11,10},{13,12},{15,14},{17,16},{19,... | collective-permute-start | bytes 368648 | tf_op jit(solution)/shard_map/ppermute | solution.py:23
  35.9 6.5 %collective-permute-start.13 = (bf16[4,24,512]{2,1,0:T(8,128)(2,1)S(1)}, bf16[4,24,512]{2,1,0:T(8,128)(2,1)S(1)}, u32[]{:S(2)}, u32[]{:S(2)}) collective-permute-start(bf16[4,24,512]{2,1,0:T(8,128)(2,1)S(1)} %get-tuple-element.67), channel_id=1, source_target_pairs={{0,6},{2,4},{4,2},{6,0},{1,7},{3,5},{5,3},{7,1},{8,14},{10,12},{12... | collective-permute-start | bytes 294920 | tf_op jit(solution)/shard_map/ppermute | solution.py:19
  37.4 6.4 %collective-permute-start.12 = (bf16[4,24,512]{2,1,0:T(8,128)(2,1)S(1)}, bf16[4,24,512]{2,1,0:T(8,128)(2,1)S(1)}, u32[]{:S(2)}, u32[]{:S(2)}) collective-permute-start(bf16[4,24,512]{2,1,0:T(8,128)(2,1)S(1)} %get-tuple-element.67), channel_id=1, source_target_pairs={{0,4},{2,6},{4,0},{6,2},{1,5},{3,7},{5,1},{7,3},{8,12},{10,14},{12... | collective-permute-start | bytes 294920 | tf_op jit(solution)/shard_map/ppermute | solution.py:19
  37.9 6.2 %collective-permute-start.10 = (bf16[4,24,512]{2,1,0:T(8,128)(2,1)S(1)}, bf16[4,24,512]{2,1,0:T(8,128)(2,1)S(1)}, u32[]{:S(2)}, u32[]{:S(2)}) collective-permute-start(bf16[4,24,512]{2,1,0:T(8,128)(2,1)S(1)} %get-tuple-element.67), channel_id=1, source_target_pairs={{0,2},{2,0},{4,6},{6,4},{1,3},{3,1},{5,7},{7,5},{8,10},{10,8},{12,... | collective-permute-start | bytes 294920 | tf_op jit(solution)/shard_map/ppermute | solution.py:19
  45.3 6.4 %collective-permute-start.15 = (bf16[24,2048]{1,0:T(8,128)(2,1)S(1)}, bf16[24,2048]{1,0:T(8,128)(2,1)S(1)}, u32[]{:S(2)}, u32[]{:S(2)}) collective-permute-start(bf16[24,2048]{1,0:T(8,128)(2,1)S(1)} %get-tuple-element.82), channel_id=1, source_target_pairs={{0,6},{2,4},{4,2},{6,0},{1,7},{3,5},{5,3},{7,1},{8,14},{10,12},{12... | collective-permute-start | bytes 294920 | tf_op jit(solution)/shard_map/ppermute | solution.py:19
  46.8 6.2 %collective-permute-start.16 = (bf16[24,2048]{1,0:T(8,128)(2,1)S(1)}, bf16[24,2048]{1,0:T(8,128)(2,1)S(1)}, u32[]{:S(2)}, u32[]{:S(2)}) collective-permute-start(bf16[24,2048]{1,0:T(8,128)(2,1)S(1)} %get-tuple-element.83), channel_id=1, source_target_pairs={{0,4},{2,6},{4,0},{6,2},{1,5},{3,7},{5,1},{7,3},{8,12},{10,14},{12... | collective-permute-start | bytes 294920 | tf_op jit(solution)/shard_map/ppermute | solution.py:19
  47.3 5.7 %collective-permute-start.17 = (bf16[24,2048]{1,0:T(8,128)(2,1)S(1)}, bf16[24,2048]{1,0:T(8,128)(2,1)S(1)}, u32[]{:S(2)}, u32[]{:S(2)}) collective-permute-start(bf16[24,2048]{1,0:T(8,128)(2,1)S(1)} %get-tuple-element.84), channel_id=1, source_target_pairs={{0,2},{2,0},{4,6},{6,4},{1,3},{3,1},{5,7},{7,5},{8,10},{10,8},{12,... | collective-permute-start | bytes 294920 | tf_op jit(solution)/shard_map/ppermute | solution.py:19
  53.1 1.3 %collective-permute-start.18 = (bf16[24,1024]{1,0:T(8,128)(2,1)S(1)}, bf16[24,1024]{1,0:T(8,128)(2,1)S(1)}, u32[]{:S(2)}, u32[]{:S(2)}) collective-permute-start(bf16[24,1024]{1,0:T(8,128)(2,1)S(1)} %get-tuple-element.87), channel_id=1, source_target_pairs={{0,1},{1,0},{2,3},{3,2},{4,5},{5,4},{6,7},{7,6},{8,9},{9,8},{10,11... | collective-permute-start | bytes 147464 | tf_op jit(solution)/shard_map/ppermute | solution.py:19
  54.6 5.8 %collective-permute-start.19 = (bf16[24,512]{1,0:T(8,128)(2,1)S(1)}, bf16[24,512]{1,0:T(8,128)(2,1)S(1)}, u32[]{:S(2)}, u32[]{:S(2)}) collective-permute-start(bf16[24,512]{1,0:T(8,128)(2,1)S(1)} %get-tuple-element.89), channel_id=1, source_target_pairs={{0,24},{8,16},{16,8},{24,0},{1,25},{9,17},{17,9},{25,1},{2,26},{10... | collective-permute-start | bytes 73736 | tf_op jit(solution)/shard_map/ppermute | solution.py:19
  57.0 4.7 %collective-permute-start.20 = (bf16[24,512]{1,0:T(8,128)(2,1)S(1)}, bf16[24,512]{1,0:T(8,128)(2,1)S(1)}, u32[]{:S(2)}, u32[]{:S(2)}) collective-permute-start(bf16[24,512]{1,0:T(8,128)(2,1)S(1)} %get-tuple-element.90), channel_id=1, source_target_pairs={{0,16},{8,24},{16,0},{24,8},{1,17},{9,25},{17,1},{25,9},{2,18},{10... | collective-permute-start | bytes 73736 | tf_op jit(solution)/shard_map/ppermute | solution.py:19
  57.4 4.4 %collective-permute-start.21 = (bf16[24,512]{1,0:T(8,128)(2,1)S(1)}, bf16[24,512]{1,0:T(8,128)(2,1)S(1)}, u32[]{:S(2)}, u32[]{:S(2)}) collective-permute-start(bf16[24,512]{1,0:T(8,128)(2,1)S(1)} %get-tuple-element.91), channel_id=1, source_target_pairs={{0,8},{8,0},{16,24},{24,16},{1,9},{9,1},{17,25},{25,17},{2,10},{10... | collective-permute-start | bytes 73736 | tf_op jit(solution)/shard_map/ppermute | solution.py:19
  (1 other events, 5.1 us)

commit v11 on v9

--- a/solution.py
+++ b/solution.py
@@ -17,6 +17,18 @@
 def send(value, axes, step):
     size = lax.axis_size(axes)
     return lax.ppermute(value, axes, [(i, i ^ step) for i in range(size)])
+
+
+def cross(value, axis, step):
+    size, pools = lax.axis_size(axis), lax.axis_size("pool")
+    pairs = [
+        (i * pools + p, (i ^ step) * pools + (p ^ (step & 1))) for i in range(size) for p in range(pools)
+    ]
+    return lax.ppermute(value, (axis, "pool"), pairs)
+
+
+def part_taken():
+    return lax.axis_index("pool") ^ (lax.axis_index("req") & 1)
 
 
 def dot(a, b, contract=((1,), (0,))):
@@ -50,8 +62,8 @@
     sources, placed_ref, targets = refs[:count], refs[count], refs[count + 1 : -1]
     residual_ref, choice_ref, route_ref = targets[7:]
     semaphores = refs[-1]
-    head, mine = lax.axis_index("head"), lax.axis_index("pool")
-    first = jnp.where(mine == 0, 1.0, 0.0)
+    head, mine = lax.axis_index("head"), part_taken()
+    first = jnp.where(lax.axis_index("pool") == 0, 1.0, 0.0)
     picked = {5: mine, 6: head}
     copies = []
     for i in range(count):
@@ -204,10 +216,9 @@
         first_ref[step] = part[:, : first_ref.shape[2]]
 
 
-def project_kernel(step, planes, block_ref, own_up_ref, other_up_ref, gain_ref, *refs):
+def projection(step, block_ref, own_up_ref, other_up_ref, gain_ref):
     head = lax.axis_index("head")
-    plane_rows = block_ref.shape[1]
-    rows = planes * plane_rows
+    rows = block_ref.shape[0] * block_ref.shape[1]
     columns = gain_ref.shape[1] // lax.axis_size("head")
     units = own_up_ref.shape[0] // 2
     at = pl.ds(pl.multiple_of((head ^ step) * columns, LANES), columns)
@@ -218,7 +229,13 @@
         axis=0,
     )
     projected = dot(scaled, weights, ((1,), (1,)))
-    squares = jnp.sum(block * block, axis=1, keepdims=True)
+    return block, projected, jnp.sum(block * block, axis=1, keepdims=True)
+
+
+def project_kernel(step, planes, block_ref, own_up_ref, other_up_ref, gain_ref, *refs):
+    block, projected, squares = projection(step, block_ref, own_up_ref, other_up_ref, gain_ref)
+    plane_rows = block_ref.shape[1]
+    rows, columns = block.shape
     if step:
         before_ref, before_squares_ref, projected_ref, squares_ref = refs
         projected_ref[...] = before_ref[...] + projected
@@ -238,12 +255,15 @@
     own_ref[...] = dot(order_ref[...], jnp.where(line < plane_rows, block, 0.0).astype(BF16))
 
 
-def expert_kernel(projected_ref, squares_ref, route_ref, own_ref, own_down_ref, other_down_ref, order_ref, *outs):
+def expert_kernel(block_ref, own_up_ref, other_up_ref, gain_ref, projected_ref, squares_ref, route_ref, own_ref, own_down_ref, other_down_ref, order_ref, *outs):
     heads = len(outs)
+    _, projected, squares = projection(1, block_ref, own_up_ref, other_up_ref, gain_ref)
+    projected = projected + projected_ref[...]
+    squares = squares + squares_ref[...]
     head = lax.axis_index("head")
     rows, columns = own_ref.shape
     units = own_down_ref.shape[0]
-    projected = projected_ref[...] * lax.rsqrt(squares_ref[...] / (heads * columns) + 1e-06)
+    projected = projected * lax.rsqrt(squares / (heads * columns) + 1e-06)
     gate, up = projected[:, : 2 * units], projected[:, 2 * units :]
     activated = (gate / (1.0 + jnp.exp(-gate)) * up * route_ref[...]).astype(BF16)
     activated = dot(order_ref[...], activated).astype(BF16)
@@ -268,7 +288,7 @@
 
 
 def spread_kernel(own_ref, other_ref, order_ref, *outs):
-    mine = lax.axis_index("pool")
+    mine = part_taken()
     own, other = own_ref[...].astype(F32), other_ref[...].astype(F32)
     both = jnp.concatenate([jnp.where(mine == 0, own, other), jnp.where(mine == 0, other, own)], axis=0)
     both = both.astype(BF16)
@@ -414,7 +434,7 @@
         held(send(pieces[1], "head", 1), total),
     )
 
-    arrived = [send(hidden[step], "req", step) for step in reversed(range(1, planes))] + [hidden[0]]
+    arrived = [cross(hidden[step], "req", step) for step in reversed(range(1, planes))] + [hidden[0]]
     marks = []
     for part_arrived in arrived[:-2]:
         marks = [kernel_call(mark_kernel, shape(16, LANES), held(part_arrived, *marks))]
@@ -431,7 +451,7 @@
         sums + [shape(total, 1, dtype=F32), shape(total, columns, dtype=F32)],
         held(plane_blocks, *weights, head_order, down_weight),
     )
-    for step in reversed(range(1, heads)):
+    for step in reversed(range(2, heads)):
         state = kernel_call(
             functools.partial(project_kernel, step, planes),
             sums,
@@ -441,7 +461,7 @@
     pieces = kernel_call(
         expert_kernel,
         [shape(planes * part, width, dtype=F32)] + [piece] * (heads - 1),
-        held(*state, route, own, down_weight, other_down, head_order),
+        held(send(sent, "head", 1), *weights, *state, route, own, down_weight, other_down, head_order),
     )
     arrived = [send(pieces[step], "head", step) for step in reversed(range(1, heads))] + [pieces[0]]
     own, other = kernel_call(
@@ -451,7 +471,12 @@
     piece = shape(2 * rows_here, width // pools // 2)
     pieces = kernel_call(spread_kernel, [piece] * planes, held(own, other, plane_order))
     arrived = [send(pieces[step], "req", step) for step in reversed(range(1, planes))] + [pieces[0]]
-    return kernel_call(total_kernel, shape(rows_here, width // pools), held(*arrived))
+    return pl.pallas_call(
+        total_kernel,
+        out_shape=shape(rows_here, width // pools),
+        in_specs=[pl.BlockSpec(memory_space=pltpu.VMEM)] * planes,
+        out_specs=pl.BlockSpec(memory_space=pltpu.VMEM),
+    )(*held(*arrived))
 
 
 def solution(mesh):

time: 48.2 us -> 49.2 us (1.021)
  waiting for transfers between devices: 18.2 us -> 19.8 us
  local copies, waits for them, and re-layouts: 0.64 us -> 0.02 us
  starting transfers between devices: 22.2 us -> 21.6 us
  Pallas kernels: 6.09 us -> 6.62 us
    ppermute x21 -> x18, starting transfers between devices: 22.2 us -> 17.7 us  [send(): return lax.ppermute(value, axes, [(i, i ^ step) for i in range(size)])]
    ppermute x0 -> x3, starting transfers between devices: none -> 3.89 us  [cross(): return lax.ppermute(value, (axis, 'pool'), pairs)]
    ppermute x0 -> x3, waiting for transfers between devices: none -> 2.94 us  [cross(): return lax.ppermute(value, (axis, 'pool'), pairs)]
    ppermute x21 -> x18, waiting for transfers between devices: 18.2 us -> 16.9 us  [send(): return lax.ppermute(value, axes, [(i, i ^ step) for i in range(size)])]
    pallas_call x0 -> x1, Pallas kernels: none -> 0.63 us  [local(): pl.pallas_call(total_kernel, out_shape=shape(rows_here, width // pools),...]
    unnamed x7 -> x6, local copies, waits for them, and re-layouts: 0.64 us -> 0.02 us
    pallas_call x17 -> x15, Pallas kernels: 6.09 us -> 5.99 us  [kernel_call(): pl.pallas_call(body, out_shape=jax.tree.map(lambda out: pltpu.VMEM(out.sh...]
  transfers between devices with their start and end apart: 21 -> 21, of which waited for: 15 -> 13; matrix products, arithmetic and copies ran while one was open for 2% -> 2% of each run, Pallas kernels for 7% -> 7%
where the time goes in v11:
time: 49.2 us; the launch traced here: 49 us
  starting transfers between devices  21.6 us (44%)
  waiting for transfers between devices  19.8 us (40%)
  Pallas kernels  6.62 us (13%)
  other arithmetic  0.78 us (2%)
    ppermute x18, starting transfers between devices, send(): return lax.ppermute(value, axes, [(i, i ^ step) for i in range(size)])  17.7 us
    ppermute x18, waiting for transfers between devices, send(): return lax.ppermute(value, axes, [(i, i ^ step) for i in range(size)])  16.9 us
    pallas_call x15, Pallas kernels, kernel_call(): pl.pallas_call(body, out_shape=jax.tree.map(lambda out: pltpu.VMEM(out.sh...  5.99 us
    ppermute x3, starting transfers between devices, cross(): return lax.ppermute(value, (axis, 'pool'), pairs)  3.89 us
    ppermute x3, waiting for transfers between devices, cross(): return lax.ppermute(value, (axis, 'pool'), pairs)  2.94 us
  transfers between devices with their start and end apart: 21, of which 13 were waited for; matrix products, arithmetic and copies ran while one was open for 2% of the time, Pallas kernels for 7%

profile of v11, /device:TPU:0, one launch (start us, length us, event | category | flops | bytes accessed | tf_op | source)
XLA Modules:
  0.0 49.0 jit_solution(7932896087637459733)
XLA Ops:
  1.3 1.9 %shard_map.163 = (bf16[48,2560]{1,0:T(8,128)(2,1)S(1)}, bf16[832,256]{1,0:T(8,128)(2,1)S(1)}, bf16[48,1024]{1,0:T(8,128)(2,1)S(1)}, bf16[512,2048]{1,0:T(8,128)(...) custom-call(bf16[832,256]{1,0:T(8,128)(2,1)} %bitcast.24, ...), custom_call_target="tpu_custom_call" | custom-call | tf_op jit(solution)/shard_map/pallas_call | solution.py:39
  3.3 1.6 %shard_map.164 = (f32[24,2560]{1,0:T(8,128)S(1)}, bf16[24,2560]{1,0:T(8,128)(2,1)S(1)}) custom-call(bf16[48,1024]{1,0:T(8,128)(2,1)S(1)} %get-tuple-element.45.q_ref, bf16[48,2,256]{2,1,0:T(2,128)(2,1)S(1)} %get-tuple-element.46.new_ref, bf16[832,256]{1,0:T(8,128)(2,1)S(1)} %get-tuple-element.47.own_ref, ...), custom_call_target="tpu_custom_call" | custom-call | tf_op jit(solution)/shard_map/pallas_call | solution.py:39
  6.9 3.9 %collective-permute-start.4 = (bf16[24,640]{1,0:T(8,128)(2,1)S(1)}, bf16[24,640]{1,0:T(8,128)(2,1)S(1)}, u32[]{:S(2)}, u32[]{:S(2)}) collective-permute-start(bf16[24,640]{1,0:T(8,128)(2,1)S(1)} %get-tuple-element.55), channel_id=1, source_target_pairs={{0,6},{2,4},{4,2},{6,0},{1,7},{3,5},{5,3},{7,1},{8,14},{10,12},{12... | collective-permute-start | bytes 92168 | tf_op jit(solution)/shard_map/ppermute | solution.py:19
  11.4 1.2 %collective-permute-done.4.part_ref = bf16[24,640]{1,0:T(8,128)(2,1)S(1)} collective-permute-done((bf16[24,640]{1,0:T(8,128)(2,1)S(1)}, bf16[24,640]{1,0:T(8,128)(2,1)S(1)}, u32[]{:S(2)}, u32[]{:S(2)}) %collective-permute-start.4) | collective-permute-done | bytes 30752 | tf_op jit(solution)/shard_map/ppermute | solution.py:19
  12.7 2.0 %collective-permute-done.5.part_ref = bf16[24,640]{1,0:T(8,128)(2,1)S(1)} collective-permute-done((bf16[24,640]{1,0:T(8,128)(2,1)S(1)}, bf16[24,640]{1,0:T(8,128)(2,1)S(1)}, u32[]{:S(2)}, u32[]{:S(2)}) %collective-permute-start.5) | collective-permute-done | bytes 30752 | tf_op jit(solution)/shard_map/ppermute | solution.py:19
  15.2 1.7 %collective-permute-start.7 = (bf16[24,640]{1,0:T(8,128)(2,1)S(1)}, bf16[24,640]{1,0:T(8,128)(2,1)S(1)}, u32[]{:S(2)}, u32[]{:S(2)}) collective-permute-start(bf16[24,640]{1,0:T(8,128)(2,1)S(1)} %get-tuple-element.58), channel_id=1, source_target_pairs={{0,25},{1,24},{8,17},{9,16},{16,9},{17,8},{24,1},{25,0},{2,27},{3,... | collective-permute-start | bytes 92168 | tf_op jit(solution)/shard_map/ppermute | solution.py:27
  16.9 1.0 %collective-permute-start.6 = (bf16[24,640]{1,0:T(8,128)(2,1)S(1)}, bf16[24,640]{1,0:T(8,128)(2,1)S(1)}, u32[]{:S(2)}, u32[]{:S(2)}) collective-permute-start(bf16[24,640]{1,0:T(8,128)(2,1)S(1)} %get-tuple-element.57), channel_id=1, source_target_pairs={{0,16},{1,17},{8,24},{9,25},{16,0},{17,1},{24,8},{25,9},{2,18},{3,... | collective-permute-start | bytes 92168 | tf_op jit(solution)/shard_map/ppermute | solution.py:27
  18.0 1.2 %collective-permute-start.8 = (bf16[24,640]{1,0:T(8,128)(2,1)S(1)}, bf16[24,640]{1,0:T(8,128)(2,1)S(1)}, u32[]{:S(2)}, u32[]{:S(2)}) collective-permute-start(bf16[24,640]{1,0:T(8,128)(2,1)S(1)} %get-tuple-element.59), channel_id=1, source_target_pairs={{0,9},{1,8},{8,1},{9,0},{16,25},{17,24},{24,17},{25,16},{2,11},{3,... | collective-permute-start | bytes 92168 | tf_op jit(solution)/shard_map/ppermute | solution.py:27
  19.1 1.3 %collective-permute-done.7.part_ref.refs_1_ = bf16[24,640]{1,0:T(8,128)(2,1)S(1)} collective-permute-done((bf16[24,640]{1,0:T(8,128)(2,1)S(1)}, bf16[24,640]{1,0:T(8,128)(2,1)S(1)}, u32[]{:S(2)}, u32[]{:S(2)}) %collective-permute-start.7) | collective-permute-done | bytes 30752 | tf_op jit(solution)/shard_map/ppermute | solution.py:27
  20.4 1.7 %collective-permute-done.6.part_ref.refs_2_ = bf16[24,640]{1,0:T(8,128)(2,1)S(1)} collective-permute-done((bf16[24,640]{1,0:T(8,128)(2,1)S(1)}, bf16[24,640]{1,0:T(8,128)(2,1)S(1)}, u32[]{:S(2)}, u32[]{:S(2)}) %collective-permute-start.6) | collective-permute-done | bytes 30752 | tf_op jit(solution)/shard_map/ppermute | solution.py:27
  22.1 1.6 %collective-permute-start.12 = (bf16[4,24,512]{2,1,0:T(8,128)(2,1)S(1)}, bf16[4,24,512]{2,1,0:T(8,128)(2,1)S(1)}, u32[]{:S(2)}, u32[]{:S(2)}) collective-permute-start(bf16[4,24,512]{2,1,0:T(8,128)(2,1)S(1)} %get-tuple-element.61), channel_id=1, source_target_pairs={{0,6},{2,4},{4,2},{6,0},{1,7},{3,5},{5,3},{7,1},{8,14},{10,12},{12... | collective-permute-start | bytes 294920 | tf_op jit(solution)/shard_map/ppermute | solution.py:19
  24.2 1.4 %collective-permute-start.9 = (bf16[4,24,512]{2,1,0:T(8,128)(2,1)S(1)}, bf16[4,24,512]{2,1,0:T(8,128)(2,1)S(1)}, u32[]{:S(2)}, u32[]{:S(2)}) collective-permute-start(bf16[4,24,512]{2,1,0:T(8,128)(2,1)S(1)} %get-tuple-element.61), channel_id=1, source_target_pairs={{0,2},{2,0},{4,6},{6,4},{1,3},{3,1},{5,7},{7,5},{8,10},{10,8},{12,... | collective-permute-start | bytes 294920 | tf_op jit(solution)/shard_map/ppermute | solution.py:19
  26.1 2.5 %collective-permute-done.12.block_ref = bf16[4,24,512]{2,1,0:T(8,128)(2,1)S(1)} collective-permute-done((bf16[4,24,512]{2,1,0:T(8,128)(2,1)S(1)}, bf16[4,24,512]{2,1,0:T(8,128)(2,1)S(1)}, u32[]{:S(2)}, u32[]{:S(2)}) %collective-permute-start.12) | collective-permute-done | bytes 98336 | tf_op jit(solution)/shard_map/ppermute | solution.py:19
  29.0 1.4 %collective-permute-done.11.block_ref = bf16[4,24,512]{2,1,0:T(8,128)(2,1)S(1)} collective-permute-done((bf16[4,24,512]{2,1,0:T(8,128)(2,1)S(1)}, bf16[4,24,512]{2,1,0:T(8,128)(2,1)S(1)}, u32[]{:S(2)}, u32[]{:S(2)}) %collective-permute-start.11) | collective-permute-done | bytes 98336 | tf_op jit(solution)/shard_map/ppermute | solution.py:19
  30.9 1.0 %shard_map.175 = (f32[24,2048]{1,0:T(8,128)S(1)}, bf16[24,2048]{1,0:T(8,128)(2,1)S(1)}, bf16[24,2048]{1,0:T(8,128)(2,1)S(1)}, bf16[24,2048]{1,0:T(8,128)(2,1)S(1)}) custom-call(bf16[4,24,512]{2,1,0:T(8,128)(2,1)S(1)} %collective-permute-done.9.block_ref, bf16[384,2048]{1,0:T(8,128)(2,1)S(1)} %bitcast.15, ...), custom_call_target="tpu_custom_call" | custom-call | tf_op jit(solution)/shard_map/pallas_call | solution.py:39
  31.9 1.6 %collective-permute-start.14 = (bf16[24,2048]{1,0:T(8,128)(2,1)S(1)}, bf16[24,2048]{1,0:T(8,128)(2,1)S(1)}, u32[]{:S(2)}, u32[]{:S(2)}) collective-permute-start(bf16[24,2048]{1,0:T(8,128)(2,1)S(1)} %get-tuple-element.74), channel_id=1, source_target_pairs={{0,6},{2,4},{4,2},{6,0},{1,7},{3,5},{5,3},{7,1},{8,14},{10,12},{12... | collective-permute-start | bytes 294920 | tf_op jit(solution)/shard_map/ppermute | solution.py:19
  33.9 1.5 %collective-permute-start.16 = (bf16[24,2048]{1,0:T(8,128)(2,1)S(1)}, bf16[24,2048]{1,0:T(8,128)(2,1)S(1)}, u32[]{:S(2)}, u32[]{:S(2)}) collective-permute-start(bf16[24,2048]{1,0:T(8,128)(2,1)S(1)} %get-tuple-element.76), channel_id=1, source_target_pairs={{0,2},{2,0},{4,6},{6,4},{1,3},{3,1},{5,7},{7,5},{8,10},{10,8},{12,... | collective-permute-start | bytes 294920 | tf_op jit(solution)/shard_map/ppermute | solution.py:19
  35.4 2.8 %collective-permute-done.14.refs_0_ = bf16[24,2048]{1,0:T(8,128)(2,1)S(1)} collective-permute-done((bf16[24,2048]{1,0:T(8,128)(2,1)S(1)}, bf16[24,2048]{1,0:T(8,128)(2,1)S(1)}, u32[]{:S(2)}, u32[]{:S(2)}) %collective-permute-start.14) | collective-permute-done | bytes 98336 | tf_op jit(solution)/shard_map/ppermute | solution.py:19
  38.2 1.5 %collective-permute-done.15.refs_1_ = bf16[24,2048]{1,0:T(8,128)(2,1)S(1)} collective-permute-done((bf16[24,2048]{1,0:T(8,128)(2,1)S(1)}, bf16[24,2048]{1,0:T(8,128)(2,1)S(1)}, u32[]{:S(2)}, u32[]{:S(2)}) %collective-permute-start.15) | collective-permute-done | bytes 98336 | tf_op jit(solution)/shard_map/ppermute | solution.py:19
  39.8 1.2 %collective-permute-done.17.other_ref = bf16[24,1024]{1,0:T(8,128)(2,1)S(1)} collective-permute-done((bf16[24,1024]{1,0:T(8,128)(2,1)S(1)}, bf16[24,1024]{1,0:T(8,128)(2,1)S(1)}, u32[]{:S(2)}, u32[]{:S(2)}) %collective-permute-start.17) | collective-permute-done | bytes 49184 | tf_op jit(solution)/shard_map/ppermute | solution.py:19
  41.2 2.5 %collective-permute-start.18 = (bf16[24,512]{1,0:T(8,128)(2,1)S(1)}, bf16[24,512]{1,0:T(8,128)(2,1)S(1)}, u32[]{:S(2)}, u32[]{:S(2)}) collective-permute-start(bf16[24,512]{1,0:T(8,128)(2,1)S(1)} %get-tuple-element.81), channel_id=1, source_target_pairs={{0,24},{8,16},{16,8},{24,0},{1,25},{9,17},{17,9},{25,1},{2,26},{10... | collective-permute-start | bytes 73736 | tf_op jit(solution)/shard_map/ppermute | solution.py:19
  43.7 2.0 %collective-permute-start.20 = (bf16[24,512]{1,0:T(8,128)(2,1)S(1)}, bf16[24,512]{1,0:T(8,128)(2,1)S(1)}, u32[]{:S(2)}, u32[]{:S(2)}) collective-permute-start(bf16[24,512]{1,0:T(8,128)(2,1)S(1)} %get-tuple-element.83), channel_id=1, source_target_pairs={{0,8},{8,0},{16,24},{24,16},{1,9},{9,1},{17,25},{25,17},{2,10},{10... | collective-permute-start | bytes 73736 | tf_op jit(solution)/shard_map/ppermute | solution.py:19
  45.7 1.2 %collective-permute-done.18.refs_0_ = bf16[24,512]{1,0:T(8,128)(2,1)S(1)} collective-permute-done((bf16[24,512]{1,0:T(8,128)(2,1)S(1)}, bf16[24,512]{1,0:T(8,128)(2,1)S(1)}, u32[]{:S(2)}, u32[]{:S(2)}) %collective-permute-start.18) | collective-permute-done | bytes 24608 | tf_op jit(solution)/shard_map/ppermute | solution.py:19
  46.9 1.5 %collective-permute-done.19.refs_1_ = bf16[24,512]{1,0:T(8,128)(2,1)S(1)} collective-permute-done((bf16[24,512]{1,0:T(8,128)(2,1)S(1)}, bf16[24,512]{1,0:T(8,128)(2,1)S(1)}, u32[]{:S(2)}, u32[]{:S(2)}) %collective-permute-start.19) | collective-permute-done | bytes 24608 | tf_op jit(solution)/shard_map/ppermute | solution.py:19
  (42 shorter events, 7.7 us)
Async XLA Ops:
  0.0 3.3 %collective-permute-start = (bf16[832,256]{1,0:T(8,128)(2,1)}, bf16[832,256]{1,0:T(8,128)(2,1)S(1)}, u32[]{:S(2)}, u32[]{:S(2)}) collective-permute-start(bf16[832,256]{1,0:T(8,128)(2,1)} %bitcast.23), channel_id=1, source_target_pairs={{0,1},{1,0},{2,3},{3,2},{4,5},{5,4},{6,7},{7,6},{8,9},{9,8},{10,11... | collective-permute-start | bytes 1277960 | tf_op jit(solution)/shard_map/ppermute | solution.py:19
  1.2 2.0 %collective-permute-start.1 = (s32[1,128]{1,0:T(1,128)S(1)}, s32[1,128]{1,0:T(1,128)S(1)}, u32[]{:S(2)}, u32[]{:S(2)}) collective-permute-start(s32[1,128]{1,0:T(1,128)S(1)} %pad_bitcast_fusion.own_ints_ref), channel_id=1, source_target_pairs={{0,1},{1,0},{2,3},{3,2},{4,5},{5,4},{6,7},{7,6},{8,9},{9,8},{10,11... | collective-permute-start | bytes 1544 | tf_op jit(solution)/shard_map/ppermute | solution.py:19
  3.3 3.1 %copy-start = (bf16[1,2,192,2048]{3,2,1,0:T(8,128)(2,1)S(1)}, bf16[1,2,192,2048]{3,2,1,0:T(8,128)(2,1)}, u32[]{:S(2)}) copy-start(bf16[1,2,192,2048]{3,2,1,0:T(8,128)(2,1)} %param.29) | copy-start | bytes 4718596
  3.3 3.5 %copy-start.1 = (bf16[1,192,2048]{2,1,0:T(8,128)(2,1)S(1)}, bf16[1,192,2048]{2,1,0:T(8,128)(2,1)}, u32[]{:S(2)}) copy-start(bf16[1,192,2048]{2,1,0:T(8,128)(2,1)} %param.30) | copy-start | bytes 2359300
  3.3 22.3 %copy-start.2 = (f32[2048]{0:T(1024)S(1)}, f32[2048]{0:T(1024)}, u32[]{:S(2)}) copy-start(f32[2048]{0:T(1024)} %param.25) | copy-start | bytes 24580
  4.9 1.5 %collective-permute-start.2 = (bf16[24,2560]{1,0:T(8,128)(2,1)S(1)}, bf16[24,2560]{1,0:T(8,128)(2,1)S(1)}, u32[]{:S(2)}, u32[]{:S(2)}) collective-permute-start(bf16[24,2560]{1,0:T(8,128)(2,1)S(1)} %get-tuple-element.52), channel_id=1, source_target_pairs={{0,1},{1,0},{2,3},{3,2},{4,5},{5,4},{6,7},{7,6},{8,9},{9,8},{10,11... | collective-permute-start | bytes 368648 | tf_op jit(solution)/shard_map/ppermute | solution.py:19
  6.4 19.2 %collective-permute-start.10 = (bf16[384,2048]{1,0:T(8,128)(2,1)S(1)}, bf16[384,2048]{1,0:T(8,128)(2,1)S(1)}, u32[]{:S(2)}, u32[]{:S(2)}) collective-permute-start(bf16[384,2048]{1,0:T(8,128)(2,1)S(1)} %bitcast.11), channel_id=1, source_target_pairs={{0,1},{1,0},{2,3},{3,2},{4,5},{5,4},{6,7},{7,6},{8,9},{9,8},{10,11... | collective-permute-start | bytes 4718600 | tf_op jit(solution)/shard_map/ppermute | solution.py:19
  6.8 24.1 %collective-permute-start.13 = (bf16[192,2048]{1,0:T(8,128)(2,1)S(1)}, bf16[192,2048]{1,0:T(8,128)(2,1)S(1)}, u32[]{:S(2)}, u32[]{:S(2)}) collective-permute-start(bf16[192,2048]{1,0:T(8,128)(2,1)S(1)} %bitcast.16), channel_id=1, source_target_pairs={{0,1},{1,0},{2,3},{3,2},{4,5},{5,4},{6,7},{7,6},{8,9},{9,8},{10,11... | collective-permute-start | bytes 2359304 | tf_op jit(solution)/shard_map/ppermute | solution.py:19
  6.9 5.7 %collective-permute-start.4 = (bf16[24,640]{1,0:T(8,128)(2,1)S(1)}, bf16[24,640]{1,0:T(8,128)(2,1)S(1)}, u32[]{:S(2)}, u32[]{:S(2)}) collective-permute-start(bf16[24,640]{1,0:T(8,128)(2,1)S(1)} %get-tuple-element.55), channel_id=1, source_target_pairs={{0,6},{2,4},{4,2},{6,0},{1,7},{3,5},{5,3},{7,1},{8,14},{10,12},{12... | collective-permute-start | bytes 92168 | tf_op jit(solution)/shard_map/ppermute | solution.py:19
  10.8 3.9 %collective-permute-start.5 = (bf16[24,640]{1,0:T(8,128)(2,1)S(1)}, bf16[24,640]{1,0:T(8,128)(2,1)S(1)}, u32[]{:S(2)}, u32[]{:S(2)}) collective-permute-start(bf16[24,640]{1,0:T(8,128)(2,1)S(1)} %get-tuple-element.56), channel_id=1, source_target_pairs={{0,4},{2,6},{4,0},{6,2},{1,5},{3,7},{5,1},{7,3},{8,12},{10,14},{12... | collective-permute-start | bytes 92168 | tf_op jit(solution)/shard_map/ppermute | solution.py:19
  11.3 3.9 %collective-permute-start.3 = (bf16[24,640]{1,0:T(8,128)(2,1)S(1)}, bf16[24,640]{1,0:T(8,128)(2,1)S(1)}, u32[]{:S(2)}, u32[]{:S(2)}) collective-permute-start(bf16[24,640]{1,0:T(8,128)(2,1)S(1)} %get-tuple-element.53), channel_id=1, source_target_pairs={{0,2},{2,0},{4,6},{6,4},{1,3},{3,1},{5,7},{7,5},{8,10},{10,8},{12,... | collective-permute-start | bytes 92168 | tf_op jit(solution)/shard_map/ppermute | solution.py:19
  15.2 5.2 %collective-permute-start.7 = (bf16[24,640]{1,0:T(8,128)(2,1)S(1)}, bf16[24,640]{1,0:T(8,128)(2,1)S(1)}, u32[]{:S(2)}, u32[]{:S(2)}) collective-permute-start(bf16[24,640]{1,0:T(8,128)(2,1)S(1)} %get-tuple-element.58), channel_id=1, source_target_pairs={{0,25},{1,24},{8,17},{9,16},{16,9},{17,8},{24,1},{25,0},{2,27},{3,... | collective-permute-start | bytes 92168 | tf_op jit(solution)/shard_map/ppermute | solution.py:27
  16.9 5.1 %collective-permute-start.6 = (bf16[24,640]{1,0:T(8,128)(2,1)S(1)}, bf16[24,640]{1,0:T(8,128)(2,1)S(1)}, u32[]{:S(2)}, u32[]{:S(2)}) collective-permute-start(bf16[24,640]{1,0:T(8,128)(2,1)S(1)} %get-tuple-element.57), channel_id=1, source_target_pairs={{0,16},{1,17},{8,24},{9,25},{16,0},{17,1},{24,8},{25,9},{2,18},{3,... | collective-permute-start | bytes 92168 | tf_op jit(solution)/shard_map/ppermute | solution.py:27
  18.0 4.1 %collective-permute-start.8 = (bf16[24,640]{1,0:T(8,128)(2,1)S(1)}, bf16[24,640]{1,0:T(8,128)(2,1)S(1)}, u32[]{:S(2)}, u32[]{:S(2)}) collective-permute-start(bf16[24,640]{1,0:T(8,128)(2,1)S(1)} %get-tuple-element.59), channel_id=1, source_target_pairs={{0,9},{1,8},{8,1},{9,0},{16,25},{17,24},{24,17},{25,16},{2,11},{3,... | collective-permute-start | bytes 92168 | tf_op jit(solution)/shard_map/ppermute | solution.py:27
  22.1 6.5 %collective-permute-start.12 = (bf16[4,24,512]{2,1,0:T(8,128)(2,1)S(1)}, bf16[4,24,512]{2,1,0:T(8,128)(2,1)S(1)}, u32[]{:S(2)}, u32[]{:S(2)}) collective-permute-start(bf16[4,24,512]{2,1,0:T(8,128)(2,1)S(1)} %get-tuple-element.61), channel_id=1, source_target_pairs={{0,6},{2,4},{4,2},{6,0},{1,7},{3,5},{5,3},{7,1},{8,14},{10,12},{12... | collective-permute-start | bytes 294920 | tf_op jit(solution)/shard_map/ppermute | solution.py:19
  23.7 6.7 %collective-permute-start.11 = (bf16[4,24,512]{2,1,0:T(8,128)(2,1)S(1)}, bf16[4,24,512]{2,1,0:T(8,128)(2,1)S(1)}, u32[]{:S(2)}, u32[]{:S(2)}) collective-permute-start(bf16[4,24,512]{2,1,0:T(8,128)(2,1)S(1)} %get-tuple-element.61), channel_id=1, source_target_pairs={{0,4},{2,6},{4,0},{6,2},{1,5},{3,7},{5,1},{7,3},{8,12},{10,14},{12... | collective-permute-start | bytes 294920 | tf_op jit(solution)/shard_map/ppermute | solution.py:19
  24.2 6.6 %collective-permute-start.9 = (bf16[4,24,512]{2,1,0:T(8,128)(2,1)S(1)}, bf16[4,24,512]{2,1,0:T(8,128)(2,1)S(1)}, u32[]{:S(2)}, u32[]{:S(2)}) collective-permute-start(bf16[4,24,512]{2,1,0:T(8,128)(2,1)S(1)} %get-tuple-element.61), channel_id=1, source_target_pairs={{0,2},{2,0},{4,6},{6,4},{1,3},{3,1},{5,7},{7,5},{8,10},{10,8},{12,... | collective-permute-start | bytes 294920 | tf_op jit(solution)/shard_map/ppermute | solution.py:19
  31.9 6.3 %collective-permute-start.14 = (bf16[24,2048]{1,0:T(8,128)(2,1)S(1)}, bf16[24,2048]{1,0:T(8,128)(2,1)S(1)}, u32[]{:S(2)}, u32[]{:S(2)}) collective-permute-start(bf16[24,2048]{1,0:T(8,128)(2,1)S(1)} %get-tuple-element.74), channel_id=1, source_target_pairs={{0,6},{2,4},{4,2},{6,0},{1,7},{3,5},{5,3},{7,1},{8,14},{10,12},{12... | collective-permute-start | bytes 294920 | tf_op jit(solution)/shard_map/ppermute | solution.py:19
  33.4 6.2 %collective-permute-start.15 = (bf16[24,2048]{1,0:T(8,128)(2,1)S(1)}, bf16[24,2048]{1,0:T(8,128)(2,1)S(1)}, u32[]{:S(2)}, u32[]{:S(2)}) collective-permute-start(bf16[24,2048]{1,0:T(8,128)(2,1)S(1)} %get-tuple-element.75), channel_id=1, source_target_pairs={{0,4},{2,6},{4,0},{6,2},{1,5},{3,7},{5,1},{7,3},{8,12},{10,14},{12... | collective-permute-start | bytes 294920 | tf_op jit(solution)/shard_map/ppermute | solution.py:19
  33.9 5.7 %collective-permute-start.16 = (bf16[24,2048]{1,0:T(8,128)(2,1)S(1)}, bf16[24,2048]{1,0:T(8,128)(2,1)S(1)}, u32[]{:S(2)}, u32[]{:S(2)}) collective-permute-start(bf16[24,2048]{1,0:T(8,128)(2,1)S(1)} %get-tuple-element.76), channel_id=1, source_target_pairs={{0,2},{2,0},{4,6},{6,4},{1,3},{3,1},{5,7},{7,5},{8,10},{10,8},{12,... | collective-permute-start | bytes 294920 | tf_op jit(solution)/shard_map/ppermute | solution.py:19
  39.7 1.3 %collective-permute-start.17 = (bf16[24,1024]{1,0:T(8,128)(2,1)S(1)}, bf16[24,1024]{1,0:T(8,128)(2,1)S(1)}, u32[]{:S(2)}, u32[]{:S(2)}) collective-permute-start(bf16[24,1024]{1,0:T(8,128)(2,1)S(1)} %get-tuple-element.79), channel_id=1, source_target_pairs={{0,1},{1,0},{2,3},{3,2},{4,5},{5,4},{6,7},{7,6},{8,9},{9,8},{10,11... | collective-permute-start | bytes 147464 | tf_op jit(solution)/shard_map/ppermute | solution.py:19
  41.2 5.7 %collective-permute-start.18 = (bf16[24,512]{1,0:T(8,128)(2,1)S(1)}, bf16[24,512]{1,0:T(8,128)(2,1)S(1)}, u32[]{:S(2)}, u32[]{:S(2)}) collective-permute-start(bf16[24,512]{1,0:T(8,128)(2,1)S(1)} %get-tuple-element.81), channel_id=1, source_target_pairs={{0,24},{8,16},{16,8},{24,0},{1,25},{9,17},{17,9},{25,1},{2,26},{10... | collective-permute-start | bytes 73736 | tf_op jit(solution)/shard_map/ppermute | solution.py:19
  43.7 4.7 %collective-permute-start.19 = (bf16[24,512]{1,0:T(8,128)(2,1)S(1)}, bf16[24,512]{1,0:T(8,128)(2,1)S(1)}, u32[]{:S(2)}, u32[]{:S(2)}) collective-permute-start(bf16[24,512]{1,0:T(8,128)(2,1)S(1)} %get-tuple-element.82), channel_id=1, source_target_pairs={{0,16},{8,24},{16,0},{24,8},{1,17},{9,25},{17,1},{25,9},{2,18},{10... | collective-permute-start | bytes 73736 | tf_op jit(solution)/shard_map/ppermute | solution.py:19
  43.7 4.7 %collective-permute-start.20 = (bf16[24,512]{1,0:T(8,128)(2,1)S(1)}, bf16[24,512]{1,0:T(8,128)(2,1)S(1)}, u32[]{:S(2)}, u32[]{:S(2)}) collective-permute-start(bf16[24,512]{1,0:T(8,128)(2,1)S(1)} %get-tuple-element.83), channel_id=1, source_target_pairs={{0,8},{8,0},{16,24},{24,16},{1,9},{9,1},{17,25},{25,17},{2,10},{10... | collective-permute-start | bytes 73736 | tf_op jit(solution)/shard_map/ppermute | solution.py:19

commit v12 on v11

--- a/solution.py
+++ b/solution.py
@@ -23,6 +23,25 @@
     size, pools = lax.axis_size(axis), lax.axis_size("pool")
     pairs = [
         (i * pools + p, (i ^ step) * pools + (p ^ (step & 1))) for i in range(size) for p in range(pools)
+    ]
+    return lax.ppermute(value, (axis, "pool"), pairs)
+
+
+def turn_step(turn, pool, size):
+    return size - 1 - (turn - pool) % (size - 1)
+
+
+def own_step(turn, size):
+    step = turn_step(turn, 0, size)
+    for pool in range(1, lax.axis_size("pool")):
+        step = jnp.where(lax.axis_index("pool") == pool, turn_step(turn, pool, size), step)
+    return step
+
+
+def send_turn(value, axis, turn):
+    size, pools = lax.axis_size(axis), lax.axis_size("pool")
+    pairs = [
+        (i * pools + p, (i ^ turn_step(turn, p, size)) * pools + p) for i in range(size) for p in range(pools)
     ]
     return lax.ppermute(value, (axis, "pool"), pairs)
 
@@ -64,7 +83,7 @@
     semaphores = refs[-1]
     head, mine = lax.axis_index("head"), part_taken()
     first = jnp.where(lax.axis_index("pool") == 0, 1.0, 0.0)
-    picked = {5: mine, 6: head}
+    picked = {5: mine, 6: head * pools + lax.axis_index("pool")}
     copies = []
     for i in range(count):
         source = sources[i].at[picked[i]] if i in picked else sources[i]
@@ -232,11 +251,12 @@
     return block, projected, jnp.sum(block * block, axis=1, keepdims=True)
 
 
-def project_kernel(step, planes, block_ref, own_up_ref, other_up_ref, gain_ref, *refs):
+def project_kernel(turn, planes, block_ref, own_up_ref, other_up_ref, gain_ref, *refs):
+    step = 0 if turn is None else own_step(turn, lax.axis_size("head"))
     block, projected, squares = projection(step, block_ref, own_up_ref, other_up_ref, gain_ref)
     plane_rows = block_ref.shape[1]
     rows, columns = block.shape
-    if step:
+    if turn is not None:
         before_ref, before_squares_ref, projected_ref, squares_ref = refs
         projected_ref[...] = before_ref[...] + projected
         squares_ref[...] = before_squares_ref[...] + squares
@@ -257,7 +277,7 @@
 
 def expert_kernel(block_ref, own_up_ref, other_up_ref, gain_ref, projected_ref, squares_ref, route_ref, own_ref, own_down_ref, other_down_ref, order_ref, *outs):
     heads = len(outs)
-    _, projected, squares = projection(1, block_ref, own_up_ref, other_up_ref, gain_ref)
+    _, projected, squares = projection(own_step(heads - 2, heads), block_ref, own_up_ref, other_up_ref, gain_ref)
     projected = projected + projected_ref[...]
     squares = squares + squares_ref[...]
     head = lax.axis_index("head")
@@ -359,8 +379,14 @@
         for here in range(pools)
     ]
     head_order = [
-        [(r * heads + (here ^ h)) * part + i for h in range(heads) for r in range(planes) for i in range(part)]
+        [
+            (r * heads + (here ^ h)) * part + i
+            for h in [0] + [turn_step(turn, p, heads) for turn in range(heads - 1)]
+            for r in range(planes)
+            for i in range(part)
+        ]
         for here in range(heads)
+        for p in range(pools)
     ]
     plane_order = [
         [
@@ -447,23 +473,23 @@
     total = planes * rows
     sums = [shape(total, 2 * gate_up.shape[0], dtype=F32), shape(total, 1, dtype=F32)]
     *state, route, own = kernel_call(
-        functools.partial(project_kernel, 0, planes),
+        functools.partial(project_kernel, None, planes),
         sums + [shape(total, 1, dtype=F32), shape(total, columns, dtype=F32)],
         held(plane_blocks, *weights, head_order, down_weight),
     )
-    for step in reversed(range(2, heads)):
+    for turn in range(heads - 2):
         state = kernel_call(
-            functools.partial(project_kernel, step, planes),
+            functools.partial(project_kernel, turn, planes),
             sums,
-            held(send(sent, "head", step), *weights, *state),
+            held(send_turn(sent, "head", turn), *weights, *state),
         )
     piece = shape(planes * part, width)
     pieces = kernel_call(
         expert_kernel,
         [shape(planes * part, width, dtype=F32)] + [piece] * (heads - 1),
-        held(send(sent, "head", 1), *weights, *state, route, own, down_weight, other_down, head_order),
-    )
-    arrived = [send(pieces[step], "head", step) for step in reversed(range(1, heads))] + [pieces[0]]
+        held(send_turn(sent, "head", heads - 2), *weights, *state, route, own, down_weight, other_down, head_order),
+    )
+    arrived = [send_turn(pieces[turn + 1], "head", turn) for turn in range(heads - 1)] + [pieces[0]]
     own, other = kernel_call(
         halve_kernel, [shape(planes * part, width // pools)] * 2, held(*arrived)
     )

time: 49.2 us -> 50.2 us (1.020)
  waiting for transfers between devices: 19.8 us -> 20.9 us
    ppermute x0 -> x6, waiting for transfers between devices: none -> 8.86 us  [send_turn(): return lax.ppermute(value, (axis, 'pool'), pairs)]
    ppermute x18 -> x12, waiting for transfers between devices: 16.9 us -> 9.1 us  [send(): return lax.ppermute(value, axes, [(i, i ^ step) for i in range(size)])]
    ppermute x18 -> x12, starting transfers between devices: 17.7 us -> 10.6 us  [send(): return lax.ppermute(value, axes, [(i, i ^ step) for i in range(size)])]
    ppermute x0 -> x6, starting transfers between devices: none -> 7.11 us  [send_turn(): return lax.ppermute(value, (axis, 'pool'), pairs)]
  transfers between devices with their start and end apart: 21 -> 21, of which waited for: 13 -> 13; matrix products, arithmetic and copies ran while one was open for 2% -> 2% of each run, Pallas kernels for 7% -> 6%
where the time goes in v12:
time: 50.2 us; the launch traced here: 50.1 us
  starting transfers between devices  21.6 us (43%)
  waiting for transfers between devices  20.9 us (42%)
  Pallas kernels  6.61 us (13%)
  other arithmetic  0.78 us (2%)
    ppermute x12, starting transfers between devices, send(): return lax.ppermute(value, axes, [(i, i ^ step) for i in range(size)])  10.6 us
    ppermute x12, waiting for transfers between devices, send(): return lax.ppermute(value, axes, [(i, i ^ step) for i in range(size)])  9.1 us
    ppermute x6, waiting for transfers between devices, send_turn(): return lax.ppermute(value, (axis, 'pool'), pairs)  8.86 us
    ppermute x6, starting transfers between devices, send_turn(): return lax.ppermute(value, (axis, 'pool'), pairs)  7.11 us
    pallas_call x15, Pallas kernels, kernel_call(): pl.pallas_call(body, out_shape=jax.tree.map(lambda out: pltpu.VMEM(out.sh...  5.98 us
    ppermute x3, starting transfers between devices, cross(): return lax.ppermute(value, (axis, 'pool'), pairs)  3.89 us
    ppermute x3, waiting for transfers between devices, cross(): return lax.ppermute(value, (axis, 'pool'), pairs)  2.94 us
  transfers between devices with their start and end apart: 21, of which 13 were waited for; matrix products, arithmetic and copies ran while one was open for 2% of the time, Pallas kernels for 6%

profile of v12, /device:TPU:0, one launch (start us, length us, event | category | flops | bytes accessed | tf_op | source)
XLA Modules:
  0.0 50.1 jit_solution(11824212103335330292)
XLA Ops:
  1.3 1.9 %shard_map.163 = (bf16[48,2560]{1,0:T(8,128)(2,1)S(1)}, bf16[832,256]{1,0:T(8,128)(2,1)S(1)}, bf16[48,1024]{1,0:T(8,128)(2,1)S(1)}, bf16[512,2048]{1,0:T(8,128)(...) custom-call(bf16[832,256]{1,0:T(8,128)(2,1)} %bitcast.24, ...), custom_call_target="tpu_custom_call" | custom-call | tf_op jit(solution)/shard_map/pallas_call | solution.py:58
  3.3 1.6 %shard_map.164 = (f32[24,2560]{1,0:T(8,128)S(1)}, bf16[24,2560]{1,0:T(8,128)(2,1)S(1)}) custom-call(bf16[48,1024]{1,0:T(8,128)(2,1)S(1)} %get-tuple-element.45.q_ref, bf16[48,2,256]{2,1,0:T(2,128)(2,1)S(1)} %get-tuple-element.46.new_ref, bf16[832,256]{1,0:T(8,128)(2,1)S(1)} %get-tuple-element.47.own_ref, ...), custom_call_target="tpu_custom_call" | custom-call | tf_op jit(solution)/shard_map/pallas_call | solution.py:58
  6.9 3.9 %collective-permute-start.4 = (bf16[24,640]{1,0:T(8,128)(2,1)S(1)}, bf16[24,640]{1,0:T(8,128)(2,1)S(1)}, u32[]{:S(2)}, u32[]{:S(2)}) collective-permute-start(bf16[24,640]{1,0:T(8,128)(2,1)S(1)} %get-tuple-element.55), channel_id=1, source_target_pairs={{0,6},{2,4},{4,2},{6,0},{1,7},{3,5},{5,3},{7,1},{8,14},{10,12},{12... | collective-permute-start | bytes 92168 | tf_op jit(solution)/shard_map/ppermute | solution.py:19
  11.4 1.2 %collective-permute-done.4.part_ref = bf16[24,640]{1,0:T(8,128)(2,1)S(1)} collective-permute-done((bf16[24,640]{1,0:T(8,128)(2,1)S(1)}, bf16[24,640]{1,0:T(8,128)(2,1)S(1)}, u32[]{:S(2)}, u32[]{:S(2)}) %collective-permute-start.4) | collective-permute-done | bytes 30752 | tf_op jit(solution)/shard_map/ppermute | solution.py:19
  12.7 2.0 %collective-permute-done.5.part_ref = bf16[24,640]{1,0:T(8,128)(2,1)S(1)} collective-permute-done((bf16[24,640]{1,0:T(8,128)(2,1)S(1)}, bf16[24,640]{1,0:T(8,128)(2,1)S(1)}, u32[]{:S(2)}, u32[]{:S(2)}) %collective-permute-start.5) | collective-permute-done | bytes 30752 | tf_op jit(solution)/shard_map/ppermute | solution.py:19
  15.2 1.7 %collective-permute-start.7 = (bf16[24,640]{1,0:T(8,128)(2,1)S(1)}, bf16[24,640]{1,0:T(8,128)(2,1)S(1)}, u32[]{:S(2)}, u32[]{:S(2)}) collective-permute-start(bf16[24,640]{1,0:T(8,128)(2,1)S(1)} %get-tuple-element.58), channel_id=1, source_target_pairs={{0,25},{1,24},{8,17},{9,16},{16,9},{17,8},{24,1},{25,0},{2,27},{3,... | collective-permute-start | bytes 92168 | tf_op jit(solution)/shard_map/ppermute | solution.py:27
  16.9 1.0 %collective-permute-start.6 = (bf16[24,640]{1,0:T(8,128)(2,1)S(1)}, bf16[24,640]{1,0:T(8,128)(2,1)S(1)}, u32[]{:S(2)}, u32[]{:S(2)}) collective-permute-start(bf16[24,640]{1,0:T(8,128)(2,1)S(1)} %get-tuple-element.57), channel_id=1, source_target_pairs={{0,16},{1,17},{8,24},{9,25},{16,0},{17,1},{24,8},{25,9},{2,18},{3,... | collective-permute-start | bytes 92168 | tf_op jit(solution)/shard_map/ppermute | solution.py:27
  18.0 1.2 %collective-permute-start.8 = (bf16[24,640]{1,0:T(8,128)(2,1)S(1)}, bf16[24,640]{1,0:T(8,128)(2,1)S(1)}, u32[]{:S(2)}, u32[]{:S(2)}) collective-permute-start(bf16[24,640]{1,0:T(8,128)(2,1)S(1)} %get-tuple-element.59), channel_id=1, source_target_pairs={{0,9},{1,8},{8,1},{9,0},{16,25},{17,24},{24,17},{25,16},{2,11},{3,... | collective-permute-start | bytes 92168 | tf_op jit(solution)/shard_map/ppermute | solution.py:27
  19.1 1.3 %collective-permute-done.7.part_ref.refs_1_ = bf16[24,640]{1,0:T(8,128)(2,1)S(1)} collective-permute-done((bf16[24,640]{1,0:T(8,128)(2,1)S(1)}, bf16[24,640]{1,0:T(8,128)(2,1)S(1)}, u32[]{:S(2)}, u32[]{:S(2)}) %collective-permute-start.7) | collective-permute-done | bytes 30752 | tf_op jit(solution)/shard_map/ppermute | solution.py:27
  20.4 1.7 %collective-permute-done.6.part_ref.refs_2_ = bf16[24,640]{1,0:T(8,128)(2,1)S(1)} collective-permute-done((bf16[24,640]{1,0:T(8,128)(2,1)S(1)}, bf16[24,640]{1,0:T(8,128)(2,1)S(1)}, u32[]{:S(2)}, u32[]{:S(2)}) %collective-permute-start.6) | collective-permute-done | bytes 30752 | tf_op jit(solution)/shard_map/ppermute | solution.py:27
  22.1 1.6 %collective-permute-start.12 = (bf16[4,24,512]{2,1,0:T(8,128)(2,1)S(1)}, bf16[4,24,512]{2,1,0:T(8,128)(2,1)S(1)}, u32[]{:S(2)}, u32[]{:S(2)}) collective-permute-start(bf16[4,24,512]{2,1,0:T(8,128)(2,1)S(1)} %get-tuple-element.61), channel_id=1, source_target_pairs={{0,6},{1,3},{2,4},{3,1},{4,2},{5,7},{6,0},{7,5},{8,14},{9,11},{10,... | collective-permute-start | bytes 294920 | tf_op jit(solution)/shard_map/ppermute | solution.py:46
  24.2 1.4 %collective-permute-start.9 = (bf16[4,24,512]{2,1,0:T(8,128)(2,1)S(1)}, bf16[4,24,512]{2,1,0:T(8,128)(2,1)S(1)}, u32[]{:S(2)}, u32[]{:S(2)}) collective-permute-start(bf16[4,24,512]{2,1,0:T(8,128)(2,1)S(1)} %get-tuple-element.61), channel_id=1, source_target_pairs={{0,2},{1,5},{2,0},{3,7},{4,6},{5,1},{6,4},{7,3},{8,10},{9,13},{10,... | collective-permute-start | bytes 294920 | tf_op jit(solution)/shard_map/ppermute | solution.py:46
  26.1 2.7 %collective-permute-done.12.block_ref = bf16[4,24,512]{2,1,0:T(8,128)(2,1)S(1)} collective-permute-done((bf16[4,24,512]{2,1,0:T(8,128)(2,1)S(1)}, bf16[4,24,512]{2,1,0:T(8,128)(2,1)S(1)}, u32[]{:S(2)}, u32[]{:S(2)}) %collective-permute-start.12) | collective-permute-done | bytes 98336 | tf_op jit(solution)/shard_map/ppermute | solution.py:46
  29.2 1.7 %collective-permute-done.11.block_ref = bf16[4,24,512]{2,1,0:T(8,128)(2,1)S(1)} collective-permute-done((bf16[4,24,512]{2,1,0:T(8,128)(2,1)S(1)}, bf16[4,24,512]{2,1,0:T(8,128)(2,1)S(1)}, u32[]{:S(2)}, u32[]{:S(2)}) %collective-permute-start.11) | collective-permute-done | bytes 98336 | tf_op jit(solution)/shard_map/ppermute | solution.py:46
  31.3 1.0 %shard_map.175 = (f32[24,2048]{1,0:T(8,128)S(1)}, bf16[24,2048]{1,0:T(8,128)(2,1)S(1)}, bf16[24,2048]{1,0:T(8,128)(2,1)S(1)}, bf16[24,2048]{1,0:T(8,128)(2,1)S(1)}) custom-call(bf16[4,24,512]{2,1,0:T(8,128)(2,1)S(1)} %collective-permute-done.9.block_ref, bf16[384,2048]{1,0:T(8,128)(2,1)S(1)} %bitcast.15, ...), custom_call_target="tpu_custom_call" | custom-call | tf_op jit(solution)/shard_map/pallas_call | solution.py:58
  32.3 1.6 %collective-permute-start.14 = (bf16[24,2048]{1,0:T(8,128)(2,1)S(1)}, bf16[24,2048]{1,0:T(8,128)(2,1)S(1)}, u32[]{:S(2)}, u32[]{:S(2)}) collective-permute-start(bf16[24,2048]{1,0:T(8,128)(2,1)S(1)} %get-tuple-element.74), channel_id=1, source_target_pairs={{0,6},{1,3},{2,4},{3,1},{4,2},{5,7},{6,0},{7,5},{8,14},{9,11},{10,... | collective-permute-start | bytes 294920 | tf_op jit(solution)/shard_map/ppermute | solution.py:46
  34.9 1.0 %collective-permute-start.16 = (bf16[24,2048]{1,0:T(8,128)(2,1)S(1)}, bf16[24,2048]{1,0:T(8,128)(2,1)S(1)}, u32[]{:S(2)}, u32[]{:S(2)}) collective-permute-start(bf16[24,2048]{1,0:T(8,128)(2,1)S(1)} %get-tuple-element.76), channel_id=1, source_target_pairs={{0,2},{1,5},{2,0},{3,7},{4,6},{5,1},{6,4},{7,3},{8,10},{9,13},{10,... | collective-permute-start | bytes 294920 | tf_op jit(solution)/shard_map/ppermute | solution.py:46
  35.9 2.4 %collective-permute-done.14.refs_0_ = bf16[24,2048]{1,0:T(8,128)(2,1)S(1)} collective-permute-done((bf16[24,2048]{1,0:T(8,128)(2,1)S(1)}, bf16[24,2048]{1,0:T(8,128)(2,1)S(1)}, u32[]{:S(2)}, u32[]{:S(2)}) %collective-permute-start.14) | collective-permute-done | bytes 98336 | tf_op jit(solution)/shard_map/ppermute | solution.py:46
  38.3 2.0 %collective-permute-done.15.refs_1_ = bf16[24,2048]{1,0:T(8,128)(2,1)S(1)} collective-permute-done((bf16[24,2048]{1,0:T(8,128)(2,1)S(1)}, bf16[24,2048]{1,0:T(8,128)(2,1)S(1)}, u32[]{:S(2)}, u32[]{:S(2)}) %collective-permute-start.15) | collective-permute-done | bytes 98336 | tf_op jit(solution)/shard_map/ppermute | solution.py:46
  40.4 1.2 %collective-permute-done.17.other_ref = bf16[24,1024]{1,0:T(8,128)(2,1)S(1)} collective-permute-done((bf16[24,1024]{1,0:T(8,128)(2,1)S(1)}, bf16[24,1024]{1,0:T(8,128)(2,1)S(1)}, u32[]{:S(2)}, u32[]{:S(2)}) %collective-permute-start.17) | collective-permute-done | bytes 49184 | tf_op jit(solution)/shard_map/ppermute | solution.py:19
  41.8 2.9 %collective-permute-start.18 = (bf16[24,512]{1,0:T(8,128)(2,1)S(1)}, bf16[24,512]{1,0:T(8,128)(2,1)S(1)}, u32[]{:S(2)}, u32[]{:S(2)}) collective-permute-start(bf16[24,512]{1,0:T(8,128)(2,1)S(1)} %get-tuple-element.81), channel_id=1, source_target_pairs={{0,24},{8,16},{16,8},{24,0},{1,25},{9,17},{17,9},{25,1},{2,26},{10... | collective-permute-start | bytes 73736 | tf_op jit(solution)/shard_map/ppermute | solution.py:19
  44.7 1.6 %collective-permute-start.20 = (bf16[24,512]{1,0:T(8,128)(2,1)S(1)}, bf16[24,512]{1,0:T(8,128)(2,1)S(1)}, u32[]{:S(2)}, u32[]{:S(2)}) collective-permute-start(bf16[24,512]{1,0:T(8,128)(2,1)S(1)} %get-tuple-element.83), channel_id=1, source_target_pairs={{0,8},{8,0},{16,24},{24,16},{1,9},{9,1},{17,25},{25,17},{2,10},{10... | collective-permute-start | bytes 73736 | tf_op jit(solution)/shard_map/ppermute | solution.py:19
  46.3 1.3 %collective-permute-done.18.refs_0_ = bf16[24,512]{1,0:T(8,128)(2,1)S(1)} collective-permute-done((bf16[24,512]{1,0:T(8,128)(2,1)S(1)}, bf16[24,512]{1,0:T(8,128)(2,1)S(1)}, u32[]{:S(2)}, u32[]{:S(2)}) %collective-permute-start.18) | collective-permute-done | bytes 24608 | tf_op jit(solution)/shard_map/ppermute | solution.py:19
  47.6 1.8 %collective-permute-done.19.refs_1_ = bf16[24,512]{1,0:T(8,128)(2,1)S(1)} collective-permute-done((bf16[24,512]{1,0:T(8,128)(2,1)S(1)}, bf16[24,512]{1,0:T(8,128)(2,1)S(1)}, u32[]{:S(2)}, u32[]{:S(2)}) %collective-permute-start.19) | collective-permute-done | bytes 24608 | tf_op jit(solution)/shard_map/ppermute | solution.py:19
  (42 shorter events, 8.2 us)
Async XLA Ops:
  0.0 3.3 %collective-permute-start = (bf16[832,256]{1,0:T(8,128)(2,1)}, bf16[832,256]{1,0:T(8,128)(2,1)S(1)}, u32[]{:S(2)}, u32[]{:S(2)}) collective-permute-start(bf16[832,256]{1,0:T(8,128)(2,1)} %bitcast.23), channel_id=1, source_target_pairs={{0,1},{1,0},{2,3},{3,2},{4,5},{5,4},{6,7},{7,6},{8,9},{9,8},{10,11... | collective-permute-start | bytes 1277960 | tf_op jit(solution)/shard_map/ppermute | solution.py:19
  1.2 2.0 %collective-permute-start.1 = (s32[1,128]{1,0:T(1,128)S(1)}, s32[1,128]{1,0:T(1,128)S(1)}, u32[]{:S(2)}, u32[]{:S(2)}) collective-permute-start(s32[1,128]{1,0:T(1,128)S(1)} %pad_bitcast_fusion.own_ints_ref), channel_id=1, source_target_pairs={{0,1},{1,0},{2,3},{3,2},{4,5},{5,4},{6,7},{7,6},{8,9},{9,8},{10,11... | collective-permute-start | bytes 1544 | tf_op jit(solution)/shard_map/ppermute | solution.py:19
  3.3 3.1 %copy-start = (bf16[1,2,192,2048]{3,2,1,0:T(8,128)(2,1)S(1)}, bf16[1,2,192,2048]{3,2,1,0:T(8,128)(2,1)}, u32[]{:S(2)}) copy-start(bf16[1,2,192,2048]{3,2,1,0:T(8,128)(2,1)} %param.29) | copy-start | bytes 4718596
  3.3 3.5 %copy-start.1 = (bf16[1,192,2048]{2,1,0:T(8,128)(2,1)S(1)}, bf16[1,192,2048]{2,1,0:T(8,128)(2,1)}, u32[]{:S(2)}) copy-start(bf16[1,192,2048]{2,1,0:T(8,128)(2,1)} %param.30) | copy-start | bytes 2359300
  3.3 22.3 %copy-start.2 = (f32[2048]{0:T(1024)S(1)}, f32[2048]{0:T(1024)}, u32[]{:S(2)}) copy-start(f32[2048]{0:T(1024)} %param.25) | copy-start | bytes 24580
  4.9 1.5 %collective-permute-start.2 = (bf16[24,2560]{1,0:T(8,128)(2,1)S(1)}, bf16[24,2560]{1,0:T(8,128)(2,1)S(1)}, u32[]{:S(2)}, u32[]{:S(2)}) collective-permute-start(bf16[24,2560]{1,0:T(8,128)(2,1)S(1)} %get-tuple-element.52), channel_id=1, source_target_pairs={{0,1},{1,0},{2,3},{3,2},{4,5},{5,4},{6,7},{7,6},{8,9},{9,8},{10,11... | collective-permute-start | bytes 368648 | tf_op jit(solution)/shard_map/ppermute | solution.py:19
  6.4 19.2 %collective-permute-start.10 = (bf16[384,2048]{1,0:T(8,128)(2,1)S(1)}, bf16[384,2048]{1,0:T(8,128)(2,1)S(1)}, u32[]{:S(2)}, u32[]{:S(2)}) collective-permute-start(bf16[384,2048]{1,0:T(8,128)(2,1)S(1)} %bitcast.11), channel_id=1, source_target_pairs={{0,1},{1,0},{2,3},{3,2},{4,5},{5,4},{6,7},{7,6},{8,9},{9,8},{10,11... | collective-permute-start | bytes 4718600 | tf_op jit(solution)/shard_map/ppermute | solution.py:19
  6.8 24.6 %collective-permute-start.13 = (bf16[192,2048]{1,0:T(8,128)(2,1)S(1)}, bf16[192,2048]{1,0:T(8,128)(2,1)S(1)}, u32[]{:S(2)}, u32[]{:S(2)}) collective-permute-start(bf16[192,2048]{1,0:T(8,128)(2,1)S(1)} %bitcast.16), channel_id=1, source_target_pairs={{0,1},{1,0},{2,3},{3,2},{4,5},{5,4},{6,7},{7,6},{8,9},{9,8},{10,11... | collective-permute-start | bytes 2359304 | tf_op jit(solution)/shard_map/ppermute | solution.py:19
  6.9 5.7 %collective-permute-start.4 = (bf16[24,640]{1,0:T(8,128)(2,1)S(1)}, bf16[24,640]{1,0:T(8,128)(2,1)S(1)}, u32[]{:S(2)}, u32[]{:S(2)}) collective-permute-start(bf16[24,640]{1,0:T(8,128)(2,1)S(1)} %get-tuple-element.55), channel_id=1, source_target_pairs={{0,6},{2,4},{4,2},{6,0},{1,7},{3,5},{5,3},{7,1},{8,14},{10,12},{12... | collective-permute-start | bytes 92168 | tf_op jit(solution)/shard_map/ppermute | solution.py:19
  10.8 3.9 %collective-permute-start.5 = (bf16[24,640]{1,0:T(8,128)(2,1)S(1)}, bf16[24,640]{1,0:T(8,128)(2,1)S(1)}, u32[]{:S(2)}, u32[]{:S(2)}) collective-permute-start(bf16[24,640]{1,0:T(8,128)(2,1)S(1)} %get-tuple-element.56), channel_id=1, source_target_pairs={{0,4},{2,6},{4,0},{6,2},{1,5},{3,7},{5,1},{7,3},{8,12},{10,14},{12... | collective-permute-start | bytes 92168 | tf_op jit(solution)/shard_map/ppermute | solution.py:19
  11.3 3.9 %collective-permute-start.3 = (bf16[24,640]{1,0:T(8,128)(2,1)S(1)}, bf16[24,640]{1,0:T(8,128)(2,1)S(1)}, u32[]{:S(2)}, u32[]{:S(2)}) collective-permute-start(bf16[24,640]{1,0:T(8,128)(2,1)S(1)} %get-tuple-element.53), channel_id=1, source_target_pairs={{0,2},{2,0},{4,6},{6,4},{1,3},{3,1},{5,7},{7,5},{8,10},{10,8},{12,... | collective-permute-start | bytes 92168 | tf_op jit(solution)/shard_map/ppermute | solution.py:19
  15.2 5.2 %collective-permute-start.7 = (bf16[24,640]{1,0:T(8,128)(2,1)S(1)}, bf16[24,640]{1,0:T(8,128)(2,1)S(1)}, u32[]{:S(2)}, u32[]{:S(2)}) collective-permute-start(bf16[24,640]{1,0:T(8,128)(2,1)S(1)} %get-tuple-element.58), channel_id=1, source_target_pairs={{0,25},{1,24},{8,17},{9,16},{16,9},{17,8},{24,1},{25,0},{2,27},{3,... | collective-permute-start | bytes 92168 | tf_op jit(solution)/shard_map/ppermute | solution.py:27
  16.9 5.1 %collective-permute-start.6 = (bf16[24,640]{1,0:T(8,128)(2,1)S(1)}, bf16[24,640]{1,0:T(8,128)(2,1)S(1)}, u32[]{:S(2)}, u32[]{:S(2)}) collective-permute-start(bf16[24,640]{1,0:T(8,128)(2,1)S(1)} %get-tuple-element.57), channel_id=1, source_target_pairs={{0,16},{1,17},{8,24},{9,25},{16,0},{17,1},{24,8},{25,9},{2,18},{3,... | collective-permute-start | bytes 92168 | tf_op jit(solution)/shard_map/ppermute | solution.py:27
  18.0 4.1 %collective-permute-start.8 = (bf16[24,640]{1,0:T(8,128)(2,1)S(1)}, bf16[24,640]{1,0:T(8,128)(2,1)S(1)}, u32[]{:S(2)}, u32[]{:S(2)}) collective-permute-start(bf16[24,640]{1,0:T(8,128)(2,1)S(1)} %get-tuple-element.59), channel_id=1, source_target_pairs={{0,9},{1,8},{8,1},{9,0},{16,25},{17,24},{24,17},{25,16},{2,11},{3,... | collective-permute-start | bytes 92168 | tf_op jit(solution)/shard_map/ppermute | solution.py:27
  22.1 6.7 %collective-permute-start.12 = (bf16[4,24,512]{2,1,0:T(8,128)(2,1)S(1)}, bf16[4,24,512]{2,1,0:T(8,128)(2,1)S(1)}, u32[]{:S(2)}, u32[]{:S(2)}) collective-permute-start(bf16[4,24,512]{2,1,0:T(8,128)(2,1)S(1)} %get-tuple-element.61), channel_id=1, source_target_pairs={{0,6},{1,3},{2,4},{3,1},{4,2},{5,7},{6,0},{7,5},{8,14},{9,11},{10,... | collective-permute-start | bytes 294920 | tf_op jit(solution)/shard_map/ppermute | solution.py:46
  23.7 7.2 %collective-permute-start.11 = (bf16[4,24,512]{2,1,0:T(8,128)(2,1)S(1)}, bf16[4,24,512]{2,1,0:T(8,128)(2,1)S(1)}, u32[]{:S(2)}, u32[]{:S(2)}) collective-permute-start(bf16[4,24,512]{2,1,0:T(8,128)(2,1)S(1)} %get-tuple-element.61), channel_id=1, source_target_pairs={{0,4},{1,7},{2,6},{3,5},{4,0},{5,3},{6,2},{7,1},{8,12},{9,15},{10,... | collective-permute-start | bytes 294920 | tf_op jit(solution)/shard_map/ppermute | solution.py:46
  24.2 7.1 %collective-permute-start.9 = (bf16[4,24,512]{2,1,0:T(8,128)(2,1)S(1)}, bf16[4,24,512]{2,1,0:T(8,128)(2,1)S(1)}, u32[]{:S(2)}, u32[]{:S(2)}) collective-permute-start(bf16[4,24,512]{2,1,0:T(8,128)(2,1)S(1)} %get-tuple-element.61), channel_id=1, source_target_pairs={{0,2},{1,5},{2,0},{3,7},{4,6},{5,1},{6,4},{7,3},{8,10},{9,13},{10,... | collective-permute-start | bytes 294920 | tf_op jit(solution)/shard_map/ppermute | solution.py:46
  32.3 5.9 %collective-permute-start.14 = (bf16[24,2048]{1,0:T(8,128)(2,1)S(1)}, bf16[24,2048]{1,0:T(8,128)(2,1)S(1)}, u32[]{:S(2)}, u32[]{:S(2)}) collective-permute-start(bf16[24,2048]{1,0:T(8,128)(2,1)S(1)} %get-tuple-element.74), channel_id=1, source_target_pairs={{0,6},{1,3},{2,4},{3,1},{4,2},{5,7},{6,0},{7,5},{8,14},{9,11},{10,... | collective-permute-start | bytes 294920 | tf_op jit(solution)/shard_map/ppermute | solution.py:46
  33.9 6.4 %collective-permute-start.15 = (bf16[24,2048]{1,0:T(8,128)(2,1)S(1)}, bf16[24,2048]{1,0:T(8,128)(2,1)S(1)}, u32[]{:S(2)}, u32[]{:S(2)}) collective-permute-start(bf16[24,2048]{1,0:T(8,128)(2,1)S(1)} %get-tuple-element.75), channel_id=1, source_target_pairs={{0,4},{1,7},{2,6},{3,5},{4,0},{5,3},{6,2},{7,1},{8,12},{9,15},{10,... | collective-permute-start | bytes 294920 | tf_op jit(solution)/shard_map/ppermute | solution.py:46
  34.9 5.4 %collective-permute-start.16 = (bf16[24,2048]{1,0:T(8,128)(2,1)S(1)}, bf16[24,2048]{1,0:T(8,128)(2,1)S(1)}, u32[]{:S(2)}, u32[]{:S(2)}) collective-permute-start(bf16[24,2048]{1,0:T(8,128)(2,1)S(1)} %get-tuple-element.76), channel_id=1, source_target_pairs={{0,2},{1,5},{2,0},{3,7},{4,6},{5,1},{6,4},{7,3},{8,10},{9,13},{10,... | collective-permute-start | bytes 294920 | tf_op jit(solution)/shard_map/ppermute | solution.py:46
  40.3 1.3 %collective-permute-start.17 = (bf16[24,1024]{1,0:T(8,128)(2,1)S(1)}, bf16[24,1024]{1,0:T(8,128)(2,1)S(1)}, u32[]{:S(2)}, u32[]{:S(2)}) collective-permute-start(bf16[24,1024]{1,0:T(8,128)(2,1)S(1)} %get-tuple-element.79), channel_id=1, source_target_pairs={{0,1},{1,0},{2,3},{3,2},{4,5},{5,4},{6,7},{7,6},{8,9},{9,8},{10,11... | collective-permute-start | bytes 147464 | tf_op jit(solution)/shard_map/ppermute | solution.py:19
  41.8 5.8 %collective-permute-start.18 = (bf16[24,512]{1,0:T(8,128)(2,1)S(1)}, bf16[24,512]{1,0:T(8,128)(2,1)S(1)}, u32[]{:S(2)}, u32[]{:S(2)}) collective-permute-start(bf16[24,512]{1,0:T(8,128)(2,1)S(1)} %get-tuple-element.81), channel_id=1, source_target_pairs={{0,24},{8,16},{16,8},{24,0},{1,25},{9,17},{17,9},{25,1},{2,26},{10... | collective-permute-start | bytes 73736 | tf_op jit(solution)/shard_map/ppermute | solution.py:19
  44.7 4.7 %collective-permute-start.19 = (bf16[24,512]{1,0:T(8,128)(2,1)S(1)}, bf16[24,512]{1,0:T(8,128)(2,1)S(1)}, u32[]{:S(2)}, u32[]{:S(2)}) collective-permute-start(bf16[24,512]{1,0:T(8,128)(2,1)S(1)} %get-tuple-element.82), channel_id=1, source_target_pairs={{0,16},{8,24},{16,0},{24,8},{1,17},{9,25},{17,1},{25,9},{2,18},{10... | collective-permute-start | bytes 73736 | tf_op jit(solution)/shard_map/ppermute | solution.py:19
  44.7 4.7 %collective-permute-start.20 = (bf16[24,512]{1,0:T(8,128)(2,1)S(1)}, bf16[24,512]{1,0:T(8,128)(2,1)S(1)}, u32[]{:S(2)}, u32[]{:S(2)}) collective-permute-start(bf16[24,512]{1,0:T(8,128)(2,1)S(1)} %get-tuple-element.83), channel_id=1, source_target_pairs={{0,8},{8,0},{16,24},{24,16},{1,9},{9,1},{17,25},{25,17},{2,10},{10... | collective-permute-start | bytes 73736 | tf_op jit(solution)/shard_map/ppermute | solution.py:19

commit v13 on v11

--- a/solution.py
+++ b/solution.py
@@ -19,16 +19,8 @@
     return lax.ppermute(value, axes, [(i, i ^ step) for i in range(size)])
 
 
-def cross(value, axis, step):
-    size, pools = lax.axis_size(axis), lax.axis_size("pool")
-    pairs = [
-        (i * pools + p, (i ^ step) * pools + (p ^ (step & 1))) for i in range(size) for p in range(pools)
-    ]
-    return lax.ppermute(value, (axis, "pool"), pairs)
-
-
 def part_taken():
-    return lax.axis_index("pool") ^ (lax.axis_index("req") & 1)
+    return lax.axis_index("pool")
 
 
 def dot(a, b, contract=((1,), (0,))):
@@ -434,7 +426,7 @@
         held(send(pieces[1], "head", 1), total),
     )
 
-    arrived = [cross(hidden[step], "req", step) for step in reversed(range(1, planes))] + [hidden[0]]
+    arrived = [send(hidden[step], "req", step) for step in reversed(range(1, planes))] + [hidden[0]]
     marks = []
     for part_arrived in arrived[:-2]:
         marks = [kernel_call(mark_kernel, shape(16, LANES), held(part_arrived, *marks))]

time: 49.2 us -> 48.1 us (0.978)
  waiting for transfers between devices: 19.8 us -> 18.2 us
  starting transfers between devices: 21.6 us -> 22.2 us
    ppermute x18 -> x21, starting transfers between devices: 17.7 us -> 22.2 us  [send(): return lax.ppermute(value, axes, [(i, i ^ step) for i in range(size)])]
    ppermute x3 -> x0, starting transfers between devices: 3.89 us -> none  [cross(): return lax.ppermute(value, (axis, 'pool'), pairs)]
    ppermute x3 -> x0, waiting for transfers between devices: 2.94 us -> none  [cross(): return lax.ppermute(value, (axis, 'pool'), pairs)]
    ppermute x18 -> x21, waiting for transfers between devices: 16.9 us -> 18.2 us  [send(): return lax.ppermute(value, axes, [(i, i ^ step) for i in range(size)])]
  transfers between devices with their start and end apart: 21 -> 21, of which waited for: 13 -> 14; matrix products, arithmetic and copies ran while one was open for 2% -> 2% of each run, Pallas kernels for 7% -> 7%
where the time goes in v13:
time: 48.1 us; the launch traced here: 48 us
  starting transfers between devices  22.2 us (46%)
  waiting for transfers between devices  18.2 us (38%)
  Pallas kernels  6.62 us (14%)
  other arithmetic  0.78 us (2%)
    ppermute x21, starting transfers between devices, send(): return lax.ppermute(value, axes, [(i, i ^ step) for i in range(size)])  22.2 us
    ppermute x21, waiting for transfers between devices, send(): return lax.ppermute(value, axes, [(i, i ^ step) for i in range(size)])  18.2 us
    pallas_call x15, Pallas kernels, kernel_call(): pl.pallas_call(body, out_shape=jax.tree.map(lambda out: pltpu.VMEM(out.sh...  5.99 us
  transfers between devices with their start and end apart: 21, of which 14 were waited for; matrix products, arithmetic and copies ran while one was open for 2% of the time, Pallas kernels for 7%

profile of v13, /device:TPU:0, one launch (start us, length us, event | category | flops | bytes accessed | tf_op | source)
XLA Modules:
  0.0 48.0 jit_solution(14339362511464368418)
XLA Ops:
  0.5 0.8 %pad_add_fusion = s32[104]{0:T(128)S(1)} fusion(s32[4]{0:T(128)} %param.23, s32[4]{0:T(128)} %param.22, s32[48]{0:T(128)} %bitcast.28, s32[48]{0:T(128)} %bitcast.29), kind=kLoop, calls=%fused_computation | loop fusion | flops 312 | bytes 832 | tf_op jit(solution)/shard_map/concatenate | solution.py:339
  1.3 1.9 %shard_map.163 = (bf16[48,2560]{1,0:T(8,128)(2,1)S(1)}, bf16[832,256]{1,0:T(8,128)(2,1)S(1)}, bf16[48,1024]{1,0:T(8,128)(2,1)S(1)}, bf16[512,2048]{1,0:T(8,128)(...) custom-call(bf16[832,256]{1,0:T(8,128)(2,1)} %bitcast.24, ...), custom_call_target="tpu_custom_call" | custom-call | tf_op jit(solution)/shard_map/pallas_call | solution.py:31
  3.3 1.6 %shard_map.164 = (f32[24,2560]{1,0:T(8,128)S(1)}, bf16[24,2560]{1,0:T(8,128)(2,1)S(1)}) custom-call(bf16[48,1024]{1,0:T(8,128)(2,1)S(1)} %get-tuple-element.45.q_ref, bf16[48,2,256]{2,1,0:T(2,128)(2,1)S(1)} %get-tuple-element.46.new_ref, bf16[832,256]{1,0:T(8,128)(2,1)S(1)} %get-tuple-element.47.own_ref, ...), custom_call_target="tpu_custom_call" | custom-call | tf_op jit(solution)/shard_map/pallas_call | solution.py:31
  5.4 1.0 %collective-permute-done.2.other_ref = bf16[24,2560]{1,0:T(8,128)(2,1)S(1)} collective-permute-done((bf16[24,2560]{1,0:T(8,128)(2,1)S(1)}, bf16[24,2560]{1,0:T(8,128)(2,1)S(1)}, u32[]{:S(2)}, u32[]{:S(2)}) %collective-permute-start.2) | collective-permute-done | bytes 122912 | tf_op jit(solution)/shard_map/ppermute | solution.py:19
  6.9 3.9 %collective-permute-start.4 = (bf16[24,640]{1,0:T(8,128)(2,1)S(1)}, bf16[24,640]{1,0:T(8,128)(2,1)S(1)}, u32[]{:S(2)}, u32[]{:S(2)}) collective-permute-start(bf16[24,640]{1,0:T(8,128)(2,1)S(1)} %get-tuple-element.55), channel_id=1, source_target_pairs={{0,6},{2,4},{4,2},{6,0},{1,7},{3,5},{5,3},{7,1},{8,14},{10,12},{12... | collective-permute-start | bytes 92168 | tf_op jit(solution)/shard_map/ppermute | solution.py:19
  11.4 1.2 %collective-permute-done.4.part_ref = bf16[24,640]{1,0:T(8,128)(2,1)S(1)} collective-permute-done((bf16[24,640]{1,0:T(8,128)(2,1)S(1)}, bf16[24,640]{1,0:T(8,128)(2,1)S(1)}, u32[]{:S(2)}, u32[]{:S(2)}) %collective-permute-start.4) | collective-permute-done | bytes 30752 | tf_op jit(solution)/shard_map/ppermute | solution.py:19
  12.7 2.0 %collective-permute-done.5.part_ref = bf16[24,640]{1,0:T(8,128)(2,1)S(1)} collective-permute-done((bf16[24,640]{1,0:T(8,128)(2,1)S(1)}, bf16[24,640]{1,0:T(8,128)(2,1)S(1)}, u32[]{:S(2)}, u32[]{:S(2)}) %collective-permute-start.5) | collective-permute-done | bytes 30752 | tf_op jit(solution)/shard_map/ppermute | solution.py:19
  15.2 3.7 %collective-permute-start.7 = (bf16[24,640]{1,0:T(8,128)(2,1)S(1)}, bf16[24,640]{1,0:T(8,128)(2,1)S(1)}, u32[]{:S(2)}, u32[]{:S(2)}) collective-permute-start(bf16[24,640]{1,0:T(8,128)(2,1)S(1)} %get-tuple-element.58), channel_id=1, source_target_pairs={{0,24},{8,16},{16,8},{24,0},{1,25},{9,17},{17,9},{25,1},{2,26},{10... | collective-permute-start | bytes 92168 | tf_op jit(solution)/shard_map/ppermute | solution.py:19
  18.9 0.8 %collective-permute-start.8 = (bf16[24,640]{1,0:T(8,128)(2,1)S(1)}, bf16[24,640]{1,0:T(8,128)(2,1)S(1)}, u32[]{:S(2)}, u32[]{:S(2)}) collective-permute-start(bf16[24,640]{1,0:T(8,128)(2,1)S(1)} %get-tuple-element.59), channel_id=1, source_target_pairs={{0,8},{8,0},{16,24},{24,16},{1,9},{9,1},{17,25},{25,17},{2,10},{10... | collective-permute-start | bytes 92168 | tf_op jit(solution)/shard_map/ppermute | solution.py:19
  19.7 1.4 %collective-permute-done.7.part_ref.refs_1_ = bf16[24,640]{1,0:T(8,128)(2,1)S(1)} collective-permute-done((bf16[24,640]{1,0:T(8,128)(2,1)S(1)}, bf16[24,640]{1,0:T(8,128)(2,1)S(1)}, u32[]{:S(2)}, u32[]{:S(2)}) %collective-permute-start.7) | collective-permute-done | bytes 30752 | tf_op jit(solution)/shard_map/ppermute | solution.py:19
  21.1 2.6 %collective-permute-done.6.part_ref.refs_2_ = bf16[24,640]{1,0:T(8,128)(2,1)S(1)} collective-permute-done((bf16[24,640]{1,0:T(8,128)(2,1)S(1)}, bf16[24,640]{1,0:T(8,128)(2,1)S(1)}, u32[]{:S(2)}, u32[]{:S(2)}) %collective-permute-start.6) | collective-permute-done | bytes 30752 | tf_op jit(solution)/shard_map/ppermute | solution.py:19
  23.7 1.6 %collective-permute-start.12 = (bf16[4,24,512]{2,1,0:T(8,128)(2,1)S(1)}, bf16[4,24,512]{2,1,0:T(8,128)(2,1)S(1)}, u32[]{:S(2)}, u32[]{:S(2)}) collective-permute-start(bf16[4,24,512]{2,1,0:T(8,128)(2,1)S(1)} %get-tuple-element.61), channel_id=1, source_target_pairs={{0,6},{2,4},{4,2},{6,0},{1,7},{3,5},{5,3},{7,1},{8,14},{10,12},{12... | collective-permute-start | bytes 294920 | tf_op jit(solution)/shard_map/ppermute | solution.py:19
  25.8 1.5 %collective-permute-start.9 = (bf16[4,24,512]{2,1,0:T(8,128)(2,1)S(1)}, bf16[4,24,512]{2,1,0:T(8,128)(2,1)S(1)}, u32[]{:S(2)}, u32[]{:S(2)}) collective-permute-start(bf16[4,24,512]{2,1,0:T(8,128)(2,1)S(1)} %get-tuple-element.61), channel_id=1, source_target_pairs={{0,2},{2,0},{4,6},{6,4},{1,3},{3,1},{5,7},{7,5},{8,10},{10,8},{12,... | collective-permute-start | bytes 294920 | tf_op jit(solution)/shard_map/ppermute | solution.py:19
  27.7 1.6 %collective-permute-done.12.block_ref = bf16[4,24,512]{2,1,0:T(8,128)(2,1)S(1)} collective-permute-done((bf16[4,24,512]{2,1,0:T(8,128)(2,1)S(1)}, bf16[4,24,512]{2,1,0:T(8,128)(2,1)S(1)}, u32[]{:S(2)}, u32[]{:S(2)}) %collective-permute-start.12) | collective-permute-done | bytes 98336 | tf_op jit(solution)/shard_map/ppermute | solution.py:19
  30.7 1.0 %shard_map.175 = (f32[24,2048]{1,0:T(8,128)S(1)}, bf16[24,2048]{1,0:T(8,128)(2,1)S(1)}, bf16[24,2048]{1,0:T(8,128)(2,1)S(1)}, bf16[24,2048]{1,0:T(8,128)(2,1)S(1)}) custom-call(bf16[4,24,512]{2,1,0:T(8,128)(2,1)S(1)} %collective-permute-done.9.block_ref, bf16[384,2048]{1,0:T(8,128)(2,1)S(1)} %bitcast.15, ...), custom_call_target="tpu_custom_call" | custom-call | tf_op jit(solution)/shard_map/pallas_call | solution.py:31
  31.7 2.7 %collective-permute-start.14 = (bf16[24,2048]{1,0:T(8,128)(2,1)S(1)}, bf16[24,2048]{1,0:T(8,128)(2,1)S(1)}, u32[]{:S(2)}, u32[]{:S(2)}) collective-permute-start(bf16[24,2048]{1,0:T(8,128)(2,1)S(1)} %get-tuple-element.74), channel_id=1, source_target_pairs={{0,6},{2,4},{4,2},{6,0},{1,7},{3,5},{5,3},{7,1},{8,14},{10,12},{12... | collective-permute-start | bytes 294920 | tf_op jit(solution)/shard_map/ppermute | solution.py:19
  34.4 0.9 %collective-permute-start.16 = (bf16[24,2048]{1,0:T(8,128)(2,1)S(1)}, bf16[24,2048]{1,0:T(8,128)(2,1)S(1)}, u32[]{:S(2)}, u32[]{:S(2)}) collective-permute-start(bf16[24,2048]{1,0:T(8,128)(2,1)S(1)} %get-tuple-element.76), channel_id=1, source_target_pairs={{0,2},{2,0},{4,6},{6,4},{1,3},{3,1},{5,7},{7,5},{8,10},{10,8},{12,... | collective-permute-start | bytes 294920 | tf_op jit(solution)/shard_map/ppermute | solution.py:19
  35.3 2.0 %collective-permute-done.14.refs_0_ = bf16[24,2048]{1,0:T(8,128)(2,1)S(1)} collective-permute-done((bf16[24,2048]{1,0:T(8,128)(2,1)S(1)}, bf16[24,2048]{1,0:T(8,128)(2,1)S(1)}, u32[]{:S(2)}, u32[]{:S(2)}) %collective-permute-start.14) | collective-permute-done | bytes 98336 | tf_op jit(solution)/shard_map/ppermute | solution.py:19
  37.3 1.7 %collective-permute-done.15.refs_1_ = bf16[24,2048]{1,0:T(8,128)(2,1)S(1)} collective-permute-done((bf16[24,2048]{1,0:T(8,128)(2,1)S(1)}, bf16[24,2048]{1,0:T(8,128)(2,1)S(1)}, u32[]{:S(2)}, u32[]{:S(2)}) %collective-permute-start.15) | collective-permute-done | bytes 98336 | tf_op jit(solution)/shard_map/ppermute | solution.py:19
  39.2 1.2 %collective-permute-done.17.other_ref = bf16[24,1024]{1,0:T(8,128)(2,1)S(1)} collective-permute-done((bf16[24,1024]{1,0:T(8,128)(2,1)S(1)}, bf16[24,1024]{1,0:T(8,128)(2,1)S(1)}, u32[]{:S(2)}, u32[]{:S(2)}) %collective-permute-start.17) | collective-permute-done | bytes 49184 | tf_op jit(solution)/shard_map/ppermute | solution.py:19
  40.6 1.7 %collective-permute-start.18 = (bf16[24,512]{1,0:T(8,128)(2,1)S(1)}, bf16[24,512]{1,0:T(8,128)(2,1)S(1)}, u32[]{:S(2)}, u32[]{:S(2)}) collective-permute-start(bf16[24,512]{1,0:T(8,128)(2,1)S(1)} %get-tuple-element.81), channel_id=1, source_target_pairs={{0,24},{8,16},{16,8},{24,0},{1,25},{9,17},{17,9},{25,1},{2,26},{10... | collective-permute-start | bytes 73736 | tf_op jit(solution)/shard_map/ppermute | solution.py:19
  42.3 0.9 %collective-permute-start.19 = (bf16[24,512]{1,0:T(8,128)(2,1)S(1)}, bf16[24,512]{1,0:T(8,128)(2,1)S(1)}, u32[]{:S(2)}, u32[]{:S(2)}) collective-permute-start(bf16[24,512]{1,0:T(8,128)(2,1)S(1)} %get-tuple-element.82), channel_id=1, source_target_pairs={{0,16},{8,24},{16,0},{24,8},{1,17},{9,25},{17,1},{25,9},{2,18},{10... | collective-permute-start | bytes 73736 | tf_op jit(solution)/shard_map/ppermute | solution.py:19
  43.2 1.8 %collective-permute-start.20 = (bf16[24,512]{1,0:T(8,128)(2,1)S(1)}, bf16[24,512]{1,0:T(8,128)(2,1)S(1)}, u32[]{:S(2)}, u32[]{:S(2)}) collective-permute-start(bf16[24,512]{1,0:T(8,128)(2,1)S(1)} %get-tuple-element.83), channel_id=1, source_target_pairs={{0,8},{8,0},{16,24},{24,16},{1,9},{9,1},{17,25},{25,17},{2,10},{10... | collective-permute-start | bytes 73736 | tf_op jit(solution)/shard_map/ppermute | solution.py:19
  45.1 1.3 %collective-permute-done.18.refs_0_ = bf16[24,512]{1,0:T(8,128)(2,1)S(1)} collective-permute-done((bf16[24,512]{1,0:T(8,128)(2,1)S(1)}, bf16[24,512]{1,0:T(8,128)(2,1)S(1)}, u32[]{:S(2)}, u32[]{:S(2)}) %collective-permute-start.18) | collective-permute-done | bytes 24608 | tf_op jit(solution)/shard_map/ppermute | solution.py:19
  (42 shorter events, 7.1 us)
Async XLA Ops:
  0.0 3.3 %collective-permute-start = (bf16[832,256]{1,0:T(8,128)(2,1)}, bf16[832,256]{1,0:T(8,128)(2,1)S(1)}, u32[]{:S(2)}, u32[]{:S(2)}) collective-permute-start(bf16[832,256]{1,0:T(8,128)(2,1)} %bitcast.23), channel_id=1, source_target_pairs={{0,1},{1,0},{2,3},{3,2},{4,5},{5,4},{6,7},{7,6},{8,9},{9,8},{10,11... | collective-permute-start | bytes 1277960 | tf_op jit(solution)/shard_map/ppermute | solution.py:19
  1.2 2.0 %collective-permute-start.1 = (s32[1,128]{1,0:T(1,128)S(1)}, s32[1,128]{1,0:T(1,128)S(1)}, u32[]{:S(2)}, u32[]{:S(2)}) collective-permute-start(s32[1,128]{1,0:T(1,128)S(1)} %pad_bitcast_fusion.own_ints_ref), channel_id=1, source_target_pairs={{0,1},{1,0},{2,3},{3,2},{4,5},{5,4},{6,7},{7,6},{8,9},{9,8},{10,11... | collective-permute-start | bytes 1544 | tf_op jit(solution)/shard_map/ppermute | solution.py:19
  3.3 3.1 %copy-start = (bf16[1,2,192,2048]{3,2,1,0:T(8,128)(2,1)S(1)}, bf16[1,2,192,2048]{3,2,1,0:T(8,128)(2,1)}, u32[]{:S(2)}) copy-start(bf16[1,2,192,2048]{3,2,1,0:T(8,128)(2,1)} %param.29) | copy-start | bytes 4718596
  3.3 3.5 %copy-start.1 = (bf16[1,192,2048]{2,1,0:T(8,128)(2,1)S(1)}, bf16[1,192,2048]{2,1,0:T(8,128)(2,1)}, u32[]{:S(2)}) copy-start(bf16[1,192,2048]{2,1,0:T(8,128)(2,1)} %param.30) | copy-start | bytes 2359300
  3.3 24.0 %copy-start.2 = (f32[2048]{0:T(1024)S(1)}, f32[2048]{0:T(1024)}, u32[]{:S(2)}) copy-start(f32[2048]{0:T(1024)} %param.25) | copy-start | bytes 24580
  4.9 1.5 %collective-permute-start.2 = (bf16[24,2560]{1,0:T(8,128)(2,1)S(1)}, bf16[24,2560]{1,0:T(8,128)(2,1)S(1)}, u32[]{:S(2)}, u32[]{:S(2)}) collective-permute-start(bf16[24,2560]{1,0:T(8,128)(2,1)S(1)} %get-tuple-element.52), channel_id=1, source_target_pairs={{0,1},{1,0},{2,3},{3,2},{4,5},{5,4},{6,7},{7,6},{8,9},{9,8},{10,11... | collective-permute-start | bytes 368648 | tf_op jit(solution)/shard_map/ppermute | solution.py:19
  6.4 20.9 %collective-permute-start.10 = (bf16[384,2048]{1,0:T(8,128)(2,1)S(1)}, bf16[384,2048]{1,0:T(8,128)(2,1)S(1)}, u32[]{:S(2)}, u32[]{:S(2)}) collective-permute-start(bf16[384,2048]{1,0:T(8,128)(2,1)S(1)} %bitcast.11), channel_id=1, source_target_pairs={{0,1},{1,0},{2,3},{3,2},{4,5},{5,4},{6,7},{7,6},{8,9},{9,8},{10,11... | collective-permute-start | bytes 4718600 | tf_op jit(solution)/shard_map/ppermute | solution.py:19
  6.8 24.0 %collective-permute-start.13 = (bf16[192,2048]{1,0:T(8,128)(2,1)S(1)}, bf16[192,2048]{1,0:T(8,128)(2,1)S(1)}, u32[]{:S(2)}, u32[]{:S(2)}) collective-permute-start(bf16[192,2048]{1,0:T(8,128)(2,1)S(1)} %bitcast.16), channel_id=1, source_target_pairs={{0,1},{1,0},{2,3},{3,2},{4,5},{5,4},{6,7},{7,6},{8,9},{9,8},{10,11... | collective-permute-start | bytes 2359304 | tf_op jit(solution)/shard_map/ppermute | solution.py:19
  6.9 5.7 %collective-permute-start.4 = (bf16[24,640]{1,0:T(8,128)(2,1)S(1)}, bf16[24,640]{1,0:T(8,128)(2,1)S(1)}, u32[]{:S(2)}, u32[]{:S(2)}) collective-permute-start(bf16[24,640]{1,0:T(8,128)(2,1)S(1)} %get-tuple-element.55), channel_id=1, source_target_pairs={{0,6},{2,4},{4,2},{6,0},{1,7},{3,5},{5,3},{7,1},{8,14},{10,12},{12... | collective-permute-start | bytes 92168 | tf_op jit(solution)/shard_map/ppermute | solution.py:19
  10.8 3.9 %collective-permute-start.5 = (bf16[24,640]{1,0:T(8,128)(2,1)S(1)}, bf16[24,640]{1,0:T(8,128)(2,1)S(1)}, u32[]{:S(2)}, u32[]{:S(2)}) collective-permute-start(bf16[24,640]{1,0:T(8,128)(2,1)S(1)} %get-tuple-element.56), channel_id=1, source_target_pairs={{0,4},{2,6},{4,0},{6,2},{1,5},{3,7},{5,1},{7,3},{8,12},{10,14},{12... | collective-permute-start | bytes 92168 | tf_op jit(solution)/shard_map/ppermute | solution.py:19
  11.3 3.9 %collective-permute-start.3 = (bf16[24,640]{1,0:T(8,128)(2,1)S(1)}, bf16[24,640]{1,0:T(8,128)(2,1)S(1)}, u32[]{:S(2)}, u32[]{:S(2)}) collective-permute-start(bf16[24,640]{1,0:T(8,128)(2,1)S(1)} %get-tuple-element.53), channel_id=1, source_target_pairs={{0,2},{2,0},{4,6},{6,4},{1,3},{3,1},{5,7},{7,5},{8,10},{10,8},{12,... | collective-permute-start | bytes 92168 | tf_op jit(solution)/shard_map/ppermute | solution.py:19
  15.2 5.9 %collective-permute-start.7 = (bf16[24,640]{1,0:T(8,128)(2,1)S(1)}, bf16[24,640]{1,0:T(8,128)(2,1)S(1)}, u32[]{:S(2)}, u32[]{:S(2)}) collective-permute-start(bf16[24,640]{1,0:T(8,128)(2,1)S(1)} %get-tuple-element.58), channel_id=1, source_target_pairs={{0,24},{8,16},{16,8},{24,0},{1,25},{9,17},{17,9},{25,1},{2,26},{10... | collective-permute-start | bytes 92168 | tf_op jit(solution)/shard_map/ppermute | solution.py:19
  18.9 4.8 %collective-permute-start.6 = (bf16[24,640]{1,0:T(8,128)(2,1)S(1)}, bf16[24,640]{1,0:T(8,128)(2,1)S(1)}, u32[]{:S(2)}, u32[]{:S(2)}) collective-permute-start(bf16[24,640]{1,0:T(8,128)(2,1)S(1)} %get-tuple-element.57), channel_id=1, source_target_pairs={{0,16},{8,24},{16,0},{24,8},{1,17},{9,25},{17,1},{25,9},{2,18},{10... | collective-permute-start | bytes 92168 | tf_op jit(solution)/shard_map/ppermute | solution.py:19
  18.9 4.8 %collective-permute-start.8 = (bf16[24,640]{1,0:T(8,128)(2,1)S(1)}, bf16[24,640]{1,0:T(8,128)(2,1)S(1)}, u32[]{:S(2)}, u32[]{:S(2)}) collective-permute-start(bf16[24,640]{1,0:T(8,128)(2,1)S(1)} %get-tuple-element.59), channel_id=1, source_target_pairs={{0,8},{8,0},{16,24},{24,16},{1,9},{9,1},{17,25},{25,17},{2,10},{10... | collective-permute-start | bytes 92168 | tf_op jit(solution)/shard_map/ppermute | solution.py:19
  23.7 5.6 %collective-permute-start.12 = (bf16[4,24,512]{2,1,0:T(8,128)(2,1)S(1)}, bf16[4,24,512]{2,1,0:T(8,128)(2,1)S(1)}, u32[]{:S(2)}, u32[]{:S(2)}) collective-permute-start(bf16[4,24,512]{2,1,0:T(8,128)(2,1)S(1)} %get-tuple-element.61), channel_id=1, source_target_pairs={{0,6},{2,4},{4,2},{6,0},{1,7},{3,5},{5,3},{7,1},{8,14},{10,12},{12... | collective-permute-start | bytes 294920 | tf_op jit(solution)/shard_map/ppermute | solution.py:19
  25.3 5.1 %collective-permute-start.11 = (bf16[4,24,512]{2,1,0:T(8,128)(2,1)S(1)}, bf16[4,24,512]{2,1,0:T(8,128)(2,1)S(1)}, u32[]{:S(2)}, u32[]{:S(2)}) collective-permute-start(bf16[4,24,512]{2,1,0:T(8,128)(2,1)S(1)} %get-tuple-element.61), channel_id=1, source_target_pairs={{0,4},{2,6},{4,0},{6,2},{1,5},{3,7},{5,1},{7,3},{8,12},{10,14},{12... | collective-permute-start | bytes 294920 | tf_op jit(solution)/shard_map/ppermute | solution.py:19
  25.8 5.0 %collective-permute-start.9 = (bf16[4,24,512]{2,1,0:T(8,128)(2,1)S(1)}, bf16[4,24,512]{2,1,0:T(8,128)(2,1)S(1)}, u32[]{:S(2)}, u32[]{:S(2)}) collective-permute-start(bf16[4,24,512]{2,1,0:T(8,128)(2,1)S(1)} %get-tuple-element.61), channel_id=1, source_target_pairs={{0,2},{2,0},{4,6},{6,4},{1,3},{3,1},{5,7},{7,5},{8,10},{10,8},{12,... | collective-permute-start | bytes 294920 | tf_op jit(solution)/shard_map/ppermute | solution.py:19
  31.7 5.6 %collective-permute-start.14 = (bf16[24,2048]{1,0:T(8,128)(2,1)S(1)}, bf16[24,2048]{1,0:T(8,128)(2,1)S(1)}, u32[]{:S(2)}, u32[]{:S(2)}) collective-permute-start(bf16[24,2048]{1,0:T(8,128)(2,1)S(1)} %get-tuple-element.74), channel_id=1, source_target_pairs={{0,6},{2,4},{4,2},{6,0},{1,7},{3,5},{5,3},{7,1},{8,14},{10,12},{12... | collective-permute-start | bytes 294920 | tf_op jit(solution)/shard_map/ppermute | solution.py:19
  34.4 4.6 %collective-permute-start.15 = (bf16[24,2048]{1,0:T(8,128)(2,1)S(1)}, bf16[24,2048]{1,0:T(8,128)(2,1)S(1)}, u32[]{:S(2)}, u32[]{:S(2)}) collective-permute-start(bf16[24,2048]{1,0:T(8,128)(2,1)S(1)} %get-tuple-element.75), channel_id=1, source_target_pairs={{0,4},{2,6},{4,0},{6,2},{1,5},{3,7},{5,1},{7,3},{8,12},{10,14},{12... | collective-permute-start | bytes 294920 | tf_op jit(solution)/shard_map/ppermute | solution.py:19
  34.4 4.6 %collective-permute-start.16 = (bf16[24,2048]{1,0:T(8,128)(2,1)S(1)}, bf16[24,2048]{1,0:T(8,128)(2,1)S(1)}, u32[]{:S(2)}, u32[]{:S(2)}) collective-permute-start(bf16[24,2048]{1,0:T(8,128)(2,1)S(1)} %get-tuple-element.76), channel_id=1, source_target_pairs={{0,2},{2,0},{4,6},{6,4},{1,3},{3,1},{5,7},{7,5},{8,10},{10,8},{12,... | collective-permute-start | bytes 294920 | tf_op jit(solution)/shard_map/ppermute | solution.py:19
  39.1 1.3 %collective-permute-start.17 = (bf16[24,1024]{1,0:T(8,128)(2,1)S(1)}, bf16[24,1024]{1,0:T(8,128)(2,1)S(1)}, u32[]{:S(2)}, u32[]{:S(2)}) collective-permute-start(bf16[24,1024]{1,0:T(8,128)(2,1)S(1)} %get-tuple-element.79), channel_id=1, source_target_pairs={{0,1},{1,0},{2,3},{3,2},{4,5},{5,4},{6,7},{7,6},{8,9},{9,8},{10,11... | collective-permute-start | bytes 147464 | tf_op jit(solution)/shard_map/ppermute | solution.py:19
  40.6 5.7 %collective-permute-start.18 = (bf16[24,512]{1,0:T(8,128)(2,1)S(1)}, bf16[24,512]{1,0:T(8,128)(2,1)S(1)}, u32[]{:S(2)}, u32[]{:S(2)}) collective-permute-start(bf16[24,512]{1,0:T(8,128)(2,1)S(1)} %get-tuple-element.81), channel_id=1, source_target_pairs={{0,24},{8,16},{16,8},{24,0},{1,25},{9,17},{17,9},{25,1},{2,26},{10... | collective-permute-start | bytes 73736 | tf_op jit(solution)/shard_map/ppermute | solution.py:19
  42.3 4.8 %collective-permute-start.19 = (bf16[24,512]{1,0:T(8,128)(2,1)S(1)}, bf16[24,512]{1,0:T(8,128)(2,1)S(1)}, u32[]{:S(2)}, u32[]{:S(2)}) collective-permute-start(bf16[24,512]{1,0:T(8,128)(2,1)S(1)} %get-tuple-element.82), channel_id=1, source_target_pairs={{0,16},{8,24},{16,0},{24,8},{1,17},{9,25},{17,1},{25,9},{2,18},{10... | collective-permute-start | bytes 73736 | tf_op jit(solution)/shard_map/ppermute | solution.py:19
  43.2 4.1 %collective-permute-start.20 = (bf16[24,512]{1,0:T(8,128)(2,1)S(1)}, bf16[24,512]{1,0:T(8,128)(2,1)S(1)}, u32[]{:S(2)}, u32[]{:S(2)}) collective-permute-start(bf16[24,512]{1,0:T(8,128)(2,1)S(1)} %get-tuple-element.83), channel_id=1, source_target_pairs={{0,8},{8,0},{16,24},{24,16},{1,9},{9,1},{17,25},{25,17},{2,10},{10... | collective-permute-start | bytes 73736 | tf_op jit(solution)/shard_map/ppermute | solution.py:19

commit v14 on v9

--- a/solution.py
+++ b/solution.py
@@ -393,14 +393,14 @@
         args,
     )
     other = send(other, "pool", 1)
-    ready = lax.optimization_barrier((gate_up, down_weight, other))
-    other_up, other_down = send(ready[0], "pool", 1), send(ready[1], "pool", 1)
     piece = shape(rows, columns + mixes)
     pieces = kernel_call(
         split_kernel,
         [shape(rows, columns + mixes, dtype=F32)] + [piece] * (heads - 1),
         held(own, other),
     )
+    ready = lax.optimization_barrier((gate_up, down_weight, pieces[1]))
+    other_up, other_down = send(ready[0], "pool", 1), send(ready[1], "pool", 1)
     total = pieces[0]
     for step in reversed(range(2, heads)):
         total = kernel_call(

time: 48.2 us -> 48.2 us (level)
  no operation moved by 1% of the time
where the time goes in v14:
time: 48.2 us; the launch traced here: 48 us
  starting transfers between devices  22.1 us (46%)
  waiting for transfers between devices  18.3 us (38%)
  Pallas kernels  6.1 us (13%)
  other arithmetic  0.78 us (2%)
  local copies, waits for them, and re-layouts  0.64 us (1%)
    ppermute x21, starting transfers between devices, send(): return lax.ppermute(value, axes, [(i, i ^ step) for i in range(size)])  22.1 us
    ppermute x21, waiting for transfers between devices, send(): return lax.ppermute(value, axes, [(i, i ^ step) for i in range(size)])  18.3 us
    pallas_call x17, Pallas kernels, kernel_call(): pl.pallas_call(body, out_shape=jax.tree.map(lambda out: pltpu.VMEM(out.sh...  6.1 us
  transfers between devices with their start and end apart: 21, of which 15 were waited for; matrix products, arithmetic and copies ran while one was open for 2% of the time, Pallas kernels for 7%

profile of v14, /device:TPU:0, one launch (start us, length us, event | category | flops | bytes accessed | tf_op | source)
XLA Modules:
  0.0 48.0 jit_solution(13010135945729858338)
XLA Ops:
  0.5 0.8 %pad_add_fusion = s32[104]{0:T(128)S(1)} fusion(s32[4]{0:T(128)} %param.23, s32[4]{0:T(128)} %param.22, s32[48]{0:T(128)} %bitcast.28, s32[48]{0:T(128)} %bitcast.29), kind=kLoop, calls=%fused_computation | loop fusion | flops 312 | bytes 832 | tf_op jit(solution)/shard_map/concatenate | solution.py:327
  1.3 1.9 %shard_map.163 = (bf16[48,2560]{1,0:T(8,128)(2,1)S(1)}, bf16[832,256]{1,0:T(8,128)(2,1)S(1)}, bf16[48,1024]{1,0:T(8,128)(2,1)S(1)}, bf16[512,2048]{1,0:T(8,128)(...) custom-call(bf16[832,256]{1,0:T(8,128)(2,1)} %bitcast.24, ...), custom_call_target="tpu_custom_call" | custom-call | tf_op jit(solution)/shard_map/pallas_call | solution.py:27
  3.3 1.6 %shard_map.164 = (f32[24,2560]{1,0:T(8,128)S(1)}, bf16[24,2560]{1,0:T(8,128)(2,1)S(1)}) custom-call(bf16[48,1024]{1,0:T(8,128)(2,1)S(1)} %get-tuple-element.47.q_ref, bf16[48,2,256]{2,1,0:T(2,128)(2,1)S(1)} %get-tuple-element.48.new_ref, bf16[832,256]{1,0:T(8,128)(2,1)S(1)} %get-tuple-element.49.own_ref, ...), custom_call_target="tpu_custom_call" | custom-call | tf_op jit(solution)/shard_map/pallas_call | solution.py:27
  5.4 1.0 %collective-permute-done.2.other_ref = bf16[24,2560]{1,0:T(8,128)(2,1)S(1)} collective-permute-done((bf16[24,2560]{1,0:T(8,128)(2,1)S(1)}, bf16[24,2560]{1,0:T(8,128)(2,1)S(1)}, u32[]{:S(2)}, u32[]{:S(2)}) %collective-permute-start.2) | collective-permute-done | bytes 122912 | tf_op jit(solution)/shard_map/ppermute | solution.py:19
  7.0 3.8 %collective-permute-start.4 = (bf16[24,640]{1,0:T(8,128)(2,1)S(1)}, bf16[24,640]{1,0:T(8,128)(2,1)S(1)}, u32[]{:S(2)}, u32[]{:S(2)}) collective-permute-start(bf16[24,640]{1,0:T(8,128)(2,1)S(1)} %get-tuple-element.57), channel_id=1, source_target_pairs={{0,6},{2,4},{4,2},{6,0},{1,7},{3,5},{5,3},{7,1},{8,14},{10,12},{12... | collective-permute-start | bytes 92168 | tf_op jit(solution)/shard_map/ppermute | solution.py:19
  11.4 1.3 %collective-permute-done.4.part_ref = bf16[24,640]{1,0:T(8,128)(2,1)S(1)} collective-permute-done((bf16[24,640]{1,0:T(8,128)(2,1)S(1)}, bf16[24,640]{1,0:T(8,128)(2,1)S(1)}, u32[]{:S(2)}, u32[]{:S(2)}) %collective-permute-start.4) | collective-permute-done | bytes 30752 | tf_op jit(solution)/shard_map/ppermute | solution.py:19
  12.7 2.0 %collective-permute-done.5.part_ref = bf16[24,640]{1,0:T(8,128)(2,1)S(1)} collective-permute-done((bf16[24,640]{1,0:T(8,128)(2,1)S(1)}, bf16[24,640]{1,0:T(8,128)(2,1)S(1)}, u32[]{:S(2)}, u32[]{:S(2)}) %collective-permute-start.5) | collective-permute-done | bytes 30752 | tf_op jit(solution)/shard_map/ppermute | solution.py:19
  15.2 3.7 %collective-permute-start.7 = (bf16[24,640]{1,0:T(8,128)(2,1)S(1)}, bf16[24,640]{1,0:T(8,128)(2,1)S(1)}, u32[]{:S(2)}, u32[]{:S(2)}) collective-permute-start(bf16[24,640]{1,0:T(8,128)(2,1)S(1)} %get-tuple-element.60), channel_id=1, source_target_pairs={{0,24},{8,16},{16,8},{24,0},{1,25},{9,17},{17,9},{25,1},{2,26},{10... | collective-permute-start | bytes 92168 | tf_op jit(solution)/shard_map/ppermute | solution.py:19
  18.9 0.8 %collective-permute-start.8 = (bf16[24,640]{1,0:T(8,128)(2,1)S(1)}, bf16[24,640]{1,0:T(8,128)(2,1)S(1)}, u32[]{:S(2)}, u32[]{:S(2)}) collective-permute-start(bf16[24,640]{1,0:T(8,128)(2,1)S(1)} %get-tuple-element.61), channel_id=1, source_target_pairs={{0,8},{8,0},{16,24},{24,16},{1,9},{9,1},{17,25},{25,17},{2,10},{10... | collective-permute-start | bytes 92168 | tf_op jit(solution)/shard_map/ppermute | solution.py:19
  19.7 1.4 %collective-permute-done.7.part_ref.refs_1_ = bf16[24,640]{1,0:T(8,128)(2,1)S(1)} collective-permute-done((bf16[24,640]{1,0:T(8,128)(2,1)S(1)}, bf16[24,640]{1,0:T(8,128)(2,1)S(1)}, u32[]{:S(2)}, u32[]{:S(2)}) %collective-permute-start.7) | collective-permute-done | bytes 30752 | tf_op jit(solution)/shard_map/ppermute | solution.py:19
  21.1 2.6 %collective-permute-done.6.part_ref.refs_2_ = bf16[24,640]{1,0:T(8,128)(2,1)S(1)} collective-permute-done((bf16[24,640]{1,0:T(8,128)(2,1)S(1)}, bf16[24,640]{1,0:T(8,128)(2,1)S(1)}, u32[]{:S(2)}, u32[]{:S(2)}) %collective-permute-start.6) | collective-permute-done | bytes 30752 | tf_op jit(solution)/shard_map/ppermute | solution.py:19
  23.7 1.6 %collective-permute-start.12 = (bf16[4,24,512]{2,1,0:T(8,128)(2,1)S(1)}, bf16[4,24,512]{2,1,0:T(8,128)(2,1)S(1)}, u32[]{:S(2)}, u32[]{:S(2)}) collective-permute-start(bf16[4,24,512]{2,1,0:T(8,128)(2,1)S(1)} %get-tuple-element.63), channel_id=1, source_target_pairs={{0,6},{2,4},{4,2},{6,0},{1,7},{3,5},{5,3},{7,1},{8,14},{10,12},{12... | collective-permute-start | bytes 294920 | tf_op jit(solution)/shard_map/ppermute | solution.py:19
  25.8 1.5 %collective-permute-start.9 = (bf16[4,24,512]{2,1,0:T(8,128)(2,1)S(1)}, bf16[4,24,512]{2,1,0:T(8,128)(2,1)S(1)}, u32[]{:S(2)}, u32[]{:S(2)}) collective-permute-start(bf16[4,24,512]{2,1,0:T(8,128)(2,1)S(1)} %get-tuple-element.63), channel_id=1, source_target_pairs={{0,2},{2,0},{4,6},{6,4},{1,3},{3,1},{5,7},{7,5},{8,10},{10,8},{12,... | collective-permute-start | bytes 294920 | tf_op jit(solution)/shard_map/ppermute | solution.py:19
  27.7 1.6 %collective-permute-done.12.block_ref = bf16[4,24,512]{2,1,0:T(8,128)(2,1)S(1)} collective-permute-done((bf16[4,24,512]{2,1,0:T(8,128)(2,1)S(1)}, bf16[4,24,512]{2,1,0:T(8,128)(2,1)S(1)}, u32[]{:S(2)}, u32[]{:S(2)}) %collective-permute-start.12) | collective-permute-done | bytes 98336 | tf_op jit(solution)/shard_map/ppermute | solution.py:19
  31.8 2.6 %collective-permute-start.14 = (bf16[24,2048]{1,0:T(8,128)(2,1)S(1)}, bf16[24,2048]{1,0:T(8,128)(2,1)S(1)}, u32[]{:S(2)}, u32[]{:S(2)}) collective-permute-start(bf16[24,2048]{1,0:T(8,128)(2,1)S(1)} %get-tuple-element.78), channel_id=1, source_target_pairs={{0,6},{2,4},{4,2},{6,0},{1,7},{3,5},{5,3},{7,1},{8,14},{10,12},{12... | collective-permute-start | bytes 294920 | tf_op jit(solution)/shard_map/ppermute | solution.py:19
  34.5 0.9 %collective-permute-start.16 = (bf16[24,2048]{1,0:T(8,128)(2,1)S(1)}, bf16[24,2048]{1,0:T(8,128)(2,1)S(1)}, u32[]{:S(2)}, u32[]{:S(2)}) collective-permute-start(bf16[24,2048]{1,0:T(8,128)(2,1)S(1)} %get-tuple-element.80), channel_id=1, source_target_pairs={{0,2},{2,0},{4,6},{6,4},{1,3},{3,1},{5,7},{7,5},{8,10},{10,8},{12,... | collective-permute-start | bytes 294920 | tf_op jit(solution)/shard_map/ppermute | solution.py:19
  35.4 2.0 %collective-permute-done.14.refs_0_ = bf16[24,2048]{1,0:T(8,128)(2,1)S(1)} collective-permute-done((bf16[24,2048]{1,0:T(8,128)(2,1)S(1)}, bf16[24,2048]{1,0:T(8,128)(2,1)S(1)}, u32[]{:S(2)}, u32[]{:S(2)}) %collective-permute-start.14) | collective-permute-done | bytes 98336 | tf_op jit(solution)/shard_map/ppermute | solution.py:19
  37.4 1.6 %collective-permute-done.15.refs_1_ = bf16[24,2048]{1,0:T(8,128)(2,1)S(1)} collective-permute-done((bf16[24,2048]{1,0:T(8,128)(2,1)S(1)}, bf16[24,2048]{1,0:T(8,128)(2,1)S(1)}, u32[]{:S(2)}, u32[]{:S(2)}) %collective-permute-start.15) | collective-permute-done | bytes 98336 | tf_op jit(solution)/shard_map/ppermute | solution.py:19
  39.2 1.2 %collective-permute-done.17.other_ref = bf16[24,1024]{1,0:T(8,128)(2,1)S(1)} collective-permute-done((bf16[24,1024]{1,0:T(8,128)(2,1)S(1)}, bf16[24,1024]{1,0:T(8,128)(2,1)S(1)}, u32[]{:S(2)}, u32[]{:S(2)}) %collective-permute-start.17) | collective-permute-done | bytes 49184 | tf_op jit(solution)/shard_map/ppermute | solution.py:19
  40.6 1.8 %collective-permute-start.18 = (bf16[24,512]{1,0:T(8,128)(2,1)S(1)}, bf16[24,512]{1,0:T(8,128)(2,1)S(1)}, u32[]{:S(2)}, u32[]{:S(2)}) collective-permute-start(bf16[24,512]{1,0:T(8,128)(2,1)S(1)} %get-tuple-element.85), channel_id=1, source_target_pairs={{0,24},{8,16},{16,8},{24,0},{1,25},{9,17},{17,9},{25,1},{2,26},{10... | collective-permute-start | bytes 73736 | tf_op jit(solution)/shard_map/ppermute | solution.py:19
  42.4 0.9 %collective-permute-start.19 = (bf16[24,512]{1,0:T(8,128)(2,1)S(1)}, bf16[24,512]{1,0:T(8,128)(2,1)S(1)}, u32[]{:S(2)}, u32[]{:S(2)}) collective-permute-start(bf16[24,512]{1,0:T(8,128)(2,1)S(1)} %get-tuple-element.86), channel_id=1, source_target_pairs={{0,16},{8,24},{16,0},{24,8},{1,17},{9,25},{17,1},{25,9},{2,18},{10... | collective-permute-start | bytes 73736 | tf_op jit(solution)/shard_map/ppermute | solution.py:19
  43.3 1.8 %collective-permute-start.20 = (bf16[24,512]{1,0:T(8,128)(2,1)S(1)}, bf16[24,512]{1,0:T(8,128)(2,1)S(1)}, u32[]{:S(2)}, u32[]{:S(2)}) collective-permute-start(bf16[24,512]{1,0:T(8,128)(2,1)S(1)} %get-tuple-element.87), channel_id=1, source_target_pairs={{0,8},{8,0},{16,24},{24,16},{1,9},{9,1},{17,25},{25,17},{2,10},{10... | collective-permute-start | bytes 73736 | tf_op jit(solution)/shard_map/ppermute | solution.py:19
  45.1 1.3 %collective-permute-done.18.refs_0_ = bf16[24,512]{1,0:T(8,128)(2,1)S(1)} collective-permute-done((bf16[24,512]{1,0:T(8,128)(2,1)S(1)}, bf16[24,512]{1,0:T(8,128)(2,1)S(1)}, u32[]{:S(2)}, u32[]{:S(2)}) %collective-permute-start.18) | collective-permute-done | bytes 24608 | tf_op jit(solution)/shard_map/ppermute | solution.py:19
  46.4 0.8 %collective-permute-done.19.refs_1_ = bf16[24,512]{1,0:T(8,128)(2,1)S(1)} collective-permute-done((bf16[24,512]{1,0:T(8,128)(2,1)S(1)}, bf16[24,512]{1,0:T(8,128)(2,1)S(1)}, u32[]{:S(2)}, u32[]{:S(2)}) %collective-permute-start.19) | collective-permute-done | bytes 24608 | tf_op jit(solution)/shard_map/ppermute | solution.py:19
  (44 shorter events, 7.4 us)
Async XLA Ops:
  0.0 3.3 %collective-permute-start = (bf16[832,256]{1,0:T(8,128)(2,1)}, bf16[832,256]{1,0:T(8,128)(2,1)S(1)}, u32[]{:S(2)}, u32[]{:S(2)}) collective-permute-start(bf16[832,256]{1,0:T(8,128)(2,1)} %bitcast.23), channel_id=1, source_target_pairs={{0,1},{1,0},{2,3},{3,2},{4,5},{5,4},{6,7},{7,6},{8,9},{9,8},{10,11... | collective-permute-start | bytes 1277960 | tf_op jit(solution)/shard_map/ppermute | solution.py:19
  1.2 2.0 %collective-permute-start.1 = (s32[1,128]{1,0:T(1,128)S(1)}, s32[1,128]{1,0:T(1,128)S(1)}, u32[]{:S(2)}, u32[]{:S(2)}) collective-permute-start(s32[1,128]{1,0:T(1,128)S(1)} %pad_bitcast_fusion.own_ints_ref), channel_id=1, source_target_pairs={{0,1},{1,0},{2,3},{3,2},{4,5},{5,4},{6,7},{7,6},{8,9},{9,8},{10,11... | collective-permute-start | bytes 1544 | tf_op jit(solution)/shard_map/ppermute | solution.py:19
  3.3 3.2 %copy-start = (bf16[1,2,192,2048]{3,2,1,0:T(8,128)(2,1)S(1)}, bf16[1,2,192,2048]{3,2,1,0:T(8,128)(2,1)}, u32[]{:S(2)}) copy-start(bf16[1,2,192,2048]{3,2,1,0:T(8,128)(2,1)} %param.29) | copy-start | bytes 4718596
  3.3 3.6 %copy-start.1 = (bf16[1,192,2048]{2,1,0:T(8,128)(2,1)S(1)}, bf16[1,192,2048]{2,1,0:T(8,128)(2,1)}, u32[]{:S(2)}) copy-start(bf16[1,192,2048]{2,1,0:T(8,128)(2,1)} %param.30) | copy-start | bytes 2359300
  3.3 24.0 %copy-start.2 = (f32[2048]{0:T(1024)S(1)}, f32[2048]{0:T(1024)}, u32[]{:S(2)}) copy-start(f32[2048]{0:T(1024)} %param.25) | copy-start | bytes 24580
  4.9 1.5 %collective-permute-start.2 = (bf16[24,2560]{1,0:T(8,128)(2,1)S(1)}, bf16[24,2560]{1,0:T(8,128)(2,1)S(1)}, u32[]{:S(2)}, u32[]{:S(2)}) collective-permute-start(bf16[24,2560]{1,0:T(8,128)(2,1)S(1)} %get-tuple-element.54), channel_id=1, source_target_pairs={{0,1},{1,0},{2,3},{3,2},{4,5},{5,4},{6,7},{7,6},{8,9},{9,8},{10,11... | collective-permute-start | bytes 368648 | tf_op jit(solution)/shard_map/ppermute | solution.py:19
  6.4 20.8 %collective-permute-start.10 = (bf16[384,2048]{1,0:T(8,128)(2,1)S(1)}, bf16[384,2048]{1,0:T(8,128)(2,1)S(1)}, u32[]{:S(2)}, u32[]{:S(2)}) collective-permute-start(bf16[384,2048]{1,0:T(8,128)(2,1)S(1)} %bitcast.11), channel_id=1, source_target_pairs={{0,1},{1,0},{2,3},{3,2},{4,5},{5,4},{6,7},{7,6},{8,9},{9,8},{10,11... | collective-permute-start | bytes 4718600 | tf_op jit(solution)/shard_map/ppermute | solution.py:19
  6.9 24.3 %collective-permute-start.13 = (bf16[192,2048]{1,0:T(8,128)(2,1)S(1)}, bf16[192,2048]{1,0:T(8,128)(2,1)S(1)}, u32[]{:S(2)}, u32[]{:S(2)}) collective-permute-start(bf16[192,2048]{1,0:T(8,128)(2,1)S(1)} %bitcast.16), channel_id=1, source_target_pairs={{0,1},{1,0},{2,3},{3,2},{4,5},{5,4},{6,7},{7,6},{8,9},{9,8},{10,11... | collective-permute-start | bytes 2359304 | tf_op jit(solution)/shard_map/ppermute | solution.py:19
  7.0 5.7 %collective-permute-start.4 = (bf16[24,640]{1,0:T(8,128)(2,1)S(1)}, bf16[24,640]{1,0:T(8,128)(2,1)S(1)}, u32[]{:S(2)}, u32[]{:S(2)}) collective-permute-start(bf16[24,640]{1,0:T(8,128)(2,1)S(1)} %get-tuple-element.57), channel_id=1, source_target_pairs={{0,6},{2,4},{4,2},{6,0},{1,7},{3,5},{5,3},{7,1},{8,14},{10,12},{12... | collective-permute-start | bytes 92168 | tf_op jit(solution)/shard_map/ppermute | solution.py:19
  10.8 3.9 %collective-permute-start.5 = (bf16[24,640]{1,0:T(8,128)(2,1)S(1)}, bf16[24,640]{1,0:T(8,128)(2,1)S(1)}, u32[]{:S(2)}, u32[]{:S(2)}) collective-permute-start(bf16[24,640]{1,0:T(8,128)(2,1)S(1)} %get-tuple-element.58), channel_id=1, source_target_pairs={{0,4},{2,6},{4,0},{6,2},{1,5},{3,7},{5,1},{7,3},{8,12},{10,14},{12... | collective-permute-start | bytes 92168 | tf_op jit(solution)/shard_map/ppermute | solution.py:19
  11.3 3.9 %collective-permute-start.3 = (bf16[24,640]{1,0:T(8,128)(2,1)S(1)}, bf16[24,640]{1,0:T(8,128)(2,1)S(1)}, u32[]{:S(2)}, u32[]{:S(2)}) collective-permute-start(bf16[24,640]{1,0:T(8,128)(2,1)S(1)} %get-tuple-element.55), channel_id=1, source_target_pairs={{0,2},{2,0},{4,6},{6,4},{1,3},{3,1},{5,7},{7,5},{8,10},{10,8},{12,... | collective-permute-start | bytes 92168 | tf_op jit(solution)/shard_map/ppermute | solution.py:19
  15.2 5.9 %collective-permute-start.7 = (bf16[24,640]{1,0:T(8,128)(2,1)S(1)}, bf16[24,640]{1,0:T(8,128)(2,1)S(1)}, u32[]{:S(2)}, u32[]{:S(2)}) collective-permute-start(bf16[24,640]{1,0:T(8,128)(2,1)S(1)} %get-tuple-element.60), channel_id=1, source_target_pairs={{0,24},{8,16},{16,8},{24,0},{1,25},{9,17},{17,9},{25,1},{2,26},{10... | collective-permute-start | bytes 92168 | tf_op jit(solution)/shard_map/ppermute | solution.py:19
  18.9 4.8 %collective-permute-start.6 = (bf16[24,640]{1,0:T(8,128)(2,1)S(1)}, bf16[24,640]{1,0:T(8,128)(2,1)S(1)}, u32[]{:S(2)}, u32[]{:S(2)}) collective-permute-start(bf16[24,640]{1,0:T(8,128)(2,1)S(1)} %get-tuple-element.59), channel_id=1, source_target_pairs={{0,16},{8,24},{16,0},{24,8},{1,17},{9,25},{17,1},{25,9},{2,18},{10... | collective-permute-start | bytes 92168 | tf_op jit(solution)/shard_map/ppermute | solution.py:19
  18.9 4.8 %collective-permute-start.8 = (bf16[24,640]{1,0:T(8,128)(2,1)S(1)}, bf16[24,640]{1,0:T(8,128)(2,1)S(1)}, u32[]{:S(2)}, u32[]{:S(2)}) collective-permute-start(bf16[24,640]{1,0:T(8,128)(2,1)S(1)} %get-tuple-element.61), channel_id=1, source_target_pairs={{0,8},{8,0},{16,24},{24,16},{1,9},{9,1},{17,25},{25,17},{2,10},{10... | collective-permute-start | bytes 92168 | tf_op jit(solution)/shard_map/ppermute | solution.py:19
  23.7 5.6 %collective-permute-start.12 = (bf16[4,24,512]{2,1,0:T(8,128)(2,1)S(1)}, bf16[4,24,512]{2,1,0:T(8,128)(2,1)S(1)}, u32[]{:S(2)}, u32[]{:S(2)}) collective-permute-start(bf16[4,24,512]{2,1,0:T(8,128)(2,1)S(1)} %get-tuple-element.63), channel_id=1, source_target_pairs={{0,6},{2,4},{4,2},{6,0},{1,7},{3,5},{5,3},{7,1},{8,14},{10,12},{12... | collective-permute-start | bytes 294920 | tf_op jit(solution)/shard_map/ppermute | solution.py:19
  25.3 5.1 %collective-permute-start.11 = (bf16[4,24,512]{2,1,0:T(8,128)(2,1)S(1)}, bf16[4,24,512]{2,1,0:T(8,128)(2,1)S(1)}, u32[]{:S(2)}, u32[]{:S(2)}) collective-permute-start(bf16[4,24,512]{2,1,0:T(8,128)(2,1)S(1)} %get-tuple-element.63), channel_id=1, source_target_pairs={{0,4},{2,6},{4,0},{6,2},{1,5},{3,7},{5,1},{7,3},{8,12},{10,14},{12... | collective-permute-start | bytes 294920 | tf_op jit(solution)/shard_map/ppermute | solution.py:19
  25.8 5.0 %collective-permute-start.9 = (bf16[4,24,512]{2,1,0:T(8,128)(2,1)S(1)}, bf16[4,24,512]{2,1,0:T(8,128)(2,1)S(1)}, u32[]{:S(2)}, u32[]{:S(2)}) collective-permute-start(bf16[4,24,512]{2,1,0:T(8,128)(2,1)S(1)} %get-tuple-element.63), channel_id=1, source_target_pairs={{0,2},{2,0},{4,6},{6,4},{1,3},{3,1},{5,7},{7,5},{8,10},{10,8},{12,... | collective-permute-start | bytes 294920 | tf_op jit(solution)/shard_map/ppermute | solution.py:19
  31.8 5.6 %collective-permute-start.14 = (bf16[24,2048]{1,0:T(8,128)(2,1)S(1)}, bf16[24,2048]{1,0:T(8,128)(2,1)S(1)}, u32[]{:S(2)}, u32[]{:S(2)}) collective-permute-start(bf16[24,2048]{1,0:T(8,128)(2,1)S(1)} %get-tuple-element.78), channel_id=1, source_target_pairs={{0,6},{2,4},{4,2},{6,0},{1,7},{3,5},{5,3},{7,1},{8,14},{10,12},{12... | collective-permute-start | bytes 294920 | tf_op jit(solution)/shard_map/ppermute | solution.py:19
  34.4 4.6 %collective-permute-start.15 = (bf16[24,2048]{1,0:T(8,128)(2,1)S(1)}, bf16[24,2048]{1,0:T(8,128)(2,1)S(1)}, u32[]{:S(2)}, u32[]{:S(2)}) collective-permute-start(bf16[24,2048]{1,0:T(8,128)(2,1)S(1)} %get-tuple-element.79), channel_id=1, source_target_pairs={{0,4},{2,6},{4,0},{6,2},{1,5},{3,7},{5,1},{7,3},{8,12},{10,14},{12... | collective-permute-start | bytes 294920 | tf_op jit(solution)/shard_map/ppermute | solution.py:19
  34.5 4.6 %collective-permute-start.16 = (bf16[24,2048]{1,0:T(8,128)(2,1)S(1)}, bf16[24,2048]{1,0:T(8,128)(2,1)S(1)}, u32[]{:S(2)}, u32[]{:S(2)}) collective-permute-start(bf16[24,2048]{1,0:T(8,128)(2,1)S(1)} %get-tuple-element.80), channel_id=1, source_target_pairs={{0,2},{2,0},{4,6},{6,4},{1,3},{3,1},{5,7},{7,5},{8,10},{10,8},{12,... | collective-permute-start | bytes 294920 | tf_op jit(solution)/shard_map/ppermute | solution.py:19
  39.2 1.3 %collective-permute-start.17 = (bf16[24,1024]{1,0:T(8,128)(2,1)S(1)}, bf16[24,1024]{1,0:T(8,128)(2,1)S(1)}, u32[]{:S(2)}, u32[]{:S(2)}) collective-permute-start(bf16[24,1024]{1,0:T(8,128)(2,1)S(1)} %get-tuple-element.83), channel_id=1, source_target_pairs={{0,1},{1,0},{2,3},{3,2},{4,5},{5,4},{6,7},{7,6},{8,9},{9,8},{10,11... | collective-permute-start | bytes 147464 | tf_op jit(solution)/shard_map/ppermute | solution.py:19
  40.6 5.8 %collective-permute-start.18 = (bf16[24,512]{1,0:T(8,128)(2,1)S(1)}, bf16[24,512]{1,0:T(8,128)(2,1)S(1)}, u32[]{:S(2)}, u32[]{:S(2)}) collective-permute-start(bf16[24,512]{1,0:T(8,128)(2,1)S(1)} %get-tuple-element.85), channel_id=1, source_target_pairs={{0,24},{8,16},{16,8},{24,0},{1,25},{9,17},{17,9},{25,1},{2,26},{10... | collective-permute-start | bytes 73736 | tf_op jit(solution)/shard_map/ppermute | solution.py:19
  42.4 4.8 %collective-permute-start.19 = (bf16[24,512]{1,0:T(8,128)(2,1)S(1)}, bf16[24,512]{1,0:T(8,128)(2,1)S(1)}, u32[]{:S(2)}, u32[]{:S(2)}) collective-permute-start(bf16[24,512]{1,0:T(8,128)(2,1)S(1)} %get-tuple-element.86), channel_id=1, source_target_pairs={{0,16},{8,24},{16,0},{24,8},{1,17},{9,25},{17,1},{25,9},{2,18},{10... | collective-permute-start | bytes 73736 | tf_op jit(solution)/shard_map/ppermute | solution.py:19
  43.3 4.1 %collective-permute-start.20 = (bf16[24,512]{1,0:T(8,128)(2,1)S(1)}, bf16[24,512]{1,0:T(8,128)(2,1)S(1)}, u32[]{:S(2)}, u32[]{:S(2)}) collective-permute-start(bf16[24,512]{1,0:T(8,128)(2,1)S(1)} %get-tuple-element.87), channel_id=1, source_target_pairs={{0,8},{8,0},{16,24},{24,16},{1,9},{9,1},{17,25},{25,17},{2,10},{10... | collective-permute-start | bytes 73736 | tf_op jit(solution)/shard_map/ppermute | solution.py:19
